TPU v7x, 32 devices: a whole 2x2x4 slice. The times are simulated.
32 devices in a mesh: dp: 8 (over z, y), seq: 4 (over x, core).
Axes of the slice: x: 2, y: 2, z: 4, core: 2. Of those that a mesh axis runs over, the one named last changes fastest.
Arguments:
- hidden_in: bfloat16 [4096, 768], P(('dp', 'seq')), may hold values from -6 to 6
- lengths: int32 [8, 4], P('dp'), may hold values from 1 to 509, as said below
- grad_out: bfloat16 [4096, 768], P(('dp', 'seq')), may hold values from -6 to 6
- attn_gain: bfloat16 [768], P(('dp', 'seq')), may hold values from 0.5 to 1.5
- attn_shift: bfloat16 [768], P(('dp', 'seq')), may hold values from -3 to 3
- mlp_gain: bfloat16 [768], P(('dp', 'seq')), may hold values from 0.5 to 1.5
- mlp_shift: bfloat16 [768], P(('dp', 'seq')), may hold values from -3 to 3
- qkv_weight: bfloat16 [768, 2304], P(('dp', 'seq')), may hold values from -0.21875 to 0.21875
- qkv_bias: bfloat16 [2304], P(('dp', 'seq')), may hold values from -3 to 3
- dense_weight: bfloat16 [768, 768], P(('dp', 'seq')), may hold values from -2.5 to 2.5
- dense_bias: bfloat16 [768], P(('dp', 'seq')), may hold values from -3 to 3
- up_weight: bfloat16 [768, 3072], P(('dp', 'seq')), may hold values from -0.21875 to 0.21875
- up_bias: bfloat16 [3072], P(('dp', 'seq')), may hold values from -3 to 3
- down_weight: bfloat16 [3072, 768], P(('dp', 'seq')), may hold values from -0.109375 to 0.109375
- down_bias: bfloat16 [768], P(('dp', 'seq')), may hold values from -3 to 3
Outputs:
- block_out: bfloat16 [4096, 768], P(('dp', 'seq'))
- grad_in: bfloat16 [4096, 768], P(('dp', 'seq'))
- attn_gain_grad: float32 [768], P(('dp', 'seq'))
- attn_shift_grad: float32 [768], P(('dp', 'seq'))
- mlp_gain_grad: float32 [768], P(('dp', 'seq'))
- mlp_shift_grad: float32 [768], P(('dp', 'seq'))
- qkv_weight_grad: float32 [768, 2304], P(('dp', 'seq'))
- qkv_bias_grad: float32 [2304], P(('dp', 'seq'))
- dense_weight_grad: float32 [768, 768], P(('dp', 'seq'))
- dense_bias_grad: float32 [768], P(('dp', 'seq'))
- up_weight_grad: float32 [768, 3072], P(('dp', 'seq'))
- up_bias_grad: float32 [3072], P(('dp', 'seq'))
- down_weight_grad: float32 [3072, 768], P(('dp', 'seq'))
- down_bias_grad: float32 [768], P(('dp', 'seq'))
Inputs may be any that keep to these rules, and one draw needn't show every extreme that they name: Each row's 4 lengths sum to 512, and one of them is more than 384; in one row all the others are 1.
All inputs are finite; a program needn't handle non-finite values.
Results may differ from a plain program's by a relative error of at most 0.028.
Values may be sent and summed in bfloat16 or wider, within the bound.
No kernel may reach another device: no remote copies, remote signals or barrier semaphores. Data moves between devices by JAX's collectives and lax.ppermute only.
A program may use at most 192 MiB of HBM per device.

v0:
```python
import jax
import jax.numpy as jnp
from jax import lax
from jax.sharding import PartitionSpec as P

HEADS = 12
HEAD_DIM = 64
ROT = 16


EPS = 1e-05
NEGATIVE = -1e30


def normalize(values, gain, shift):
    center = jnp.mean(values, axis=-1, keepdims=True)
    centered = values - center
    spread = jnp.mean(centered * centered, axis=-1, keepdims=True)
    inverse = lax.rsqrt(spread + EPS)
    unit = centered * inverse
    return (unit * gain + shift, unit, inverse)


def normalize_back(upstream, unit, inverse, gain):
    scaled = upstream * gain
    inner = (
        scaled
        - jnp.mean(scaled, axis=-1, keepdims=True)
        - unit * jnp.mean(scaled * unit, axis=-1, keepdims=True)
    )
    return (inverse * inner, jnp.sum(upstream * unit, axis=0), jnp.sum(upstream, axis=0))


def frequencies():
    steps = jnp.arange(ROT // 2, dtype=jnp.float32)
    return jnp.power(jnp.float32(10000.0), -(2.0 * steps) / ROT)


def rotate(values, cosine, sine, sign):
    half = ROT // 2
    first = values[..., :half]
    second = values[..., half:ROT]
    turned_one = first * cosine - sign * second * sine
    turned_two = second * cosine + sign * first * sine
    return jnp.concatenate([turned_one, turned_two, values[..., ROT:]], axis=-1)


def place(row_lengths, index):
    ends = jnp.cumsum(row_lengths)
    after = (index[:, None] >= ends[None, :]).astype(jnp.int32)
    segment = jnp.sum(after, axis=1)
    start = jnp.sum(after * row_lengths[None, :], axis=1)
    return (segment, index - start)


def regroup(values, outer_count, inner_count):
    total = values.shape[0]
    rest = values.shape[1:]
    blocks = values.reshape((outer_count, inner_count, total // (outer_count * inner_count)) + rest)
    return jnp.swapaxes(blocks, 0, 1).reshape((total,) + rest)


def collect(
    attn_gain,
    attn_shift,
    mlp_gain,
    mlp_shift,
    qkv_weight,
    qkv_bias,
    dense_weight,
    dense_bias,
    up_weight,
    up_bias,
    down_weight,
    down_bias,
):
    inner = (
        lax.all_gather(attn_gain, "seq", axis=0, tiled=True),
        lax.all_gather(attn_shift, "seq", axis=0, tiled=True),
        lax.all_gather(mlp_gain, "seq", axis=0, tiled=True),
        lax.all_gather(mlp_shift, "seq", axis=0, tiled=True),
        lax.all_gather(qkv_weight, "seq", axis=0, tiled=True),
        lax.all_gather(qkv_bias, "seq", axis=0, tiled=True),
        lax.all_gather(dense_weight, "seq", axis=0, tiled=True),
        lax.all_gather(dense_bias, "seq", axis=0, tiled=True),
        lax.all_gather(up_weight, "seq", axis=0, tiled=True),
        lax.all_gather(up_bias, "seq", axis=0, tiled=True),
        lax.all_gather(down_weight, "seq", axis=0, tiled=True),
        lax.all_gather(down_bias, "seq", axis=0, tiled=True),
    )
    return (
        lax.all_gather(inner[0], "dp", axis=0, tiled=True),
        lax.all_gather(inner[1], "dp", axis=0, tiled=True),
        lax.all_gather(inner[2], "dp", axis=0, tiled=True),
        lax.all_gather(inner[3], "dp", axis=0, tiled=True),
        lax.all_gather(inner[4], "dp", axis=0, tiled=True),
        lax.all_gather(inner[5], "dp", axis=0, tiled=True),
        lax.all_gather(inner[6], "dp", axis=0, tiled=True),
        lax.all_gather(inner[7], "dp", axis=0, tiled=True),
        lax.all_gather(inner[8], "dp", axis=0, tiled=True),
        lax.all_gather(inner[9], "dp", axis=0, tiled=True),
        lax.all_gather(inner[10], "dp", axis=0, tiled=True),
        lax.all_gather(inner[11], "dp", axis=0, tiled=True),
    )


def per_device(
    hidden_in,
    lengths,
    grad_out,
    attn_gain,
    attn_shift,
    mlp_gain,
    mlp_shift,
    qkv_weight,
    qkv_bias,
    dense_weight,
    dense_bias,
    up_weight,
    up_bias,
    down_weight,
    down_bias,
):
    rows = hidden_in.shape[0]
    width = hidden_in.shape[1]
    group = rows * lax.axis_size("seq")
    scale = HEAD_DIM ** (-0.5)
    piece_index = lax.axis_index("seq")
    row_lengths = lengths[0]
    query_index = piece_index * rows + jnp.arange(rows, dtype=jnp.int32)
    last_query = piece_index * rows + rows - 1
    query_segment, query_position = place(row_lengths, query_index)
    angles = query_position.astype(jnp.float32)[:, None] * frequencies()[None, :]
    cosine = jnp.cos(angles)[:, None, :]
    sine = jnp.sin(angles)[:, None, :]
    params = collect(
        attn_gain,
        attn_shift,
        mlp_gain,
        mlp_shift,
        qkv_weight,
        qkv_bias,
        dense_weight,
        dense_bias,
        up_weight,
        up_bias,
        down_weight,
        down_bias,
    )
    full_attn_gain = params[0].astype(jnp.float32)
    full_attn_shift = params[1].astype(jnp.float32)
    full_mlp_gain = params[2].astype(jnp.float32)
    full_mlp_shift = params[3].astype(jnp.float32)
    hidden = hidden_in.astype(jnp.float32)
    attn_norm, attn_unit, attn_inverse = normalize(hidden, full_attn_gain, full_attn_shift)
    attn_in = attn_norm.astype(jnp.bfloat16)
    joined = jnp.dot(attn_in, params[4], preferred_element_type=jnp.float32) + params[5].astype(
        jnp.float32
    )
    joined = joined.reshape(rows, 3, HEADS, HEAD_DIM)
    queries = rotate(joined[:, 0], cosine, sine, 1.0).astype(jnp.bfloat16)
    keys_flat = rotate(joined[:, 1], cosine, sine, 1.0).astype(jnp.bfloat16).reshape(rows, width)
    values_flat = joined[:, 2].astype(jnp.bfloat16).reshape(rows, width)

    def update(carry, key_block, value_block, key_index):
        run_max, run_sum, totals = carry
        key_segment, unused = place(row_lengths, key_index)
        scores = (
            jnp.einsum("thd,nhd->htn", queries, key_block, preferred_element_type=jnp.float32)
            * scale
        )
        allowed = (query_segment[:, None] == key_segment[None, :]) & (
            key_index[None, :] <= query_index[:, None]
        )
        masked = jnp.where(allowed[None], scores, NEGATIVE)
        new_max = jnp.maximum(run_max, jnp.max(masked, axis=-1))
        weights = jnp.where(allowed[None], jnp.exp(masked - new_max[..., None]), 0.0)
        factor = jnp.exp(run_max - new_max)
        run_sum = run_sum * factor + jnp.sum(weights, axis=-1)
        totals = totals * factor[..., None] + jnp.einsum(
            "htn,nhd->htd",
            weights.astype(jnp.bfloat16),
            value_block,
            preferred_element_type=jnp.float32,
        )
        return (new_max, run_sum, totals)

    initial = (
        jnp.full((HEADS, rows), NEGATIVE, jnp.float32),
        jnp.zeros((HEADS, rows), jnp.float32),
        jnp.zeros((HEADS, rows, HEAD_DIM), jnp.float32),
    )
    carry = initial
    start = jnp.int32(0)
    key_piece = lax.all_gather(keys_flat, "seq", axis=0, tiled=True)
    value_piece = lax.all_gather(values_flat, "seq", axis=0, tiled=True)
    count = key_piece.shape[0]
    step = min(count, 512)
    for offset in range(0, count, step):
        size = min(step, count - offset)
        key_block = key_piece[offset : offset + size].reshape(size, HEADS, HEAD_DIM)
        value_block = value_piece[offset : offset + size].reshape(size, HEADS, HEAD_DIM)
        key_index = start + offset + jnp.arange(size, dtype=jnp.int32)
        carry = lax.cond(
            start + offset > last_query,
            lambda held: held,
            lambda held: update(held, key_block, value_block, key_index),
            carry,
        )
    run_max, run_sum, totals = carry
    logsum = run_max + jnp.log(run_sum)
    attended_heads = jnp.transpose(totals / run_sum[..., None], (1, 0, 2))
    attended_full = attended_heads.reshape(rows, width)
    attended = attended_full.astype(jnp.bfloat16)
    attn_out = jnp.dot(attended, params[6], preferred_element_type=jnp.float32) + params[7].astype(
        jnp.float32
    )
    mlp_norm, mlp_unit, mlp_inverse = normalize(hidden, full_mlp_gain, full_mlp_shift)
    mlp_in = mlp_norm.astype(jnp.bfloat16)
    upper = jnp.dot(mlp_in, params[8], preferred_element_type=jnp.float32) + params[9].astype(
        jnp.float32
    )
    act = jax.nn.gelu(upper, approximate=False).astype(jnp.bfloat16)
    mlp_out = jnp.dot(act, params[10], preferred_element_type=jnp.float32) + params[11].astype(
        jnp.float32
    )
    block_out = (hidden + attn_out + mlp_out).astype(jnp.bfloat16)
    back_attn_gain = params[0].astype(jnp.float32)
    back_mlp_gain = params[2].astype(jnp.float32)
    upstream = grad_out.astype(jnp.float32)
    dense_weight_grad = jnp.einsum(
        "td,te->de", attended, grad_out, preferred_element_type=jnp.float32
    )
    down_weight_grad = jnp.einsum("tf,td->fd", act, grad_out, preferred_element_type=jnp.float32)
    bias_sum = jnp.sum(upstream, axis=0)
    d_attended = jnp.einsum(
        "td,ed->te", grad_out, params[6], preferred_element_type=jnp.float32
    ).astype(jnp.bfloat16)
    d_act = jnp.einsum("td,fd->tf", grad_out, params[10], preferred_element_type=jnp.float32)
    gelu_pull = jax.vjp(lambda value: jax.nn.gelu(value, approximate=False), upper)[1]
    d_up = gelu_pull(d_act)[0].astype(jnp.bfloat16)
    up_weight_grad = jnp.einsum("td,tf->df", mlp_in, d_up, preferred_element_type=jnp.float32)
    up_bias_grad = jnp.sum(d_up.astype(jnp.float32), axis=0)
    d_mlp_in = jnp.einsum("tf,df->td", d_up, params[8], preferred_element_type=jnp.float32)
    d_heads = d_attended.reshape(rows, HEADS, HEAD_DIM)
    delta = jnp.transpose(jnp.sum(d_heads.astype(jnp.float32) * attended_heads, axis=-1), (1, 0))
    keys_all, values_all = (
        lax.all_gather(keys_flat, "seq", axis=0, tiled=True),
        lax.all_gather(values_flat, "seq", axis=0, tiled=True),
    )
    block = min(group, 512)
    count = group // block
    key_blocks = keys_all.reshape(count, block, HEADS, HEAD_DIM)
    value_blocks = values_all.reshape(count, block, HEADS, HEAD_DIM)
    block_starts = jnp.arange(count, dtype=jnp.int32) * block

    def pair_terms(
        query_block,
        d_block,
        logsum_block,
        delta_block,
        query_idx,
        query_seg,
        key_block,
        value_block,
        key_index,
        key_segment,
    ):
        scores = (
            jnp.einsum("thd,nhd->htn", query_block, key_block, preferred_element_type=jnp.float32)
            * scale
        )
        allowed = (query_seg[:, None] == key_segment[None, :]) & (
            key_index[None, :] <= query_idx[:, None]
        )
        probs = jnp.where(allowed[None], jnp.exp(scores - logsum_block[..., None]), 0.0)
        d_probs = jnp.einsum(
            "thd,nhd->htn", d_block, value_block, preferred_element_type=jnp.float32
        )
        d_scores = (probs * (d_probs - delta_block[..., None])).astype(jnp.bfloat16)
        return (probs, d_scores)

    def back_step(d_queries, inputs):
        key_block, value_block, block_start = inputs

        def work(held):
            key_index = block_start + jnp.arange(block, dtype=jnp.int32)
            key_segment, unused = place(row_lengths, key_index)
            probs, d_scores = pair_terms(
                queries,
                d_heads,
                logsum,
                delta,
                query_index,
                query_segment,
                key_block,
                value_block,
                key_index,
                key_segment,
            )
            held = held + scale * jnp.einsum(
                "htn,nhd->thd", d_scores, key_block, preferred_element_type=jnp.float32
            )
            d_keys = scale * jnp.einsum(
                "htn,thd->nhd", d_scores, queries, preferred_element_type=jnp.float32
            )
            d_values = jnp.einsum(
                "htn,thd->nhd",
                probs.astype(jnp.bfloat16),
                d_heads,
                preferred_element_type=jnp.float32,
            )
            return (
                held,
                jnp.concatenate(
                    [d_keys.reshape(block, width), d_values.reshape(block, width)], axis=1
                ),
            )

        def skip(held):
            return (held, jnp.zeros((block, 2 * width), jnp.float32))

        return lax.cond(block_start > last_query, skip, work, d_queries)

    d_queries, key_terms = lax.scan(
        back_step,
        jnp.zeros((rows, HEADS, HEAD_DIM), jnp.float32),
        (key_blocks, value_blocks, block_starts),
    )
    own_keys = lax.psum_scatter(
        key_terms.reshape(group, 2 * width).astype(jnp.bfloat16),
        "seq",
        scatter_dimension=0,
        tiled=True,
    ).astype(jnp.float32)
    d_keys_own = own_keys[:, :width].reshape(rows, HEADS, HEAD_DIM)
    d_values_own = own_keys[:, width:].reshape(rows, HEADS, HEAD_DIM)
    d_joined = jnp.stack(
        [
            rotate(d_queries, cosine, sine, -1.0),
            rotate(d_keys_own, cosine, sine, -1.0),
            d_values_own,
        ],
        axis=1,
    )
    d_joined = d_joined.reshape(rows, 3 * width).astype(jnp.bfloat16)
    qkv_weight_grad = jnp.einsum("td,te->de", attn_in, d_joined, preferred_element_type=jnp.float32)
    qkv_bias_grad = jnp.sum(d_joined.astype(jnp.float32), axis=0)
    d_attn_in = jnp.einsum("te,de->td", d_joined, params[4], preferred_element_type=jnp.float32)
    attn_back, attn_gain_grad, attn_shift_grad = normalize_back(
        d_attn_in, attn_unit, attn_inverse, back_attn_gain
    )
    mlp_back, mlp_gain_grad, mlp_shift_grad = normalize_back(
        d_mlp_in, mlp_unit, mlp_inverse, back_mlp_gain
    )
    grad_in = (upstream + attn_back + mlp_back).astype(jnp.bfloat16)
    outer_count = lax.axis_size("dp")
    inner_count = lax.axis_size("seq")
    moved = [
        regroup(item, outer_count, inner_count)
        for item in (
            attn_gain_grad,
            attn_shift_grad,
            mlp_gain_grad,
            mlp_shift_grad,
            qkv_weight_grad,
            qkv_bias_grad,
            dense_weight_grad,
            bias_sum,
            up_weight_grad,
            up_bias_grad,
            down_weight_grad,
            bias_sum,
        )
    ]
    partial_sums = (
        lax.psum_scatter(
            moved[0].astype(jnp.bfloat16), "seq", scatter_dimension=0, tiled=True
        ).astype(jnp.float32),
        lax.psum_scatter(
            moved[1].astype(jnp.bfloat16), "seq", scatter_dimension=0, tiled=True
        ).astype(jnp.float32),
        lax.psum_scatter(
            moved[2].astype(jnp.bfloat16), "seq", scatter_dimension=0, tiled=True
        ).astype(jnp.float32),
        lax.psum_scatter(
            moved[3].astype(jnp.bfloat16), "seq", scatter_dimension=0, tiled=True
        ).astype(jnp.float32),
        lax.psum_scatter(
            moved[4].astype(jnp.bfloat16), "seq", scatter_dimension=0, tiled=True
        ).astype(jnp.float32),
        lax.psum_scatter(
            moved[5].astype(jnp.bfloat16), "seq", scatter_dimension=0, tiled=True
        ).astype(jnp.float32),
        lax.psum_scatter(
            moved[6].astype(jnp.bfloat16), "seq", scatter_dimension=0, tiled=True
        ).astype(jnp.float32),
        lax.psum_scatter(
            moved[7].astype(jnp.bfloat16), "seq", scatter_dimension=0, tiled=True
        ).astype(jnp.float32),
        lax.psum_scatter(
            moved[8].astype(jnp.bfloat16), "seq", scatter_dimension=0, tiled=True
        ).astype(jnp.float32),
        lax.psum_scatter(
            moved[9].astype(jnp.bfloat16), "seq", scatter_dimension=0, tiled=True
        ).astype(jnp.float32),
        lax.psum_scatter(
            moved[10].astype(jnp.bfloat16), "seq", scatter_dimension=0, tiled=True
        ).astype(jnp.float32),
        lax.psum_scatter(
            moved[11].astype(jnp.bfloat16), "seq", scatter_dimension=0, tiled=True
        ).astype(jnp.float32),
    )
    owned = (
        lax.psum_scatter(
            partial_sums[0].astype(jnp.bfloat16), "dp", scatter_dimension=0, tiled=True
        ).astype(jnp.float32),
        lax.psum_scatter(
            partial_sums[1].astype(jnp.bfloat16), "dp", scatter_dimension=0, tiled=True
        ).astype(jnp.float32),
        lax.psum_scatter(
            partial_sums[2].astype(jnp.bfloat16), "dp", scatter_dimension=0, tiled=True
        ).astype(jnp.float32),
        lax.psum_scatter(
            partial_sums[3].astype(jnp.bfloat16), "dp", scatter_dimension=0, tiled=True
        ).astype(jnp.float32),
        lax.psum_scatter(
            partial_sums[4].astype(jnp.bfloat16), "dp", scatter_dimension=0, tiled=True
        ).astype(jnp.float32),
        lax.psum_scatter(
            partial_sums[5].astype(jnp.bfloat16), "dp", scatter_dimension=0, tiled=True
        ).astype(jnp.float32),
        lax.psum_scatter(
            partial_sums[6].astype(jnp.bfloat16), "dp", scatter_dimension=0, tiled=True
        ).astype(jnp.float32),
        lax.psum_scatter(
            partial_sums[7].astype(jnp.bfloat16), "dp", scatter_dimension=0, tiled=True
        ).astype(jnp.float32),
        lax.psum_scatter(
            partial_sums[8].astype(jnp.bfloat16), "dp", scatter_dimension=0, tiled=True
        ).astype(jnp.float32),
        lax.psum_scatter(
            partial_sums[9].astype(jnp.bfloat16), "dp", scatter_dimension=0, tiled=True
        ).astype(jnp.float32),
        lax.psum_scatter(
            partial_sums[10].astype(jnp.bfloat16), "dp", scatter_dimension=0, tiled=True
        ).astype(jnp.float32),
        lax.psum_scatter(
            partial_sums[11].astype(jnp.bfloat16), "dp", scatter_dimension=0, tiled=True
        ).astype(jnp.float32),
    )
    return (
        block_out,
        grad_in,
        owned[0],
        owned[1],
        owned[2],
        owned[3],
        owned[4],
        owned[5],
        owned[6],
        owned[7],
        owned[8],
        owned[9],
        owned[10],
        owned[11],
    )


def solution(mesh):
    in_specs = (
        P(("dp", "seq"), None),
        P("dp", None),
        P(("dp", "seq"), None),
        P(("dp", "seq")),
        P(("dp", "seq")),
        P(("dp", "seq")),
        P(("dp", "seq")),
        P(("dp", "seq"), None),
        P(("dp", "seq")),
        P(("dp", "seq"), None),
        P(("dp", "seq")),
        P(("dp", "seq"), None),
        P(("dp", "seq")),
        P(("dp", "seq"), None),
        P(("dp", "seq")),
    )
    out_specs = (
        P(("dp", "seq"), None),
        P(("dp", "seq"), None),
        P(("dp", "seq")),
        P(("dp", "seq")),
        P(("dp", "seq")),
        P(("dp", "seq")),
        P(("dp", "seq"), None),
        P(("dp", "seq")),
        P(("dp", "seq"), None),
        P(("dp", "seq")),
        P(("dp", "seq"), None),
        P(("dp", "seq")),
        P(("dp", "seq"), None),
        P(("dp", "seq")),
    )
    return jax.shard_map(
        per_device, mesh=mesh, in_specs=in_specs, out_specs=out_specs, check_vma=False
    )
```

profile of v0, /device:TPU:0, one launch (start us, length us, event | category | flops | bytes accessed | tf_op | source)
XLA Modules:
  0.0 753.8 jit_solution(7452630809966027847)
XLA Ops:
  7.2 8.4 %all_gather.90 = bf16[96,768]{1,0:T(8,128)(2,1)} all-gather(bf16[24,768]{1,0:T(8,128)(2,1)} %param.28), channel_id=1, replica_groups=mesh['dp'=8,'seq'=4] {'seq'}, dimensions={0}, use_global_device_ids=true | all-gather | bytes 184320 | tf_op jit(solution)/shard_map/all_gather | solution.py:84
  15.7 8.0 %all_gather.84 = bf16[96,2304]{1,0:T(8,128)(2,1)} all-gather(bf16[24,2304]{1,0:T(8,128)(2,1)} %param.26), channel_id=1, replica_groups=mesh['dp'=8,'seq'=4] {'seq'}, dimensions={0}, use_global_device_ids=true | all-gather | bytes 552960 | tf_op jit(solution)/shard_map/all_gather | solution.py:82
  23.8 9.6 %all_gather.98 = bf16[96,3072]{1,0:T(8,128)(2,1)} all-gather(bf16[24,3072]{1,0:T(8,128)(2,1)} %param.30), channel_id=1, replica_groups=mesh['dp'=8,'seq'=4] {'seq'}, dimensions={0}, use_global_device_ids=true | all-gather | bytes 737280 | tf_op jit(solution)/shard_map/all_gather | solution.py:86
  33.5 8.1 %all_gather.102 = bf16[384,768]{1,0:T(8,128)(2,1)} all-gather(bf16[96,768]{1,0:T(8,128)(2,1)S(1)} %copy-done.12), channel_id=1, replica_groups=mesh['dp'=8,'seq'=4] {'seq'}, dimensions={0}, use_global_device_ids=true | all-gather | bytes 737280 | tf_op jit(solution)/shard_map/all_gather | solution.py:88
  47.1 7.2 all-reduce.32
  55.3 37.7 %all-reduce.30 = (bf16[768]{0:T(1024)(128)(2,1)}, bf16[768]{0:T(1024)(128)(2,1)}, bf16[2304]{0:T(1024)(128)(2,1)S(1)}, bf16[768]{0:T(1024)(128)(2,1)S(1)}, bf16[768]{0:T(1024)(128)(2,1)S(1)}) all-reduce(bf16[768]{0:T(1024)(128)(2,1)S(1)} %dynamic-update-slice.11, ...), channel_id=1, replica_groups=mesh['dp'=8,'seq'=4] {'dp'}, use_global_device_ids=true, to_apply=%add.11 | all-reduce | flops 5376 | bytes 21504
  94.5 1.8 convolution_convert_fusion.4
  97.1 26.8 %all-gather.6.cloned.1.call-done = bf16[768,2304]{1,0:T(8,128)(2,1)} async-done(((bf16[96,2304]{1,0:T(8,128)(2,1)}), bf16[768,2304]{1,0:T(8,128)(2,1)}) %all-gather.6.cloned.1.call-update) | async-done | bytes 3538960 | tf_op jit(solution)/shard_map/all_gather | solution.py:96
  123.9 2.7 convolution_add_fusion
  127.3 8.6 %all_gather.88 = bf16[512,768]{0,1:T(8,128)(2,1)S(1)} all-gather(bf16[128,768]{0,1:T(8,128)(2,1)S(1)} %bitcast.142), channel_id=1, replica_groups=mesh['dp'=8,'seq'=4] {'seq'}, dimensions={0}, use_global_device_ids=true | all-gather | bytes 983040 | tf_op jit(solution)/shard_map/all_gather | solution.py:195
  135.9 8.9 %all_gather.89 = bf16[512,768]{0,1:T(8,128)(2,1)S(1)} all-gather(bf16[128,768]{0,1:T(8,128)(2,1)S(1)} %bitcast.141), channel_id=1, replica_groups=mesh['dp'=8,'seq'=4] {'seq'}, dimensions={0}, use_global_device_ids=true | all-gather | bytes 983040 | tf_op jit(solution)/shard_map/all_gather | solution.py:196
  144.8 3.3 conditional.2
  148.8 7.7 %conditional.3 = (bf16[512,1536]{0,1:T(8,128)(2,1)S(1)}, f32[128,12,64]{0,2,1:T(8,128)S(1)}) conditional(s32[]{:T(128)} %convert_element_type.334, (s32[128]{0:T(128)}, s32[4]{0:T(128)S(1)}, s32[128]{0:T(128)}, bf16[128,12,64]{0,2,1:T(8,128)(2,1)S(1)}, bf16[512,12,64]{0,2,1:T(8,128)(2,1)S(1)}, /*index=5*/f32[12,128]{1,0:T(8,128)S(1)}, ...), branch_computations={%region_12.15_spmd.clone, %region_15.16_spmd.clone} | conditional | flops 515513344 | bytes 35632280 | solution.py:323
  148.8 2.3 fusion.77
  151.5 2.9 multiply_convert_fusion
  156.5 1.6 copy.94
  158.8 26.5 %all-gather = bf16[8,1,384]{2,1,0:T(2,128)(2,1)S(1)} all-gather(bf16[1,1,384]{2,1,0:T(2,128)(2,1)S(1)} %reshape.484), channel_id=1, replica_groups=mesh['dp'=8,'seq'=4] {'dp'}, dimensions={0}, use_global_device_ids=true | all-gather | bytes 6912 | tf_op jit(solution)/shard_map/all_gather | solution.py:101
  186.5 1.1 copy.86
  188.0 16.8 %all-gather.10.cloned.1.call-done = bf16[768,3072]{1,0:T(8,128)(2,1)} async-done(((bf16[96,3072]{1,0:T(8,128)(2,1)}), bf16[768,3072]{1,0:T(8,128)(2,1)}) %all-gather.10.cloned.1.call-update) | async-done | bytes 4718608 | tf_op jit(solution)/shard_map/all_gather | solution.py:100
  204.8 3.2 convolution_add_fusion.1
  207.9 76.9 %all-gather.12.cloned.1.call-done = bf16[3072,768]{1,0:T(8,128)(2,1)} async-done(((bf16[384,768]{1,0:T(8,128)(2,1)}), bf16[3072,768]{1,0:T(8,128)(2,1)}) %all-gather.12.cloned.1.call-update) | async-done | bytes 4718608 | tf_op jit(solution)/shard_map/all_gather | solution.py:102
  284.8 8.8 %fusion.72 = (bf16[3072]{0:T(1024)(128)(2,1)}, bf16[128,3072]{1,0:T(8,128)(2,1)S(1)}, f32[128,3072]{1,0:T(8,128)}) fusion(f32[128,3072]{1,0:T(8,128)S(1)} %convolution_add_fusion.1, bf16[128,768]{1,0:T(8,128)(2,1)S(1)} %copy-done.2, bf16[3072,768]{1,0:T(8,128)(2,1)} %all-gather.12.cloned.1.call-done), kind=kOutput, calls=%fused_computation.144 | convolution fusion | flops 632681472 | bytes 8853504 | tf_op jit(solution)/shard_map/td,fd->tf/dot_general | solution.py:239
  293.6 1.7 fusion.79
  295.3 18.2 %reduce-scatter.28.cloned.1.call-done = bf16[128,1536]{1,0:T(8,128)(2,1)} async-done(((bf16[512,1536]{1,0:T(8,128)(2,1)}), bf16[128,1536]{1,0:T(8,128)(2,1)}) %reduce-scatter.28.cloned.1.call-update) | async-done | bytes 393232
  318.1 1.9 fusion.74
  320.0 3.5 fusion.78
  323.5 1.6 fusion.59
  326.2 1.1 fusion.25
  327.3 2.0 copy.84
  330.4 2.2 convolution_convert_fusion.1
  332.6 2.6 copy.88
  335.4 6.5 reduce-scatter.16.cloned.1.call-done
  342.2 1.6 multiply_convert_fusion.1
  343.7 1.4 convolution_convert_fusion
  345.2 2.5 copy.90
  347.9 37.0 %reduce-scatter.12.cloned.1.call-done = bf16[192,2304]{1,0:T(8,128)(2,1)} async-done(((bf16[768,2304]{1,0:T(8,128)(2,1)}), bf16[192,2304]{1,0:T(8,128)(2,1)}) %reduce-scatter.12.cloned.1.call-update) | async-done | bytes 884752 | tf_op jit(solution)/shard_map/reduce_scatter | solution.py:389
  384.9 50.5 %reduce-scatter.20.cloned.1.call-done = bf16[192,3072]{1,0:T(8,128)(2,1)} async-done(((bf16[768,3072]{1,0:T(8,128)(2,1)}), bf16[192,3072]{1,0:T(8,128)(2,1)}) %reduce-scatter.20.cloned.1.call-update) | async-done | bytes 1179664 | tf_op jit(solution)/shard_map/reduce_scatter | solution.py:401
  440.4 57.1 %reduce-scatter.18.cloned.1.call-done = bf16[24,768]{1,0:T(8,128)(2,1)} async-done(((bf16[192,768]{1,0:T(8,128)(2,1)}), bf16[24,768]{1,0:T(8,128)(2,1)}) %reduce-scatter.18.cloned.1.call-update) | async-done | bytes 36880 | tf_op jit(solution)/shard_map/reduce_scatter | solution.py:433
  497.5 1.4 convert_element_type.374
  500.0 10.3 %all-reduce.31 = (bf16[96]{0:T(256)(128)(2,1)S(1)}, bf16[96]{0:T(256)(128)(2,1)S(1)}, bf16[768]{0:T(1024)(128)(2,1)S(1)}, bf16[768]{0:T(1024)(128)(2,1)S(1)}, bf...) all-reduce(bf16[96]{0:T(256)(128)(2,1)S(1)} %dynamic-update-slice.1, ...), channel_id=1, replica_groups=mesh['dp'=8,'seq'=4] {'seq'}, use_global_device_ids=true, to_apply=%add.13 | all-reduce | flops 9408 | bytes 37632
  511.2 35.1 %all-reduce.29 = (bf16[768]{0:T(1024)(128)(2,1)S(1)}, bf16[768]{0:T(1024)(128)(2,1)S(1)}, bf16[192]{0:T(256)(128)(2,1)S(1)}, bf16[192]{0:T(256)(128)(2,1)S(1)}, ...) all-reduce(bf16[768]{0:T(1024)(128)(2,1)S(1)} %dynamic-update-slice, ...), channel_id=1, replica_groups=mesh['dp'=8,'seq'=4] {'dp'}, use_global_device_ids=true, to_apply=%add.14 | all-reduce | flops 3840 | bytes 15360
  550.9 3.2 convolution_add_fusion.3
  555.3 56.4 %reduce-scatter.14.cloned.1.call-done = bf16[24,2304]{1,0:T(8,128)(2,1)} async-done(((bf16[192,2304]{1,0:T(8,128)(2,1)}), bf16[24,2304]{1,0:T(8,128)(2,1)}) %reduce-scatter.14.cloned.1.call-update) | async-done | bytes 110608 | tf_op jit(solution)/shard_map/reduce_scatter | solution.py:427
  611.7 1.6 convert_element_type.366
  613.3 65.0 %reduce-scatter.22.cloned.1.call-done = bf16[24,3072]{1,0:T(8,128)(2,1)} async-done(((bf16[192,3072]{1,0:T(8,128)(2,1)}), bf16[24,3072]{1,0:T(8,128)(2,1)}) %reduce-scatter.22.cloned.1.call-update) | async-done | bytes 147472 | tf_op jit(solution)/shard_map/reduce_scatter | solution.py:439
  678.3 1.6 convert_element_type.383
  679.9 65.2 %reduce-scatter.26.cloned.1.call-done = bf16[96,768]{1,0:T(8,128)(2,1)} async-done(((bf16[768,768]{1,0:T(8,128)(2,1)}), bf16[96,768]{1,0:T(8,128)(2,1)}) %reduce-scatter.26.cloned.1.call-update) | async-done | bytes 147472 | tf_op jit(solution)/shard_map/reduce_scatter | solution.py:445
  745.2 1.6 convert_element_type.392
  (271 shorter events, 31.0 us)
Async XLA Ops:
  7.2 26.4 %copy-start.12 = (bf16[96,768]{1,0:T(8,128)(2,1)S(1)}, bf16[96,768]{1,0:T(8,128)(2,1)}, u32[]{:S(2)}) copy-start(bf16[96,768]{1,0:T(8,128)(2,1)} %param.32) | copy-start | bytes 442372
  7.2 87.3 %all-gather.8.cloned.1.call-start = ((), (), s32[]{:S(2)}) async-start(), calls=%async_computation.10 | async-start | bytes 1327104 | tf_op jit(solution)/shard_map/all_gather | solution.py:98
  15.7 108.2 %all-gather.6.cloned.1.call-start = ((), (), s32[]{:S(2)}) async-start(), calls=%async_computation.9 | async-start | bytes 3981312 | tf_op jit(solution)/shard_map/all_gather | solution.py:96
  23.7 21.9 %copy-start.46 = (bf16[24]{0:T(256)(128)(2,1)S(1)}, bf16[24]{0:T(256)(128)(2,1)}, u32[]{:S(2)}) copy-start(bf16[24]{0:T(256)(128)(2,1)} %param.22) | copy-start | bytes 148
  23.7 22.2 %copy-start.47 = (bf16[24]{0:T(256)(128)(2,1)S(1)}, bf16[24]{0:T(256)(128)(2,1)}, u32[]{:S(2)}) copy-start(bf16[24]{0:T(256)(128)(2,1)} %param.25) | copy-start | bytes 148
  23.7 22.4 %copy-start.48 = (bf16[24]{0:T(256)(128)(2,1)S(1)}, bf16[24]{0:T(256)(128)(2,1)}, u32[]{:S(2)}) copy-start(bf16[24]{0:T(256)(128)(2,1)} %param.23) | copy-start | bytes 148
  23.7 22.7 %copy-start.49 = (bf16[24]{0:T(256)(128)(2,1)S(1)}, bf16[24]{0:T(256)(128)(2,1)}, u32[]{:S(2)}) copy-start(bf16[24]{0:T(256)(128)(2,1)} %param.24) | copy-start | bytes 148
  23.7 22.9 %copy-start.50 = (bf16[96]{0:T(256)(128)(2,1)S(1)}, bf16[96]{0:T(256)(128)(2,1)}, u32[]{:S(2)}) copy-start(bf16[96]{0:T(256)(128)(2,1)} %param.31) | copy-start | bytes 580
  23.7 23.1 %copy-start.51 = (bf16[72]{0:T(256)(128)(2,1)S(1)}, bf16[72]{0:T(256)(128)(2,1)}, u32[]{:S(2)}) copy-start(bf16[72]{0:T(256)(128)(2,1)} %param.27) | copy-start | bytes 436
  23.7 69.4 %copy-start.44 = (s32[1,4]{1,0:T(1,128)S(1)}, s32[1,4]{1,0:T(1,128)}, u32[]{:S(2)}) copy-start(s32[1,4]{1,0:T(1,128)} %param.20) | copy-start | bytes 52
  23.7 69.6 %copy-start.1 = (bf16[128,768]{1,0:T(8,128)(2,1)S(1)}, bf16[128,768]{1,0:T(8,128)(2,1)}, u32[]{:S(2)}) copy-start(bf16[128,768]{1,0:T(8,128)(2,1)} %param.19) | copy-start | bytes 589828
  23.8 70.7 %copy-start.2 = (bf16[128,768]{1,0:T(8,128)(2,1)S(1)}, bf16[128,768]{1,0:T(8,128)(2,1)}, u32[]{:S(2)}) copy-start(bf16[128,768]{1,0:T(8,128)(2,1)} %param.21) | copy-start | bytes 589828
  23.8 181.0 %all-gather.10.cloned.1.call-start = ((), (), s32[]{:S(2)}) async-start(), calls=%async_computation.11 | async-start | bytes 5308416 | tf_op jit(solution)/shard_map/all_gather | solution.py:100
  33.5 251.3 %all-gather.12.cloned.1.call-start = ((), (), s32[]{:S(2)}) async-start(), calls=%async_computation.12 | async-start | bytes 5308416 | tf_op jit(solution)/shard_map/all_gather | solution.py:102
  41.7 271.8 %reduce-scatter.28.cloned.1.call-start = ((), (), s32[]{:S(2)}) async-start(), calls=%async_computation.21 | async-start | bytes 1966080
  93.1 33.5 %copy-start.13 = (f32[768]{0:T(1024)}, f32[768]{0:T(1024)S(1)}, u32[]{:S(2)}) copy-start(f32[768]{0:T(1024)S(1)} %convert_element_type.316) | copy-start | bytes 9220
  93.1 33.5 %copy-start.16 = (f32[768]{0:T(1024)}, f32[768]{0:T(1024)S(1)}, u32[]{:S(2)}) copy-start(f32[768]{0:T(1024)S(1)} %convert_element_type.317) | copy-start | bytes 9220
  93.3 51.5 %copy-start.31 = (s32[128]{0:T(128)}, s32[128]{0:T(128)S(1)}, u32[]{:S(2)}) copy-start(s32[128]{0:T(128)S(1)} %iota_add_fusion) | copy-start | bytes 1540
  93.4 51.4 %copy-start.33 = (s32[128]{0:T(128)}, s32[128]{0:T(128)S(1)}, u32[]{:S(2)}) copy-start(s32[128]{0:T(128)S(1)} %get-tuple-element.225) | copy-start | bytes 1540
  93.5 33.1 %copy-start.20 = (f32[128]{0:T(128)}, f32[128]{0:T(128)S(1)}, u32[]{:S(2)}) copy-start(f32[128]{0:T(128)S(1)} %broadcast_multiply_fusion.5) | copy-start | bytes 1540
  93.7 32.9 %copy-start.22 = (f32[128]{0:T(128)}, f32[128]{0:T(128)S(1)}, u32[]{:S(2)}) copy-start(f32[128]{0:T(128)S(1)} %add_rsqrt_fusion) | copy-start | bytes 1540
  94.5 32.7 %copy-start.18 = (f32[128,8]{0,1:T(8,128)}, f32[128,8]{0,1:T(8,128)S(1)}, u32[]{:S(2)}) copy-start(f32[128,8]{0,1:T(8,128)S(1)} %get-tuple-element.283) | copy-start | bytes 12292
  158.1 27.9 %copy-start.10 = (f32[12,128,64]{1,2,0:T(8,128)S(1)}, f32[12,128,64]{1,2,0:T(8,128)}, u32[]{:S(2)}) copy-start(f32[12,128,64]{1,2,0:T(8,128)} %copy-done.9) | copy-start | bytes 1179652
  158.1 183.7 %reduce-scatter.16.cloned.1.call-start = ((), (), s32[]{:S(2)}) async-start(), calls=%async_computation.15 | async-start | bytes 1474560 | tf_op jit(solution)/shard_map/reduce_scatter | solution.py:395
  186.5 18.3 %copy-start.21 = (f32[128]{0:T(128)S(1)}, f32[128]{0:T(128)}, u32[]{:S(2)}) copy-start(f32[128]{0:T(128)} %copy-done.20) | copy-start | bytes 1540
  186.5 18.3 %copy-start.23 = (f32[128]{0:T(128)S(1)}, f32[128]{0:T(128)}, u32[]{:S(2)}) copy-start(f32[128]{0:T(128)} %copy-done.22) | copy-start | bytes 1540
  187.7 197.2 %reduce-scatter.12.cloned.1.call-start = ((), (), s32[]{:S(2)}) async-start(), calls=%async_computation.13 | async-start | bytes 4423680 | tf_op jit(solution)/shard_map/reduce_scatter | solution.py:389
  295.3 21.1 %copy-start.19 = (f32[128,8]{0,1:T(8,128)S(1)}, f32[128,8]{0,1:T(8,128)}, u32[]{:S(2)}) copy-start(f32[128,8]{0,1:T(8,128)} %copy-done.18) | copy-start | bytes 12292
  329.3 106.1 %reduce-scatter.20.cloned.1.call-start = ((), (), s32[]{:S(2)}) async-start(), calls=%async_computation.17 | async-start | bytes 5898240 | tf_op jit(solution)/shard_map/reduce_scatter | solution.py:401
  335.3 162.2 %reduce-scatter.18.cloned.1.call-start = ((), (), s32[]{:S(2)}) async-start(), calls=%async_computation.16 | async-start | bytes 331776 | tf_op jit(solution)/shard_map/reduce_scatter | solution.py:433
  341.9 205.1 %reduce-scatter.24.cloned.1.call-start = ((), (), s32[]{:S(2)}) async-start(), calls=%async_computation.19 | async-start | bytes 5898240 | tf_op jit(solution)/shard_map/reduce_scatter | solution.py:407
  347.7 92.0 %copy-start.52 = (bf16[24]{0:T(256)(128)(2,1)S(1)}, bf16[24]{0:T(256)(128)(2,1)}, u32[]{:S(2)}) copy-start(bf16[24]{0:T(256)(128)(2,1)} %param.33) | copy-start | bytes 148
  347.7 92.2 %copy-start.53 = (bf16[24]{0:T(256)(128)(2,1)S(1)}, bf16[24]{0:T(256)(128)(2,1)}, u32[]{:S(2)}) copy-start(bf16[24]{0:T(256)(128)(2,1)} %param.29) | copy-start | bytes 148
  347.8 92.5 %copy-start.30 = (bf16[3072]{0:T(1024)(128)(2,1)S(1)}, bf16[3072]{0:T(1024)(128)(2,1)}, u32[]{:S(2)}) copy-start(bf16[3072]{0:T(1024)(128)(2,1)} %get-tuple-element.259) | copy-start | bytes 18436
  347.8 151.2 %copy-start.29 = (bf16[768]{0:T(1024)(128)(2,1)S(1)}, bf16[768]{0:T(1024)(128)(2,1)}, u32[]{:S(2)}) copy-start(bf16[768]{0:T(1024)(128)(2,1)} %get-tuple-element.214) | copy-start | bytes 4612
  347.8 151.4 %copy-start.28 = (bf16[768]{0:T(1024)(128)(2,1)S(1)}, bf16[768]{0:T(1024)(128)(2,1)}, u32[]{:S(2)}) copy-start(bf16[768]{0:T(1024)(128)(2,1)} %get-tuple-element.219) | copy-start | bytes 4612
  347.8 151.6 %copy-start.27 = (bf16[768]{0:T(1024)(128)(2,1)S(1)}, bf16[768]{0:T(1024)(128)(2,1)}, u32[]{:S(2)}) copy-start(bf16[768]{0:T(1024)(128)(2,1)} %get-tuple-element.223) | copy-start | bytes 4612
  347.8 151.8 %copy-start.26 = (bf16[768]{0:T(1024)(128)(2,1)S(1)}, bf16[768]{0:T(1024)(128)(2,1)}, u32[]{:S(2)}) copy-start(bf16[768]{0:T(1024)(128)(2,1)} %get-tuple-element.220) | copy-start | bytes 4612
  347.8 152.0 %copy-start.15 = (bf16[3,12,64]{2,1,0:T(8,128)(2,1)S(1)}, bf16[3,12,64]{2,1,0:T(8,128)(2,1)}, u32[]{:S(2)}) copy-start(bf16[3,12,64]{2,1,0:T(8,128)(2,1)} %get-tuple-element.262) | copy-start | bytes 13828
  347.8 263.9 %reduce-scatter.14.cloned.1.call-start = ((), (), s32[]{:S(2)}) async-start(), calls=%async_computation.14 | async-start | bytes 995328 | tf_op jit(solution)/shard_map/reduce_scatter | solution.py:427
  384.9 293.4 %reduce-scatter.22.cloned.1.call-start = ((), (), s32[]{:S(2)}) async-start(), calls=%async_computation.18 | async-start | bytes 1327104 | tf_op jit(solution)/shard_map/reduce_scatter | solution.py:439
  435.5 114.5 %copy-start.43 = (f32[128]{0:T(128)S(1)}, f32[128]{0:T(128)}, u32[]{:S(2)}) copy-start(f32[128]{0:T(128)} %get-tuple-element.222) | copy-start | bytes 1540
  435.5 114.5 %copy-start.42 = (f32[128]{0:T(128)S(1)}, f32[128]{0:T(128)}, u32[]{:S(2)}) copy-start(f32[128]{0:T(128)} %get-tuple-element.221) | copy-start | bytes 1540
  435.5 114.5 %copy-start.41 = (f32[128]{0:T(128)S(1)}, f32[128]{0:T(128)}, u32[]{:S(2)}) copy-start(f32[128]{0:T(128)} %get-tuple-element.215) | copy-start | bytes 1540
  435.5 114.5 %copy-start.40 = (f32[128]{0:T(128)S(1)}, f32[128]{0:T(128)}, u32[]{:S(2)}) copy-start(f32[128]{0:T(128)} %get-tuple-element.216) | copy-start | bytes 1540
  435.5 114.5 %copy-start.25 = (f32[128]{0:T(128)S(1)}, f32[128]{0:T(128)}, u32[]{:S(2)}) copy-start(f32[128]{0:T(128)} %copy-done.22) | copy-start | bytes 1540
  435.5 309.7 %reduce-scatter.26.cloned.1.call-start = ((), (), s32[]{:S(2)}) async-start(), calls=%async_computation.20 | async-start | bytes 1327104 | tf_op jit(solution)/shard_map/reduce_scatter | solution.py:445
  546.4 200.4 %copy-start.54 = (f32[24]{0:T(128)}, f32[24]{0:T(128)S(1)}, u32[]{:S(2)}) copy-start(f32[24]{0:T(128)S(1)} %dynamic-slice_convert_fusion.1) | copy-start | bytes 292
  (20 other events, 98.5 us)
Sparse Core Ops, SparseCore 0:
  15.8 41.4 all-gather.7
  59.5 64.3 all-gather.5
  126.1 78.6 all-gather.9
  206.8 77.9 all-gather.11
  287.2 26.2 reduce-scatter.27
  316.1 25.7 reduce-scatter.15
  344.4 40.4 reduce-scatter.11
  387.6 47.8 reduce-scatter.19
  438.7 58.7 reduce-scatter.17
  499.9 46.8 reduce-scatter.23
  550.6 61.0 reduce-scatter.13
  615.3 62.9 reduce-scatter.21
  682.1 63.0 reduce-scatter.25
where the time goes:
time: 755 us; the launch traced here: 754 us
  waiting for transfers between devices  477 us (63%)
  blocking collectives  168 us (22%)
  matrix products  40 us (5%)
  local copies, waits for them, and re-layouts  24.7 us (3%)
  between operations  21.9 us (3%)
  other arithmetic  21 us (3%)
    unnamed x4, blocking collectives  90.3 us
    all_gather x1, waiting for transfers between devices, collect(): lax.all_gather(inner[10], 'dp', axis=0, tiled=True)  76.9 us
    reduce_scatter x1, waiting for transfers between devices, per_device(): lax.psum_scatter(partial_sums[10].astype(jnp.bfloat16), 'dp', scatter_dim...  65.2 us
    reduce_scatter x1, waiting for transfers between devices, per_device(): lax.psum_scatter(partial_sums[8].astype(jnp.bfloat16), 'dp', scatter_dime...  65 us
    reduce_scatter x1, waiting for transfers between devices, per_device(): lax.psum_scatter(partial_sums[6].astype(jnp.bfloat16), 'dp', scatter_dime...  57.1 us
    reduce_scatter x1, waiting for transfers between devices, per_device(): lax.psum_scatter(partial_sums[4].astype(jnp.bfloat16), 'dp', scatter_dime...  56.4 us
    reduce_scatter x1, waiting for transfers between devices, per_device(): lax.psum_scatter(moved[8].astype(jnp.bfloat16), 'seq', scatter_dimension=...  50.5 us
    reduce_scatter x1, waiting for transfers between devices, per_device(): lax.psum_scatter(moved[4].astype(jnp.bfloat16), 'seq', scatter_dimension=...  37 us
  transfers between devices with their start and end apart: 13, of which 11 were waited for; matrix products, arithmetic and copies ran while one was open for 11% of the time, Pallas kernels for 0%

commit v1 on v0

v1 whole, which is shorter than its diff:
```python
import jax
import jax.numpy as jnp
from jax import lax
from jax.sharding import PartitionSpec as P

HEADS = 12
HEAD_DIM = 64
ROT = 16
EPS = 1e-05
NEGATIVE = -1e30
BF = jnp.bfloat16
F32 = jnp.float32


def dot(spec, a, b):
    return jnp.einsum(spec, a, b, preferred_element_type=F32)


def frequencies():
    steps = jnp.arange(ROT // 2, dtype=F32)
    return jnp.power(F32(10000.0), -(2.0 * steps) / ROT)


def rotate(values, cosine, sine, sign):
    half = ROT // 2
    first = values[..., :half]
    second = values[..., half:ROT]
    turned_one = first * cosine - sign * second * sine
    turned_two = second * cosine + sign * first * sine
    return jnp.concatenate([turned_one, turned_two, values[..., ROT:]], axis=-1)


def place(row_lengths, index):
    ends = jnp.cumsum(row_lengths)
    after = (index[:, None] >= ends[None, :]).astype(jnp.int32)
    segment = jnp.sum(after, axis=1)
    start = jnp.sum(after * row_lengths[None, :], axis=1)
    return (segment, index - start)


def pick(values, index):
    return lax.dynamic_index_in_dim(values, index, 0, keepdims=False)


def seq_exchange(blocks):
    n = lax.axis_size("seq")
    if n != 4:
        return lax.all_to_all(blocks, "seq", 0, 0)
    me = lax.axis_index("seq")
    got = [pick(blocks, me)]
    for other in (1, 2, 3):
        pairs = [(i, i ^ other) for i in range(n)]
        got.append(lax.ppermute(pick(blocks, me ^ other), "seq", pairs))
    return jnp.stack(
        [
            jnp.where(
                me < 2,
                jnp.where(me == 0, got[j], got[j ^ 1]),
                jnp.where(me == 2, got[j ^ 2], got[j ^ 3]),
            )
            for j in range(n)
        ]
    )


CHIP_SWAP = [(0, 2), (2, 0), (1, 3), (3, 1)]
CORE_SWAP = [(0, 1), (1, 0), (2, 3), (3, 2)]


def seq_gather(values):
    n = lax.axis_size("seq")
    if n != 4:
        return lax.all_gather(values, "seq", axis=0, tiled=True)
    me = lax.axis_index("seq")
    chip, core = me // 2, me % 2
    far = lax.ppermute(values, "seq", CHIP_SWAP)
    mine = jnp.stack([jnp.where(chip == 0, values, far), jnp.where(chip == 0, far, values)])
    other = lax.ppermute(mine, "seq", CORE_SWAP)
    full = jnp.stack([jnp.where(core == 0, mine, other), jnp.where(core == 0, other, mine)], axis=1)
    return full.reshape((n * values.shape[0],) + values.shape[1:])


def seq_reduce(values):
    n = lax.axis_size("seq")
    if n != 4:
        return lax.psum_scatter(values.astype(BF), "seq", scatter_dimension=0, tiled=True).astype(F32)
    me = lax.axis_index("seq")
    chip, core = me // 2, me % 2
    rows = values.shape[0] // n
    parts = values.reshape((2, 2, rows) + values.shape[1:])
    keep = lax.dynamic_index_in_dim(parts, core, 1, keepdims=False)
    give = lax.dynamic_index_in_dim(parts, 1 - core, 1, keepdims=False).astype(BF)
    both = keep.astype(F32) + lax.ppermute(give, "seq", CORE_SWAP).astype(F32)
    far = lax.ppermute(pick(both, 1 - chip).astype(BF), "seq", CHIP_SWAP)
    return pick(both, chip) + far.astype(F32)


SIDE_SWAP = [(i, i ^ 1) for i in range(8)]


def up_pairs(*places):
    return [(2 * p + y, 2 * p + 2 + y) for p in places for y in (0, 1)]


def down_pairs(*places):
    return [(2 * p + y, 2 * p - 2 + y) for p in places for y in (0, 1)]


def dp_gather(block):
    n = lax.axis_size("dp")
    if n != 8:
        return lax.all_gather(block, "dp", axis=0)
    me = lax.axis_index("dp")
    line, side = me // 2, me % 2

    def send(values, pairs):
        return lax.ppermute(values, "dp", pairs)

    up1 = send(block, up_pairs(0, 1, 2))
    down1 = send(block, down_pairs(1, 2, 3))
    side0 = send(block, SIDE_SWAP)
    up2 = send(up1, up_pairs(1, 2))
    down2 = send(down1, down_pairs(2, 1))
    first = jnp.where(line == 0, down1, up1)
    side1 = send(first, SIDE_SWAP)
    second = jnp.where(line < 2, down2, up2)
    end3 = send(second, up_pairs(2) + down_pairs(1))
    side2 = send(second, SIDE_SWAP)
    third = jnp.where((line == 0) | (line == 3), end3, down1)
    side3 = send(third, SIDE_SWAP)
    source1 = jnp.where(line == 0, 1, line - 1)
    source2 = jnp.where(line < 2, line + 2, line - 2)
    source3 = jnp.where(line == 0, 3, jnp.where(line == 3, 0, line + 1))
    full = jnp.zeros((4, 2) + block.shape, block.dtype)
    zero = jnp.int32(0)
    for where, near, far in (
        (line, block, side0),
        (source1, first, side1),
        (source2, second, side2),
        (source3, third, side3),
    ):
        pair = jnp.stack([jnp.where(side == 0, near, far), jnp.where(side == 0, far, near)])
        full = lax.dynamic_update_slice(full, pair[None], (where, zero, zero, zero))
    return full.reshape((n,) + block.shape)


def dp_reduce(block_of):
    n = lax.axis_size("dp")
    if n != 8:
        blocks = jnp.stack([block_of(jnp.int32(i)).astype(BF) for i in range(n)])
        return lax.psum_scatter(blocks, "dp", scatter_dimension=0).astype(F32)
    me = lax.axis_index("dp")
    line, side = me // 2, me % 2

    def send(values, pairs):
        return lax.ppermute(values.astype(BF), "dp", pairs).astype(F32)

    ahead = line < 2

    def over_side(target):
        moved = send(block_of(2 * target + 1 - side), SIDE_SWAP)
        return block_of(2 * target + side).astype(F32) + moved

    sum_a = over_side(jnp.where(ahead, 3, 0))
    sum_b = over_side(jnp.where(ahead, 2, 1))
    sum_c = over_side(jnp.where(ahead, 1 - line, 5 - line))
    sum_d = over_side(line)
    sum_a = sum_a + send(sum_a, up_pairs(0) + down_pairs(3))
    end = (line == 0) | (line == 3)
    second = jnp.where(end, sum_b, sum_a)
    up2 = send(second, up_pairs(0, 1))
    down2 = send(second, down_pairs(3, 2))
    sum_b = sum_b + jnp.where(ahead, up2, down2)
    sum_c = sum_c + jnp.where(ahead, down2, up2)
    up3 = send(jnp.where(line == 1, sum_b, sum_c), up_pairs(0, 1, 2))
    down3 = send(jnp.where(line == 2, sum_b, sum_c), down_pairs(3, 2, 1))
    return sum_d + up3 + down3


def attention(queries, keys, values, d_out, segment, scale):
    tokens = queries.shape[1]
    index = jnp.arange(tokens, dtype=jnp.int32)
    allowed = (segment[:, None] == segment[None, :]) & (index[None, :] <= index[:, None])
    scores = dot("htd,hnd->htn", queries, keys) * scale
    masked = jnp.where(allowed[None], scores, NEGATIVE)
    top = jnp.max(masked, axis=-1, keepdims=True)
    weights = jnp.where(allowed[None], jnp.exp(masked - top), 0.0)
    probs = weights / jnp.sum(weights, axis=-1, keepdims=True)
    probs_r = probs.astype(BF)
    attended = dot("htn,hnd->htd", probs_r, values)
    d_probs = dot("htd,hnd->htn", d_out, values)
    delta = jnp.sum(probs * d_probs, axis=-1, keepdims=True)
    d_scores = (probs * (d_probs - delta)).astype(BF)
    d_queries = dot("htn,hnd->htd", d_scores, keys) * scale
    d_keys = dot("htn,htd->hnd", d_scores, queries) * scale
    d_values = dot("htn,htd->hnd", probs_r, d_out)
    return attended, d_queries, d_keys, d_values


def per_device(
    hidden_in,
    lengths,
    grad_out,
    attn_gain,
    attn_shift,
    mlp_gain,
    mlp_shift,
    qkv_weight,
    qkv_bias,
    dense_weight,
    dense_bias,
    up_weight,
    up_bias,
    down_weight,
    down_bias,
):
    n_dp, n_seq = lax.axis_size("dp"), lax.axis_size("seq")
    me = lax.axis_index("seq")
    rows, width = hidden_in.shape
    group = rows * n_seq
    scale = HEAD_DIM ** (-0.5)
    hidden_units = up_weight.shape[1]
    own_units = hidden_units // n_seq
    deep = width // (n_dp * n_seq)
    unit_rows = hidden_units // (n_dp * n_seq)
    heads = -(-HEADS // n_seq)
    own = heads * HEAD_DIM
    spare = heads * n_seq - HEADS

    def by_head(values):
        lead = values.shape[:-1]
        split = values.reshape(lead + (3, HEADS, HEAD_DIM))
        if spare:
            split = jnp.pad(split, [(0, 0)] * (len(lead) + 1) + [(0, spare), (0, 0)])
        split = split.reshape(lead + (3, n_seq, own))
        return jnp.moveaxis(split, -2, 0).reshape((n_seq,) + lead + (3 * own,))

    def from_heads(blocks):
        lead = blocks.shape[1:-1]
        split = jnp.moveaxis(blocks.reshape((n_seq,) + lead + (3, own)), 0, -2)
        split = split.reshape(lead + (3, HEADS + spare, HEAD_DIM))[..., :HEADS, :]
        return split.reshape(lead + (3 * width,))

    vectors = (attn_gain, attn_shift, mlp_gain, mlp_shift, qkv_bias, dense_bias, up_bias, down_bias)
    sizes = [v.shape[0] for v in vectors]
    length = sum(sizes)
    wide = own_units + 3 * own
    up_blocks = jnp.moveaxis(up_weight.reshape(deep, n_dp, n_seq, unit_rows), 2, 0)
    up_blocks = up_blocks.reshape(n_seq, deep, own_units)
    vector = jnp.pad(jnp.concatenate(vectors), (0, wide - length))
    blocks = jnp.concatenate(
        [
            jnp.concatenate([up_blocks, by_head(qkv_weight)], axis=2),
            jnp.broadcast_to(vector, (n_seq, 1, wide)),
        ],
        axis=1,
    )
    got = seq_exchange(blocks)
    up_piece = got[:, :deep, :own_units].reshape(n_seq * deep, own_units)
    qkv_piece = got[:, :deep, own_units:].reshape(n_seq * deep, 3 * own)
    group_vector = got[:, deep, :length]

    hidden_group = seq_gather(hidden_in)
    grad_group = seq_gather(grad_out)

    up_rows = n_seq * deep * own_units // width
    mlp_all = dp_gather(jnp.concatenate([up_piece.reshape(up_rows, width), down_weight], axis=0))
    qkv_all = dp_gather(qkv_piece)
    vec_rows = -(-n_seq * length // width)
    vec_piece = jnp.pad(group_vector.reshape(-1), (0, vec_rows * width - n_seq * length))
    dense_all = dp_gather(jnp.concatenate([dense_weight, vec_piece.reshape(vec_rows, width)], axis=0))
    up_full = mlp_all[:, :up_rows].reshape(width, own_units)
    down_full = mlp_all[:, up_rows:].reshape(own_units, width)
    qkv_full = qkv_all.reshape(width, 3 * own)
    dense_rows = dense_all[:, :deep].reshape(n_dp * deep, width)
    every = dense_all[:, deep:].reshape(n_dp, vec_rows * width)[:, : n_seq * length]
    every = every.reshape(n_dp * n_seq, length).astype(F32)
    whole = []
    start = 0
    for size in sizes:
        whole.append(every[:, start : start + size].reshape(-1))
        start += size
    f_attn_gain, f_attn_shift, f_mlp_gain, f_mlp_shift, f_qkv_bias, f_dense_bias, f_up_bias, f_down_bias = whole
    own_qkv_bias = pick(by_head(f_qkv_bias), me)
    own_up_bias = lax.dynamic_index_in_dim(
        f_up_bias.reshape(n_dp, n_seq, unit_rows), me, 1, keepdims=False
    ).reshape(-1)

    row_lengths = lengths[0]
    index = jnp.arange(group, dtype=jnp.int32)
    segment, position = place(row_lengths, index)
    angles = position.astype(F32)[:, None] * frequencies()[None, :]
    cosine = jnp.cos(angles)[:, None, :]
    sine = jnp.sin(angles)[:, None, :]

    tokens = hidden_group.astype(F32)
    center = jnp.mean(tokens, axis=-1, keepdims=True)
    centered = tokens - center
    spread = jnp.mean(centered * centered, axis=-1, keepdims=True)
    unit = centered * lax.rsqrt(spread + EPS)
    attn_in = (unit * f_attn_gain + f_attn_shift).astype(BF)
    mlp_in = (unit * f_mlp_gain + f_mlp_shift).astype(BF)

    upper = dot("td,df->tf", mlp_in, up_full) + own_up_bias
    cdf = 0.5 * (1.0 + lax.erf(upper * F32(0.7071067811865476)))
    pdf = jnp.exp(-0.5 * upper * upper) * F32(0.3989422804014327)
    act = (upper * cdf).astype(BF)
    d_act = dot("td,fd->tf", grad_group, down_full)
    d_up = (d_act * (cdf + upper * pdf)).astype(BF)
    down_grad = dot("tf,td->fd", act, grad_group).astype(BF).reshape(n_dp, unit_rows, width)
    up_grad = dot("td,tf->df", mlp_in, d_up).astype(BF).reshape(n_dp, up_rows, width)
    mlp_out = dot("tf,fd->td", act, down_full)
    d_mlp_in = dot("tf,df->td", d_up, up_full)
    mlp_sum = dp_reduce(lambda i: jnp.concatenate([pick(up_grad, i), pick(down_grad, i)], axis=0))

    joined = dot("td,de->te", attn_in, qkv_full) + own_qkv_bias
    joined = joined.reshape(group, 3, heads, HEAD_DIM)
    queries = jnp.moveaxis(rotate(joined[:, 0], cosine, sine, 1.0).astype(BF), 1, 0)
    keys = jnp.moveaxis(rotate(joined[:, 1], cosine, sine, 1.0).astype(BF), 1, 0)
    values = jnp.moveaxis(joined[:, 2].astype(BF), 1, 0)
    feature_rows = n_dp * deep
    per_line = n_seq * deep
    direct = spare == 0 and own % per_line == 0
    d_rows = dot("fe,te->ft", dense_rows, grad_group).astype(BF)
    if direct:
        runs = own // per_line
        moved = seq_exchange(d_rows.reshape(n_seq, runs * deep, group))
        moved = moved.reshape(n_seq, runs, deep, group)
        d_attended = jnp.moveaxis(moved, 0, 1).reshape(heads, HEAD_DIM, group)
    else:
        moved = lax.all_gather(d_rows.reshape(n_dp, deep, group), "seq", axis=1)
        moved = moved.reshape(width, group)
        moved = jnp.pad(moved, ((0, spare * HEAD_DIM), (0, 0)))
        d_attended = pick(moved.reshape(n_seq, heads, HEAD_DIM, group), me)
    d_attended = jnp.swapaxes(d_attended, 1, 2)
    attended, d_queries, d_keys, d_values = attention(queries, keys, values, d_attended, segment, scale)
    attended = jnp.swapaxes(attended.astype(BF), 1, 2).reshape(own, group)
    if direct:
        given = jnp.moveaxis(attended.reshape(runs, n_seq, deep, group), 1, 0)
        rows_attended = seq_exchange(given.reshape(n_seq, runs * deep, group)).reshape(feature_rows, group)
    else:
        given = lax.all_gather(attended, "seq", axis=0, tiled=True)[:width]
        rows_attended = lax.dynamic_index_in_dim(
            given.reshape(n_dp, n_seq, deep, group), me, 1, keepdims=False
        ).reshape(feature_rows, group)
    attn_out = dot("ft,fe->te", rows_attended, dense_rows)
    dense_grad = dot("ft,te->fe", rows_attended, grad_group).reshape(n_dp, deep, width)
    d_queries = rotate(jnp.moveaxis(d_queries, 0, 1), cosine, sine, -1.0)
    d_keys = rotate(jnp.moveaxis(d_keys, 0, 1), cosine, sine, -1.0)
    d_joined = jnp.stack([d_queries, d_keys, jnp.moveaxis(d_values, 0, 1)], axis=1)
    d_joined = d_joined.astype(BF).reshape(group, 3 * own)
    qkv_grad = dot("td,te->de", attn_in, d_joined).astype(BF).reshape(n_dp, n_seq * deep, 3 * own)
    d_attn_in = dot("te,de->td", d_joined, qkv_full)

    mine = jnp.arange(n_seq) == me
    qkv_bias_grad = jnp.sum(d_joined.astype(F32), axis=0)
    qkv_bias_grad = from_heads(jnp.where(mine[:, None], qkv_bias_grad[None], 0.0))
    up_bias_grad = jnp.sum(d_up.astype(F32), axis=0).reshape(n_dp, 1, unit_rows)
    up_bias_grad = jnp.where(mine[None, :, None], up_bias_grad, 0.0)
    bias_sum = jnp.sum(grad_out.astype(F32), axis=0)
    terms = (
        jnp.sum(d_attn_in * unit, axis=0),
        jnp.sum(d_attn_in, axis=0),
        jnp.sum(d_mlp_in * unit, axis=0),
        jnp.sum(d_mlp_in, axis=0),
        qkv_bias_grad,
        bias_sum,
        up_bias_grad,
        bias_sum,
    )
    terms = [t.reshape(n_dp, n_seq, size) for t, size in zip(terms, sizes)]
    terms = jnp.concatenate(terms, axis=2).reshape(n_dp, n_seq * length)
    terms = jnp.pad(terms, ((0, 0), (0, vec_rows * width - n_seq * length)))
    terms = terms.reshape(n_dp, vec_rows, width)
    dense_terms = jnp.concatenate([dense_grad, terms], axis=1).astype(BF)
    qkv_sum = dp_reduce(lambda i: pick(qkv_grad, i))
    dense_sum = dp_reduce(lambda i: pick(dense_terms, i))

    block_out = hidden_in.astype(F32) + f_dense_bias + f_down_bias + seq_reduce(attn_out + mlp_out)
    upstream = seq_reduce(d_attn_in * f_attn_gain + d_mlp_in * f_mlp_gain)
    x = hidden_in.astype(F32)
    centered = x - jnp.mean(x, axis=-1, keepdims=True)
    inverse = lax.rsqrt(jnp.mean(centered * centered, axis=-1, keepdims=True) + EPS)
    own_unit = centered * inverse
    inner = (
        upstream
        - jnp.mean(upstream, axis=-1, keepdims=True)
        - own_unit * jnp.mean(upstream * own_unit, axis=-1, keepdims=True)
    )
    grad_in = grad_out.astype(F32) + inverse * inner

    vec_sum = dense_sum[deep:].reshape(-1)[: n_seq * length].reshape(n_seq, 1, length)
    vec_sum = jnp.pad(vec_sum, ((0, 0), (0, 0), (0, wide - length)))
    back = jnp.concatenate(
        [
            jnp.concatenate(
                [
                    mlp_sum[:up_rows].reshape(n_seq, deep, own_units),
                    qkv_sum.reshape(n_seq, deep, 3 * own),
                ],
                axis=2,
            ),
            vec_sum,
        ],
        axis=1,
    )
    back = seq_exchange(back.astype(BF)).astype(F32)
    up_own = jnp.moveaxis(back[:, :deep, :own_units].reshape(n_seq, deep, n_dp, unit_rows), 0, 2)
    qkv_own = from_heads(back[:, :deep, own_units:])
    vec_own = jnp.sum(back[:, deep, :length], axis=0)
    owned = []
    start = 0
    for size in sizes:
        owned.append(vec_own[start : start + size])
        start += size
    return (
        block_out.astype(BF),
        grad_in.astype(BF),
        owned[0],
        owned[1],
        owned[2],
        owned[3],
        qkv_own,
        owned[4],
        dense_sum[:deep],
        owned[5],
        up_own.reshape(deep, hidden_units),
        owned[6],
        mlp_sum[up_rows:],
        owned[7],
    )


def solution(mesh):
    both = ("dp", "seq")
    matrix, vector = P(both, None), P(both)
    params = (vector, vector, vector, vector, matrix, vector, matrix, vector, matrix, vector, matrix, vector)
    return jax.shard_map(
        per_device,
        mesh=mesh,
        in_specs=(matrix, P("dp", None), matrix) + params,
        out_specs=(matrix, matrix) + params,
        check_vma=False,
    )
```

time: 755 us -> 271 us (0.36)
  waiting for transfers between devices: 477 us -> 63.9 us
  blocking collectives: 168 us -> 0 us
  starting transfers between devices: 1.01 us -> 114 us
  between operations: 21.9 us -> 2.8 us
  matrix products: 40 us -> 27.5 us
  other arithmetic: 21 us -> 30.1 us
    reduce_scatter x8 -> x0, waiting for transfers between devices: 338 us -> none  [the longest x1 65.2 us: per_device(): lax.psum_scatter(partial_sums[10].astype(jnp.bfloat16), 'dp', scatter_dim...]
    all_gather x4 -> x0, waiting for transfers between devices: 120 us -> none  [the longest x1 76.9 us: collect(): lax.all_gather(inner[10], 'dp', axis=0, tiled=True)]
    ppermute x0 -> x74, starting transfers between devices: none -> 114 us  [the longest x27 60.3 us: send(): return lax.ppermute(values.astype(BF), 'dp', pairs).astype(F32)]
    unnamed x4 -> x0, blocking collectives: 90.3 us -> none
    all_gather x7 -> x0, blocking collectives: 78 us -> none  [the longest x1 26.5 us: collect(): lax.all_gather(inner[9], 'dp', axis=0, tiled=True)]
    ppermute x0 -> x74, waiting for transfers between devices: none -> 63.9 us  [the longest x27 35.3 us: send(): return lax.ppermute(values, 'dp', pairs)]
    unnamed x14 -> x0, waiting for transfers between devices: 18.4 us -> none
    dot_general x19 -> x17, matrix products: 40 us -> 22.7 us  [dot(): return jnp.einsum(spec, a, b, preferred_element_type=F32)]
  transfers between devices with their start and end apart: 13 -> 74, of which waited for: 11 -> 24; matrix products, arithmetic and copies ran while one was open for 11% -> 26% of each run, Pallas kernels for 0% -> 0%
where the time goes in v1:
time: 271 us; the launch traced here: 269 us
  starting transfers between devices  114 us (42%)
  waiting for transfers between devices  63.9 us (24%)
  local copies, waits for them, and re-layouts  30.9 us (11%)
  other arithmetic  30.1 us (11%)
  matrix products  27.5 us (10%)
  between operations  2.8 us (1%)
    ppermute x27, starting transfers between devices, send(): return lax.ppermute(values.astype(BF), 'dp', pairs).astype(F32)  60.3 us
    ppermute x27, starting transfers between devices, send(): return lax.ppermute(values, 'dp', pairs)  39 us
    ppermute x27, waiting for transfers between devices, send(): return lax.ppermute(values, 'dp', pairs)  35.3 us
    dot_general x17, matrix products, dot(): return jnp.einsum(spec, a, b, preferred_element_type=F32)  22.7 us
    ppermute x27, waiting for transfers between devices, send(): return lax.ppermute(values.astype(BF), 'dp', pairs).astype(F32)  22 us
    ppermute x12, starting transfers between devices, seq_exchange(): got.append(lax.ppermute(pick(blocks, me ^ other), 'seq', pairs))  8.69 us
    ppermute x12, waiting for transfers between devices, seq_exchange(): got.append(lax.ppermute(pick(blocks, me ^ other), 'seq', pairs))  6.41 us
    unnamed x167, local copies, waits for them, and re-layouts  6.1 us
  transfers between devices with their start and end apart: 74, of which 24 were waited for; matrix products, arithmetic and copies ran while one was open for 26% of the time, Pallas kernels for 0%

profile of v1, /device:TPU:0, one launch (start us, length us, event | category | flops | bytes accessed | tf_op | source)
XLA Modules:
  0.0 269.2 jit_solution(18175715114264997707)
XLA Ops:
  0.7 3.0 %collective-permute-start.37 = (bf16[128,768]{1,0:T(8,128)(2,1)}, bf16[128,768]{1,0:T(8,128)(2,1)S(1)}, u32[]{:S(2)}, u32[]{:S(2)}) collective-permute-start(bf16[128,768]{1,0:T(8,128)(2,1)} %param.17), channel_id=1, source_target_pairs={{0,2},{2,0},{1,3},{3,1},{4,6},{6,4},{5,7},{7,5},{8,10},{10,8},{9,1... | collective-permute-start | bytes 589832 | tf_op jit(solution)/shard_map/ppermute | solution.py:76
  6.8 2.0 collective-permute-start.1
  12.4 3.4 %collective-permute-done.1 = bf16[25,1344]{1,0:T(8,128)(2,1)S(1)} collective-permute-done((bf16[25,1344]{1,0:T(8,128)(2,1)S(1)}, bf16[25,1344]{1,0:T(8,128)(2,1)S(1)}, u32[]{:S(2)}, u32[]{:S(2)}) %collective-permute-start.1) | collective-permute-done | bytes 67232 | tf_op jit(solution)/shard_map/ppermute | solution.py:53
  17.7 4.6 %collective-permute-start.5 = (bf16[26,768]{1,0:T(8,128)(2,1)S(1)}, bf16[26,768]{1,0:T(8,128)(2,1)S(1)}, u32[]{:S(2)}, u32[]{:S(2)}) collective-permute-start(bf16[26,768]{1,0:T(8,128)(2,1)S(1)} %constant_dynamic-update-slice_fusion), channel_id=1, source_target_pairs={{0,8},{4,12},{8,16},{12,20},{16,24},{20,28},{1,9},{5,13},{9,17},{1... | collective-permute-start | bytes 119816 | tf_op jit(solution)/shard_map/ppermute | solution.py:117
  22.3 1.6 collective-permute-start.3
  24.7 1.8 collective-permute-done.3
  26.4 3.5 %collective-permute-start.16 = (bf16[96,576]{1,0:T(8,128)(2,1)S(1)}, bf16[96,576]{1,0:T(8,128)(2,1)S(1)}, u32[]{:S(2)}, u32[]{:S(2)}) collective-permute-start(bf16[96,576]{1,0:T(8,128)(2,1)S(1)} %bitcast.544), channel_id=1, source_target_pairs={{0,8},{4,12},{8,16},{12,20},{16,24},{20,28},{1,9},{5,13},{9,17},{1... | collective-permute-start | bytes 331784 | tf_op jit(solution)/shard_map/ppermute | solution.py:117
  32.3 3.7 %collective-permute-done.7 = bf16[26,768]{1,0:T(8,128)(2,1)S(1)} collective-permute-done((bf16[26,768]{1,0:T(8,128)(2,1)S(1)}, bf16[26,768]{1,0:T(8,128)(2,1)S(1)}, u32[]{:S(2)}, u32[]{:S(2)}) %collective-permute-start.7) | collective-permute-done | bytes 39968 | tf_op jit(solution)/shard_map/ppermute | solution.py:117
  37.3 1.6 collective-permute-start.14
  38.9 3.9 %collective-permute-done.14 = bf16[96,576]{1,0:T(8,128)(2,1)S(1)} collective-permute-done((bf16[96,576]{1,0:T(8,128)(2,1)S(1)}, bf16[96,576]{1,0:T(8,128)(2,1)S(1)}, u32[]{:S(2)}, u32[]{:S(2)}) %collective-permute-start.14) | collective-permute-done | bytes 110624 | tf_op jit(solution)/shard_map/ppermute | solution.py:117
  44.5 2.4 collective-permute-done.9
  48.2 4.6 %collective-permute-done.10 = bf16[26,768]{1,0:T(8,128)(2,1)S(1)} collective-permute-done((bf16[26,768]{1,0:T(8,128)(2,1)S(1)}, bf16[26,768]{1,0:T(8,128)(2,1)S(1)}, u32[]{:S(2)}, u32[]{:S(2)}) %collective-permute-start.10) | collective-permute-done | bytes 39968 | tf_op jit(solution)/shard_map/ppermute | solution.py:117
  52.8 2.3 collective-permute-start.28
  71.7 4.7 %collective-permute-done.18 = bf16[96,576]{1,0:T(8,128)(2,1)S(1)} collective-permute-done((bf16[96,576]{1,0:T(8,128)(2,1)S(1)}, bf16[96,576]{1,0:T(8,128)(2,1)S(1)}, u32[]{:S(2)}, u32[]{:S(2)}) %collective-permute-start.18) | collective-permute-done | bytes 110624 | tf_op jit(solution)/shard_map/ppermute | solution.py:117
  80.4 3.6 %collective-permute-done.21 = bf16[96,576]{1,0:T(8,128)(2,1)S(1)} collective-permute-done((bf16[96,576]{1,0:T(8,128)(2,1)S(1)}, bf16[96,576]{1,0:T(8,128)(2,1)S(1)}, u32[]{:S(2)}, u32[]{:S(2)}) %collective-permute-start.21) | collective-permute-done | bytes 110624 | tf_op jit(solution)/shard_map/ppermute | solution.py:117
  86.6 4.0 %collective-permute-done.17 = bf16[96,576]{1,0:T(8,128)(2,1)S(1)} collective-permute-done((bf16[96,576]{1,0:T(8,128)(2,1)S(1)}, bf16[96,576]{1,0:T(8,128)(2,1)S(1)}, u32[]{:S(2)}, u32[]{:S(2)}) %collective-permute-start.17) | collective-permute-done | bytes 110624 | tf_op jit(solution)/shard_map/ppermute | solution.py:117
  91.6 3.8 %collective-permute-done.22 = bf16[96,576]{1,0:T(8,128)(2,1)S(1)} collective-permute-done((bf16[96,576]{1,0:T(8,128)(2,1)S(1)}, bf16[96,576]{1,0:T(8,128)(2,1)S(1)}, u32[]{:S(2)}, u32[]{:S(2)}) %collective-permute-start.22) | collective-permute-done | bytes 110624 | tf_op jit(solution)/shard_map/ppermute | solution.py:117
  103.2 4.9 %fusion.116 = (f32[3,512]{1,0:T(4,128)}, f32[3,512,512]{1,2,0:T(8,128)}) fusion(pred[512,512]{0,1:T(8,128)(4,1)} %fusion.15, bf16[512,3,48]{0,2,1:T(8,128)(2,1)S(1)} %slice.262, bf16[512,3,8]{0,2,1:T(8,128)(2,1)S(1)} %get-tuple-element.149, bf16[512,3,8]{0,2,1:T(8,128)(2,1)S(1)} %get-tuple-element.150, bf16[512,3,48]{0,2,1:T(8,128)(2,1)S(1)} %slice.263, ...), kind=kOutput, calls=%fused_computation.375 | convolution fusion | flops 105775616 | bytes 3807232 | tf_op jit(solution)/shard_map/sub | solution.py:187
  108.1 2.5 convolution_convert_fusion.5
  115.0 1.6 multiply_reduce_fusion
  121.5 2.2 copy.118
  123.8 1.9 dynamic-slice_bitcast_fusion.19
  130.6 2.6 fusion.117
  133.3 1.7 broadcast_select_fusion.1
  136.3 1.6 fusion.53
  137.9 5.9 %collective-permute-start.56 = (bf16[96,576]{1,0:T(8,128)(2,1)}, bf16[96,576]{1,0:T(8,128)(2,1)}, u32[]{:S(2)}, u32[]{:S(2)}) collective-permute-start(bf16[96,576]{1,0:T(8,128)(2,1)} %fusion.53), channel_id=1, source_target_pairs={{0,8},{4,12},{24,16},{28,20},{1,9},{5,13},{25,17},{29,21},{2,10},{... | collective-permute-start | bytes 331784 | tf_op jit(solution)/shard_map/ppermute | solution.py:156
  148.0 4.8 %collective-permute-start.57 = (bf16[96,576]{1,0:T(8,128)(2,1)S(1)}, bf16[96,576]{1,0:T(8,128)(2,1)S(1)}, u32[]{:S(2)}, u32[]{:S(2)}) collective-permute-start(bf16[96,576]{1,0:T(8,128)(2,1)S(1)} %select_convert_fusion.5), channel_id=1, source_target_pairs={{0,8},{4,12},{8,16},{12,20},{1,9},{5,13},{9,17},{13,21},{2,10},{6,... | collective-permute-start | bytes 331784 | tf_op jit(solution)/shard_map/ppermute | solution.py:156
  157.2 4.8 %collective-permute-start.60 = (bf16[96,576]{1,0:T(8,128)(2,1)S(1)}, bf16[96,576]{1,0:T(8,128)(2,1)S(1)}, u32[]{:S(2)}, u32[]{:S(2)}) collective-permute-start(bf16[96,576]{1,0:T(8,128)(2,1)S(1)} %get-tuple-element.31), channel_id=1, source_target_pairs={{0,8},{4,12},{8,16},{12,20},{16,24},{20,28},{1,9},{5,13},{9,17},{1... | collective-permute-start | bytes 331784 | tf_op jit(solution)/shard_map/ppermute | solution.py:156
  164.6 4.2 %collective-permute-done.61 = bf16[96,576]{1,0:T(8,128)(2,1)S(1)} collective-permute-done((bf16[96,576]{1,0:T(8,128)(2,1)S(1)}, bf16[96,576]{1,0:T(8,128)(2,1)S(1)}, u32[]{:S(2)}, u32[]{:S(2)}) %collective-permute-start.61) | collective-permute-done | bytes 110624 | tf_op jit(solution)/shard_map/ppermute | solution.py:156
  168.9 1.6 fusion.52
  172.9 2.0 convert_reduce_fusion
  175.1 1.9 fusion.118
  181.7 2.8 %fusion.111 = (bf16[768]{0:T(1024)(128)(2,1)S(1)}, bf16[768]{0:T(1024)(128)(2,1)S(1)}, f32[512,768]{1,0:T(8,128)}, bf16[768]{0:T(1024)(128)(2,1)S(1)}, bf16[768]{0:T(1024)(128)(2,1)S(1)}, /*index=5*/bf16[512,768]{1,0:T(8,128)(2,1)}) fusion(f32[512,768]{1,0:T(8,128)S(1)} %fusion.118, f32[512]{0:T(512)S(1)} %bitcast.559, f32[512]{0:T(512)S(1)} %bitcast.557, ...), kind=kOutput, calls=%fused_computation.370 | convolution fusion | flops 460059648 | bytes 6212608 | tf_op jit(solution)/shard_map/te,de->td/dot_general | solution.py:16
  189.3 1.9 fusion.40
  191.2 2.2 convolution_convert_fusion.1
  195.1 3.5 %collective-permute-start.65 = (bf16[26,768]{1,0:T(8,128)(2,1)S(1)}, bf16[26,768]{1,0:T(8,128)(2,1)S(1)}, u32[]{:S(2)}, u32[]{:S(2)}) collective-permute-start(bf16[26,768]{1,0:T(8,128)(2,1)S(1)} %fusion.63), channel_id=1, source_target_pairs={{0,8},{4,12},{24,16},{28,20},{1,9},{5,13},{25,17},{29,21},{2,10},{... | collective-permute-start | bytes 119816 | tf_op jit(solution)/shard_map/ppermute | solution.py:156
  201.1 4.9 %collective-permute-start.66 = (bf16[26,768]{1,0:T(8,128)(2,1)S(1)}, bf16[26,768]{1,0:T(8,128)(2,1)S(1)}, u32[]{:S(2)}, u32[]{:S(2)}) collective-permute-start(bf16[26,768]{1,0:T(8,128)(2,1)S(1)} %select_convert_fusion.8), channel_id=1, source_target_pairs={{0,8},{4,12},{8,16},{12,20},{1,9},{5,13},{9,17},{13,21},{2,10},{6,... | collective-permute-start | bytes 119816 | tf_op jit(solution)/shard_map/ppermute | solution.py:156
  207.7 4.5 %collective-permute-start.69 = (bf16[26,768]{1,0:T(8,128)(2,1)S(1)}, bf16[26,768]{1,0:T(8,128)(2,1)S(1)}, u32[]{:S(2)}, u32[]{:S(2)}) collective-permute-start(bf16[26,768]{1,0:T(8,128)(2,1)S(1)} %get-tuple-element.78), channel_id=1, source_target_pairs={{0,8},{4,12},{8,16},{12,20},{16,24},{20,28},{1,9},{5,13},{9,17},{1... | collective-permute-start | bytes 119816 | tf_op jit(solution)/shard_map/ppermute | solution.py:156
  216.4 2.2 collective-permute-done.70
  220.7 3.9 %collective-permute-start.47 = (bf16[192,768]{1,0:T(8,128)(2,1)S(1)}, bf16[192,768]{1,0:T(8,128)(2,1)S(1)}, u32[]{:S(2)}, u32[]{:S(2)}) collective-permute-start(bf16[192,768]{1,0:T(8,128)(2,1)S(1)} %fusion.25), channel_id=1, source_target_pairs={{0,8},{4,12},{24,16},{28,20},{1,9},{5,13},{25,17},{29,21},{2,10},{... | collective-permute-start | bytes 884744 | tf_op jit(solution)/shard_map/ppermute | solution.py:156
  226.0 4.0 %collective-permute-done.45 = bf16[192,768]{1,0:T(8,128)(2,1)S(1)} collective-permute-done((bf16[192,768]{1,0:T(8,128)(2,1)}, bf16[192,768]{1,0:T(8,128)(2,1)S(1)}, u32[]{:S(2)}, u32[]{:S(2)}) %collective-permute-start.45) | collective-permute-done | bytes 294944 | tf_op jit(solution)/shard_map/ppermute | solution.py:156
  232.6 5.0 %collective-permute-start.48 = (bf16[192,768]{1,0:T(8,128)(2,1)S(1)}, bf16[192,768]{1,0:T(8,128)(2,1)S(1)}, u32[]{:S(2)}, u32[]{:S(2)}) collective-permute-start(bf16[192,768]{1,0:T(8,128)(2,1)S(1)} %select_convert_fusion.2), channel_id=1, source_target_pairs={{0,8},{4,12},{8,16},{12,20},{1,9},{5,13},{9,17},{13,21},{2,10},{6,... | collective-permute-start | bytes 884744 | tf_op jit(solution)/shard_map/ppermute | solution.py:156
  240.2 2.8 %collective-permute-done.48 = bf16[192,768]{1,0:T(8,128)(2,1)S(1)} collective-permute-done((bf16[192,768]{1,0:T(8,128)(2,1)S(1)}, bf16[192,768]{1,0:T(8,128)(2,1)S(1)}, u32[]{:S(2)}, u32[]{:S(2)}) %collective-permute-start.48) | collective-permute-done | bytes 294944 | tf_op jit(solution)/shard_map/ppermute | solution.py:156
  243.2 4.5 %collective-permute-start.51 = (bf16[192,768]{1,0:T(8,128)(2,1)S(1)}, bf16[192,768]{1,0:T(8,128)(2,1)S(1)}, u32[]{:S(2)}, u32[]{:S(2)}) collective-permute-start(bf16[192,768]{1,0:T(8,128)(2,1)S(1)} %get-tuple-element.26), channel_id=1, source_target_pairs={{0,8},{4,12},{8,16},{12,20},{16,24},{20,28},{1,9},{5,13},{9,17},{1... | collective-permute-start | bytes 884744 | tf_op jit(solution)/shard_map/ppermute | solution.py:156
  249.1 3.1 %collective-permute-done.51 = bf16[192,768]{1,0:T(8,128)(2,1)S(1)} collective-permute-done((bf16[192,768]{1,0:T(8,128)(2,1)S(1)}, bf16[192,768]{1,0:T(8,128)(2,1)S(1)}, u32[]{:S(2)}, u32[]{:S(2)}) %collective-permute-start.51) | collective-permute-done | bytes 294944 | tf_op jit(solution)/shard_map/ppermute | solution.py:156
  252.2 4.5 %collective-permute-done.52 = bf16[192,768]{1,0:T(8,128)(2,1)S(1)} collective-permute-done((bf16[192,768]{1,0:T(8,128)(2,1)S(1)}, bf16[192,768]{1,0:T(8,128)(2,1)S(1)}, u32[]{:S(2)}, u32[]{:S(2)}) %collective-permute-start.52) | collective-permute-done | bytes 294944 | tf_op jit(solution)/shard_map/ppermute | solution.py:156
  258.0 1.9 collective-permute-start.72
  262.6 1.9 collective-permute-done.73
  (471 shorter events, 114.0 us)
Async XLA Ops:
  0.7 57.2 %collective-permute-start.37 = (bf16[128,768]{1,0:T(8,128)(2,1)}, bf16[128,768]{1,0:T(8,128)(2,1)S(1)}, u32[]{:S(2)}, u32[]{:S(2)}) collective-permute-start(bf16[128,768]{1,0:T(8,128)(2,1)} %param.17), channel_id=1, source_target_pairs={{0,2},{2,0},{1,3},{3,1},{4,6},{6,4},{5,7},{7,5},{8,10},{10,8},{9,1... | collective-permute-start | bytes 589832 | tf_op jit(solution)/shard_map/ppermute | solution.py:76
  3.7 51.4 %collective-permute-start.12 = (bf16[128,768]{1,0:T(8,128)(2,1)}, bf16[128,768]{1,0:T(8,128)(2,1)S(1)}, u32[]{:S(2)}, u32[]{:S(2)}) collective-permute-start(bf16[128,768]{1,0:T(8,128)(2,1)} %param.15), channel_id=1, source_target_pairs={{0,2},{2,0},{1,3},{3,1},{4,6},{6,4},{5,7},{7,5},{8,10},{10,8},{9,1... | collective-permute-start | bytes 589832 | tf_op jit(solution)/shard_map/ppermute | solution.py:76
  6.8 9.0 %collective-permute-start.1 = (bf16[25,1344]{1,0:T(8,128)(2,1)S(1)}, bf16[25,1344]{1,0:T(8,128)(2,1)S(1)}, u32[]{:S(2)}, u32[]{:S(2)}) collective-permute-start(bf16[25,1344]{1,0:T(8,128)(2,1)S(1)} %get-tuple-element.95), channel_id=1, source_target_pairs={{0,2},{1,3},{2,0},{3,1},{4,6},{5,7},{6,4},{7,5},{8,10},{9,11},{10,... | collective-permute-start | bytes 201608 | tf_op jit(solution)/shard_map/ppermute | solution.py:53
  16.4 13.6 %collective-permute-start.4 = (bf16[26,768]{1,0:T(8,128)(2,1)S(1)}, bf16[26,768]{1,0:T(8,128)(2,1)S(1)}, u32[]{:S(2)}, u32[]{:S(2)}) collective-permute-start(bf16[26,768]{1,0:T(8,128)(2,1)S(1)} %constant_dynamic-update-slice_fusion), channel_id=1, source_target_pairs={{8,0},{12,4},{16,8},{20,12},{24,16},{28,20},{9,1},{13,5},{17,9},{2... | collective-permute-start | bytes 119816 | tf_op jit(solution)/shard_map/ppermute | solution.py:117
  17.7 13.6 %collective-permute-start.5 = (bf16[26,768]{1,0:T(8,128)(2,1)S(1)}, bf16[26,768]{1,0:T(8,128)(2,1)S(1)}, u32[]{:S(2)}, u32[]{:S(2)}) collective-permute-start(bf16[26,768]{1,0:T(8,128)(2,1)S(1)} %constant_dynamic-update-slice_fusion), channel_id=1, source_target_pairs={{0,8},{4,12},{8,16},{12,20},{16,24},{20,28},{1,9},{5,13},{9,17},{1... | collective-permute-start | bytes 119816 | tf_op jit(solution)/shard_map/ppermute | solution.py:117
  26.4 37.8 %collective-permute-start.16 = (bf16[96,576]{1,0:T(8,128)(2,1)S(1)}, bf16[96,576]{1,0:T(8,128)(2,1)S(1)}, u32[]{:S(2)}, u32[]{:S(2)}) collective-permute-start(bf16[96,576]{1,0:T(8,128)(2,1)S(1)} %bitcast.544), channel_id=1, source_target_pairs={{0,8},{4,12},{8,16},{12,20},{16,24},{20,28},{1,9},{5,13},{9,17},{1... | collective-permute-start | bytes 331784 | tf_op jit(solution)/shard_map/ppermute | solution.py:117
  36.0 28.8 %collective-permute-start.15 = (bf16[96,576]{1,0:T(8,128)(2,1)S(1)}, bf16[96,576]{1,0:T(8,128)(2,1)S(1)}, u32[]{:S(2)}, u32[]{:S(2)}) collective-permute-start(bf16[96,576]{1,0:T(8,128)(2,1)S(1)} %bitcast.545), channel_id=1, source_target_pairs={{8,0},{12,4},{16,8},{20,12},{24,16},{28,20},{9,1},{13,5},{17,9},{2... | collective-permute-start | bytes 331784 | tf_op jit(solution)/shard_map/ppermute | solution.py:117
  52.8 25.3 %collective-permute-start.28 = (bf16[192,768]{1,0:T(8,128)(2,1)}, bf16[192,768]{1,0:T(8,128)(2,1)}, u32[]{:S(2)}, u32[]{:S(2)}) collective-permute-start(bf16[192,768]{1,0:T(8,128)(2,1)} %pad_maximum_fusion.6), channel_id=1, source_target_pairs={{0,8},{4,12},{8,16},{12,20},{16,24},{20,28},{1,9},{5,13},{9,17},{1... | collective-permute-start | bytes 884744 | tf_op jit(solution)/shard_map/ppermute | solution.py:117
  55.1 23.9 %collective-permute-start.27 = (bf16[192,768]{1,0:T(8,128)(2,1)}, bf16[192,768]{1,0:T(8,128)(2,1)}, u32[]{:S(2)}, u32[]{:S(2)}) collective-permute-start(bf16[192,768]{1,0:T(8,128)(2,1)} %pad_maximum_fusion.6), channel_id=1, source_target_pairs={{8,0},{12,4},{16,8},{20,12},{24,16},{28,20},{9,1},{13,5},{17,9},{2... | collective-permute-start | bytes 884744 | tf_op jit(solution)/shard_map/ppermute | solution.py:117
  64.2 12.2 %collective-permute-start.26 = (bf16[192,768]{1,0:T(8,128)(2,1)}, bf16[192,768]{1,0:T(8,128)(2,1)S(1)}, u32[]{:S(2)}, u32[]{:S(2)}) collective-permute-start(bf16[192,768]{1,0:T(8,128)(2,1)} %pad_maximum_fusion.6), channel_id=1, source_target_pairs={{0,4},{4,0},{8,12},{12,8},{16,20},{20,16},{24,28},{28,24},{1,5},{5... | collective-permute-start | bytes 884744 | tf_op jit(solution)/shard_map/ppermute | solution.py:117
  66.7 9.6 %collective-permute-start.18 = (bf16[96,576]{1,0:T(8,128)(2,1)S(1)}, bf16[96,576]{1,0:T(8,128)(2,1)S(1)}, u32[]{:S(2)}, u32[]{:S(2)}) collective-permute-start(bf16[96,576]{1,0:T(8,128)(2,1)S(1)} %collective-permute-done.15), channel_id=1, source_target_pairs={{16,8},{20,12},{8,0},{12,4},{17,9},{21,13},{9,1},{13,5},{18,10},{2... | collective-permute-start | bytes 331784 | tf_op jit(solution)/shard_map/ppermute | solution.py:117
  71.6 24.0 %collective-permute-start.38 = (bf16[2,128,768]{2,1,0:T(8,128)(2,1)}, bf16[2,128,768]{2,1,0:T(8,128)(2,1)S(1)}, u32[]{:S(2)}, u32[]{:S(2)}) collective-permute-start(bf16[2,128,768]{2,1,0:T(8,128)(2,1)} %pad_maximum_fusion.4), channel_id=1, source_target_pairs={{0,1},{1,0},{2,3},{3,2},{4,5},{5,4},{6,7},{7,6},{8,9},{9,8},{10,11... | collective-permute-start | bytes 1179656 | tf_op jit(solution)/shard_map/ppermute | solution.py:78
  76.4 22.1 %collective-permute-start.13 = (bf16[2,128,768]{2,1,0:T(8,128)(2,1)}, bf16[2,128,768]{2,1,0:T(8,128)(2,1)S(1)}, u32[]{:S(2)}, u32[]{:S(2)}) collective-permute-start(bf16[2,128,768]{2,1,0:T(8,128)(2,1)} %pad_maximum_fusion.3), channel_id=1, source_target_pairs={{0,1},{1,0},{2,3},{3,2},{4,5},{5,4},{6,7},{7,6},{8,9},{9,8},{10,11... | collective-permute-start | bytes 1179656 | tf_op jit(solution)/shard_map/ppermute | solution.py:78
  79.1 54.2 %collective-permute-start.31 = (bf16[192,768]{1,0:T(8,128)(2,1)}, bf16[192,768]{1,0:T(8,128)(2,1)}, u32[]{:S(2)}, u32[]{:S(2)}) collective-permute-start(bf16[192,768]{1,0:T(8,128)(2,1)} %collective-permute-done.28), channel_id=1, source_target_pairs={{8,16},{12,20},{16,24},{20,28},{9,17},{13,21},{17,25},{21,29},{10,... | collective-permute-start | bytes 884744 | tf_op jit(solution)/shard_map/ppermute | solution.py:117
  84.0 49.2 %collective-permute-start.30 = (bf16[192,768]{1,0:T(8,128)(2,1)}, bf16[192,768]{1,0:T(8,128)(2,1)}, u32[]{:S(2)}, u32[]{:S(2)}) collective-permute-start(bf16[192,768]{1,0:T(8,128)(2,1)} %collective-permute-done.27), channel_id=1, source_target_pairs={{16,8},{20,12},{8,0},{12,4},{17,9},{21,13},{9,1},{13,5},{18,10},{2... | collective-permute-start | bytes 884744 | tf_op jit(solution)/shard_map/ppermute | solution.py:117
  96.9 14.3 %collective-permute-start.40 = (bf16[48,512]{1,0:T(8,128)(2,1)}, bf16[48,512]{1,0:T(8,128)(2,1)}, u32[]{:S(2)}, u32[]{:S(2)}) collective-permute-start(bf16[48,512]{1,0:T(8,128)(2,1)} %get-tuple-element.123), channel_id=1, source_target_pairs={{0,2},{1,3},{2,0},{3,1},{4,6},{5,7},{6,4},{7,5},{8,10},{9,11},{10,... | collective-permute-start | bytes 147464 | tf_op jit(solution)/shard_map/ppermute | solution.py:53
  98.4 14.4 %collective-permute-start.41 = (bf16[48,512]{1,0:T(8,128)(2,1)}, bf16[48,512]{1,0:T(8,128)(2,1)}, u32[]{:S(2)}, u32[]{:S(2)}) collective-permute-start(bf16[48,512]{1,0:T(8,128)(2,1)} %get-tuple-element.124), channel_id=1, source_target_pairs={{0,3},{1,2},{2,1},{3,0},{4,7},{5,6},{6,5},{7,4},{8,11},{9,10},{10,... | collective-permute-start | bytes 147464 | tf_op jit(solution)/shard_map/ppermute | solution.py:53
  98.4 14.4 %collective-permute-start.39 = (bf16[48,512]{1,0:T(8,128)(2,1)}, bf16[48,512]{1,0:T(8,128)(2,1)}, u32[]{:S(2)}, u32[]{:S(2)}) collective-permute-start(bf16[48,512]{1,0:T(8,128)(2,1)} %get-tuple-element.125), channel_id=1, source_target_pairs={{0,1},{1,0},{2,3},{3,2},{4,5},{5,4},{6,7},{7,6},{8,9},{9,8},{10,11... | collective-permute-start | bytes 147464 | tf_op jit(solution)/shard_map/ppermute | solution.py:53
  111.3 14.3 %collective-permute-start.24 = (bf16[48,512]{1,0:T(8,128)(2,1)}, bf16[48,512]{1,0:T(8,128)(2,1)}, u32[]{:S(2)}, u32[]{:S(2)}) collective-permute-start(bf16[48,512]{1,0:T(8,128)(2,1)} %get-tuple-element.126), channel_id=1, source_target_pairs={{0,2},{1,3},{2,0},{3,1},{4,6},{5,7},{6,4},{7,5},{8,10},{9,11},{10,... | collective-permute-start | bytes 147464 | tf_op jit(solution)/shard_map/ppermute | solution.py:53
  112.8 13.8 %collective-permute-start.25 = (bf16[48,512]{1,0:T(8,128)(2,1)}, bf16[48,512]{1,0:T(8,128)(2,1)}, u32[]{:S(2)}, u32[]{:S(2)}) collective-permute-start(bf16[48,512]{1,0:T(8,128)(2,1)} %get-tuple-element.127), channel_id=1, source_target_pairs={{0,3},{1,2},{2,1},{3,0},{4,7},{5,6},{6,5},{7,4},{8,11},{9,10},{10,... | collective-permute-start | bytes 147464 | tf_op jit(solution)/shard_map/ppermute | solution.py:53
  112.8 14.9 %collective-permute-start.23 = (bf16[48,512]{1,0:T(8,128)(2,1)}, bf16[48,512]{1,0:T(8,128)(2,1)}, u32[]{:S(2)}, u32[]{:S(2)}) collective-permute-start(bf16[48,512]{1,0:T(8,128)(2,1)} %get-tuple-element.128), channel_id=1, source_target_pairs={{0,1},{1,0},{2,3},{3,2},{4,5},{5,4},{6,7},{7,6},{8,9},{9,8},{10,11... | collective-permute-start | bytes 147464 | tf_op jit(solution)/shard_map/ppermute | solution.py:53
  125.6 28.3 %collective-permute-start.59 = (bf16[96,576]{1,0:T(8,128)(2,1)}, bf16[96,576]{1,0:T(8,128)(2,1)}, u32[]{:S(2)}, u32[]{:S(2)}) collective-permute-start(bf16[96,576]{1,0:T(8,128)(2,1)} %get-tuple-element.52), channel_id=1, source_target_pairs={{0,4},{4,0},{8,12},{12,8},{16,20},{20,16},{24,28},{28,24},{1,5},{5... | collective-permute-start | bytes 331784 | tf_op jit(solution)/shard_map/ppermute | solution.py:156
  126.6 9.7 %collective-permute-start.55 = (bf16[96,576]{1,0:T(8,128)(2,1)}, bf16[96,576]{1,0:T(8,128)(2,1)}, u32[]{:S(2)}, u32[]{:S(2)}) collective-permute-start(bf16[96,576]{1,0:T(8,128)(2,1)} %get-tuple-element.53), channel_id=1, source_target_pairs={{0,4},{4,0},{8,12},{12,8},{16,20},{20,16},{24,28},{28,24},{1,5},{5... | collective-permute-start | bytes 331784 | tf_op jit(solution)/shard_map/ppermute | solution.py:156
  127.7 17.5 %collective-permute-start.54 = (bf16[96,576]{1,0:T(8,128)(2,1)}, bf16[96,576]{1,0:T(8,128)(2,1)}, u32[]{:S(2)}, u32[]{:S(2)}) collective-permute-start(bf16[96,576]{1,0:T(8,128)(2,1)} %get-tuple-element.54), channel_id=1, source_target_pairs={{0,4},{4,0},{8,12},{12,8},{16,20},{20,16},{24,28},{28,24},{1,5},{5... | collective-permute-start | bytes 331784 | tf_op jit(solution)/shard_map/ppermute | solution.py:156
  135.0 13.0 %collective-permute-start.33 = (bf16[192,768]{1,0:T(8,128)(2,1)}, bf16[192,768]{1,0:T(8,128)(2,1)}, u32[]{:S(2)}, u32[]{:S(2)}) collective-permute-start(bf16[192,768]{1,0:T(8,128)(2,1)} %broadcast_select_fusion.1), channel_id=1, source_target_pairs={{16,24},{20,28},{8,0},{12,4},{17,25},{21,29},{9,1},{13,5},{18,26},... | collective-permute-start | bytes 884744 | tf_op jit(solution)/shard_map/ppermute | solution.py:117
  137.9 8.2 %collective-permute-start.56 = (bf16[96,576]{1,0:T(8,128)(2,1)}, bf16[96,576]{1,0:T(8,128)(2,1)}, u32[]{:S(2)}, u32[]{:S(2)}) collective-permute-start(bf16[96,576]{1,0:T(8,128)(2,1)} %fusion.53), channel_id=1, source_target_pairs={{0,8},{4,12},{24,16},{28,20},{1,9},{5,13},{25,17},{29,21},{2,10},{... | collective-permute-start | bytes 331784 | tf_op jit(solution)/shard_map/ppermute | solution.py:156
  144.0 20.6 %collective-permute-start.53 = (bf16[96,576]{1,0:T(8,128)(2,1)}, bf16[96,576]{1,0:T(8,128)(2,1)S(1)}, u32[]{:S(2)}, u32[]{:S(2)}) collective-permute-start(bf16[96,576]{1,0:T(8,128)(2,1)} %get-tuple-element.51), channel_id=1, source_target_pairs={{0,4},{4,0},{8,12},{12,8},{16,20},{20,16},{24,28},{28,24},{1,5},{5... | collective-permute-start | bytes 331784 | tf_op jit(solution)/shard_map/ppermute | solution.py:156
  145.2 16.9 %collective-permute-start.32 = (bf16[192,768]{1,0:T(8,128)(2,1)}, bf16[192,768]{1,0:T(8,128)(2,1)S(1)}, u32[]{:S(2)}, u32[]{:S(2)}) collective-permute-start(bf16[192,768]{1,0:T(8,128)(2,1)} %broadcast_select_fusion.1), channel_id=1, source_target_pairs={{0,4},{4,0},{8,12},{12,8},{16,20},{20,16},{24,28},{28,24},{1,5},{5... | collective-permute-start | bytes 884744 | tf_op jit(solution)/shard_map/ppermute | solution.py:117
  147.3 7.8 %collective-permute-start.58 = (bf16[96,576]{1,0:T(8,128)(2,1)S(1)}, bf16[96,576]{1,0:T(8,128)(2,1)S(1)}, u32[]{:S(2)}, u32[]{:S(2)}) collective-permute-start(bf16[96,576]{1,0:T(8,128)(2,1)S(1)} %select_convert_fusion.5), channel_id=1, source_target_pairs={{24,16},{28,20},{16,8},{20,12},{25,17},{29,21},{17,9},{21,13},{26,... | collective-permute-start | bytes 331784 | tf_op jit(solution)/shard_map/ppermute | solution.py:156
  148.0 8.0 %collective-permute-start.57 = (bf16[96,576]{1,0:T(8,128)(2,1)S(1)}, bf16[96,576]{1,0:T(8,128)(2,1)S(1)}, u32[]{:S(2)}, u32[]{:S(2)}) collective-permute-start(bf16[96,576]{1,0:T(8,128)(2,1)S(1)} %select_convert_fusion.5), channel_id=1, source_target_pairs={{0,8},{4,12},{8,16},{12,20},{1,9},{5,13},{9,17},{13,21},{2,10},{6,... | collective-permute-start | bytes 331784 | tf_op jit(solution)/shard_map/ppermute | solution.py:156
  153.9 16.7 %collective-permute-start.34 = (bf16[192,768]{1,0:T(8,128)(2,1)S(1)}, bf16[192,768]{1,0:T(8,128)(2,1)S(1)}, u32[]{:S(2)}, u32[]{:S(2)}) collective-permute-start(bf16[192,768]{1,0:T(8,128)(2,1)S(1)} %get-tuple-element.110), channel_id=1, source_target_pairs={{0,4},{4,0},{8,12},{12,8},{16,20},{20,16},{24,28},{28,24},{1,5},{5... | collective-permute-start | bytes 884744 | tf_op jit(solution)/shard_map/ppermute | solution.py:117
  155.1 15.4 %collective-permute-start.29 = (bf16[192,768]{1,0:T(8,128)(2,1)S(1)}, bf16[192,768]{1,0:T(8,128)(2,1)S(1)}, u32[]{:S(2)}, u32[]{:S(2)}) collective-permute-start(bf16[192,768]{1,0:T(8,128)(2,1)S(1)} %get-tuple-element.111), channel_id=1, source_target_pairs={{0,4},{4,0},{8,12},{12,8},{16,20},{20,16},{24,28},{28,24},{1,5},{5... | collective-permute-start | bytes 884744 | tf_op jit(solution)/shard_map/ppermute | solution.py:117
  181.6 51.0 %collective-permute-start.35 = (bf16[2,128,768]{2,1,0:T(8,128)(2,1)}, bf16[2,128,768]{2,1,0:T(8,128)(2,1)}, u32[]{:S(2)}, u32[]{:S(2)}) collective-permute-start(bf16[2,128,768]{2,1,0:T(8,128)(2,1)} %fusion.39), channel_id=1, source_target_pairs={{0,1},{1,0},{2,3},{3,2},{4,5},{5,4},{6,7},{7,6},{8,9},{9,8},{10,11... | collective-permute-start | bytes 1179656 | tf_op jit(solution)/shard_map/ppermute | solution.py:93
  185.2 29.2 %collective-permute-start.62 = (bf16[26,768]{1,0:T(8,128)(2,1)S(1)}, bf16[26,768]{1,0:T(8,128)(2,1)S(1)}, u32[]{:S(2)}, u32[]{:S(2)}) collective-permute-start(bf16[26,768]{1,0:T(8,128)(2,1)S(1)} %get-tuple-element.106), channel_id=1, source_target_pairs={{0,4},{4,0},{8,12},{12,8},{16,20},{20,16},{24,28},{28,24},{1,5},{5... | collective-permute-start | bytes 119816 | tf_op jit(solution)/shard_map/ppermute | solution.py:156
  186.1 13.2 %collective-permute-start.63 = (bf16[26,768]{1,0:T(8,128)(2,1)S(1)}, bf16[26,768]{1,0:T(8,128)(2,1)S(1)}, u32[]{:S(2)}, u32[]{:S(2)}) collective-permute-start(bf16[26,768]{1,0:T(8,128)(2,1)S(1)} %get-tuple-element.107), channel_id=1, source_target_pairs={{0,4},{4,0},{8,12},{12,8},{16,20},{20,16},{24,28},{28,24},{1,5},{5... | collective-permute-start | bytes 119816 | tf_op jit(solution)/shard_map/ppermute | solution.py:156
  187.3 7.8 %collective-permute-start.64 = (bf16[26,768]{1,0:T(8,128)(2,1)S(1)}, bf16[26,768]{1,0:T(8,128)(2,1)S(1)}, u32[]{:S(2)}, u32[]{:S(2)}) collective-permute-start(bf16[26,768]{1,0:T(8,128)(2,1)S(1)} %get-tuple-element.108), channel_id=1, source_target_pairs={{0,4},{4,0},{8,12},{12,8},{16,20},{20,16},{24,28},{28,24},{1,5},{5... | collective-permute-start | bytes 119816 | tf_op jit(solution)/shard_map/ppermute | solution.py:156
  188.2 18.5 %collective-permute-start.68 = (bf16[26,768]{1,0:T(8,128)(2,1)S(1)}, bf16[26,768]{1,0:T(8,128)(2,1)S(1)}, u32[]{:S(2)}, u32[]{:S(2)}) collective-permute-start(bf16[26,768]{1,0:T(8,128)(2,1)S(1)} %get-tuple-element.109), channel_id=1, source_target_pairs={{0,4},{4,0},{8,12},{12,8},{16,20},{20,16},{24,28},{28,24},{1,5},{5... | collective-permute-start | bytes 119816 | tf_op jit(solution)/shard_map/ppermute | solution.py:156
  206.7 12.7 %collective-permute-start.46 = (bf16[192,768]{1,0:T(8,128)(2,1)}, bf16[192,768]{1,0:T(8,128)(2,1)S(1)}, u32[]{:S(2)}, u32[]{:S(2)}) collective-permute-start(bf16[192,768]{1,0:T(8,128)(2,1)} %pad_maximum_fusion.11), channel_id=1, source_target_pairs={{0,4},{4,0},{8,12},{12,8},{16,20},{20,16},{24,28},{28,24},{1,5},{5... | collective-permute-start | bytes 884744 | tf_op jit(solution)/shard_map/ppermute | solution.py:156
  214.4 34.8 %collective-permute-start.44 = (bf16[192,768]{1,0:T(8,128)(2,1)}, bf16[192,768]{1,0:T(8,128)(2,1)}, u32[]{:S(2)}, u32[]{:S(2)}) collective-permute-start(bf16[192,768]{1,0:T(8,128)(2,1)} %pad_maximum_fusion.7), channel_id=1, source_target_pairs={{0,4},{4,0},{8,12},{12,8},{16,20},{20,16},{24,28},{28,24},{1,5},{5... | collective-permute-start | bytes 884744 | tf_op jit(solution)/shard_map/ppermute | solution.py:156
  215.4 14.6 %collective-permute-start.45 = (bf16[192,768]{1,0:T(8,128)(2,1)}, bf16[192,768]{1,0:T(8,128)(2,1)S(1)}, u32[]{:S(2)}, u32[]{:S(2)}) collective-permute-start(bf16[192,768]{1,0:T(8,128)(2,1)} %pad_maximum_fusion.9), channel_id=1, source_target_pairs={{0,4},{4,0},{8,12},{12,8},{16,20},{20,16},{24,28},{28,24},{1,5},{5... | collective-permute-start | bytes 884744 | tf_op jit(solution)/shard_map/ppermute | solution.py:156
  219.4 20.7 %collective-permute-start.50 = (bf16[192,768]{1,0:T(8,128)(2,1)}, bf16[192,768]{1,0:T(8,128)(2,1)S(1)}, u32[]{:S(2)}, u32[]{:S(2)}) collective-permute-start(bf16[192,768]{1,0:T(8,128)(2,1)} %pad_maximum_fusion.12), channel_id=1, source_target_pairs={{0,4},{4,0},{8,12},{12,8},{16,20},{20,16},{24,28},{28,24},{1,5},{5... | collective-permute-start | bytes 884744 | tf_op jit(solution)/shard_map/ppermute | solution.py:156
  220.7 10.9 %collective-permute-start.47 = (bf16[192,768]{1,0:T(8,128)(2,1)S(1)}, bf16[192,768]{1,0:T(8,128)(2,1)S(1)}, u32[]{:S(2)}, u32[]{:S(2)}) collective-permute-start(bf16[192,768]{1,0:T(8,128)(2,1)S(1)} %fusion.25), channel_id=1, source_target_pairs={{0,8},{4,12},{24,16},{28,20},{1,9},{5,13},{25,17},{29,21},{2,10},{... | collective-permute-start | bytes 884744 | tf_op jit(solution)/shard_map/ppermute | solution.py:156
  230.0 8.7 %collective-permute-start.43 = (bf16[128,768]{1,0:T(8,128)(2,1)S(1)}, bf16[128,768]{1,0:T(8,128)(2,1)S(1)}, u32[]{:S(2)}, u32[]{:S(2)}) collective-permute-start(bf16[128,768]{1,0:T(8,128)(2,1)S(1)} %fusion.55), channel_id=1, source_target_pairs={{0,2},{2,0},{1,3},{3,1},{4,6},{6,4},{5,7},{7,5},{8,10},{10,8},{9,1... | collective-permute-start | bytes 589832 | tf_op jit(solution)/shard_map/ppermute | solution.py:94
  231.8 8.4 %collective-permute-start.49 = (bf16[192,768]{1,0:T(8,128)(2,1)S(1)}, bf16[192,768]{1,0:T(8,128)(2,1)S(1)}, u32[]{:S(2)}, u32[]{:S(2)}) collective-permute-start(bf16[192,768]{1,0:T(8,128)(2,1)S(1)} %select_convert_fusion.2), channel_id=1, source_target_pairs={{24,16},{28,20},{16,8},{20,12},{25,17},{29,21},{17,9},{21,13},{26,... | collective-permute-start | bytes 884744 | tf_op jit(solution)/shard_map/ppermute | solution.py:156
  232.6 10.3 %collective-permute-start.48 = (bf16[192,768]{1,0:T(8,128)(2,1)S(1)}, bf16[192,768]{1,0:T(8,128)(2,1)S(1)}, u32[]{:S(2)}, u32[]{:S(2)}) collective-permute-start(bf16[192,768]{1,0:T(8,128)(2,1)S(1)} %select_convert_fusion.2), channel_id=1, source_target_pairs={{0,8},{4,12},{8,16},{12,20},{1,9},{5,13},{9,17},{13,21},{2,10},{6,... | collective-permute-start | bytes 884744 | tf_op jit(solution)/shard_map/ppermute | solution.py:156
  238.7 21.5 %collective-permute-start.36 = (bf16[128,768]{1,0:T(8,128)(2,1)S(1)}, bf16[128,768]{1,0:T(8,128)(2,1)S(1)}, u32[]{:S(2)}, u32[]{:S(2)}) collective-permute-start(bf16[128,768]{1,0:T(8,128)(2,1)S(1)} %fusion.54), channel_id=1, source_target_pairs={{0,2},{2,0},{1,3},{3,1},{4,6},{6,4},{5,7},{7,5},{8,10},{10,8},{9,1... | collective-permute-start | bytes 589832 | tf_op jit(solution)/shard_map/ppermute | solution.py:94
  243.2 9.0 %collective-permute-start.51 = (bf16[192,768]{1,0:T(8,128)(2,1)S(1)}, bf16[192,768]{1,0:T(8,128)(2,1)S(1)}, u32[]{:S(2)}, u32[]{:S(2)}) collective-permute-start(bf16[192,768]{1,0:T(8,128)(2,1)S(1)} %get-tuple-element.26), channel_id=1, source_target_pairs={{0,8},{4,12},{8,16},{12,20},{16,24},{20,28},{1,9},{5,13},{9,17},{1... | collective-permute-start | bytes 884744 | tf_op jit(solution)/shard_map/ppermute | solution.py:156
  247.8 9.0 %collective-permute-start.52 = (bf16[192,768]{1,0:T(8,128)(2,1)S(1)}, bf16[192,768]{1,0:T(8,128)(2,1)S(1)}, u32[]{:S(2)}, u32[]{:S(2)}) collective-permute-start(bf16[192,768]{1,0:T(8,128)(2,1)S(1)} %get-tuple-element.27), channel_id=1, source_target_pairs={{24,16},{28,20},{16,8},{20,12},{8,0},{12,4},{25,17},{29,21},{17,9}... | collective-permute-start | bytes 884744 | tf_op jit(solution)/shard_map/ppermute | solution.py:156
  (109 other events, 665.9 us)

commit v2 on v1

--- a/solution.py
+++ b/solution.py
@@ -42,52 +42,46 @@
     return lax.dynamic_index_in_dim(values, index, 0, keepdims=False)
 
 
+CHIP_SWAP = [(0, 2), (2, 0), (1, 3), (3, 1)]
+CORE_SWAP = [(0, 1), (1, 0), (2, 3), (3, 2)]
+
+
+def in_order(second, mine, other, axis=0):
+    return jnp.stack([jnp.where(second, other, mine), jnp.where(second, mine, other)], axis=axis)
+
+
 def seq_exchange(blocks):
     n = lax.axis_size("seq")
     if n != 4:
         return lax.all_to_all(blocks, "seq", 0, 0)
     me = lax.axis_index("seq")
-    got = [pick(blocks, me)]
-    for other in (1, 2, 3):
-        pairs = [(i, i ^ other) for i in range(n)]
-        got.append(lax.ppermute(pick(blocks, me ^ other), "seq", pairs))
-    return jnp.stack(
-        [
-            jnp.where(
-                me < 2,
-                jnp.where(me == 0, got[j], got[j ^ 1]),
-                jnp.where(me == 2, got[j ^ 2], got[j ^ 3]),
-            )
-            for j in range(n)
-        ]
-    )
-
-
-CHIP_SWAP = [(0, 2), (2, 0), (1, 3), (3, 1)]
-CORE_SWAP = [(0, 1), (1, 0), (2, 3), (3, 2)]
+    chip, core = me // 2, me % 2
+    halves = blocks.reshape((2, 2) + blocks.shape[1:])
+    far = lax.ppermute(pick(halves, 1 - chip), "seq", CHIP_SWAP)
+    by_chip = in_order(chip == 1, pick(halves, chip), far, axis=1)
+    other = lax.ppermute(pick(by_chip, 1 - core), "seq", CORE_SWAP)
+    return in_order(core == 1, pick(by_chip, core), other, axis=1).reshape(blocks.shape)
 
 
 def seq_gather(values):
     n = lax.axis_size("seq")
     if n != 4:
-        return lax.all_gather(values, "seq", axis=0, tiled=True)
+        return lax.all_gather(values, "seq", axis=0)
     me = lax.axis_index("seq")
     chip, core = me // 2, me % 2
     far = lax.ppermute(values, "seq", CHIP_SWAP)
-    mine = jnp.stack([jnp.where(chip == 0, values, far), jnp.where(chip == 0, far, values)])
+    mine = in_order(chip == 1, values, far)
     other = lax.ppermute(mine, "seq", CORE_SWAP)
-    full = jnp.stack([jnp.where(core == 0, mine, other), jnp.where(core == 0, other, mine)], axis=1)
-    return full.reshape((n * values.shape[0],) + values.shape[1:])
+    return in_order(core == 1, mine, other, axis=1).reshape((n,) + values.shape)
 
 
 def seq_reduce(values):
     n = lax.axis_size("seq")
     if n != 4:
-        return lax.psum_scatter(values.astype(BF), "seq", scatter_dimension=0, tiled=True).astype(F32)
+        return lax.psum_scatter(values.astype(BF), "seq", scatter_dimension=0).astype(F32)
     me = lax.axis_index("seq")
     chip, core = me // 2, me % 2
-    rows = values.shape[0] // n
-    parts = values.reshape((2, 2, rows) + values.shape[1:])
+    parts = values.reshape((2, 2) + values.shape[1:])
     keep = lax.dynamic_index_in_dim(parts, core, 1, keepdims=False)
     give = lax.dynamic_index_in_dim(parts, 1 - core, 1, keepdims=False).astype(BF)
     both = keep.astype(F32) + lax.ppermute(give, "seq", CORE_SWAP).astype(F32)
@@ -98,12 +92,8 @@
 SIDE_SWAP = [(i, i ^ 1) for i in range(8)]
 
 
-def up_pairs(*places):
-    return [(2 * p + y, 2 * p + 2 + y) for p in places for y in (0, 1)]
-
-
-def down_pairs(*places):
-    return [(2 * p + y, 2 * p - 2 + y) for p in places for y in (0, 1)]
+def along(step):
+    return [(i, (i + 2 * step) % 8) for i in range(8)]
 
 
 def dp_gather(block):
@@ -112,35 +102,17 @@
         return lax.all_gather(block, "dp", axis=0)
     me = lax.axis_index("dp")
     line, side = me // 2, me % 2
-
-    def send(values, pairs):
-        return lax.ppermute(values, "dp", pairs)
-
-    up1 = send(block, up_pairs(0, 1, 2))
-    down1 = send(block, down_pairs(1, 2, 3))
-    side0 = send(block, SIDE_SWAP)
-    up2 = send(up1, up_pairs(1, 2))
-    down2 = send(down1, down_pairs(2, 1))
-    first = jnp.where(line == 0, down1, up1)
-    side1 = send(first, SIDE_SWAP)
-    second = jnp.where(line < 2, down2, up2)
-    end3 = send(second, up_pairs(2) + down_pairs(1))
-    side2 = send(second, SIDE_SWAP)
-    third = jnp.where((line == 0) | (line == 3), end3, down1)
-    side3 = send(third, SIDE_SWAP)
-    source1 = jnp.where(line == 0, 1, line - 1)
-    source2 = jnp.where(line < 2, line + 2, line - 2)
-    source3 = jnp.where(line == 0, 3, jnp.where(line == 3, 0, line + 1))
+    near1 = lax.ppermute(block, "dp", along(1))
+    near3 = lax.ppermute(block, "dp", along(3))
+    near2 = lax.ppermute(block, "dp", along(2))
+    far0 = lax.ppermute(block, "dp", SIDE_SWAP)
+    far13 = lax.ppermute(jnp.stack([near1, near3]), "dp", SIDE_SWAP)
+    far2 = lax.ppermute(near2, "dp", SIDE_SWAP)
     full = jnp.zeros((4, 2) + block.shape, block.dtype)
     zero = jnp.int32(0)
-    for where, near, far in (
-        (line, block, side0),
-        (source1, first, side1),
-        (source2, second, side2),
-        (source3, third, side3),
-    ):
-        pair = jnp.stack([jnp.where(side == 0, near, far), jnp.where(side == 0, far, near)])
-        full = lax.dynamic_update_slice(full, pair[None], (where, zero, zero, zero))
+    for step, near, far in ((0, block, far0), (1, near1, far13[0]), (3, near3, far13[1]), (2, near2, far2)):
+        pair = in_order(side == 1, near, far)
+        full = lax.dynamic_update_slice(full, pair[None], ((line - step) % 4, zero, zero, zero))
     return full.reshape((n,) + block.shape)
 
 
@@ -152,29 +124,18 @@
     me = lax.axis_index("dp")
     line, side = me // 2, me % 2
 
-    def send(values, pairs):
-        return lax.ppermute(values.astype(BF), "dp", pairs).astype(F32)
-
-    ahead = line < 2
-
-    def over_side(target):
-        moved = send(block_of(2 * target + 1 - side), SIDE_SWAP)
-        return block_of(2 * target + side).astype(F32) + moved
-
-    sum_a = over_side(jnp.where(ahead, 3, 0))
-    sum_b = over_side(jnp.where(ahead, 2, 1))
-    sum_c = over_side(jnp.where(ahead, 1 - line, 5 - line))
-    sum_d = over_side(line)
-    sum_a = sum_a + send(sum_a, up_pairs(0) + down_pairs(3))
-    end = (line == 0) | (line == 3)
-    second = jnp.where(end, sum_b, sum_a)
-    up2 = send(second, up_pairs(0, 1))
-    down2 = send(second, down_pairs(3, 2))
-    sum_b = sum_b + jnp.where(ahead, up2, down2)
-    sum_c = sum_c + jnp.where(ahead, down2, up2)
-    up3 = send(jnp.where(line == 1, sum_b, sum_c), up_pairs(0, 1, 2))
-    down3 = send(jnp.where(line == 2, sum_b, sum_c), down_pairs(3, 2, 1))
-    return sum_d + up3 + down3
+    def over_side(*steps):
+        targets = [2 * ((line + step) % 4) for step in steps]
+        moved = lax.ppermute(jnp.stack([block_of(t + 1 - side) for t in targets]), "dp", SIDE_SWAP)
+        return [block_of(t + side).astype(F32) + moved[j].astype(F32) for j, t in enumerate(targets)]
+
+    (sum2,) = over_side(2)
+    sum1, sum3 = over_side(1, 3)
+    (sum0,) = over_side(0)
+    got2 = lax.ppermute(sum2.astype(BF), "dp", along(2)).astype(F32)
+    got1 = lax.ppermute(sum1.astype(BF), "dp", along(1)).astype(F32)
+    got3 = lax.ppermute(sum3.astype(BF), "dp", along(3)).astype(F32)
+    return sum0 + got1 + got2 + got3
 
 
 def attention(queries, keys, values, d_out, segment, scale):
@@ -256,24 +217,39 @@
         axis=1,
     )
     got = seq_exchange(blocks)
-    up_piece = got[:, :deep, :own_units].reshape(n_seq * deep, own_units)
-    qkv_piece = got[:, :deep, own_units:].reshape(n_seq * deep, 3 * own)
+    per_line = n_seq * deep
+    up_rows = per_line * own_units // width
+    up_piece = got[:, :deep, :own_units].reshape(up_rows, width)
+    qkv_piece = got[:, :deep, own_units:].reshape(per_line, 3 * own)
     group_vector = got[:, deep, :length]
 
-    hidden_group = seq_gather(hidden_in)
-    grad_group = seq_gather(grad_out)
-
-    up_rows = n_seq * deep * own_units // width
-    mlp_all = dp_gather(jnp.concatenate([up_piece.reshape(up_rows, width), down_weight], axis=0))
-    qkv_all = dp_gather(qkv_piece)
-    vec_rows = -(-n_seq * length // width)
-    vec_piece = jnp.pad(group_vector.reshape(-1), (0, vec_rows * width - n_seq * length))
-    dense_all = dp_gather(jnp.concatenate([dense_weight, vec_piece.reshape(vec_rows, width)], axis=0))
+    both = seq_gather(jnp.concatenate([hidden_in, grad_out], axis=0))
+    hidden_group = both[:, :rows].reshape(group, width)
+    grad_group = both[:, rows:].reshape(group, width)
+
+    def beside(values):
+        lead = values.shape[:-2]
+        split = values.reshape(lead + (deep, n_seq, width // n_seq))
+        return jnp.swapaxes(split, -3, -2).reshape(lead + (per_line, width // n_seq))
+
+    def from_beside(values):
+        lead = values.shape[:-2]
+        split = values.reshape(lead + (n_seq, deep, width // n_seq))
+        return jnp.swapaxes(split, -3, -2).reshape(lead + (deep, width))
+
+    attn_wide = 3 * own + width // n_seq
+    vec_rows = -(-n_seq * length // attn_wide)
+    vec_rows += -vec_rows % 8
+    vec_piece = jnp.pad(group_vector.reshape(-1), (0, vec_rows * attn_wide - n_seq * length))
+    attn_piece = jnp.concatenate([qkv_piece, beside(dense_weight)], axis=1)
+    attn_piece = jnp.concatenate([attn_piece, vec_piece.reshape(vec_rows, attn_wide)], axis=0)
+    attn_all = dp_gather(attn_piece)
+    mlp_all = dp_gather(jnp.concatenate([up_piece, down_weight], axis=0))
+    qkv_full = attn_all[:, :per_line, : 3 * own].reshape(width, 3 * own)
+    dense_rows = from_beside(attn_all[:, :per_line, 3 * own :]).reshape(n_dp * deep, width)
     up_full = mlp_all[:, :up_rows].reshape(width, own_units)
     down_full = mlp_all[:, up_rows:].reshape(own_units, width)
-    qkv_full = qkv_all.reshape(width, 3 * own)
-    dense_rows = dense_all[:, :deep].reshape(n_dp * deep, width)
-    every = dense_all[:, deep:].reshape(n_dp, vec_rows * width)[:, : n_seq * length]
+    every = attn_all[:, per_line:].reshape(n_dp, vec_rows * attn_wide)[:, : n_seq * length]
     every = every.reshape(n_dp * n_seq, length).astype(F32)
     whole = []
     start = 0
@@ -301,25 +277,12 @@
     attn_in = (unit * f_attn_gain + f_attn_shift).astype(BF)
     mlp_in = (unit * f_mlp_gain + f_mlp_shift).astype(BF)
 
-    upper = dot("td,df->tf", mlp_in, up_full) + own_up_bias
-    cdf = 0.5 * (1.0 + lax.erf(upper * F32(0.7071067811865476)))
-    pdf = jnp.exp(-0.5 * upper * upper) * F32(0.3989422804014327)
-    act = (upper * cdf).astype(BF)
-    d_act = dot("td,fd->tf", grad_group, down_full)
-    d_up = (d_act * (cdf + upper * pdf)).astype(BF)
-    down_grad = dot("tf,td->fd", act, grad_group).astype(BF).reshape(n_dp, unit_rows, width)
-    up_grad = dot("td,tf->df", mlp_in, d_up).astype(BF).reshape(n_dp, up_rows, width)
-    mlp_out = dot("tf,fd->td", act, down_full)
-    d_mlp_in = dot("tf,df->td", d_up, up_full)
-    mlp_sum = dp_reduce(lambda i: jnp.concatenate([pick(up_grad, i), pick(down_grad, i)], axis=0))
-
     joined = dot("td,de->te", attn_in, qkv_full) + own_qkv_bias
     joined = joined.reshape(group, 3, heads, HEAD_DIM)
     queries = jnp.moveaxis(rotate(joined[:, 0], cosine, sine, 1.0).astype(BF), 1, 0)
     keys = jnp.moveaxis(rotate(joined[:, 1], cosine, sine, 1.0).astype(BF), 1, 0)
     values = jnp.moveaxis(joined[:, 2].astype(BF), 1, 0)
     feature_rows = n_dp * deep
-    per_line = n_seq * deep
     direct = spare == 0 and own % per_line == 0
     d_rows = dot("fe,te->ft", dense_rows, grad_group).astype(BF)
     if direct:
@@ -344,13 +307,26 @@
             given.reshape(n_dp, n_seq, deep, group), me, 1, keepdims=False
         ).reshape(feature_rows, group)
     attn_out = dot("ft,fe->te", rows_attended, dense_rows)
-    dense_grad = dot("ft,te->fe", rows_attended, grad_group).reshape(n_dp, deep, width)
+    dense_grad = dot("ft,te->fe", rows_attended, grad_group).astype(BF).reshape(n_dp, deep, width)
     d_queries = rotate(jnp.moveaxis(d_queries, 0, 1), cosine, sine, -1.0)
     d_keys = rotate(jnp.moveaxis(d_keys, 0, 1), cosine, sine, -1.0)
     d_joined = jnp.stack([d_queries, d_keys, jnp.moveaxis(d_values, 0, 1)], axis=1)
     d_joined = d_joined.astype(BF).reshape(group, 3 * own)
     qkv_grad = dot("td,te->de", attn_in, d_joined).astype(BF).reshape(n_dp, n_seq * deep, 3 * own)
     d_attn_in = dot("te,de->td", d_joined, qkv_full)
+    attn_terms = jnp.concatenate([qkv_grad, beside(dense_grad)], axis=2)
+    attn_sum = dp_reduce(lambda i: pick(attn_terms, i))
+
+    upper = dot("td,df->tf", mlp_in, up_full) + own_up_bias
+    cdf = 0.5 * (1.0 + lax.erf(upper * F32(0.7071067811865476)))
+    pdf = jnp.exp(-0.5 * upper * upper) * F32(0.3989422804014327)
+    act = (upper * cdf).astype(BF)
+    d_act = dot("td,fd->tf", grad_group, down_full)
+    d_up = (d_act * (cdf + upper * pdf)).astype(BF)
+    down_grad = dot("tf,td->fd", act, grad_group).astype(BF).reshape(n_dp, unit_rows, width)
+    up_grad = dot("td,tf->df", mlp_in, d_up).astype(BF).reshape(n_dp, up_rows, width)
+    mlp_out = dot("tf,fd->td", act, down_full)
+    d_mlp_in = dot("tf,df->td", d_up, up_full)
 
     mine = jnp.arange(n_seq) == me
     qkv_bias_grad = jnp.sum(d_joined.astype(F32), axis=0)
@@ -370,14 +346,17 @@
     )
     terms = [t.reshape(n_dp, n_seq, size) for t, size in zip(terms, sizes)]
     terms = jnp.concatenate(terms, axis=2).reshape(n_dp, n_seq * length)
-    terms = jnp.pad(terms, ((0, 0), (0, vec_rows * width - n_seq * length)))
-    terms = terms.reshape(n_dp, vec_rows, width)
-    dense_terms = jnp.concatenate([dense_grad, terms], axis=1).astype(BF)
-    qkv_sum = dp_reduce(lambda i: pick(qkv_grad, i))
-    dense_sum = dp_reduce(lambda i: pick(dense_terms, i))
-
-    block_out = hidden_in.astype(F32) + f_dense_bias + f_down_bias + seq_reduce(attn_out + mlp_out)
-    upstream = seq_reduce(d_attn_in * f_attn_gain + d_mlp_in * f_mlp_gain)
+    tail_rows = -(-n_seq * length // width)
+    tail_rows += -tail_rows % 8
+    terms = jnp.pad(terms, ((0, 0), (0, tail_rows * width - n_seq * length)))
+    terms = terms.reshape(n_dp, tail_rows, width).astype(BF)
+    mlp_sum = dp_reduce(lambda i: jnp.concatenate([pick(up_grad, i), pick(down_grad, i), pick(terms, i)], axis=0))
+
+    upstream = d_attn_in * f_attn_gain + d_mlp_in * f_mlp_gain
+    pair = jnp.concatenate([(attn_out + mlp_out).astype(BF), upstream.astype(BF)], axis=1)
+    pair = seq_reduce(pair.reshape(n_seq, rows, 2 * width))
+    block_out = hidden_in.astype(F32) + f_dense_bias + f_down_bias + pair[:, :width]
+    upstream = pair[:, width:]
     x = hidden_in.astype(F32)
     centered = x - jnp.mean(x, axis=-1, keepdims=True)
     inverse = lax.rsqrt(jnp.mean(centered * centered, axis=-1, keepdims=True) + EPS)
@@ -389,25 +368,16 @@
     )
     grad_in = grad_out.astype(F32) + inverse * inner
 
-    vec_sum = dense_sum[deep:].reshape(-1)[: n_seq * length].reshape(n_seq, 1, length)
-    vec_sum = jnp.pad(vec_sum, ((0, 0), (0, 0), (0, wide - length)))
-    back = jnp.concatenate(
-        [
-            jnp.concatenate(
-                [
-                    mlp_sum[:up_rows].reshape(n_seq, deep, own_units),
-                    qkv_sum.reshape(n_seq, deep, 3 * own),
-                ],
-                axis=2,
-            ),
-            vec_sum,
-        ],
-        axis=1,
-    )
+    qkv_back = attn_sum[:, : 3 * own].reshape(n_seq, deep, 3 * own).astype(BF)
+    qkv_own = from_heads(seq_exchange(qkv_back).astype(F32))
+    dense_own = from_beside(attn_sum[:, 3 * own :])
+    vec_sum = mlp_sum[up_rows + unit_rows :].reshape(-1)[: n_seq * length].reshape(n_seq, 1, length)
+    vec_sum = jnp.pad(vec_sum, ((0, 0), (0, 0), (0, -length % own_units)))
+    vec_sum = vec_sum.reshape(n_seq, -1, own_units)
+    back = jnp.concatenate([mlp_sum[:up_rows].reshape(n_seq, deep, own_units), vec_sum], axis=1)
     back = seq_exchange(back.astype(BF)).astype(F32)
-    up_own = jnp.moveaxis(back[:, :deep, :own_units].reshape(n_seq, deep, n_dp, unit_rows), 0, 2)
-    qkv_own = from_heads(back[:, :deep, own_units:])
-    vec_own = jnp.sum(back[:, deep, :length], axis=0)
+    up_own = jnp.moveaxis(back[:, :deep].reshape(n_seq, deep, n_dp, unit_rows), 0, 2)
+    vec_own = jnp.sum(back[:, deep:].reshape(n_seq, -1), axis=0)
     owned = []
     start = 0
     for size in sizes:
@@ -422,11 +392,11 @@
         owned[3],
         qkv_own,
         owned[4],
-        dense_sum[:deep],
+        dense_own,
         owned[5],
         up_own.reshape(deep, hidden_units),
         owned[6],
-        mlp_sum[up_rows:],
+        mlp_sum[up_rows : up_rows + unit_rows],
         owned[7],
     )
 

time: 271 us -> 234 us (0.86)
  starting transfers between devices: 114 us -> 49.2 us
  local copies, waits for them, and re-layouts: 30.9 us -> 56.1 us
  other arithmetic: 30.1 us -> 34.4 us
    ppermute x66 -> x34, starting transfers between devices: 108 us -> 48.4 us  [the longest x5 7.16 us: seq_exchange(): far = lax.ppermute(pick(halves, 1 - chip), 'seq', CHIP_SWAP)]
    another operation x31 -> x41, other arithmetic: 6.37 us -> 17 us  [the longest x26 9.53 us: in_order(): jnp.stack([jnp.where(second, other, mine), jnp.where(second, mine, other)...]
    ppermute x66 -> x34, waiting for transfers between devices: 63.7 us -> 55.8 us  [the longest x2 11.7 us: dp_gather(): near3 = lax.ppermute(block, 'dp', along(3))]
    ppermute x2 -> x1, waiting for transfers between devices: 0.01 us -> 5.98 us  [seq_reduce(): far = lax.ppermute(pick(both, 1 - chip).astype(BF), 'seq', CHIP_SWAP)]
    slice x3, local copies, waits for them, and re-layouts: 0.22 us -> 4.43 us  [per_device(): whole.append(every[:, start:start + size].reshape(-1))]
    select_n x7 -> x0, other arithmetic: 3.79 us -> none  [the longest x3 1.74 us: dp_gather(): second = jnp.where(line < 2, down2, up2)]
    ppermute x2 -> x1, starting transfers between devices: 3.08 us -> 0.09 us  [seq_gather(): far = lax.ppermute(values, 'seq', CHIP_SWAP)]
    unnamed x167 -> x146, local copies, waits for them, and re-layouts: 6.1 us -> 3.21 us
  transfers between devices with their start and end apart: 74 -> 38, of which waited for: 24 -> 12; matrix products, arithmetic and copies ran while one was open for 26% -> 40% of each run, Pallas kernels for 0% -> 0%
where the time goes in v2:
time: 234 us; the launch traced here: 232 us
  waiting for transfers between devices  61.8 us (26%)
  local copies, waits for them, and re-layouts  56.1 us (24%)
  starting transfers between devices  49.2 us (21%)
  other arithmetic  34.4 us (15%)
  matrix products  28.2 us (12%)
  between operations  2.58 us (1%)
    dot_general x17, matrix products, dot(): return jnp.einsum(spec, a, b, preferred_element_type=F32)  24.5 us
    ppermute x2, waiting for transfers between devices, dp_gather(): near3 = lax.ppermute(block, 'dp', along(3))  11.7 us
    ppermute x2, waiting for transfers between devices, dp_gather(): near2 = lax.ppermute(block, 'dp', along(2))  11.6 us
    ppermute x2, waiting for transfers between devices, dp_reduce(): got2 = lax.ppermute(sum2.astype(BF), 'dp', along(2)).astype(F32)  10 us
    another operation x26, other arithmetic, in_order(): jnp.stack([jnp.where(second, other, mine), jnp.where(second, mine, other)...  9.53 us
    ppermute x6, waiting for transfers between devices, over_side(): lax.ppermute(jnp.stack([block_of(t + 1 - side) for t in targets]), 'dp',...  8.99 us
    ppermute x5, starting transfers between devices, seq_exchange(): far = lax.ppermute(pick(halves, 1 - chip), 'seq', CHIP_SWAP)  7.16 us
    ppermute x2, starting transfers between devices, dp_reduce(): got3 = lax.ppermute(sum3.astype(BF), 'dp', along(3)).astype(F32)  6.67 us
  transfers between devices with their start and end apart: 38, of which 12 were waited for; matrix products, arithmetic and copies ran while one was open for 40% of the time, Pallas kernels for 0%

profile of v2, /device:TPU:0, one launch (start us, length us, event | category | flops | bytes accessed | tf_op | source)
XLA Modules:
  0.0 232.3 jit_solution(12293790409436354763)
XLA Ops:
  3.9 3.0 %collective-permute-start = (bf16[2,25,1344]{2,0,1:T(2,128)(2,1)S(1)}, bf16[2,25,1344]{2,0,1:T(2,128)(2,1)S(1)}, u32[]{:S(2)}, u32[]{:S(2)}) collective-permute-start(bf16[2,25,1344]{2,0,1:T(2,128)(2,1)S(1)} %bitcast.552), channel_id=1, source_target_pairs={{0,2},{2,0},{1,3},{3,1},{4,6},{6,4},{5,7},{7,5},{8,10},{10,8},{9,1... | collective-permute-start | bytes 403208 | tf_op jit(solution)/shard_map/ppermute | solution.py:60
  9.4 2.1 collective-permute-done
  16.4 3.2 %collective-permute-start.6 = (bf16[104,768]{1,0:T(8,128)(2,1)S(1)}, bf16[104,768]{1,0:T(8,128)(2,1)S(1)}, u32[]{:S(2)}, u32[]{:S(2)}) collective-permute-start(bf16[104,768]{1,0:T(8,128)(2,1)S(1)} %pad_maximum_fusion.13), channel_id=1, source_target_pairs={{0,16},{4,20},{8,24},{12,28},{16,0},{20,4},{24,8},{28,12},{1,17},{... | collective-permute-start | bytes 479240 | tf_op jit(solution)/shard_map/ppermute | solution.py:107
  19.6 1.6 collective-permute-start.3
  21.2 2.2 collective-permute-start.4
  23.4 1.5 collective-permute-start.2
  26.2 2.9 %collective-permute-done.2 = bf16[104,768]{1,0:T(8,128)(2,1)S(1)} collective-permute-done((bf16[104,768]{1,0:T(8,128)(2,1)S(1)}, bf16[104,768]{1,0:T(8,128)(2,1)S(1)}, u32[]{:S(2)}, u32[]{:S(2)}) %collective-permute-start.2) | collective-permute-done | bytes 159776 | tf_op jit(solution)/shard_map/ppermute | solution.py:108
  31.1 9.1 %collective-permute-done.4 = bf16[104,768]{1,0:T(8,128)(2,1)S(1)} collective-permute-done((bf16[104,768]{1,0:T(8,128)(2,1)S(1)}, bf16[104,768]{1,0:T(8,128)(2,1)S(1)}, u32[]{:S(2)}, u32[]{:S(2)}) %collective-permute-start.4) | collective-permute-done | bytes 159776 | tf_op jit(solution)/shard_map/ppermute | solution.py:106
  41.0 1.8 collective-permute-start.5
  42.9 2.6 %collective-permute-done.14 = bf16[192,768]{1,0:T(8,128)(2,1)S(1)} collective-permute-done((bf16[192,768]{1,0:T(8,128)(2,1)S(1)}, bf16[192,768]{1,0:T(8,128)(2,1)S(1)}, u32[]{:S(2)}, u32[]{:S(2)}) %collective-permute-start.14) | collective-permute-done | bytes 294944 | tf_op jit(solution)/shard_map/ppermute | solution.py:106
  45.5 1.6 collective-permute-start.7
  48.5 11.6 %collective-permute-done.16 = bf16[192,768]{1,0:T(8,128)(2,1)} collective-permute-done((bf16[192,768]{1,0:T(8,128)(2,1)S(1)}, bf16[192,768]{1,0:T(8,128)(2,1)}, u32[]{:S(2)}, u32[]{:S(2)}) %collective-permute-start.16) | collective-permute-done | bytes 294944 | tf_op jit(solution)/shard_map/ppermute | solution.py:107
  60.1 1.6 collective-permute-start.17
  69.1 1.6 fusion.113
  80.3 1.9 copy.183
  82.3 2.0 reshape_reshape.40
  93.1 1.6 fusion.111
  101.4 3.8 %fusion.115 = (f32[3,512]{1,0:T(4,128)}, f32[3,512,512]{1,2,0:T(8,128)}) fusion(pred[512,512]{0,1:T(8,128)(4,1)S(1)} %copy-done.37, bf16[512,3,48]{0,2,1:T(8,128)(2,1)S(1)} %slice.373, bf16[512,3,8]{0,2,1:T(8,128)(2,1)S(1)} %get-tuple-element.137, bf16[512,3,8]{0,2,1:T(8,128)(2,1)S(1)} %get-tuple-element.138, bf16[512,3,48]{0,2,1:T(8,128)(2,1)S(1)} %slice.374, ...), kind=kOutput, calls=%fused_computation.348 | convolution fusion | flops 105775616 | bytes 3807232 | tf_op jit(solution)/shard_map/sub | solution.py:148
  105.2 2.4 %convolution_convert_fusion.5 = bf16[3,64,512]{2,1,0:T(8,128)(2,1)S(1)} fusion(f32[512,3,3,64]{0,3,2,1:T(8,128)} %bitcast.537, f32[3,512,512]{1,2,0:T(8,128)} %get-tuple-element.153, f32[3,512]{1,0:T(4,128)} %get-tuple-element.152), kind=kOutput, calls=%fused_computation.54 | convolution fusion | flops 102334464 | bytes 3547136 | tf_op jit(solution)/shard_map/htn,hnd->htd/dot_general | solution.py:16
  108.3 1.5 collective-permute-start.10
  112.3 1.9 convolution_convert_fusion
  114.2 2.6 %convert_reduce_fusion = (bf16[768]{0:T(1024)(128)(2,1)}, bf16[512,768]{1,0:T(8,128)(2,1)}) fusion(f32[512,768]{1,0:T(8,128)S(1)} %get-tuple-element.157, bf16[512,768]{1,0:T(8,128)(2,1)S(1)} %bitcast.491, bf16[768,768]{1,0:T(8,128)(2,1)S(1)} %bitcast.518), kind=kOutput, calls=%fused_computation.26 | convolution fusion | flops 608697600 | bytes 4326912 | tf_op jit(solution)/shard_map/td,fd->tf/dot_general | solution.py:16
  119.5 2.5 %dynamic-slice_bitcast_fusion.15 = (bf16[96,768]{1,0:T(8,128)(2,1)}, bf16[96,768]{1,0:T(8,128)(2,1)}, bf16[96,768]{1,0:T(8,128)(2,1)}, bf16[96,768]{1,0:T(8,128)...) fusion(bf16[8,96,768]{2,1,0:T(8,128)(2,1)} %bitcast.515, ...), kind=kLoop, calls=%fused_computation.228 | loop fusion | bytes 2359328 | tf_op jit(solution)/shard_map/jit(dynamic_index_in_dim)/squeeze | solution.py:42
  124.6 1.6 multiply_reduce_fusion
  130.5 2.0 fusion.117
  132.4 1.5 convolution_convert_fusion.2
  134.3 1.6 fusion.116
  136.3 1.5 copy.196
  140.0 1.6 collective-permute-start.33
  142.0 4.0 %multiply_reduce_fusion.1 = (bf16[768]{0:T(1024)(128)(2,1)S(1)}, bf16[768]{0:T(1024)(128)(2,1)S(1)}, bf16[768]{0:T(1024)(128)(2,1)S(1)}, bf16[768]{0:T(1024)(128...) fusion(f32[512]{0:T(512)S(1)} %copy-done.57, f32[512]{0:T(512)S(1)} %copy-done.56, ...), kind=kOutput, calls=%fused_computation.27 | convolution fusion | flops 610268160 | bytes 5917696 | tf_op jit(solution)/shard_map/tf,df->td/dot_general | solution.py:16
  150.2 1.7 maximum_bitcast_fusion.8
  151.9 1.6 collective-permute-start.22
  153.4 2.3 add_convert_fusion.2
  158.6 6.4 %collective-permute-start.32 = (bf16[96,768]{1,0:T(8,128)(2,1)S(1)}, bf16[96,768]{1,0:T(8,128)(2,1)S(1)}, u32[]{:S(2)}, u32[]{:S(2)}) collective-permute-start(bf16[96,768]{1,0:T(8,128)(2,1)S(1)} %get-tuple-element.31), channel_id=1, source_target_pairs={{0,8},{4,12},{8,16},{12,20},{16,24},{20,28},{24,0},{28,4},{1,9},{5... | collective-permute-start | bytes 442376 | tf_op jit(solution)/shard_map/ppermute | solution.py:136
  165.0 2.0 collective-permute-start.34
  167.0 2.8 %collective-permute-start.35 = (bf16[96,768]{1,0:T(8,128)(2,1)S(1)}, bf16[96,768]{1,0:T(8,128)(2,1)S(1)}, u32[]{:S(2)}, u32[]{:S(2)}) collective-permute-start(bf16[96,768]{1,0:T(8,128)(2,1)S(1)} %get-tuple-element.32), channel_id=1, source_target_pairs={{0,24},{4,28},{8,0},{12,4},{16,8},{20,12},{24,16},{28,20},{1,25},{... | collective-permute-start | bytes 442376 | tf_op jit(solution)/shard_map/ppermute | solution.py:137
  170.7 1.5 collective-permute-start.25
  172.8 2.3 collective-permute-done.34
  176.2 1.5 collective-permute-start.36
  177.7 3.2 %collective-permute-done.25 = bf16[1,200,768]{2,1,0:T(8,128)(2,1)S(1)} collective-permute-done((bf16[1,200,768]{2,1,0:T(8,128)(2,1)S(1)}, bf16[1,200,768]{2,1,0:T(8,128)(2,1)S(1)}, u32[]{:S(2)}, u32[]{:S(2)}) %collective-permute-start.25) | collective-permute-done | bytes 307232 | tf_op jit(solution)/shard_map/ppermute | solution.py:129
  181.7 2.8 %collective-permute-start.26 = (bf16[200,768]{1,0:T(8,128)(2,1)}, bf16[200,768]{1,0:T(8,128)(2,1)}, u32[]{:S(2)}, u32[]{:S(2)}) collective-permute-start(bf16[200,768]{1,0:T(8,128)(2,1)} %fusion.19), channel_id=1, source_target_pairs={{0,16},{4,20},{8,24},{12,28},{16,0},{20,4},{24,8},{28,12},{1,17},{... | collective-permute-start | bytes 921608 | tf_op jit(solution)/shard_map/ppermute | solution.py:135
  185.5 5.8 %collective-permute-done.23 = bf16[2,200,768]{2,1,0:T(8,128)(2,1)} collective-permute-done((bf16[2,200,768]{2,1,0:T(8,128)(2,1)}, bf16[2,200,768]{2,1,0:T(8,128)(2,1)}, u32[]{:S(2)}, u32[]{:S(2)}) %collective-permute-start.23) | collective-permute-done | bytes 614432 | tf_op jit(solution)/shard_map/ppermute | solution.py:129
  191.3 2.0 fusion.20
  193.3 3.8 %collective-permute-start.27 = (bf16[200,768]{1,0:T(8,128)(2,1)}, bf16[200,768]{1,0:T(8,128)(2,1)}, u32[]{:S(2)}, u32[]{:S(2)}) collective-permute-start(bf16[200,768]{1,0:T(8,128)(2,1)} %get-tuple-element.70), channel_id=1, source_target_pairs={{0,24},{4,28},{8,0},{12,4},{16,8},{20,12},{24,16},{28,20},{1,25},{... | collective-permute-start | bytes 921608 | tf_op jit(solution)/shard_map/ppermute | solution.py:137
  198.5 7.8 %collective-permute-done.26 = bf16[200,768]{1,0:T(8,128)(2,1)} collective-permute-done((bf16[200,768]{1,0:T(8,128)(2,1)}, bf16[200,768]{1,0:T(8,128)(2,1)}, u32[]{:S(2)}, u32[]{:S(2)}) %collective-permute-start.26) | collective-permute-done | bytes 307232 | tf_op jit(solution)/shard_map/ppermute | solution.py:135
  206.3 6.0 %collective-permute-done.27 = bf16[200,768]{1,0:T(8,128)(2,1)} collective-permute-done((bf16[200,768]{1,0:T(8,128)(2,1)}, bf16[200,768]{1,0:T(8,128)(2,1)}, u32[]{:S(2)}, u32[]{:S(2)}) %collective-permute-start.27) | collective-permute-done | bytes 307232 | tf_op jit(solution)/shard_map/ppermute | solution.py:137
  216.1 2.5 %collective-permute-done.28 = bf16[2,25,768]{2,0,1:T(2,128)(2,1)S(1)} collective-permute-done((bf16[2,25,768]{2,0,1:T(2,128)(2,1)S(1)}, bf16[2,25,768]{2,0,1:T(2,128)(2,1)S(1)}, u32[]{:S(2)}, u32[]{:S(2)}) %collective-permute-start.28) | collective-permute-done | bytes 76832 | tf_op jit(solution)/shard_map/ppermute | solution.py:60
  225.0 6.0 %collective-permute-done.21 = bf16[128,1536]{1,0:T(8,128)(2,1)S(1)} collective-permute-done((bf16[128,1536]{1,0:T(8,128)(2,1)S(1)}, bf16[128,1536]{1,0:T(8,128)(2,1)S(1)}, u32[]{:S(2)}, u32[]{:S(2)}) %collective-permute-start.21) | collective-permute-done | bytes 393248 | tf_op jit(solution)/shard_map/ppermute | solution.py:88
  (388 shorter events, 87.4 us)
Async XLA Ops:
  3.9 7.5 %collective-permute-start = (bf16[2,25,1344]{2,0,1:T(2,128)(2,1)S(1)}, bf16[2,25,1344]{2,0,1:T(2,128)(2,1)S(1)}, u32[]{:S(2)}, u32[]{:S(2)}) collective-permute-start(bf16[2,25,1344]{2,0,1:T(2,128)(2,1)S(1)} %bitcast.552), channel_id=1, source_target_pairs={{0,2},{2,0},{1,3},{3,1},{4,6},{6,4},{5,7},{7,5},{8,10},{10,8},{9,1... | collective-permute-start | bytes 403208 | tf_op jit(solution)/shard_map/ppermute | solution.py:60
  7.0 18.0 %collective-permute-start.8 = (bf16[256,768]{1,0:T(8,128)(2,1)S(1)}, bf16[256,768]{1,0:T(8,128)(2,1)S(1)}, u32[]{:S(2)}, u32[]{:S(2)}) collective-permute-start(bf16[256,768]{1,0:T(8,128)(2,1)S(1)} %get-tuple-element.114), channel_id=1, source_target_pairs={{0,2},{2,0},{1,3},{3,1},{4,6},{6,4},{5,7},{7,5},{8,10},{10,8},{9,1... | collective-permute-start | bytes 1179656 | tf_op jit(solution)/shard_map/ppermute | solution.py:72
  12.7 2.0 collective-permute-start.1
  16.4 24.5 %collective-permute-start.6 = (bf16[104,768]{1,0:T(8,128)(2,1)S(1)}, bf16[104,768]{1,0:T(8,128)(2,1)S(1)}, u32[]{:S(2)}, u32[]{:S(2)}) collective-permute-start(bf16[104,768]{1,0:T(8,128)(2,1)S(1)} %pad_maximum_fusion.13), channel_id=1, source_target_pairs={{0,16},{4,20},{8,24},{12,28},{16,0},{20,4},{24,8},{28,12},{1,17},{... | collective-permute-start | bytes 479240 | tf_op jit(solution)/shard_map/ppermute | solution.py:107
  19.6 10.5 %collective-permute-start.3 = (bf16[104,768]{1,0:T(8,128)(2,1)S(1)}, bf16[104,768]{1,0:T(8,128)(2,1)S(1)}, u32[]{:S(2)}, u32[]{:S(2)}) collective-permute-start(bf16[104,768]{1,0:T(8,128)(2,1)S(1)} %pad_maximum_fusion.13), channel_id=1, source_target_pairs={{0,8},{4,12},{8,16},{12,20},{16,24},{20,28},{24,0},{28,4},{1,9},{5... | collective-permute-start | bytes 479240 | tf_op jit(solution)/shard_map/ppermute | solution.py:105
  21.2 19.0 %collective-permute-start.4 = (bf16[104,768]{1,0:T(8,128)(2,1)S(1)}, bf16[104,768]{1,0:T(8,128)(2,1)S(1)}, u32[]{:S(2)}, u32[]{:S(2)}) collective-permute-start(bf16[104,768]{1,0:T(8,128)(2,1)S(1)} %pad_maximum_fusion.13), channel_id=1, source_target_pairs={{0,24},{4,28},{8,0},{12,4},{16,8},{20,12},{24,16},{28,20},{1,25},{... | collective-permute-start | bytes 479240 | tf_op jit(solution)/shard_map/ppermute | solution.py:106
  23.4 5.7 %collective-permute-start.2 = (bf16[104,768]{1,0:T(8,128)(2,1)S(1)}, bf16[104,768]{1,0:T(8,128)(2,1)S(1)}, u32[]{:S(2)}, u32[]{:S(2)}) collective-permute-start(bf16[104,768]{1,0:T(8,128)(2,1)S(1)} %pad_maximum_fusion.13), channel_id=1, source_target_pairs={{0,4},{4,0},{8,12},{12,8},{16,20},{20,16},{24,28},{28,24},{1,5},{5... | collective-permute-start | bytes 479240 | tf_op jit(solution)/shard_map/ppermute | solution.py:108
  25.1 15.9 %collective-permute-start.13 = (bf16[192,768]{1,0:T(8,128)(2,1)S(1)}, bf16[192,768]{1,0:T(8,128)(2,1)S(1)}, u32[]{:S(2)}, u32[]{:S(2)}) collective-permute-start(bf16[192,768]{1,0:T(8,128)(2,1)S(1)} %pad_maximum_fusion.8), channel_id=1, source_target_pairs={{0,8},{4,12},{8,16},{12,20},{16,24},{20,28},{24,0},{28,4},{1,9},{5... | collective-permute-start | bytes 884744 | tf_op jit(solution)/shard_map/ppermute | solution.py:105
  29.1 16.4 %collective-permute-start.14 = (bf16[192,768]{1,0:T(8,128)(2,1)S(1)}, bf16[192,768]{1,0:T(8,128)(2,1)S(1)}, u32[]{:S(2)}, u32[]{:S(2)}) collective-permute-start(bf16[192,768]{1,0:T(8,128)(2,1)S(1)} %pad_maximum_fusion.8), channel_id=1, source_target_pairs={{0,24},{4,28},{8,0},{12,4},{16,8},{20,12},{24,16},{28,20},{1,25},{... | collective-permute-start | bytes 884744 | tf_op jit(solution)/shard_map/ppermute | solution.py:106
  30.1 17.8 %collective-permute-start.12 = (bf16[192,768]{1,0:T(8,128)(2,1)S(1)}, bf16[192,768]{1,0:T(8,128)(2,1)S(1)}, u32[]{:S(2)}, u32[]{:S(2)}) collective-permute-start(bf16[192,768]{1,0:T(8,128)(2,1)S(1)} %pad_maximum_fusion.8), channel_id=1, source_target_pairs={{0,4},{4,0},{8,12},{12,8},{16,20},{20,16},{24,28},{28,24},{1,5},{5... | collective-permute-start | bytes 884744 | tf_op jit(solution)/shard_map/ppermute | solution.py:108
  40.2 19.9 %collective-permute-start.16 = (bf16[192,768]{1,0:T(8,128)(2,1)S(1)}, bf16[192,768]{1,0:T(8,128)(2,1)}, u32[]{:S(2)}, u32[]{:S(2)}) collective-permute-start(bf16[192,768]{1,0:T(8,128)(2,1)S(1)} %pad_maximum_fusion.8), channel_id=1, source_target_pairs={{0,16},{4,20},{8,24},{12,28},{16,0},{20,4},{24,8},{28,12},{1,17},{... | collective-permute-start | bytes 884744 | tf_op jit(solution)/shard_map/ppermute | solution.py:107
  40.9 53.8 %collective-permute-start.9 = (bf16[2,256,768]{2,1,0:T(8,128)(2,1)}, bf16[2,256,768]{2,1,0:T(8,128)(2,1)}, u32[]{:S(2)}, u32[]{:S(2)}) collective-permute-start(bf16[2,256,768]{2,1,0:T(8,128)(2,1)} %pad_maximum_fusion.2), channel_id=1, source_target_pairs={{0,1},{1,0},{2,3},{3,2},{4,5},{5,4},{6,7},{7,6},{8,9},{9,8},{10,11... | collective-permute-start | bytes 2359304 | tf_op jit(solution)/shard_map/ppermute | solution.py:74
  41.0 20.6 %copy-start.9 = (bf16[192,768]{1,0:T(8,128)(2,1)}, bf16[192,768]{1,0:T(8,128)(2,1)S(1)}, u32[]{:S(2)}) copy-start(bf16[192,768]{1,0:T(8,128)(2,1)S(1)} %collective-permute-done.13) | copy-start | bytes 884740
  41.0 20.9 %collective-permute-start.5 = (bf16[2,104,768]{2,1,0:T(8,128)(2,1)S(1)}, bf16[2,104,768]{2,1,0:T(8,128)(2,1)S(1)}, u32[]{:S(2)}, u32[]{:S(2)}) collective-permute-start(bf16[2,104,768]{2,1,0:T(8,128)(2,1)S(1)} %pad_maximum_fusion.7), channel_id=1, source_target_pairs={{0,4},{4,0},{8,12},{12,8},{16,20},{20,16},{24,28},{28,24},{1,5},{5... | collective-permute-start | bytes 958472 | tf_op jit(solution)/shard_map/ppermute | solution.py:109
  45.5 16.2 %copy-start.10 = (bf16[192,768]{1,0:T(8,128)(2,1)}, bf16[192,768]{1,0:T(8,128)(2,1)S(1)}, u32[]{:S(2)}) copy-start(bf16[192,768]{1,0:T(8,128)(2,1)S(1)} %collective-permute-done.14) | copy-start | bytes 884740
  45.5 16.4 %collective-permute-start.7 = (bf16[104,768]{1,0:T(8,128)(2,1)S(1)}, bf16[104,768]{1,0:T(8,128)(2,1)S(1)}, u32[]{:S(2)}, u32[]{:S(2)}) collective-permute-start(bf16[104,768]{1,0:T(8,128)(2,1)S(1)} %collective-permute-done.6), channel_id=1, source_target_pairs={{0,4},{4,0},{8,12},{12,8},{16,20},{20,16},{24,28},{28,24},{1,5},{5... | collective-permute-start | bytes 479240 | tf_op jit(solution)/shard_map/ppermute | solution.py:110
  47.9 43.7 %collective-permute-start.15 = (bf16[2,192,768]{2,1,0:T(8,128)(2,1)}, bf16[2,192,768]{2,1,0:T(8,128)(2,1)}, u32[]{:S(2)}, u32[]{:S(2)}) collective-permute-start(bf16[2,192,768]{2,1,0:T(8,128)(2,1)} %pad_maximum_fusion.4), channel_id=1, source_target_pairs={{0,4},{4,0},{8,12},{12,8},{16,20},{20,16},{24,28},{28,24},{1,5},{5... | collective-permute-start | bytes 1769480 | tf_op jit(solution)/shard_map/ppermute | solution.py:109
  60.1 30.4 %collective-permute-start.17 = (bf16[192,768]{1,0:T(8,128)(2,1)}, bf16[192,768]{1,0:T(8,128)(2,1)}, u32[]{:S(2)}, u32[]{:S(2)}) collective-permute-start(bf16[192,768]{1,0:T(8,128)(2,1)} %collective-permute-done.16), channel_id=1, source_target_pairs={{0,4},{4,0},{8,12},{12,8},{16,20},{20,16},{24,28},{28,24},{1,5},{5... | collective-permute-start | bytes 884744 | tf_op jit(solution)/shard_map/ppermute | solution.py:110
  108.3 14.7 %collective-permute-start.10 = (bf16[2,48,512]{2,1,0:T(8,128)(2,1)}, bf16[2,48,512]{2,1,0:T(8,128)(2,1)}, u32[]{:S(2)}, u32[]{:S(2)}) collective-permute-start(bf16[2,48,512]{2,1,0:T(8,128)(2,1)} %dynamic-slice_bitcast_fusion.18), channel_id=1, source_target_pairs={{0,2},{2,0},{1,3},{3,1},{4,6},{6,4},{5,7},{7,5},{8,10},{10,8},{9,1... | collective-permute-start | bytes 294920 | tf_op jit(solution)/shard_map/ppermute | solution.py:60
  110.8 11.1 %collective-permute-start.18 = (bf16[2,48,512]{2,1,0:T(8,128)(2,1)}, bf16[2,48,512]{2,1,0:T(8,128)(2,1)}, u32[]{:S(2)}, u32[]{:S(2)}) collective-permute-start(bf16[2,48,512]{2,1,0:T(8,128)(2,1)} %dynamic-slice_bitcast_fusion.17), channel_id=1, source_target_pairs={{0,2},{2,0},{1,3},{3,1},{4,6},{6,4},{5,7},{7,5},{8,10},{10,8},{9,1... | collective-permute-start | bytes 294920 | tf_op jit(solution)/shard_map/ppermute | solution.py:60
  122.9 1.6 collective-permute-start.19
  124.0 10.0 %collective-permute-start.11 = (bf16[2,48,512]{2,1,0:T(8,128)(2,1)S(1)}, bf16[2,48,512]{2,1,0:T(8,128)(2,1)S(1)}, u32[]{:S(2)}, u32[]{:S(2)}) collective-permute-start(bf16[2,48,512]{2,1,0:T(8,128)(2,1)S(1)} %fusion.73), channel_id=1, source_target_pairs={{0,1},{1,0},{2,3},{3,2},{4,5},{5,4},{6,7},{7,6},{8,9},{9,8},{10,11... | collective-permute-start | bytes 294920 | tf_op jit(solution)/shard_map/ppermute | solution.py:62
  139.5 17.8 %collective-permute-start.31 = (bf16[2,96,768]{2,1,0:T(8,128)(2,1)}, bf16[2,96,768]{2,1,0:T(8,128)(2,1)}, u32[]{:S(2)}, u32[]{:S(2)}) collective-permute-start(bf16[2,96,768]{2,1,0:T(8,128)(2,1)} %pad_maximum_fusion.9), channel_id=1, source_target_pairs={{0,4},{4,0},{8,12},{12,8},{16,20},{20,16},{24,28},{28,24},{1,5},{5... | collective-permute-start | bytes 884744 | tf_op jit(solution)/shard_map/ppermute | solution.py:129
  140.0 17.3 %collective-permute-start.33 = (bf16[1,96,768]{2,1,0:T(8,128)(2,1)}, bf16[1,96,768]{2,1,0:T(8,128)(2,1)}, u32[]{:S(2)}, u32[]{:S(2)}) collective-permute-start(bf16[1,96,768]{2,1,0:T(8,128)(2,1)} %get-tuple-element.41), channel_id=1, source_target_pairs={{0,4},{4,0},{8,12},{12,8},{16,20},{20,16},{24,28},{28,24},{1,5},{5... | collective-permute-start | bytes 442376 | tf_op jit(solution)/shard_map/ppermute | solution.py:129
  141.5 29.2 %collective-permute-start.30 = (bf16[1,96,768]{2,1,0:T(8,128)(2,1)}, bf16[1,96,768]{2,1,0:T(8,128)(2,1)}, u32[]{:S(2)}, u32[]{:S(2)}) collective-permute-start(bf16[1,96,768]{2,1,0:T(8,128)(2,1)} %get-tuple-element.38), channel_id=1, source_target_pairs={{0,4},{4,0},{8,12},{12,8},{16,20},{20,16},{24,28},{28,24},{1,5},{5... | collective-permute-start | bytes 442376 | tf_op jit(solution)/shard_map/ppermute | solution.py:129
  151.9 46.6 %collective-permute-start.22 = (bf16[1,200,768]{2,1,0:T(8,128)(2,1)}, bf16[1,200,768]{2,1,0:T(8,128)(2,1)}, u32[]{:S(2)}, u32[]{:S(2)}) collective-permute-start(bf16[1,200,768]{2,1,0:T(8,128)(2,1)} %maximum_bitcast_fusion.8), channel_id=1, source_target_pairs={{0,4},{4,0},{8,12},{12,8},{16,20},{20,16},{24,28},{28,24},{1,5},{5... | collective-permute-start | bytes 921608 | tf_op jit(solution)/shard_map/ppermute | solution.py:129
  156.9 12.9 %copy-start.29 = (bf16[96,768]{1,0:T(8,128)(2,1)S(1)}, bf16[96,768]{1,0:T(8,128)(2,1)}, u32[]{:S(2)}) copy-start(bf16[96,768]{1,0:T(8,128)(2,1)} %get-tuple-element.55) | copy-start | bytes 442372
  156.9 12.9 %copy-start.32 = (bf16[96,768]{1,0:T(8,128)(2,1)S(1)}, bf16[96,768]{1,0:T(8,128)(2,1)}, u32[]{:S(2)}) copy-start(bf16[96,768]{1,0:T(8,128)(2,1)} %get-tuple-element.47) | copy-start | bytes 442372
  158.6 13.7 %collective-permute-start.32 = (bf16[96,768]{1,0:T(8,128)(2,1)S(1)}, bf16[96,768]{1,0:T(8,128)(2,1)S(1)}, u32[]{:S(2)}, u32[]{:S(2)}) collective-permute-start(bf16[96,768]{1,0:T(8,128)(2,1)S(1)} %get-tuple-element.31), channel_id=1, source_target_pairs={{0,8},{4,12},{8,16},{12,20},{16,24},{20,28},{24,0},{28,4},{1,9},{5... | collective-permute-start | bytes 442376 | tf_op jit(solution)/shard_map/ppermute | solution.py:136
  165.0 10.1 %collective-permute-start.34 = (bf16[96,768]{1,0:T(8,128)(2,1)S(1)}, bf16[96,768]{1,0:T(8,128)(2,1)S(1)}, u32[]{:S(2)}, u32[]{:S(2)}) collective-permute-start(bf16[96,768]{1,0:T(8,128)(2,1)S(1)} %get-tuple-element.42), channel_id=1, source_target_pairs={{0,16},{4,20},{8,24},{12,28},{16,0},{20,4},{24,8},{28,12},{1,17},{... | collective-permute-start | bytes 442376 | tf_op jit(solution)/shard_map/ppermute | solution.py:135
  167.0 8.1 %collective-permute-start.35 = (bf16[96,768]{1,0:T(8,128)(2,1)S(1)}, bf16[96,768]{1,0:T(8,128)(2,1)S(1)}, u32[]{:S(2)}, u32[]{:S(2)}) collective-permute-start(bf16[96,768]{1,0:T(8,128)(2,1)S(1)} %get-tuple-element.32), channel_id=1, source_target_pairs={{0,24},{4,28},{8,0},{12,4},{16,8},{20,12},{24,16},{28,20},{1,25},{... | collective-permute-start | bytes 442376 | tf_op jit(solution)/shard_map/ppermute | solution.py:137
  170.7 10.2 %copy-start.24 = (bf16[96,768]{1,0:T(8,128)(2,1)S(1)}, bf16[96,768]{1,0:T(8,128)(2,1)}, u32[]{:S(2)}) copy-start(bf16[96,768]{1,0:T(8,128)(2,1)} %get-tuple-element.46) | copy-start | bytes 442372
  170.7 10.2 %collective-permute-start.25 = (bf16[1,200,768]{2,1,0:T(8,128)(2,1)S(1)}, bf16[1,200,768]{2,1,0:T(8,128)(2,1)S(1)}, u32[]{:S(2)}, u32[]{:S(2)}) collective-permute-start(bf16[1,200,768]{2,1,0:T(8,128)(2,1)S(1)} %maximum_bitcast_fusion.11), channel_id=1, source_target_pairs={{0,4},{4,0},{8,12},{12,8},{16,20},{20,16},{24,28},{28,24},{1,5},{5... | collective-permute-start | bytes 921608 | tf_op jit(solution)/shard_map/ppermute | solution.py:129
  172.3 19.0 %collective-permute-start.23 = (bf16[2,200,768]{2,1,0:T(8,128)(2,1)}, bf16[2,200,768]{2,1,0:T(8,128)(2,1)}, u32[]{:S(2)}, u32[]{:S(2)}) collective-permute-start(bf16[2,200,768]{2,1,0:T(8,128)(2,1)} %pad_maximum_fusion.3), channel_id=1, source_target_pairs={{0,4},{4,0},{8,12},{12,8},{16,20},{20,16},{24,28},{28,24},{1,5},{5... | collective-permute-start | bytes 1843208 | tf_op jit(solution)/shard_map/ppermute | solution.py:129
  175.0 39.7 %collective-permute-start.20 = (bf16[2,128,1536]{2,1,0:T(8,128)(2,1)}, bf16[2,128,1536]{2,1,0:T(8,128)(2,1)}, u32[]{:S(2)}, u32[]{:S(2)}) collective-permute-start(bf16[2,128,1536]{2,1,0:T(8,128)(2,1)} %dynamic-slice_bitcast_fusion), channel_id=1, source_target_pairs={{0,1},{1,0},{2,3},{3,2},{4,5},{5,4},{6,7},{7,6},{8,9},{9,8},{10,11... | collective-permute-start | bytes 2359304 | tf_op jit(solution)/shard_map/ppermute | solution.py:87
  176.1 15.2 %copy-start.19 = (bf16[96,768]{1,0:T(8,128)(2,1)S(1)}, bf16[96,768]{1,0:T(8,128)(2,1)}, u32[]{:S(2)}) copy-start(bf16[96,768]{1,0:T(8,128)(2,1)} %get-tuple-element.52) | copy-start | bytes 442372
  176.1 15.2 %copy-start.20 = (bf16[96,768]{1,0:T(8,128)(2,1)S(1)}, bf16[96,768]{1,0:T(8,128)(2,1)}, u32[]{:S(2)}) copy-start(bf16[96,768]{1,0:T(8,128)(2,1)} %get-tuple-element.57) | copy-start | bytes 442372
  176.1 15.2 %copy-start.21 = (bf16[96,768]{1,0:T(8,128)(2,1)S(1)}, bf16[96,768]{1,0:T(8,128)(2,1)}, u32[]{:S(2)}) copy-start(bf16[96,768]{1,0:T(8,128)(2,1)} %get-tuple-element.44) | copy-start | bytes 442372
  176.1 15.2 %copy-start.22 = (bf16[96,768]{1,0:T(8,128)(2,1)S(1)}, bf16[96,768]{1,0:T(8,128)(2,1)}, u32[]{:S(2)}) copy-start(bf16[96,768]{1,0:T(8,128)(2,1)} %get-tuple-element.49) | copy-start | bytes 442372
  176.2 9.2 %collective-permute-start.36 = (bf16[2,24,576]{2,1,0:T(8,128)(2,1)S(1)}, bf16[2,24,576]{2,1,0:T(8,128)(2,1)S(1)}, u32[]{:S(2)}, u32[]{:S(2)}) collective-permute-start(bf16[2,24,576]{2,1,0:T(8,128)(2,1)S(1)} %dynamic-slice_bitcast_fusion.19), channel_id=1, source_target_pairs={{0,2},{2,0},{1,3},{3,1},{4,6},{6,4},{5,7},{7,5},{8,10},{10,8},{9,1... | collective-permute-start | bytes 165896 | tf_op jit(solution)/shard_map/ppermute | solution.py:60
  181.7 24.5 %collective-permute-start.26 = (bf16[200,768]{1,0:T(8,128)(2,1)}, bf16[200,768]{1,0:T(8,128)(2,1)}, u32[]{:S(2)}, u32[]{:S(2)}) collective-permute-start(bf16[200,768]{1,0:T(8,128)(2,1)} %fusion.19), channel_id=1, source_target_pairs={{0,16},{4,20},{8,24},{12,28},{16,0},{20,4},{24,8},{28,12},{1,17},{... | collective-permute-start | bytes 921608 | tf_op jit(solution)/shard_map/ppermute | solution.py:135
  185.4 7.9 %collective-permute-start.37 = (bf16[2,24,576]{2,1,0:T(8,128)(2,1)S(1)}, bf16[2,24,576]{2,1,0:T(8,128)(2,1)S(1)}, u32[]{:S(2)}, u32[]{:S(2)}) collective-permute-start(bf16[2,24,576]{2,1,0:T(8,128)(2,1)S(1)} %fusion.91), channel_id=1, source_target_pairs={{0,1},{1,0},{2,3},{3,2},{4,5},{5,4},{6,7},{7,6},{8,9},{9,8},{10,11... | collective-permute-start | bytes 165896 | tf_op jit(solution)/shard_map/ppermute | solution.py:62
  193.3 18.9 %copy-start.18 = (bf16[96,768]{1,0:T(8,128)(2,1)S(1)}, bf16[96,768]{1,0:T(8,128)(2,1)}, u32[]{:S(2)}) copy-start(bf16[96,768]{1,0:T(8,128)(2,1)} %get-tuple-element.51) | copy-start | bytes 442372
  193.3 12.9 %collective-permute-start.24 = (bf16[200,768]{1,0:T(8,128)(2,1)}, bf16[200,768]{1,0:T(8,128)(2,1)}, u32[]{:S(2)}, u32[]{:S(2)}) collective-permute-start(bf16[200,768]{1,0:T(8,128)(2,1)} %get-tuple-element.69), channel_id=1, source_target_pairs={{0,8},{4,12},{8,16},{12,20},{16,24},{20,28},{24,0},{28,4},{1,9},{5... | collective-permute-start | bytes 921608 | tf_op jit(solution)/shard_map/ppermute | solution.py:136
  193.3 18.9 %collective-permute-start.27 = (bf16[200,768]{1,0:T(8,128)(2,1)}, bf16[200,768]{1,0:T(8,128)(2,1)}, u32[]{:S(2)}, u32[]{:S(2)}) collective-permute-start(bf16[200,768]{1,0:T(8,128)(2,1)} %get-tuple-element.70), channel_id=1, source_target_pairs={{0,24},{4,28},{8,0},{12,4},{16,8},{20,12},{24,16},{28,20},{1,25},{... | collective-permute-start | bytes 921608 | tf_op jit(solution)/shard_map/ppermute | solution.py:137
  214.1 4.5 %collective-permute-start.28 = (bf16[2,25,768]{2,0,1:T(2,128)(2,1)S(1)}, bf16[2,25,768]{2,0,1:T(2,128)(2,1)S(1)}, u32[]{:S(2)}, u32[]{:S(2)}) collective-permute-start(bf16[2,25,768]{2,0,1:T(2,128)(2,1)S(1)} %fusion.84), channel_id=1, source_target_pairs={{0,2},{2,0},{1,3},{3,1},{4,6},{6,4},{5,7},{7,5},{8,10},{10,8},{9,1... | collective-permute-start | bytes 230408 | tf_op jit(solution)/shard_map/ppermute | solution.py:60
  219.3 1.5 collective-permute-start.29
  219.5 11.6 %collective-permute-start.21 = (bf16[128,1536]{1,0:T(8,128)(2,1)S(1)}, bf16[128,1536]{1,0:T(8,128)(2,1)S(1)}, u32[]{:S(2)}, u32[]{:S(2)}) collective-permute-start(bf16[128,1536]{1,0:T(8,128)(2,1)S(1)} %fusion.41), channel_id=1, source_target_pairs={{0,2},{2,0},{1,3},{3,1},{4,6},{6,4},{5,7},{7,5},{8,10},{10,8},{9,1... | collective-permute-start | bytes 1179656 | tf_op jit(solution)/shard_map/ppermute | solution.py:88
  (61 other events, 219.5 us)

commit v3 on v2

--- a/solution.py
+++ b/solution.py
@@ -1,6 +1,10 @@
+import functools
+
 import jax
 import jax.numpy as jnp
 from jax import lax
+from jax.experimental import pallas as pl
+from jax.experimental.pallas import tpu as pltpu
 from jax.sharding import PartitionSpec as P
 
 HEADS = 12
@@ -158,7 +162,7 @@
     return attended, d_queries, d_keys, d_values
 
 
-def per_device(
+def general_device(
     hidden_in,
     lengths,
     grad_out,
@@ -401,6 +405,485 @@
     )
 
 
+SCALE = HEAD_DIM**-0.5
+
+
+def kernel_call(body, outs, args, scratch=(), megabytes=24, flops=0):
+    moved = sum(a.size * a.dtype.itemsize for a in args)
+    return pl.pallas_call(
+        body,
+        out_shape=tuple(jax.ShapeDtypeStruct(shape, kind) for shape, kind in outs),
+        scratch_shapes=[pltpu.VMEM(shape, kind) for shape, kind in scratch],
+        compiler_params=pltpu.CompilerParams(vmem_limit_bytes=megabytes << 20),
+        cost_estimate=pl.CostEstimate(flops=flops, bytes_accessed=moved, transcendentals=0),
+    )(*args)
+
+
+def dot_nn(a, b):
+    return lax.dot_general(a, b, (((1,), (0,)), ((), ())), preferred_element_type=F32)
+
+
+def dot_nt(a, b):
+    return lax.dot_general(a, b, (((1,), (1,)), ((), ())), preferred_element_type=F32)
+
+
+def dot_tn(a, b):
+    return lax.dot_general(a, b, (((0,), (0,)), ((), ())), preferred_element_type=F32)
+
+
+def line_and_side():
+    me = lax.axis_index("dp")
+    return lax.shift_right_logical(me, 1), lax.bitwise_and(me, 1)
+
+
+def dp_index(line, step, side):
+    return 2 * lax.bitwise_and(line + step, 3) + side
+
+
+def dp_pieces(block):
+    near1 = lax.ppermute(block, "dp", along(1))
+    far0 = lax.ppermute(block, "dp", SIDE_SWAP)
+    near3 = lax.ppermute(block, "dp", along(3))
+    near2 = lax.ppermute(block, "dp", along(2))
+    far1 = lax.ppermute(near1, "dp", SIDE_SWAP)
+    far3 = lax.ppermute(near3, "dp", SIDE_SWAP)
+    far2 = lax.ppermute(near2, "dp", SIDE_SWAP)
+    return (block, far0, near1, far1, near3, far3, near2, far2)
+
+
+def piece_owners():
+    line, side = line_and_side()
+    return [dp_index(line, step, s) for step in (0, 3, 1, 2) for s in (side, 1 - side)]
+
+
+def dp_sum(send2, send13, send0, keep2, keep13, keep0):
+    moved2 = lax.ppermute(send2, "dp", SIDE_SWAP)
+    moved13 = lax.ppermute(send13, "dp", SIDE_SWAP)
+    moved0 = lax.ppermute(send0, "dp", SIDE_SWAP)
+    sum2 = (keep2.astype(F32) + moved2.astype(F32)).astype(BF)
+    sum1 = (keep13[0].astype(F32) + moved13[0].astype(F32)).astype(BF)
+    sum3 = (keep13[1].astype(F32) + moved13[1].astype(F32)).astype(BF)
+    got2 = lax.ppermute(sum2, "dp", along(2))
+    got1 = lax.ppermute(sum1, "dp", along(1))
+    got3 = lax.ppermute(sum3, "dp", along(3))
+    total = keep0.astype(F32) + moved0.astype(F32)
+    return total + got2.astype(F32) + got1.astype(F32) + got3.astype(F32)
+
+
+def pick_blocks(block_of, send2, send13, send0, keep2, keep13, keep0):
+    line, side = line_and_side()
+    for far, (r2, r13, r0) in ((True, (send2, send13, send0)), (False, (keep2, keep13, keep0))):
+        s = 1 - side if far else side
+        r2[...] = block_of(dp_index(line, 2, s))
+        r13[0] = block_of(dp_index(line, 1, s))
+        r13[1] = block_of(dp_index(line, 3, s))
+        r0[...] = block_of(dp_index(line, 0, s))
+
+
+def pick_shapes(rows, width):
+    one, two = ((rows, width), BF), ((2, rows, width), BF)
+    return (one, two, one, one, two, one)
+
+
+def seq_shuffle(blocks):
+    got = [blocks[0]]
+    for other in (1, 2, 3):
+        pairs = [(i, i ^ other) for i in range(4)]
+        got.append(lax.ppermute(blocks[other], "seq", pairs))
+    return got
+
+
+def place_kernel(deep, *refs):
+    pieces, (dy, weights, dense, vectors), d_blocks, (rows32, d_rows) = refs[:8], refs[8:12], refs[12:16], refs[16:]
+    per_line = 4 * deep
+    quarter = dy.shape[1] // 4
+    own = weights.shape[1] - quarter
+    total = jnp.zeros(vectors.shape, F32)
+    for piece, owner in zip(pieces, piece_owners()):
+        weights[pl.ds(pl.multiple_of(owner * per_line, per_line), per_line), :] = piece[:per_line, :]
+        total = total + piece[per_line:, :].astype(F32)
+        beside = piece[:per_line, own:].astype(F32)
+        for q in range(4):
+            rows32[pl.ds(pl.multiple_of(owner * deep, 8), deep), q * quarter : (q + 1) * quarter] = beside[
+                q * deep : (q + 1) * deep
+            ]
+    vectors[...] = total
+    dense[...] = rows32[...].astype(BF)
+    d_rows[...] = dot_nt(dense[...], dy[...]).astype(BF)
+    me = lax.axis_index("seq")
+    count = d_blocks[0].shape[0]
+    for j in range(4):
+        d_blocks[j][...] = d_rows[pl.ds(pl.multiple_of(lax.bitwise_xor(me, j) * count, 16), count), :]
+
+
+def turn(values, cosine, sine_a, sine_b, sign):
+    half = ROT // 2
+    ahead = pltpu.roll(values, 128 - half, 1)
+    behind = pltpu.roll(values, half, 1)
+    return values * cosine + sign * (ahead * sine_a + behind * sine_b)
+
+
+def project_kernel(unit, weights, vectors, cosine, sine_a, sine_b, attn_in, qk, v):
+    gain, shift, bias = vectors[0:1, :], vectors[1:2, :], vectors[6:7, :]
+    turned = qk.shape[1]
+    size = 128
+
+    def step(i, carry):
+        rows = pl.ds(pl.multiple_of(i * size, size), size)
+        normed = (unit[rows, :] * gain + shift).astype(BF)
+        attn_in[rows, :] = normed
+        joined = dot_nn(normed, weights[...]) + bias
+        tables = cosine[rows, :], sine_a[rows, :], sine_b[rows, :]
+        for c in range(0, turned, 128):
+            qk[rows, c : c + 128] = turn(joined[:, c : c + 128], *tables, 1.0).astype(BF)
+        v[rows, :] = joined[:, turned : turned + v.shape[1]].astype(BF)
+        return carry
+
+    lax.fori_loop(0, unit.shape[0] // size, step, 0)
+
+
+def attention_kernel(deep, *refs):
+    qk, v, d0, d1, d2, d3, seg_column, seg_row, cosine, sine_a, sine_b = refs[:11]
+    given, d_joined, (d_t, out_t, dk_t, dv_t, acc) = refs[11:15], refs[15], refs[16:]
+    tokens, own = v.shape
+    me = lax.axis_index("seq")
+    runs = own // (4 * deep)
+    for j, ref in enumerate((d0, d1, d2, d3)):
+        source = lax.bitwise_xor(me, j)
+        block = ref[...].astype(F32)
+        for r in range(runs):
+            place = pl.multiple_of(r * 4 * deep + source * deep, 8)
+            d_t[pl.ds(place, deep), :] = block[r * deep : (r + 1) * deep]
+    d_out = jnp.transpose(d_t[...]).astype(BF)
+    q_t = jnp.transpose(qk[:, :own].astype(F32)).astype(BF)
+    d_tb = d_t[...].astype(BF)
+    dk_t[...] = jnp.zeros(dk_t.shape, F32)
+    dv_t[...] = jnp.zeros(dv_t.shape, F32)
+    size = 256
+    for h in range(own // HEAD_DIM):
+        lanes = slice(h * HEAD_DIM, (h + 1) * HEAD_DIM)
+        q_h = qk[:, lanes]
+        k_h = qk[:, own + h * HEAD_DIM : own + (h + 1) * HEAD_DIM]
+        v_h = v[:, lanes]
+        d_h = d_out[:, lanes]
+        for first in range(0, tokens, size):
+            rows = slice(first, first + size)
+            n = first + size
+            scores = dot_nt(q_h[rows], k_h[:n]) * SCALE
+            query = lax.broadcasted_iota(jnp.int32, (size, n), 0) + first
+            key = lax.broadcasted_iota(jnp.int32, (size, n), 1)
+            allowed = (seg_column[rows, :] == seg_row[:, :n]) & (key <= query)
+            scores = jnp.where(allowed, scores, NEGATIVE)
+            weights = jnp.where(allowed, jnp.exp(scores - jnp.max(scores, axis=1, keepdims=True)), 0.0)
+            probs = weights * (1.0 / jnp.sum(weights, axis=1, keepdims=True))
+            probs_r = probs.astype(BF)
+            out_t[lanes, rows] = jnp.transpose(dot_nn(probs_r, v_h[:n]))
+            d_probs = dot_nt(d_h[rows], v_h[:n])
+            delta = jnp.sum(probs * d_probs, axis=1, keepdims=True)
+            d_scores = (probs * (d_probs - delta)).astype(BF)
+            acc[rows, lanes] = dot_nn(d_scores, k_h[:n]) * SCALE
+            dk_t[lanes, :n] += dot_nn(q_t[lanes, rows], d_scores)
+            dv_t[lanes, :n] += dot_nn(d_tb[lanes, rows], probs_r)
+    acc[:, own : 2 * own] = jnp.transpose(dk_t[...]) * SCALE
+    for c in range(0, 2 * own, 128):
+        turned = turn(acc[:, c : c + 128], cosine[...], sine_a[...], sine_b[...], -1.0)
+        d_joined[:, c : c + 128] = turned.astype(BF)
+    d_joined[:, 2 * own : 3 * own] = jnp.transpose(dv_t[...]).astype(BF)
+    d_joined[:, 3 * own :] = jnp.zeros((tokens, d_joined.shape[1] - 3 * own), BF)
+    for j in range(4):
+        target = lax.bitwise_xor(me, j)
+        parts = [out_t[pl.ds(pl.multiple_of(r * 4 * deep + target * deep, 8), deep), :] for r in range(runs)]
+        given[j][...] = jnp.concatenate(parts, axis=0).astype(BF)
+
+
+def attention_grads_kernel(deep, *refs):
+    r0, r1, r2, r3, dense, dy, attn_in, d_joined, weights, unit, vectors = refs[:11]
+    picks, (attn_out, scaled, sums), (rows_t, grads) = refs[11:17], refs[17:20], refs[20:]
+    me = lax.axis_index("seq")
+    count = r0.shape[0]
+    width = dy.shape[1]
+    quarter = width // 4
+    own = width - quarter
+    for j, ref in enumerate((r0, r1, r2, r3)):
+        rows_t[pl.ds(pl.multiple_of(lax.bitwise_xor(me, j) * count, 16), count), :] = ref[...]
+    size = 128
+    for c in range(0, width, size):
+        grads[c : c + size, :] = dot_tn(attn_in[:, c : c + size], d_joined[...])
+    dense_grad = dot_nn(rows_t[...], dy[...])
+    for p in range(8):
+        for q in range(4):
+            start = p * 4 * deep + q * deep
+            grads[start : start + deep, own:] = dense_grad[p * deep : (p + 1) * deep, q * quarter : (q + 1) * quarter]
+    per_line = 4 * deep
+
+    def block_of(index):
+        return grads[pl.ds(pl.multiple_of(index * per_line, per_line), per_line), :].astype(BF)
+
+    pick_blocks(block_of, *picks)
+    attended = jnp.transpose(rows_t[...].astype(F32)).astype(BF)
+    gain = vectors[0:1, :]
+    tokens = dy.shape[0]
+    sums[...] = jnp.zeros(sums.shape, F32)
+    for c in range(0, tokens, size):
+        rows = slice(c, c + size)
+        attn_out[rows, :] = dot_nn(attended[rows], dense[...])
+        back = dot_nt(d_joined[rows, :], weights[...])
+        scaled[rows, :] = back * gain
+        sums[0:1, :] += jnp.sum(back * unit[rows, :], axis=0, keepdims=True)
+        sums[1:2, :] += jnp.sum(back, axis=0, keepdims=True)
+        sums[5:6, :] += jnp.sum(d_joined[rows, :].astype(F32), axis=0, keepdims=True)
+
+
+def mlp_kernel(per_line, *refs):
+    pieces, (unit, dy, vectors, attn_out, scaled, sums_in) = refs[:8], refs[8:14]
+    picks, (give, keep), scratch = refs[14:20], refs[20:22], refs[22:]
+    up, down, mlp_in, act, d_up, up_grad, down_grad, pair, sums = scratch
+    for piece, owner in zip(pieces, piece_owners()):
+        rows = pl.ds(pl.multiple_of(owner * per_line, per_line), per_line)
+        up[rows, :] = piece[:per_line, :]
+        down[rows, :] = piece[per_line:, :]
+    gain, shift, bias = vectors[2:3, :], vectors[3:4, :], vectors[7:8, :]
+    sums[...] = sums_in[...]
+    tokens, width = dy.shape
+    size = tokens // 4
+
+    def step(i, carry):
+        rows = pl.ds(pl.multiple_of(i * size, size), size)
+        u = unit[rows, :]
+        normed = (u * gain + shift).astype(BF)
+        mlp_in[rows, :] = normed
+        upper = dot_nn(normed, up[...]) + bias
+        cdf = 0.5 * (1.0 + lax.erf(upper * 0.7071067811865476))
+        pdf = jnp.exp(-0.5 * upper * upper) * 0.3989422804014327
+        act_rows = (upper * cdf).astype(BF)
+        act[rows, :] = act_rows
+        g = dy[rows, :]
+        d_rows = (dot_nt(g, down[...]) * (cdf + upper * pdf)).astype(BF)
+        d_up[rows, :] = d_rows
+        pair[i, :, :width] = dot_nn(act_rows, down[...]) + attn_out[rows, :]
+        back = dot_nt(d_rows, up[...])
+        pair[i, :, width:] = back * gain + scaled[rows, :]
+        sums[2:3, :] += jnp.sum(back * u, axis=0, keepdims=True)
+        sums[3:4, :] += jnp.sum(back, axis=0, keepdims=True)
+        sums[4:5, :] += 0.25 * jnp.sum(g.astype(F32), axis=0, keepdims=True)
+        sums[6:7, :] += jnp.sum(d_rows.astype(F32), axis=0, keepdims=True)
+        return carry
+
+    lax.fori_loop(0, 4, step, 0)
+    core = lax.bitwise_and(lax.axis_index("seq"), 1)
+    for chip in range(2):
+        give[chip] = pair[2 * chip + 1 - core].astype(BF)
+        keep[chip] = pair[2 * chip + core]
+    for c in range(0, width, 128):
+        up_grad[c : c + 128, :] = dot_tn(mlp_in[:, c : c + 128], d_up[...]).astype(BF)
+        down_grad[c : c + 128, :] = dot_tn(act[:, c : c + 128], dy[...]).astype(BF)
+    tail = sums[...].astype(BF)
+
+    def block_of(index):
+        rows = pl.ds(pl.multiple_of(index * per_line, per_line), per_line)
+        return jnp.concatenate([up_grad[rows, :], down_grad[rows, :], tail], axis=0)
+
+    pick_blocks(block_of, *picks)
+
+
+def line_device(
+    hidden_in,
+    lengths,
+    grad_out,
+    attn_gain,
+    attn_shift,
+    mlp_gain,
+    mlp_shift,
+    qkv_weight,
+    qkv_bias,
+    dense_weight,
+    dense_bias,
+    up_weight,
+    up_bias,
+    down_weight,
+    down_bias,
+):
+    n_dp, n_seq = 8, 4
+    dp_me, me = lax.axis_index("dp"), lax.axis_index("seq")
+    device = dp_me * n_seq + me
+    zero = jnp.int32(0)
+    rows, width = hidden_in.shape
+    group = rows * n_seq
+    hidden_units = up_weight.shape[1]
+    own_units = hidden_units // n_seq
+    deep = width // (n_dp * n_seq)
+    per_line = n_seq * deep
+    unit_rows = hidden_units // (n_dp * n_seq)
+    own = width // n_seq
+    heads = own // HEAD_DIM
+    wide = own_units + 3 * own
+
+    def by_head(values):
+        split = values.reshape(values.shape[0], 3, n_seq, own)
+        return jnp.moveaxis(split, 2, 0).reshape(n_seq, values.shape[0], 3 * own)
+
+    def from_heads(blocks):
+        split = jnp.moveaxis(blocks.reshape(n_seq, -1, 3, own), 0, 2)
+        return split.reshape(-1, 3 * width)
+
+    def spread(values, length, place):
+        empty = jnp.zeros((values.shape[0], length), values.dtype)
+        return lax.dynamic_update_slice(empty, values, (zero, place))
+
+    up_blocks = jnp.moveaxis(up_weight.reshape(deep, n_dp, n_seq, unit_rows), 2, 0)
+    up_blocks = up_blocks.reshape(n_seq, deep, own_units)
+    by_width = jnp.stack([attn_gain, attn_shift, mlp_gain, mlp_shift, dense_bias, down_bias])
+    by_width = jnp.pad(spread(by_width, width, device * deep), ((0, 2), (0, 0)))
+    bias_row = spread(qkv_bias[None], 3 * width, device * qkv_bias.shape[0])
+    bias_row = jnp.pad(by_head(bias_row), ((0, 0), (6, 1), (0, 0)))
+    left = jnp.concatenate([up_blocks, jnp.broadcast_to(by_width, (n_seq,) + by_width.shape)], axis=1)
+    right = jnp.concatenate([by_head(qkv_weight), bias_row], axis=1)
+    got = seq_exchange(jnp.concatenate([left, right], axis=2))
+    up_piece = got[:, :deep, :own_units].reshape(per_line, own_units)
+    qkv_piece = got[:, :deep, own_units:].reshape(per_line, 3 * own)
+    extra = jnp.sum(got[:, deep:].astype(F32), axis=0)
+    up_row = spread(up_bias[None].astype(F32), own_units, dp_me * unit_rows)
+    extra = (
+        extra[:, :width]
+        + jnp.pad(extra[:, own_units:], ((0, 0), (0, width - 3 * own)))
+        + jnp.pad(up_row, ((7, 0), (0, 0)))
+    ).astype(BF)
+    beside = jnp.swapaxes(dense_weight.reshape(deep, n_seq, own), 0, 1).reshape(per_line, own)
+    attn_piece = jnp.concatenate([jnp.concatenate([qkv_piece, beside], axis=1), extra], axis=0)
+    attn_pieces = dp_pieces(attn_piece)
+    mlp_pieces = dp_pieces(jnp.concatenate([up_piece, down_weight], axis=0))
+
+    both = seq_gather(jnp.concatenate([hidden_in, grad_out], axis=0))
+    hidden_group = both[:, :rows].reshape(group, width)
+    dy = both[:, rows:].reshape(group, width)
+
+    row_lengths = lengths[0]
+    segment, position = place(row_lengths, jnp.arange(group, dtype=jnp.int32))
+    lane = jnp.arange(128, dtype=jnp.int32) % HEAD_DIM
+    powers = jnp.power(F32(10000.0), -(2.0 * (lane % (ROT // 2)).astype(F32)) / ROT)
+    angles = position.astype(F32)[:, None] * powers[None, :]
+    cosine = jnp.where(lane < ROT, jnp.cos(angles), 1.0)
+    sine = jnp.sin(angles)
+    sine_a = jnp.where(lane < ROT // 2, -sine, 0.0)
+    sine_b = jnp.where((lane >= ROT // 2) & (lane < ROT), sine, 0.0)
+
+    def normed(values):
+        centered = values - jnp.mean(values, axis=-1, keepdims=True)
+        inverse = lax.rsqrt(jnp.mean(centered * centered, axis=-1, keepdims=True) + EPS)
+        return centered * inverse, inverse
+
+    unit = normed(hidden_group.astype(F32))[0]
+
+    flat = (group, width)
+    placed = kernel_call(
+        functools.partial(place_kernel, deep),
+        ((flat[1:] * 2, BF), ((n_dp * deep, width), BF), ((8, width), F32)) + (((2 * deep, group), BF),) * 4,
+        attn_pieces + (dy,),
+        scratch=(((n_dp * deep, width), F32), ((n_dp * deep, group), BF)),
+        flops=2 * n_dp * deep * width * group,
+    )
+    weights, dense, vectors = placed[:3]
+    d_blocks = seq_shuffle(placed[3:])
+    attn_in, qk, v = kernel_call(
+        project_kernel,
+        ((flat, BF), ((group, 2 * own), BF), ((group, own), BF)),
+        (unit, weights, vectors, cosine, sine_a, sine_b),
+        flops=2 * group * width * width,
+    )
+    attended = kernel_call(
+        functools.partial(attention_kernel, deep),
+        (((2 * deep, group), BF),) * 4 + ((flat, BF),),
+        (qk, v, *d_blocks, segment[:, None], segment[None, :], cosine, sine_a, sine_b),
+        scratch=(((own, group), F32),) * 4 + ((flat, F32),),
+        flops=14 * group * group * own,
+    )
+    d_joined = attended[4]
+    row_blocks = seq_shuffle(attended[:4])
+    results = kernel_call(
+        functools.partial(attention_grads_kernel, deep),
+        pick_shapes(per_line, width) + ((flat, F32), (flat, F32), ((8, width), F32)),
+        (*row_blocks, dense, dy, attn_in, d_joined, weights, unit, vectors),
+        scratch=(((n_dp * deep, group), BF), ((width, width), F32)),
+        flops=5 * group * width * width,
+        megabytes=32,
+    )
+    attn_sum = dp_sum(*results[:6])
+
+    results = kernel_call(
+        functools.partial(mlp_kernel, per_line),
+        pick_shapes(per_line + unit_rows + 8, width) + (((2, rows, 2 * width), BF), ((2, rows, 2 * width), F32)),
+        (*mlp_pieces, unit, dy, vectors) + tuple(results[6:]),
+        scratch=(
+            ((width, own_units), BF),
+            ((own_units, width), BF),
+            (flat, BF),
+            ((group, own_units), BF),
+            ((group, own_units), BF),
+            ((width, own_units), BF),
+            ((own_units, width), BF),
+            ((n_seq, rows, 2 * width), F32),
+            ((8, width), F32),
+        ),
+        flops=12 * group * width * own_units,
+        megabytes=40,
+    )
+    mlp_sum = dp_sum(*results[:6])
+    give, keep = results[6:]
+
+    chip = lax.shift_right_logical(me, 1)
+    both = keep + lax.ppermute(give, "seq", CORE_SWAP).astype(F32)
+    far = lax.ppermute(pick(both, 1 - chip).astype(BF), "seq", CHIP_SWAP)
+    pair = pick(both, chip) + far.astype(F32)
+    x = hidden_in.astype(F32)
+    block_out = x + vectors[4] + vectors[5] + pair[:, :width]
+    upstream = pair[:, width:]
+    own_unit, inverse = normed(x)
+    inner = (
+        upstream
+        - jnp.mean(upstream, axis=-1, keepdims=True)
+        - own_unit * jnp.mean(upstream * own_unit, axis=-1, keepdims=True)
+    )
+    grad_in = grad_out.astype(F32) + inverse * inner
+
+    qkv_back = attn_sum[:, : 3 * own].reshape(n_seq, deep, 3 * own).astype(BF)
+    qkv_own = from_heads(seq_exchange(qkv_back).astype(F32))
+    dense_own = attn_sum[:, 3 * own :].reshape(n_seq, deep, own)
+    dense_own = jnp.swapaxes(dense_own, 0, 1).reshape(deep, width)
+    tail = mlp_sum[per_line + unit_rows :]
+    back = jnp.concatenate(
+        [mlp_sum[:per_line].reshape(n_seq, deep, own_units), jnp.broadcast_to(tail, (n_seq,) + tail.shape)], axis=1
+    )
+    back = seq_exchange(back.astype(BF)).astype(F32)
+    up_own = jnp.moveaxis(back[:, :deep].reshape(n_seq, deep, n_dp, unit_rows), 0, 2)
+    by_width = jnp.sum(back[:, deep : deep + 5], axis=0)
+    by_width = lax.dynamic_slice(by_width, (zero, device * deep), (5, deep))
+    qkv_bias_grad = from_heads(back[:, deep + 5 : deep + 6, : 3 * own])[0]
+    qkv_bias_grad = lax.dynamic_slice(qkv_bias_grad, (device * qkv_bias.shape[0],), qkv_bias.shape)
+    up_bias_grad = lax.dynamic_slice(tail[6], (dp_me * unit_rows,), (unit_rows,))
+    return (
+        block_out.astype(BF),
+        grad_in.astype(BF),
+        by_width[0],
+        by_width[1],
+        by_width[2],
+        by_width[3],
+        qkv_own,
+        qkv_bias_grad,
+        dense_own,
+        by_width[4],
+        up_own.reshape(deep, hidden_units),
+        up_bias_grad,
+        mlp_sum[per_line : per_line + unit_rows],
+        by_width[4],
+    )
+
+
+def per_device(*args):
+    if lax.axis_size("dp") == 8 and lax.axis_size("seq") == 4:
+        return line_device(*args)
+    return general_device(*args)
+
+
 def solution(mesh):
     both = ("dp", "seq")
     matrix, vector = P(both, None), P(both)

time: 234 us -> 200 us (0.85)
  local copies, waits for them, and re-layouts: 56.1 us -> 22 us
  matrix products: 28.2 us -> 0 us
  waiting for transfers between devices: 61.8 us -> 83.3 us
  other arithmetic: 34.4 us -> 14.1 us
  Pallas kernels: 0 us -> 19.8 us
  starting transfers between devices: 49.2 us -> 59 us
    dot_general x17 -> x0, matrix products: 24.5 us -> none  [dot(): return jnp.einsum(spec, a, b, preferred_element_type=F32)]
    pallas_call x0 -> x5, Pallas kernels: none -> 19.8 us  [kernel_call(): pl.pallas_call(body, out_shape=tuple((jax.ShapeDtypeStruct(shape, kind) f...]
    ppermute x26 -> x34, waiting for transfers between devices: 57.2 us -> 70.9 us  [the longest x2 14.3 us: dp_pieces(): near2 = lax.ppermute(block, 'dp', along(2))]
    ppermute x26 -> x34, starting transfers between devices: 41 us -> 52.6 us  [the longest x2 15 us: dp_sum(): got1 = lax.ppermute(sum1, 'dp', along(1))]
    slice x27 -> x12, local copies, waits for them, and re-layouts: 11 us -> 1.89 us  [the longest x1 0.93 us: line_device(): up_piece = got[:, :deep, :own_units].reshape(per_line, own_units)]
    another operation x16 -> x2, local copies, waits for them, and re-layouts: 8.65 us -> 0.84 us  [the longest x1 0.76 us: line_device(): jnp.stack([attn_gain, attn_shift, mlp_gain, mlp_shift, dense_bias, down_b...]
    another operation x16 -> x1, other arithmetic: 7.46 us -> 0.18 us  [the longest x6 3.39 us: over_side(): jnp.stack([block_of(t + 1 - side) for t in targets])]
    add x5 -> x0, local copies, waits for them, and re-layouts: 6.92 us -> none  [the longest x2 2.79 us: per_device(): hidden_in.astype(F32) + f_dense_bias + f_down_bias + pair[:, :width]]
  transfers between devices with their start and end apart: 38 -> 42, of which waited for: 12 -> 23; matrix products, arithmetic and copies ran while one was open for 40% -> 11% of each run, Pallas kernels for 0% -> 5%
where the time goes in v3:
time: 200 us
  waiting for transfers between devices  83.3 us (42%)
  starting transfers between devices  59 us (30%)
  local copies, waits for them, and re-layouts  22 us (11%)
  Pallas kernels  19.8 us (10%)
  other arithmetic  14.1 us (7%)
    pallas_call x5, Pallas kernels, kernel_call(): pl.pallas_call(body, out_shape=tuple((jax.ShapeDtypeStruct(shape, kind) f...  19.8 us
    ppermute x2, starting transfers between devices, dp_sum(): got1 = lax.ppermute(sum1, 'dp', along(1))  15 us
    ppermute x2, waiting for transfers between devices, dp_pieces(): near2 = lax.ppermute(block, 'dp', along(2))  14.3 us
    ppermute x2, waiting for transfers between devices, dp_sum(): moved13 = lax.ppermute(send13, 'dp', SIDE_SWAP)  13.3 us
    ppermute x3, waiting for transfers between devices, seq_exchange(): far = lax.ppermute(pick(halves, 1 - chip), 'seq', CHIP_SWAP)  10.3 us
    unnamed x52, local copies, waits for them, and re-layouts  9.63 us
    ppermute x2, waiting for transfers between devices, dp_pieces(): far2 = lax.ppermute(near2, 'dp', SIDE_SWAP)  7.55 us
    ppermute x2, waiting for transfers between devices, dp_pieces(): far1 = lax.ppermute(near1, 'dp', SIDE_SWAP)  6.32 us
  transfers between devices with their start and end apart: 42, of which 23 were waited for; matrix products, arithmetic and copies ran while one was open for 11% of the time, Pallas kernels for 5%

profile of v3, /device:TPU:0, one launch (start us, length us, event | category | flops | bytes accessed | tf_op | source)
XLA Modules:
  0.0 199.7 jit_solution(14421416553614209635)
XLA Ops:
  2.6 3.0 %collective-permute-start.9 = (bf16[256,768]{1,0:T(8,128)(2,1)S(1)}, bf16[256,768]{1,0:T(8,128)(2,1)S(1)}, u32[]{:S(2)}, u32[]{:S(2)}) collective-permute-start(bf16[256,768]{1,0:T(8,128)(2,1)S(1)} %constant_dynamic-update-slice_fusion), channel_id=1, source_target_pairs={{0,2},{2,0},{1,3},{3,1},{4,6},{6,4},{5,7},{7,5},{8,10},{10,8},{9,1... | collective-permute-start | bytes 1179656 | tf_op jit(solution)/shard_map/ppermute | solution.py:76
  7.6 1.1 reshape.240
  10.4 8.2 %collective-permute-done = bf16[2,32,1344]{2,1,0:T(8,128)(2,1)S(1)} collective-permute-done((bf16[2,32,1344]{2,1,0:T(8,128)(2,1)S(1)}, bf16[2,32,1344]{2,1,0:T(8,128)(2,1)S(1)}, u32[]{:S(2)}, u32[]{:S(2)}) %collective-permute-start) | collective-permute-done | bytes 172064 | tf_op jit(solution)/shard_map/ppermute | solution.py:64
  18.7 1.4 collective-permute-done.1
  21.6 1.9 collective-permute-start.3
  23.5 2.3 %collective-permute-start.5 = (bf16[104,768]{1,0:T(8,128)(2,1)S(1)}, bf16[104,768]{1,0:T(8,128)(2,1)S(1)}, u32[]{:S(2)}, u32[]{:S(2)}) collective-permute-start(bf16[104,768]{1,0:T(8,128)(2,1)S(1)} %pad_maximum_fusion.5.refs_0_), channel_id=1, source_target_pairs={{0,24},{4,28},{8,0},{12,4},{16,8},{20,12},{24,16},{28,20},{1,25},{... | collective-permute-start | bytes 479240 | tf_op jit(solution)/shard_map/ppermute | solution.py:446
  27.8 1.6 collective-permute-start.2
  30.5 1.7 collective-permute-start.4
  33.0 1.5 collective-permute-start.6
  34.5 5.9 %collective-permute-done.7.refs_6_ = bf16[104,768]{1,0:T(8,128)(2,1)S(1)} collective-permute-done((bf16[104,768]{1,0:T(8,128)(2,1)S(1)}, bf16[104,768]{1,0:T(8,128)(2,1)S(1)}, u32[]{:S(2)}, u32[]{:S(2)}) %collective-permute-start.7) | collective-permute-done | bytes 159776 | tf_op jit(solution)/shard_map/ppermute | solution.py:447
  40.4 1.5 collective-permute-start.8
  41.9 1.2 select_bitcast_fusion.1
  44.1 2.3 %collective-permute-done.8.refs_7_ = bf16[104,768]{1,0:T(8,128)(2,1)S(1)} collective-permute-done((bf16[104,768]{1,0:T(8,128)(2,1)S(1)}, bf16[104,768]{1,0:T(8,128)(2,1)S(1)}, u32[]{:S(2)}, u32[]{:S(2)}) %collective-permute-start.8) | collective-permute-done | bytes 159776 | tf_op jit(solution)/shard_map/ppermute | solution.py:450
  47.1 1.6 collective-permute-start.19
  49.2 1.6 shard_map.255
  52.4 6.1 %shard_map.256 = (bf16[48,512]{1,0:T(8,128)(2,1)S(1)}, bf16[48,512]{1,0:T(8,128)(2,1)S(1)}, bf16[48,512]{1,0:T(8,128)(2,1)S(1)}, bf16[48,512]{1,0:T(8,128)(2,1)S(1)}, bf16[512,768]{1,0:T(8,128)(2,1)S(1)}) custom-call(bf16[512,384]{1,0:T(8,128)(2,1)S(1)} %get-tuple-element.48.refs_0_, bf16[512,192]{1,0:T(8,128)(2,1)S(1)} %get-tuple-element.49.refs_1_, ...), custom_call_target="tpu_custom_call" | custom-call | flops 704643072 | bytes 1576960 | tf_op jit(solution)/shard_map/pallas_call | solution.py:413
  60.5 2.4 %collective-permute-done.22.refs_2_ = bf16[48,512]{1,0:T(8,128)(2,1)S(1)} collective-permute-done((bf16[48,512]{1,0:T(8,128)(2,1)S(1)}, bf16[48,512]{1,0:T(8,128)(2,1)S(1)}, u32[]{:S(2)}, u32[]{:S(2)}) %collective-permute-start.22) | collective-permute-done | bytes 49184 | tf_op jit(solution)/shard_map/ppermute | solution.py:492
  63.8 2.9 %shard_map.257 = (bf16[96,768]{1,0:T(8,128)(2,1)S(1)}, bf16[2,96,768]{2,1,0:T(8,128)(2,1)S(1)}, bf16[96,768]{1,0:T(8,128)(2,1)}, bf16[96,768]{1,0:T(8,128)(2,1)S...) custom-call(bf16[48,512]{1,0:T(8,128)(2,1)S(1)} %get-tuple-element.5, ...), custom_call_target="tpu_custom_call" | custom-call | flops 1509949440 | bytes 5627904 | tf_op jit(solution)/shard_map/pallas_call | solution.py:413
  66.7 1.2 copy-done.6
  67.9 1.5 collective-permute-start.35
  71.4 3.7 %collective-permute-start.14 = (bf16[192,768]{1,0:T(8,128)(2,1)S(1)}, bf16[192,768]{1,0:T(8,128)(2,1)S(1)}, u32[]{:S(2)}, u32[]{:S(2)}) collective-permute-start(bf16[192,768]{1,0:T(8,128)(2,1)S(1)} %pad_maximum_fusion.3.refs_0_), channel_id=1, source_target_pairs={{0,24},{4,28},{8,0},{12,4},{16,8},{20,12},{24,16},{28,20},{1,25},{... | collective-permute-start | bytes 884744 | tf_op jit(solution)/shard_map/ppermute | solution.py:446
  75.5 1.5 collective-permute-start.34
  77.7 3.1 %collective-permute-done.37 = bf16[2,96,768]{2,1,0:T(8,128)(2,1)S(1)} collective-permute-done((bf16[2,96,768]{2,1,0:T(8,128)(2,1)S(1)}, bf16[2,96,768]{2,1,0:T(8,128)(2,1)S(1)}, u32[]{:S(2)}, u32[]{:S(2)}) %collective-permute-start.37) | collective-permute-done | bytes 294944 | tf_op jit(solution)/shard_map/ppermute | solution.py:461
  80.7 2.2 %collective-permute-start.36 = (bf16[96,768]{1,0:T(8,128)(2,1)}, bf16[96,768]{1,0:T(8,128)(2,1)}, u32[]{:S(2)}, u32[]{:S(2)}) collective-permute-start(bf16[96,768]{1,0:T(8,128)(2,1)} %add_convert_fusion.5), channel_id=1, source_target_pairs={{0,16},{4,20},{8,24},{12,28},{16,0},{20,4},{24,8},{28,12},{1,17},{... | collective-permute-start | bytes 442376 | tf_op jit(solution)/shard_map/ppermute | solution.py:466
  83.7 14.9 %collective-permute-start.38 = (bf16[96,768]{1,0:T(8,128)(2,1)}, bf16[96,768]{1,0:T(8,128)(2,1)}, u32[]{:S(2)}, u32[]{:S(2)}) collective-permute-start(bf16[96,768]{1,0:T(8,128)(2,1)} %get-tuple-element.94), channel_id=1, source_target_pairs={{0,8},{4,12},{8,16},{12,20},{16,24},{20,28},{24,0},{28,4},{1,9},{5... | collective-permute-start | bytes 442376 | tf_op jit(solution)/shard_map/ppermute | solution.py:467
  98.8 8.4 %collective-permute-done.16.refs_6_ = bf16[192,768]{1,0:T(8,128)(2,1)} collective-permute-done((bf16[192,768]{1,0:T(8,128)(2,1)S(1)}, bf16[192,768]{1,0:T(8,128)(2,1)}, u32[]{:S(2)}, u32[]{:S(2)}) %collective-permute-start.16) | collective-permute-done | bytes 294944 | tf_op jit(solution)/shard_map/ppermute | solution.py:447
  107.1 1.4 collective-permute-start.11
  110.3 1.4 collective-permute-start.15
  112.3 1.2 convert_add_fusion.3
  114.7 2.4 %collective-permute-done.11.refs_1_ = bf16[192,768]{1,0:T(8,128)(2,1)S(1)} collective-permute-done((bf16[192,768]{1,0:T(8,128)(2,1)S(1)}, bf16[192,768]{1,0:T(8,128)(2,1)S(1)}, u32[]{:S(2)}, u32[]{:S(2)}) %collective-permute-start.11) | collective-permute-done | bytes 294944 | tf_op jit(solution)/shard_map/ppermute | solution.py:445
  117.0 6.3 %collective-permute-done.13.refs_3_ = bf16[192,768]{1,0:T(8,128)(2,1)S(1)} collective-permute-done((bf16[192,768]{1,0:T(8,128)(2,1)S(1)}, bf16[192,768]{1,0:T(8,128)(2,1)S(1)}, u32[]{:S(2)}, u32[]{:S(2)}) %collective-permute-start.13) | collective-permute-done | bytes 294944 | tf_op jit(solution)/shard_map/ppermute | solution.py:448
  123.4 6.3 %collective-permute-done.15.refs_5_ = bf16[192,768]{1,0:T(8,128)(2,1)S(1)} collective-permute-done((bf16[192,768]{1,0:T(8,128)(2,1)S(1)}, bf16[192,768]{1,0:T(8,128)(2,1)S(1)}, u32[]{:S(2)}, u32[]{:S(2)}) %collective-permute-start.15) | collective-permute-done | bytes 294944 | tf_op jit(solution)/shard_map/ppermute | solution.py:449
  129.7 5.2 %collective-permute-done.17.refs_7_ = bf16[192,768]{1,0:T(8,128)(2,1)S(1)} collective-permute-done((bf16[192,768]{1,0:T(8,128)(2,1)}, bf16[192,768]{1,0:T(8,128)(2,1)S(1)}, u32[]{:S(2)}, u32[]{:S(2)}) %collective-permute-start.17) | collective-permute-done | bytes 294944 | tf_op jit(solution)/shard_map/ppermute | solution.py:450
  135.9 1.4 copy-done.5
  137.3 1.4 copy-done.7
  140.6 8.6 %shard_map.258 = (bf16[200,768]{1,0:T(8,128)(2,1)S(1)}, bf16[2,200,768]{2,1,0:T(8,128)(2,1)}, bf16[200,768]{1,0:T(8,128)(2,1)}, bf16[200,768]{1,0:T(8,128)(2,1)S...) custom-call(bf16[192,768]{1,0:T(8,128)(2,1)S(1)} %copy-done.3, ...), custom_call_target="tpu_custom_call" | custom-call | flops 3623878656 | bytes 7913472 | tf_op jit(solution)/shard_map/pallas_call | solution.py:413
  149.2 1.2 copy-done
  150.4 1.4 collective-permute-start.27
  152.4 1.4 collective-permute-start.26
  154.5 6.1 %collective-permute-done.27 = bf16[200,768]{1,0:T(8,128)(2,1)S(1)} collective-permute-done((bf16[200,768]{1,0:T(8,128)(2,1)S(1)}, bf16[200,768]{1,0:T(8,128)(2,1)S(1)}, u32[]{:S(2)}, u32[]{:S(2)}) %collective-permute-start.27) | collective-permute-done | bytes 307232 | tf_op jit(solution)/shard_map/ppermute | solution.py:460
  163.6 10.3 %collective-permute-done.29 = bf16[2,200,768]{2,1,0:T(8,128)(2,1)} collective-permute-done((bf16[2,200,768]{2,1,0:T(8,128)(2,1)}, bf16[2,200,768]{2,1,0:T(8,128)(2,1)}, u32[]{:S(2)}, u32[]{:S(2)}) %collective-permute-start.29) | collective-permute-done | bytes 614432 | tf_op jit(solution)/shard_map/ppermute | solution.py:461
  173.9 1.2 fusion.23
  175.2 3.8 %collective-permute-start.31 = (bf16[200,768]{1,0:T(8,128)(2,1)S(1)}, bf16[200,768]{1,0:T(8,128)(2,1)S(1)}, u32[]{:S(2)}, u32[]{:S(2)}) collective-permute-start(bf16[200,768]{1,0:T(8,128)(2,1)S(1)} %get-tuple-element.89), channel_id=1, source_target_pairs={{0,24},{4,28},{8,0},{12,4},{16,8},{20,12},{24,16},{28,20},{1,25},{... | collective-permute-start | bytes 921608 | tf_op jit(solution)/shard_map/ppermute | solution.py:468
  179.0 1.3 convert_add_fusion
  180.3 5.3 %collective-permute-done.30 = bf16[200,768]{1,0:T(8,128)(2,1)S(1)} collective-permute-done((bf16[200,768]{1,0:T(8,128)(2,1)S(1)}, bf16[200,768]{1,0:T(8,128)(2,1)S(1)}, u32[]{:S(2)}, u32[]{:S(2)}) %collective-permute-start.30) | collective-permute-done | bytes 307232 | tf_op jit(solution)/shard_map/ppermute | solution.py:467
  185.7 1.4 collective-permute-done.31
  187.0 1.3 convert_add_fusion.1
  191.3 2.1 %collective-permute-done.32 = bf16[2,32,768]{2,1,0:T(8,128)(2,1)S(1)} collective-permute-done((bf16[2,32,768]{2,1,0:T(8,128)(2,1)S(1)}, bf16[2,32,768]{2,1,0:T(8,128)(2,1)S(1)}, u32[]{:S(2)}, u32[]{:S(2)}) %collective-permute-start.32) | collective-permute-done | bytes 98336 | tf_op jit(solution)/shard_map/ppermute | solution.py:64
  (200 shorter events, 41.1 us)
Async XLA Ops:
  2.6 17.7 %collective-permute-start.9 = (bf16[256,768]{1,0:T(8,128)(2,1)S(1)}, bf16[256,768]{1,0:T(8,128)(2,1)S(1)}, u32[]{:S(2)}, u32[]{:S(2)}) collective-permute-start(bf16[256,768]{1,0:T(8,128)(2,1)S(1)} %constant_dynamic-update-slice_fusion), channel_id=1, source_target_pairs={{0,2},{2,0},{1,3},{3,1},{4,6},{6,4},{5,7},{7,5},{8,10},{10,8},{9,1... | collective-permute-start | bytes 1179656 | tf_op jit(solution)/shard_map/ppermute | solution.py:76
  9.5 9.1 %collective-permute-start = (bf16[2,32,1344]{2,1,0:T(8,128)(2,1)S(1)}, bf16[2,32,1344]{2,1,0:T(8,128)(2,1)S(1)}, u32[]{:S(2)}, u32[]{:S(2)}) collective-permute-start(bf16[2,32,1344]{2,1,0:T(8,128)(2,1)S(1)} %dynamic-slice_bitcast_fusion), channel_id=1, source_target_pairs={{0,2},{2,0},{1,3},{3,1},{4,6},{6,4},{5,7},{7,5},{8,10},{10,8},{9,1... | collective-permute-start | bytes 516104 | tf_op jit(solution)/shard_map/ppermute | solution.py:64
  18.6 1.5 collective-permute-start.1
  21.3 20.6 %collective-permute-start.10 = (bf16[2,256,768]{2,1,0:T(8,128)(2,1)}, bf16[2,256,768]{2,1,0:T(8,128)(2,1)}, u32[]{:S(2)}, u32[]{:S(2)}) collective-permute-start(bf16[2,256,768]{2,1,0:T(8,128)(2,1)} %pad_maximum_fusion.1), channel_id=1, source_target_pairs={{0,1},{1,0},{2,3},{3,2},{4,5},{5,4},{6,7},{7,6},{8,9},{9,8},{10,11... | collective-permute-start | bytes 2359304 | tf_op jit(solution)/shard_map/ppermute | solution.py:78
  21.6 8.9 %collective-permute-start.3 = (bf16[104,768]{1,0:T(8,128)(2,1)S(1)}, bf16[104,768]{1,0:T(8,128)(2,1)S(1)}, u32[]{:S(2)}, u32[]{:S(2)}) collective-permute-start(bf16[104,768]{1,0:T(8,128)(2,1)S(1)} %pad_maximum_fusion.5.refs_0_), channel_id=1, source_target_pairs={{0,8},{4,12},{8,16},{12,20},{16,24},{20,28},{24,0},{28,4},{1,9},{5... | collective-permute-start | bytes 479240 | tf_op jit(solution)/shard_map/ppermute | solution.py:444
  23.5 9.5 %collective-permute-start.5 = (bf16[104,768]{1,0:T(8,128)(2,1)S(1)}, bf16[104,768]{1,0:T(8,128)(2,1)S(1)}, u32[]{:S(2)}, u32[]{:S(2)}) collective-permute-start(bf16[104,768]{1,0:T(8,128)(2,1)S(1)} %pad_maximum_fusion.5.refs_0_), channel_id=1, source_target_pairs={{0,24},{4,28},{8,0},{12,4},{16,8},{20,12},{24,16},{28,20},{1,25},{... | collective-permute-start | bytes 479240 | tf_op jit(solution)/shard_map/ppermute | solution.py:446
  25.8 14.7 %collective-permute-start.7 = (bf16[104,768]{1,0:T(8,128)(2,1)S(1)}, bf16[104,768]{1,0:T(8,128)(2,1)S(1)}, u32[]{:S(2)}, u32[]{:S(2)}) collective-permute-start(bf16[104,768]{1,0:T(8,128)(2,1)S(1)} %pad_maximum_fusion.5.refs_0_), channel_id=1, source_target_pairs={{0,16},{4,20},{8,24},{12,28},{16,0},{20,4},{24,8},{28,12},{1,17},{... | collective-permute-start | bytes 479240 | tf_op jit(solution)/shard_map/ppermute | solution.py:447
  27.8 16.3 %collective-permute-start.2 = (bf16[104,768]{1,0:T(8,128)(2,1)S(1)}, bf16[104,768]{1,0:T(8,128)(2,1)S(1)}, u32[]{:S(2)}, u32[]{:S(2)}) collective-permute-start(bf16[104,768]{1,0:T(8,128)(2,1)S(1)} %pad_maximum_fusion.5.refs_0_), channel_id=1, source_target_pairs={{0,4},{4,0},{8,12},{12,8},{16,20},{20,16},{24,28},{28,24},{1,5},{5... | collective-permute-start | bytes 479240 | tf_op jit(solution)/shard_map/ppermute | solution.py:445
  30.5 13.6 %collective-permute-start.4 = (bf16[104,768]{1,0:T(8,128)(2,1)S(1)}, bf16[104,768]{1,0:T(8,128)(2,1)S(1)}, u32[]{:S(2)}, u32[]{:S(2)}) collective-permute-start(bf16[104,768]{1,0:T(8,128)(2,1)S(1)} %collective-permute-done.3.refs_2_), channel_id=1, source_target_pairs={{0,4},{4,0},{8,12},{12,8},{16,20},{20,16},{24,28},{28,24},{1,5},{5... | collective-permute-start | bytes 479240 | tf_op jit(solution)/shard_map/ppermute | solution.py:448
  33.0 11.1 %collective-permute-start.6 = (bf16[104,768]{1,0:T(8,128)(2,1)S(1)}, bf16[104,768]{1,0:T(8,128)(2,1)S(1)}, u32[]{:S(2)}, u32[]{:S(2)}) collective-permute-start(bf16[104,768]{1,0:T(8,128)(2,1)S(1)} %collective-permute-done.5.refs_4_), channel_id=1, source_target_pairs={{0,4},{4,0},{8,12},{12,8},{16,20},{20,16},{24,28},{28,24},{1,5},{5... | collective-permute-start | bytes 479240 | tf_op jit(solution)/shard_map/ppermute | solution.py:449
  40.4 6.0 %collective-permute-start.8 = (bf16[104,768]{1,0:T(8,128)(2,1)S(1)}, bf16[104,768]{1,0:T(8,128)(2,1)S(1)}, u32[]{:S(2)}, u32[]{:S(2)}) collective-permute-start(bf16[104,768]{1,0:T(8,128)(2,1)S(1)} %collective-permute-done.7.refs_6_), channel_id=1, source_target_pairs={{0,4},{4,0},{8,12},{12,8},{16,20},{20,16},{24,28},{28,24},{1,5},{5... | collective-permute-start | bytes 479240 | tf_op jit(solution)/shard_map/ppermute | solution.py:450
  47.0 3.8 %collective-permute-start.18 = (bf16[48,512]{1,0:T(8,128)(2,1)S(1)}, bf16[48,512]{1,0:T(8,128)(2,1)S(1)}, u32[]{:S(2)}, u32[]{:S(2)}) collective-permute-start(bf16[48,512]{1,0:T(8,128)(2,1)S(1)} %get-tuple-element.51), channel_id=1, source_target_pairs={{0,1},{1,0},{2,3},{3,2},{4,5},{5,4},{6,7},{7,6},{8,9},{9,8},{10,11... | collective-permute-start | bytes 147464 | tf_op jit(solution)/shard_map/ppermute | solution.py:492
  47.1 4.2 %collective-permute-start.19 = (bf16[48,512]{1,0:T(8,128)(2,1)S(1)}, bf16[48,512]{1,0:T(8,128)(2,1)S(1)}, u32[]{:S(2)}, u32[]{:S(2)}) collective-permute-start(bf16[48,512]{1,0:T(8,128)(2,1)S(1)} %get-tuple-element.52), channel_id=1, source_target_pairs={{0,2},{1,3},{2,0},{3,1},{4,6},{5,7},{6,4},{7,5},{8,10},{9,11},{10,... | collective-permute-start | bytes 147464 | tf_op jit(solution)/shard_map/ppermute | solution.py:492
  48.7 3.7 %collective-permute-start.20 = (bf16[48,512]{1,0:T(8,128)(2,1)S(1)}, bf16[48,512]{1,0:T(8,128)(2,1)S(1)}, u32[]{:S(2)}, u32[]{:S(2)}) collective-permute-start(bf16[48,512]{1,0:T(8,128)(2,1)S(1)} %get-tuple-element.53), channel_id=1, source_target_pairs={{0,3},{1,2},{2,1},{3,0},{4,7},{5,6},{6,5},{7,4},{8,11},{9,10},{10,... | collective-permute-start | bytes 147464 | tf_op jit(solution)/shard_map/ppermute | solution.py:492
  58.5 1.9 collective-permute-start.21
  58.8 4.1 %collective-permute-start.22 = (bf16[48,512]{1,0:T(8,128)(2,1)S(1)}, bf16[48,512]{1,0:T(8,128)(2,1)S(1)}, u32[]{:S(2)}, u32[]{:S(2)}) collective-permute-start(bf16[48,512]{1,0:T(8,128)(2,1)S(1)} %get-tuple-element.56), channel_id=1, source_target_pairs={{0,2},{1,3},{2,0},{3,1},{4,6},{5,7},{6,4},{7,5},{8,10},{9,11},{10,... | collective-permute-start | bytes 147464 | tf_op jit(solution)/shard_map/ppermute | solution.py:492
  59.9 3.9 %collective-permute-start.23 = (bf16[48,512]{1,0:T(8,128)(2,1)S(1)}, bf16[48,512]{1,0:T(8,128)(2,1)S(1)}, u32[]{:S(2)}, u32[]{:S(2)}) collective-permute-start(bf16[48,512]{1,0:T(8,128)(2,1)S(1)} %get-tuple-element.57), channel_id=1, source_target_pairs={{0,3},{1,2},{2,1},{3,0},{4,7},{5,6},{6,5},{7,4},{8,11},{9,10},{10,... | collective-permute-start | bytes 147464 | tf_op jit(solution)/shard_map/ppermute | solution.py:492
  67.9 30.8 %copy-start.4 = (f32[512,768]{1,0:T(8,128)}, f32[512,768]{1,0:T(8,128)S(1)}, u32[]{:S(2)}) copy-start(f32[512,768]{1,0:T(8,128)S(1)} %get-tuple-element.61.refs_11_) | copy-start | bytes 4718596
  67.9 7.6 %collective-permute-start.35 = (bf16[96,768]{1,0:T(8,128)(2,1)S(1)}, bf16[96,768]{1,0:T(8,128)(2,1)S(1)}, u32[]{:S(2)}, u32[]{:S(2)}) collective-permute-start(bf16[96,768]{1,0:T(8,128)(2,1)S(1)} %get-tuple-element.75), channel_id=1, source_target_pairs={{0,4},{4,0},{8,12},{12,8},{16,20},{20,16},{24,28},{28,24},{1,5},{5... | collective-permute-start | bytes 442376 | tf_op jit(solution)/shard_map/ppermute | solution.py:460
  70.5 10.2 %collective-permute-start.37 = (bf16[2,96,768]{2,1,0:T(8,128)(2,1)S(1)}, bf16[2,96,768]{2,1,0:T(8,128)(2,1)S(1)}, u32[]{:S(2)}, u32[]{:S(2)}) collective-permute-start(bf16[2,96,768]{2,1,0:T(8,128)(2,1)S(1)} %get-tuple-element.77), channel_id=1, source_target_pairs={{0,4},{4,0},{8,12},{12,8},{16,20},{20,16},{24,28},{28,24},{1,5},{5... | collective-permute-start | bytes 884744 | tf_op jit(solution)/shard_map/ppermute | solution.py:461
  71.1 63.8 %copy-start.2 = (bf16[192,768]{1,0:T(8,128)(2,1)}, bf16[192,768]{1,0:T(8,128)(2,1)S(1)}, u32[]{:S(2)}) copy-start(bf16[192,768]{1,0:T(8,128)(2,1)S(1)} %pad_maximum_fusion.3.refs_0_) | copy-start | bytes 884740
  71.1 12.6 %collective-permute-start.12 = (bf16[192,768]{1,0:T(8,128)(2,1)S(1)}, bf16[192,768]{1,0:T(8,128)(2,1)S(1)}, u32[]{:S(2)}, u32[]{:S(2)}) collective-permute-start(bf16[192,768]{1,0:T(8,128)(2,1)S(1)} %pad_maximum_fusion.3.refs_0_), channel_id=1, source_target_pairs={{0,8},{4,12},{8,16},{12,20},{16,24},{20,28},{24,0},{28,4},{1,9},{5... | collective-permute-start | bytes 884744 | tf_op jit(solution)/shard_map/ppermute | solution.py:444
  71.4 27.3 %collective-permute-start.14 = (bf16[192,768]{1,0:T(8,128)(2,1)S(1)}, bf16[192,768]{1,0:T(8,128)(2,1)S(1)}, u32[]{:S(2)}, u32[]{:S(2)}) collective-permute-start(bf16[192,768]{1,0:T(8,128)(2,1)S(1)} %pad_maximum_fusion.3.refs_0_), channel_id=1, source_target_pairs={{0,24},{4,28},{8,0},{12,4},{16,8},{20,12},{24,16},{28,20},{1,25},{... | collective-permute-start | bytes 884744 | tf_op jit(solution)/shard_map/ppermute | solution.py:446
  75.0 32.1 %collective-permute-start.16 = (bf16[192,768]{1,0:T(8,128)(2,1)S(1)}, bf16[192,768]{1,0:T(8,128)(2,1)}, u32[]{:S(2)}, u32[]{:S(2)}) collective-permute-start(bf16[192,768]{1,0:T(8,128)(2,1)S(1)} %pad_maximum_fusion.3.refs_0_), channel_id=1, source_target_pairs={{0,16},{4,20},{8,24},{12,28},{16,0},{20,4},{24,8},{28,12},{1,17},{... | collective-permute-start | bytes 884744 | tf_op jit(solution)/shard_map/ppermute | solution.py:447
  75.5 33.1 %collective-permute-start.34 = (bf16[96,768]{1,0:T(8,128)(2,1)}, bf16[96,768]{1,0:T(8,128)(2,1)}, u32[]{:S(2)}, u32[]{:S(2)}) collective-permute-start(bf16[96,768]{1,0:T(8,128)(2,1)} %get-tuple-element.73), channel_id=1, source_target_pairs={{0,4},{4,0},{8,12},{12,8},{16,20},{20,16},{24,28},{28,24},{1,5},{5... | collective-permute-start | bytes 442376 | tf_op jit(solution)/shard_map/ppermute | solution.py:462
  80.7 29.5 %collective-permute-start.36 = (bf16[96,768]{1,0:T(8,128)(2,1)}, bf16[96,768]{1,0:T(8,128)(2,1)}, u32[]{:S(2)}, u32[]{:S(2)}) collective-permute-start(bf16[96,768]{1,0:T(8,128)(2,1)} %add_convert_fusion.5), channel_id=1, source_target_pairs={{0,16},{4,20},{8,24},{12,28},{16,0},{20,4},{24,8},{28,12},{1,17},{... | collective-permute-start | bytes 442376 | tf_op jit(solution)/shard_map/ppermute | solution.py:466
  83.7 51.1 %copy-start.8 = (bf16[192,768]{1,0:T(8,128)(2,1)}, bf16[192,768]{1,0:T(8,128)(2,1)S(1)}, u32[]{:S(2)}) copy-start(bf16[192,768]{1,0:T(8,128)(2,1)S(1)} %collective-permute-done.12.refs_2_) | copy-start | bytes 884740
  83.7 27.9 %collective-permute-start.38 = (bf16[96,768]{1,0:T(8,128)(2,1)}, bf16[96,768]{1,0:T(8,128)(2,1)}, u32[]{:S(2)}, u32[]{:S(2)}) collective-permute-start(bf16[96,768]{1,0:T(8,128)(2,1)} %get-tuple-element.94), channel_id=1, source_target_pairs={{0,8},{4,12},{8,16},{12,20},{16,24},{20,28},{24,0},{28,4},{1,9},{5... | collective-permute-start | bytes 442376 | tf_op jit(solution)/shard_map/ppermute | solution.py:467
  98.7 36.2 %copy-start.10 = (bf16[192,768]{1,0:T(8,128)(2,1)}, bf16[192,768]{1,0:T(8,128)(2,1)S(1)}, u32[]{:S(2)}) copy-start(bf16[192,768]{1,0:T(8,128)(2,1)S(1)} %collective-permute-done.14.refs_4_) | copy-start | bytes 884740
  98.7 13.6 %collective-permute-start.39 = (bf16[96,768]{1,0:T(8,128)(2,1)}, bf16[96,768]{1,0:T(8,128)(2,1)}, u32[]{:S(2)}, u32[]{:S(2)}) collective-permute-start(bf16[96,768]{1,0:T(8,128)(2,1)} %get-tuple-element.95), channel_id=1, source_target_pairs={{0,24},{4,28},{8,0},{12,4},{16,8},{20,12},{24,16},{28,20},{1,25},{... | collective-permute-start | bytes 442376 | tf_op jit(solution)/shard_map/ppermute | solution.py:468
  107.1 9.9 %collective-permute-start.11 = (bf16[192,768]{1,0:T(8,128)(2,1)S(1)}, bf16[192,768]{1,0:T(8,128)(2,1)S(1)}, u32[]{:S(2)}, u32[]{:S(2)}) collective-permute-start(bf16[192,768]{1,0:T(8,128)(2,1)S(1)} %pad_maximum_fusion.3.refs_0_), channel_id=1, source_target_pairs={{0,4},{4,0},{8,12},{12,8},{16,20},{20,16},{24,28},{28,24},{1,5},{5... | collective-permute-start | bytes 884744 | tf_op jit(solution)/shard_map/ppermute | solution.py:445
  108.6 14.8 %collective-permute-start.13 = (bf16[192,768]{1,0:T(8,128)(2,1)S(1)}, bf16[192,768]{1,0:T(8,128)(2,1)S(1)}, u32[]{:S(2)}, u32[]{:S(2)}) collective-permute-start(bf16[192,768]{1,0:T(8,128)(2,1)S(1)} %collective-permute-done.12.refs_2_), channel_id=1, source_target_pairs={{0,4},{4,0},{8,12},{12,8},{16,20},{20,16},{24,28},{28,24},{1,5},{5... | collective-permute-start | bytes 884744 | tf_op jit(solution)/shard_map/ppermute | solution.py:448
  110.3 19.4 %collective-permute-start.15 = (bf16[192,768]{1,0:T(8,128)(2,1)S(1)}, bf16[192,768]{1,0:T(8,128)(2,1)S(1)}, u32[]{:S(2)}, u32[]{:S(2)}) collective-permute-start(bf16[192,768]{1,0:T(8,128)(2,1)S(1)} %collective-permute-done.14.refs_4_), channel_id=1, source_target_pairs={{0,4},{4,0},{8,12},{12,8},{16,20},{20,16},{24,28},{28,24},{1,5},{5... | collective-permute-start | bytes 884744 | tf_op jit(solution)/shard_map/ppermute | solution.py:449
  111.7 23.2 %collective-permute-start.17 = (bf16[192,768]{1,0:T(8,128)(2,1)}, bf16[192,768]{1,0:T(8,128)(2,1)S(1)}, u32[]{:S(2)}, u32[]{:S(2)}) collective-permute-start(bf16[192,768]{1,0:T(8,128)(2,1)} %collective-permute-done.16.refs_6_), channel_id=1, source_target_pairs={{0,4},{4,0},{8,12},{12,8},{16,20},{20,16},{24,28},{28,24},{1,5},{5... | collective-permute-start | bytes 884744 | tf_op jit(solution)/shard_map/ppermute | solution.py:450
  113.5 40.3 %collective-permute-start.40 = (bf16[2,24,576]{2,1,0:T(8,128)(2,1)S(1)}, bf16[2,24,576]{2,1,0:T(8,128)(2,1)S(1)}, u32[]{:S(2)}, u32[]{:S(2)}) collective-permute-start(bf16[2,24,576]{2,1,0:T(8,128)(2,1)S(1)} %dynamic-slice_bitcast_fusion.1), channel_id=1, source_target_pairs={{0,2},{2,0},{1,3},{3,1},{4,6},{6,4},{5,7},{7,5},{8,10},{10,8},{9,1... | collective-permute-start | bytes 165896 | tf_op jit(solution)/shard_map/ppermute | solution.py:64
  150.4 10.2 %collective-permute-start.27 = (bf16[200,768]{1,0:T(8,128)(2,1)S(1)}, bf16[200,768]{1,0:T(8,128)(2,1)S(1)}, u32[]{:S(2)}, u32[]{:S(2)}) collective-permute-start(bf16[200,768]{1,0:T(8,128)(2,1)S(1)} %get-tuple-element.69), channel_id=1, source_target_pairs={{0,4},{4,0},{8,12},{12,8},{16,20},{20,16},{24,28},{28,24},{1,5},{5... | collective-permute-start | bytes 921608 | tf_op jit(solution)/shard_map/ppermute | solution.py:460
  151.8 22.1 %collective-permute-start.29 = (bf16[2,200,768]{2,1,0:T(8,128)(2,1)}, bf16[2,200,768]{2,1,0:T(8,128)(2,1)}, u32[]{:S(2)}, u32[]{:S(2)}) collective-permute-start(bf16[2,200,768]{2,1,0:T(8,128)(2,1)} %get-tuple-element.71), channel_id=1, source_target_pairs={{0,4},{4,0},{8,12},{12,8},{16,20},{20,16},{24,28},{28,24},{1,5},{5... | collective-permute-start | bytes 1843208 | tf_op jit(solution)/shard_map/ppermute | solution.py:461
  152.4 27.9 %collective-permute-start.26 = (bf16[200,768]{1,0:T(8,128)(2,1)}, bf16[200,768]{1,0:T(8,128)(2,1)}, u32[]{:S(2)}, u32[]{:S(2)}) collective-permute-start(bf16[200,768]{1,0:T(8,128)(2,1)} %get-tuple-element.67), channel_id=1, source_target_pairs={{0,4},{4,0},{8,12},{12,8},{16,20},{20,16},{24,28},{28,24},{1,5},{5... | collective-permute-start | bytes 921608 | tf_op jit(solution)/shard_map/ppermute | solution.py:462
  153.8 25.1 %collective-permute-start.24 = (bf16[2,128,1536]{2,1,0:T(8,128)(2,1)}, bf16[2,128,1536]{2,1,0:T(8,128)(2,1)}, u32[]{:S(2)}, u32[]{:S(2)}) collective-permute-start(bf16[2,128,1536]{2,1,0:T(8,128)(2,1)} %get-tuple-element.65), channel_id=1, source_target_pairs={{0,1},{1,0},{2,3},{3,2},{4,5},{5,4},{6,7},{7,6},{8,9},{9,8},{10,11... | collective-permute-start | bytes 2359304 | tf_op jit(solution)/shard_map/ppermute | solution.py:834
  153.9 8.4 %collective-permute-start.41 = (bf16[2,24,576]{2,1,0:T(8,128)(2,1)S(1)}, bf16[2,24,576]{2,1,0:T(8,128)(2,1)S(1)}, u32[]{:S(2)}, u32[]{:S(2)}) collective-permute-start(bf16[2,24,576]{2,1,0:T(8,128)(2,1)S(1)} %fusion.49), channel_id=1, source_target_pairs={{0,1},{1,0},{2,3},{3,2},{4,5},{5,4},{6,7},{7,6},{8,9},{9,8},{10,11... | collective-permute-start | bytes 165896 | tf_op jit(solution)/shard_map/ppermute | solution.py:66
  161.4 18.9 %collective-permute-start.28 = (bf16[200,768]{1,0:T(8,128)(2,1)}, bf16[200,768]{1,0:T(8,128)(2,1)}, u32[]{:S(2)}, u32[]{:S(2)}) collective-permute-start(bf16[200,768]{1,0:T(8,128)(2,1)} %add_convert_fusion.2), channel_id=1, source_target_pairs={{0,16},{4,20},{8,24},{12,28},{16,0},{20,4},{24,8},{28,12},{1,17},{... | collective-permute-start | bytes 921608 | tf_op jit(solution)/shard_map/ppermute | solution.py:466
  162.5 16.4 %copy-start.1 = (f32[2,128,1536]{2,1,0:T(8,128)S(1)}, f32[2,128,1536]{2,1,0:T(8,128)}, u32[]{:S(2)}) copy-start(f32[2,128,1536]{2,1,0:T(8,128)} %copy-done) | copy-start | bytes 4718596
  175.1 10.6 %collective-permute-start.30 = (bf16[200,768]{1,0:T(8,128)(2,1)S(1)}, bf16[200,768]{1,0:T(8,128)(2,1)S(1)}, u32[]{:S(2)}, u32[]{:S(2)}) collective-permute-start(bf16[200,768]{1,0:T(8,128)(2,1)S(1)} %get-tuple-element.88), channel_id=1, source_target_pairs={{0,8},{4,12},{8,16},{12,20},{16,24},{20,28},{24,0},{28,4},{1,9},{5... | collective-permute-start | bytes 921608 | tf_op jit(solution)/shard_map/ppermute | solution.py:467
  175.2 11.9 %collective-permute-start.31 = (bf16[200,768]{1,0:T(8,128)(2,1)S(1)}, bf16[200,768]{1,0:T(8,128)(2,1)S(1)}, u32[]{:S(2)}, u32[]{:S(2)}) collective-permute-start(bf16[200,768]{1,0:T(8,128)(2,1)S(1)} %get-tuple-element.89), channel_id=1, source_target_pairs={{0,24},{4,28},{8,0},{12,4},{16,8},{20,12},{24,16},{28,20},{1,25},{... | collective-permute-start | bytes 921608 | tf_op jit(solution)/shard_map/ppermute | solution.py:468
  180.3 9.2 %copy-start.15 = (f32[2,128,1536]{2,1,0:T(8,128)}, f32[2,128,1536]{2,1,0:T(8,128)S(1)}, u32[]{:S(2)}) copy-start(f32[2,128,1536]{2,1,0:T(8,128)S(1)} %convert_add_fusion) | copy-start | bytes 4718596
  188.4 5.1 %collective-permute-start.32 = (bf16[2,32,768]{2,1,0:T(8,128)(2,1)S(1)}, bf16[2,32,768]{2,1,0:T(8,128)(2,1)S(1)}, u32[]{:S(2)}, u32[]{:S(2)}) collective-permute-start(bf16[2,32,768]{2,1,0:T(8,128)(2,1)S(1)} %fusion.41), channel_id=1, source_target_pairs={{0,2},{2,0},{1,3},{3,1},{4,6},{6,4},{5,7},{7,5},{8,10},{10,8},{9,1... | collective-permute-start | bytes 294920 | tf_op jit(solution)/shard_map/ppermute | solution.py:64
  189.5 8.5 %collective-permute-start.25 = (bf16[128,1536]{1,0:T(8,128)(2,1)S(1)}, bf16[128,1536]{1,0:T(8,128)(2,1)S(1)}, u32[]{:S(2)}, u32[]{:S(2)}) collective-permute-start(bf16[128,1536]{1,0:T(8,128)(2,1)S(1)} %fusion.18), channel_id=1, source_target_pairs={{0,2},{2,0},{1,3},{3,1},{4,6},{6,4},{5,7},{7,5},{8,10},{10,8},{9,1... | collective-permute-start | bytes 1179656 | tf_op jit(solution)/shard_map/ppermute | solution.py:835
  193.5 1.4 collective-permute-start.33
  (19 other events, 53.2 us)

commit v4 on v3

--- a/solution.py
+++ b/solution.py
@@ -408,12 +408,15 @@
 SCALE = HEAD_DIM**-0.5
 
 
-def kernel_call(body, outs, args, scratch=(), megabytes=24, flops=0):
+def kernel_call(body, outs, args, scratch=(), megabytes=24, flops=0, apart=0):
     moved = sum(a.size * a.dtype.itemsize for a in args)
+    held = [pl.BlockSpec(memory_space=pl.ANY)] * apart
+    held += [pl.BlockSpec(memory_space=pltpu.VMEM)] * (len(args) - apart)
     return pl.pallas_call(
         body,
         out_shape=tuple(jax.ShapeDtypeStruct(shape, kind) for shape, kind in outs),
-        scratch_shapes=[pltpu.VMEM(shape, kind) for shape, kind in scratch],
+        in_specs=held,
+        scratch_shapes=[pltpu.VMEM(*item) if isinstance(item, tuple) else item for item in scratch],
         compiler_params=pltpu.CompilerParams(vmem_limit_bytes=megabytes << 20),
         cost_estimate=pl.CostEstimate(flops=flops, bytes_accessed=moved, transcendentals=0),
     )(*args)
@@ -447,7 +450,7 @@
     near2 = lax.ppermute(block, "dp", along(2))
     far1 = lax.ppermute(near1, "dp", SIDE_SWAP)
     far3 = lax.ppermute(near3, "dp", SIDE_SWAP)
-    far2 = lax.ppermute(near2, "dp", SIDE_SWAP)
+    far2 = lax.ppermute(once(near2, far3), "dp", SIDE_SWAP)
     return (block, far0, near1, far1, near3, far3, near2, far2)
 
 
@@ -467,7 +470,7 @@
     got1 = lax.ppermute(sum1, "dp", along(1))
     got3 = lax.ppermute(sum3, "dp", along(3))
     total = keep0.astype(F32) + moved0.astype(F32)
-    return total + got2.astype(F32) + got1.astype(F32) + got3.astype(F32)
+    return (moved2, moved13), total + got2.astype(F32) + got1.astype(F32) + got3.astype(F32)
 
 
 def pick_blocks(block_of, send2, send13, send0, keep2, keep13, keep0):
@@ -483,6 +486,10 @@
 def pick_shapes(rows, width):
     one, two = ((rows, width), BF), ((2, rows, width), BF)
     return (one, two, one, one, two, one)
+
+
+def once(values, *others):
+    return lax.optimization_barrier((values, *others))[0]
 
 
 def seq_shuffle(blocks):
@@ -634,56 +641,225 @@
         sums[5:6, :] += jnp.sum(d_joined[rows, :].astype(F32), axis=0, keepdims=True)
 
 
-def mlp_kernel(per_line, *refs):
-    pieces, (unit, dy, vectors, attn_out, scaled, sums_in) = refs[:8], refs[8:14]
-    picks, (give, keep), scratch = refs[14:20], refs[20:22], refs[22:]
-    up, down, mlp_in, act, d_up, up_grad, down_grad, pair, sums = scratch
-    for piece, owner in zip(pieces, piece_owners()):
-        rows = pl.ds(pl.multiple_of(owner * per_line, per_line), per_line)
-        up[rows, :] = piece[:per_line, :]
-        down[rows, :] = piece[per_line:, :]
-    gain, shift, bias = vectors[2:3, :], vectors[3:4, :], vectors[7:8, :]
+def pack_kernel(deep, *refs):
+    qkv, up, vectors_in, blocks, (all_blocks, row_block) = *refs[:2], refs[2:9], refs[9:13], refs[13:]
+    width = qkv.shape[1] // 3
+    own = width // 4
+    units = up.shape[1] // 32
+    half = up.shape[1] // 8
+    me = lax.axis_index("seq")
+    device = 4 * lax.axis_index("dp") + me
+    row_block[...] = jnp.zeros(row_block.shape, F32)
+    for r in range(6):
+        row_block[r : r + 1, :deep] = vectors_in[r][...].astype(F32)
+    vectors = pltpu.roll(row_block[:, :width], device * deep, 1)
+    row_block[0:6, :] = jnp.zeros((6, row_block.shape[1]), F32)
+    row_block[6:7, : 3 * deep] = vectors_in[6][...].astype(F32)
+    bias_rows = pltpu.roll(row_block[...], device * (3 * deep), 1)
+    up_values, qkv_values = up[...].astype(F32), qkv[...].astype(F32)
+    for t in range(4):
+        parts = [up_values[:, ((l * 2 + y) * 4 + t) * units :][:, :units] for y in range(2) for l in range(4)]
+        all_blocks[t, :deep, : 2 * half] = jnp.concatenate(parts, axis=1)
+        all_blocks[t, deep:, : 2 * half] = vectors
+        for part in range(3):
+            lanes = slice(part * width + t * own, part * width + (t + 1) * own)
+            place = slice(2 * half + part * own, 2 * half + (part + 1) * own)
+            all_blocks[t, :deep, place] = qkv_values[:, lanes]
+            all_blocks[t, deep:, place] = bias_rows[:, lanes]
+    for j in range(4):
+        blocks[j][...] = all_blocks[lax.bitwise_xor(me, j)].astype(BF)
+
+
+def unpack_kernel(deep, r0, r1, r2, r3, dense, up_bias, attn_piece, up_keep, up_give, rows32, row_block):
+    me = lax.axis_index("seq")
+    line, side = line_and_side()
+    width = dense.shape[1]
+    quarter = width // 4
+    half = up_keep.shape[1]
+    own = 3 * quarter
+    extra = jnp.zeros((8, rows32.shape[1]), F32)
+    for j, ref in enumerate((r0, r1, r2, r3)):
+        block = ref[...].astype(F32)
+        source = lax.bitwise_xor(me, j)
+        rows32[pl.ds(pl.multiple_of(source * deep, 8), deep), :] = block[:deep]
+        extra = extra + block[deep:]
+    rows = 4 * deep
+    first, second = rows32[:, :half], rows32[:, half : 2 * half]
+    up_keep[...] = jnp.where(side == 0, first, second).astype(BF)
+    up_give[...] = jnp.where(side == 0, second, first).astype(BF)
+    attn_piece[:rows, :own] = rows32[:, 2 * half :].astype(BF)
+    dense_values = dense[...].astype(F32)
+    beside = [dense_values[:, q * quarter : (q + 1) * quarter] for q in range(4)]
+    attn_piece[:rows, own:] = jnp.concatenate(beside, axis=0).astype(BF)
+    units = half // 4
+    row_block[...] = jnp.zeros(row_block.shape, F32)
+    row_block[7:8, :units] = up_bias[...].astype(F32)
+    up_row = pltpu.roll(row_block[...], side * half + line * units, 1)
+    qkv_row = jnp.concatenate([extra[:, 2 * half :], jnp.zeros((8, quarter), F32)], axis=1)
+    attn_piece[rows:, :] = (extra[:, : 2 * half] + up_row + qkv_row).astype(BF)
+
+
+def mlp_kernel(*refs):
+    pieces, (unit_own, unit_other, dy_own, dy_other, vectors, attn_out, scaled, sums_in) = refs[:4], refs[4:12]
+    give, keep, mlp_in, act, d_up, sums, up, down, done = refs[12:]
+    line, side = line_and_side()
+    width, half = up.shape
+    units = half // 4
+    copies = []
+    for step, piece in zip((0, 3, 1, 2), pieces):
+        l = lax.bitwise_and(line + step, 3)
+        top, low = pl.ds(0, units), pl.ds(units, units)
+        for source, target in (
+            (piece.at[top, :], down.at[pl.ds(pl.multiple_of(l * units, 32), units), :]),
+            (piece.at[low, pl.ds(0, half)], up.at[pl.ds(pl.multiple_of(2 * l * units, 32), units), :]),
+            (piece.at[low, pl.ds(half, half)], up.at[pl.ds(pl.multiple_of((2 * l + 1) * units, 32), units), :]),
+        ):
+            copies.append(pltpu.make_async_copy(source, target, done.at[len(copies)]))
+    for copy in copies:
+        copy.start()
+    gain, shift = vectors[2:3, :], vectors[3:4, :]
+    bias = jnp.where(side == 0, vectors[7:8, :half], vectors[7:8, half:])
     sums[...] = sums_in[...]
-    tokens, width = dy.shape
-    size = tokens // 4
-
-    def step(i, carry):
-        rows = pl.ds(pl.multiple_of(i * size, size), size)
-        u = unit[rows, :]
-        normed = (u * gain + shift).astype(BF)
-        mlp_in[rows, :] = normed
-        upper = dot_nn(normed, up[...]) + bias
-        cdf = 0.5 * (1.0 + lax.erf(upper * 0.7071067811865476))
-        pdf = jnp.exp(-0.5 * upper * upper) * 0.3989422804014327
-        act_rows = (upper * cdf).astype(BF)
-        act[rows, :] = act_rows
-        g = dy[rows, :]
-        d_rows = (dot_nt(g, down[...]) * (cdf + upper * pdf)).astype(BF)
-        d_up[rows, :] = d_rows
-        pair[i, :, :width] = dot_nn(act_rows, down[...]) + attn_out[rows, :]
-        back = dot_nt(d_rows, up[...])
-        pair[i, :, width:] = back * gain + scaled[rows, :]
-        sums[2:3, :] += jnp.sum(back * u, axis=0, keepdims=True)
-        sums[3:4, :] += jnp.sum(back, axis=0, keepdims=True)
-        sums[4:5, :] += 0.25 * jnp.sum(g.astype(F32), axis=0, keepdims=True)
-        sums[6:7, :] += jnp.sum(d_rows.astype(F32), axis=0, keepdims=True)
-        return carry
-
-    lax.fori_loop(0, 4, step, 0)
+    group = unit_own.shape[0]
+    size = group // 4
     core = lax.bitwise_and(lax.axis_index("seq"), 1)
-    for chip in range(2):
-        give[chip] = pair[2 * chip + 1 - core].astype(BF)
-        keep[chip] = pair[2 * chip + core]
+    for copy in copies:
+        copy.wait()
+
+    def tokens(unit, dy, offset, own):
+        def step(i, carry):
+            rows = pl.ds(pl.multiple_of(i * size, size), size)
+            all_rows = pl.ds(pl.multiple_of(offset + i * size, size), size)
+            u = unit[rows, :]
+            normed = (u * gain + shift).astype(BF)
+            mlp_in[all_rows, :] = normed
+            upper = dot_nn(normed, up[...]) + bias
+            cdf = 0.5 * (1.0 + lax.erf(upper * 0.7071067811865476))
+            pdf = jnp.exp(-0.5 * upper * upper) * 0.3989422804014327
+            act_rows = (upper * cdf).astype(BF)
+            act[all_rows, :] = act_rows
+            g = dy[rows, :]
+            d_rows = (dot_nt(g, down[...]) * (cdf + upper * pdf)).astype(BF)
+            d_up[all_rows, :] = d_rows
+            out = dot_nn(act_rows, down[...])
+            back = dot_nt(d_rows, up[...])
+            sums[2:3, :] += jnp.sum(back * u, axis=0, keepdims=True)
+            sums[3:4, :] += jnp.sum(back, axis=0, keepdims=True)
+            sums[6:7, :half] += jnp.sum(d_rows.astype(F32), axis=0, keepdims=True)
+            back = back * gain
+            if own:
+                out = out + attn_out[rows, :]
+                back = back + scaled[rows, :]
+                sums[4:5, :] += 0.25 * jnp.sum(g.astype(F32), axis=0, keepdims=True)
+            place = (0 if own else 2) + lax.shift_right_logical(i, 1)
+            out, back = out.astype(BF), back.astype(BF)
+
+            @pl.when(lax.bitwise_and(i, 1) == core)
+            def _():
+                keep[place, :, :width] = out
+                keep[place, :, width:] = back
+
+            @pl.when(lax.bitwise_and(i, 1) != core)
+            def _():
+                give[place, :, :width] = out
+                give[place, :, width:] = back
+
+            return carry
+
+        lax.fori_loop(0, 4, step, 0)
+
+    tokens(unit_own, dy_own, 0, True)
+    tokens(unit_other, dy_other, group, False)
+
+
+def mlp_grads_kernel(mlp_in, act, d_up, dy_own, dy_other, sums, send1, send2, send3, own_terms, up_grad, down_grad):
+    line, _ = line_and_side()
+    sends = (send1, send2, send3)
+    group, width = dy_own.shape
+    half = act.shape[1]
+    units = half // 4
     for c in range(0, width, 128):
         up_grad[c : c + 128, :] = dot_tn(mlp_in[:, c : c + 128], d_up[...]).astype(BF)
-        down_grad[c : c + 128, :] = dot_tn(act[:, c : c + 128], dy[...]).astype(BF)
+    for c in range(0, half, 128):
+        total = dot_tn(act[:group, c : c + 128], dy_own[...]) + dot_tn(act[group:, c : c + 128], dy_other[...])
+        down_grad[c : c + 128, :] = total.astype(BF)
     tail = sums[...].astype(BF)
-
-    def block_of(index):
-        rows = pl.ds(pl.multiple_of(index * per_line, per_line), per_line)
-        return jnp.concatenate([up_grad[rows, :], down_grad[rows, :], tail], axis=0)
-
-    pick_blocks(block_of, *picks)
+    for step, ref in zip((1, 2, 3, 0), (*sends, own_terms)):
+        l = lax.bitwise_and(line + step, 3)
+        ref[:units, :] = down_grad[pl.ds(pl.multiple_of(l * units, 32), units), :]
+        ref[units : 2 * units, :half] = up_grad[pl.ds(pl.multiple_of(2 * l * units, 32), units), :]
+        ref[units : 2 * units, half:] = up_grad[pl.ds(pl.multiple_of((2 * l + 1) * units, 32), units), :]
+        ref[2 * units :, :] = tail
+
+
+def mlp_sum_kernel(own, g1, g2, g3, down_own, up_keep, up_give, tail):
+    units, width = down_own.shape
+    half = width // 2
+    _, side = line_and_side()
+    refs = (own, g1, g2, g3)
+
+    def total(rows, lanes):
+        return sum(ref[rows, lanes].astype(F32) for ref in refs)
+
+    down_own[...] = total(slice(0, units), slice(None))
+    first = total(slice(units, 2 * units), slice(0, half))
+    second = total(slice(units, 2 * units), slice(half, width))
+    last = total(slice(2 * units, 2 * units + 8), slice(None))
+    tail[...] = last
+    up_keep[...] = jnp.where(side == 0, first, second).astype(BF)
+    up_give[:units, :] = jnp.where(side == 0, second, first).astype(BF)
+    up_give[units:, :] = jnp.concatenate([last[:, :half], last[:, half:]], axis=0).astype(BF)
+
+
+def owners_kernel(deep, keep, far, tail, b0, b1, b2, b3, rows32):
+    _, side = line_and_side()
+    me = lax.axis_index("seq")
+    rows, half = keep.shape
+    here, there = keep[...].astype(F32), far[:rows, :].astype(F32)
+    rows32[:, :half] = jnp.where(side == 0, here, there)
+    rows32[:, half:] = jnp.where(side == 0, there, here)
+    far_tail = far[rows:, :].astype(F32)
+    last = tail[...] + jnp.concatenate([far_tail[:8], far_tail[8:]], axis=1)
+    for j, ref in enumerate((b0, b1, b2, b3)):
+        target = lax.bitwise_xor(me, j)
+        block = rows32[pl.ds(pl.multiple_of(target * deep, 8), deep), :]
+        ref[...] = jnp.concatenate([block, last], axis=0).astype(BF)
+
+
+def owned_kernel(deep, b0, b1, b2, b3, tail, up_own, vec_own, sources, row_block):
+    line, _ = line_and_side()
+    me = lax.axis_index("seq")
+    device = 4 * lax.axis_index("dp") + me
+    width = tail.shape[1]
+    half, own = width // 2, width // 4
+    units = half // 4
+    for j, ref in enumerate((b0, b1, b2, b3)):
+        sources[lax.bitwise_xor(me, j)] = ref[...].astype(F32)
+    for l in range(4):
+        parts = [
+            sources[t, :deep, y * half + l * units : y * half + (l + 1) * units] for y in range(2) for t in range(4)
+        ]
+        up_own[:, l * 2 * half : (l + 1) * 2 * half] = jnp.concatenate(parts, axis=1)
+    total = sources[0, deep:] + sources[1, deep:] + sources[2, deep:] + sources[3, deep:]
+    rolled = pltpu.roll(total, width - device * deep, 1)
+    vec_own[...] = rolled[:, :128]
+    row_block[...] = jnp.zeros(row_block.shape, F32)
+    for t in range(4):
+        row = sources[t, deep + 5 : deep + 6, :]
+        for part in range(3):
+            place = part * width + t * own
+            row_block[5:6, place : place + own] = row[:, part * own : (part + 1) * own]
+    rolled = pltpu.roll(row_block[...], 3 * width - device * (3 * deep), 1)
+    vec_own[5:6, :] = rolled[5:6, :128]
+    rolled = pltpu.roll(tail[...], width - line * units, 1)
+    vec_own[6:7, :] = rolled[6:7, :128]
+
+
+def with_waits(count, body):
+    def wrapped(*refs):
+        body(*refs[count:])
+
+    return wrapped
 
 
 def line_device(
@@ -705,57 +881,58 @@
 ):
     n_dp, n_seq = 8, 4
     dp_me, me = lax.axis_index("dp"), lax.axis_index("seq")
+    line, side = lax.shift_right_logical(dp_me, 1), lax.bitwise_and(dp_me, 1)
+    chip, core = lax.shift_right_logical(me, 1), lax.bitwise_and(me, 1)
     device = dp_me * n_seq + me
     zero = jnp.int32(0)
     rows, width = hidden_in.shape
     group = rows * n_seq
     hidden_units = up_weight.shape[1]
-    own_units = hidden_units // n_seq
+    units = hidden_units // (n_dp * n_seq)
+    half = hidden_units // 8
     deep = width // (n_dp * n_seq)
     per_line = n_seq * deep
-    unit_rows = hidden_units // (n_dp * n_seq)
     own = width // n_seq
-    heads = own // HEAD_DIM
-    wide = own_units + 3 * own
-
-    def by_head(values):
-        split = values.reshape(values.shape[0], 3, n_seq, own)
-        return jnp.moveaxis(split, 2, 0).reshape(n_seq, values.shape[0], 3 * own)
-
-    def from_heads(blocks):
-        split = jnp.moveaxis(blocks.reshape(n_seq, -1, 3, own), 0, 2)
-        return split.reshape(-1, 3 * width)
-
-    def spread(values, length, place):
-        empty = jnp.zeros((values.shape[0], length), values.dtype)
-        return lax.dynamic_update_slice(empty, values, (zero, place))
-
-    up_blocks = jnp.moveaxis(up_weight.reshape(deep, n_dp, n_seq, unit_rows), 2, 0)
-    up_blocks = up_blocks.reshape(n_seq, deep, own_units)
-    by_width = jnp.stack([attn_gain, attn_shift, mlp_gain, mlp_shift, dense_bias, down_bias])
-    by_width = jnp.pad(spread(by_width, width, device * deep), ((0, 2), (0, 0)))
-    bias_row = spread(qkv_bias[None], 3 * width, device * qkv_bias.shape[0])
-    bias_row = jnp.pad(by_head(bias_row), ((0, 0), (6, 1), (0, 0)))
-    left = jnp.concatenate([up_blocks, jnp.broadcast_to(by_width, (n_seq,) + by_width.shape)], axis=1)
-    right = jnp.concatenate([by_head(qkv_weight), bias_row], axis=1)
-    got = seq_exchange(jnp.concatenate([left, right], axis=2))
-    up_piece = got[:, :deep, :own_units].reshape(per_line, own_units)
-    qkv_piece = got[:, :deep, own_units:].reshape(per_line, 3 * own)
-    extra = jnp.sum(got[:, deep:].astype(F32), axis=0)
-    up_row = spread(up_bias[None].astype(F32), own_units, dp_me * unit_rows)
-    extra = (
-        extra[:, :width]
-        + jnp.pad(extra[:, own_units:], ((0, 0), (0, width - 3 * own)))
-        + jnp.pad(up_row, ((7, 0), (0, 0)))
-    ).astype(BF)
-    beside = jnp.swapaxes(dense_weight.reshape(deep, n_seq, own), 0, 1).reshape(per_line, own)
-    attn_piece = jnp.concatenate([jnp.concatenate([qkv_piece, beside], axis=1), extra], axis=0)
+    wide = 2 * half + 3 * own
+    flat = (group, width)
+
+    vectors_in = (attn_gain, attn_shift, mlp_gain, mlp_shift, dense_bias, down_bias, qkv_bias)
+    blocks = kernel_call(
+        functools.partial(pack_kernel, deep),
+        (((deep + 8, wide), BF),) * 4,
+        (qkv_weight, up_weight, *[v[None] for v in vectors_in]),
+        scratch=(((4, deep + 8, wide), F32), ((8, 3 * width), F32)),
+        megabytes=16,
+    )
+    got = seq_shuffle(blocks)
+    attn_piece, up_keep, up_give = kernel_call(
+        functools.partial(unpack_kernel, deep),
+        (((per_line + 8, width), BF), ((per_line, half), BF), ((per_line, half), BF)),
+        (*got, dense_weight, up_bias[None]),
+        scratch=(((per_line, wide), F32), ((8, width), F32)),
+        megabytes=16,
+    )
     attn_pieces = dp_pieces(attn_piece)
-    mlp_pieces = dp_pieces(jnp.concatenate([up_piece, down_weight], axis=0))
-
-    both = seq_gather(jnp.concatenate([hidden_in, grad_out], axis=0))
-    hidden_group = both[:, :rows].reshape(group, width)
-    dy = both[:, rows:].reshape(group, width)
+    up_far = lax.ppermute(up_give, "dp", SIDE_SWAP)
+    up_both = jnp.concatenate(
+        [jnp.where(side == 0, up_keep, up_far), jnp.where(side == 0, up_far, up_keep)], axis=1
+    )
+    mlp_piece = jnp.concatenate([down_weight, up_both], axis=0)
+    from2, from1, from3 = [lax.ppermute(mlp_piece, "dp", along(k)) for k in (2, 1, 3)]
+    mlp_pieces = (mlp_piece, from1, from3, from2)
+
+    mine = jnp.concatenate([hidden_in, grad_out], axis=0)
+    across = lax.ppermute(mine, "dp", SIDE_SWAP)
+
+    def whole_group(values):
+        far = lax.ppermute(values, "seq", CHIP_SWAP)
+        by_chip = in_order(chip == 1, values, far)
+        over = lax.ppermute(by_chip, "seq", CORE_SWAP)
+        full = in_order(core == 1, by_chip, over, axis=1).reshape(n_seq, 2, rows, width)
+        return full[:, 0].reshape(flat), full[:, 1].reshape(flat)
+
+    hidden_group, dy = whole_group(once(mine, attn_pieces[2]))
+    hidden_other, dy_other = whole_group(once(across, attn_pieces[6]))
 
     row_lengths = lengths[0]
     segment, position = place(row_lengths, jnp.arange(group, dtype=jnp.int32))
@@ -773,8 +950,8 @@
         return centered * inverse, inverse
 
     unit = normed(hidden_group.astype(F32))[0]
-
-    flat = (group, width)
+    unit_other = normed(hidden_other.astype(F32))[0]
+
     placed = kernel_call(
         functools.partial(place_kernel, deep),
         ((flat[1:] * 2, BF), ((n_dp * deep, width), BF), ((8, width), F32)) + (((2 * deep, group), BF),) * 4,
@@ -791,47 +968,51 @@
         flops=2 * group * width * width,
     )
     attended = kernel_call(
-        functools.partial(attention_kernel, deep),
+        with_waits(1, functools.partial(attention_kernel, deep)),
         (((2 * deep, group), BF),) * 4 + ((flat, BF),),
-        (qk, v, *d_blocks, segment[:, None], segment[None, :], cosine, sine_a, sine_b),
+        (from2, qk, v, *d_blocks, segment[:, None], segment[None, :], cosine, sine_a, sine_b),
         scratch=(((own, group), F32),) * 4 + ((flat, F32),),
         flops=14 * group * group * own,
+        apart=1,
     )
     d_joined = attended[4]
     row_blocks = seq_shuffle(attended[:4])
     results = kernel_call(
-        functools.partial(attention_grads_kernel, deep),
+        with_waits(2, functools.partial(attention_grads_kernel, deep)),
         pick_shapes(per_line, width) + ((flat, F32), (flat, F32), ((8, width), F32)),
-        (*row_blocks, dense, dy, attn_in, d_joined, weights, unit, vectors),
+        (from1, from3, *row_blocks, dense, dy, attn_in, d_joined, weights, unit, vectors),
         scratch=(((n_dp * deep, group), BF), ((width, width), F32)),
         flops=5 * group * width * width,
         megabytes=32,
-    )
-    attn_sum = dp_sum(*results[:6])
-
+        apart=2,
+    )
+    moved, attn_sum = dp_sum(*results[:6])
+
+    units_shape = ((2 * group, half), BF)
+    give, keep, *held = kernel_call(
+        mlp_kernel,
+        (((4, rows, 2 * width), BF),) * 2 + (((2 * group, width), BF), units_shape, units_shape, ((8, width), F32)),
+        (*mlp_pieces, unit, unit_other, dy, dy_other, vectors) + tuple(results[6:]),
+        scratch=(((width, half), BF), ((half, width), BF), pltpu.SemaphoreType.DMA((12,))),
+        flops=8 * group * width * 2 * half,
+        megabytes=32,
+        apart=4,
+    )
     results = kernel_call(
-        functools.partial(mlp_kernel, per_line),
-        pick_shapes(per_line + unit_rows + 8, width) + (((2, rows, 2 * width), BF), ((2, rows, 2 * width), F32)),
-        (*mlp_pieces, unit, dy, vectors) + tuple(results[6:]),
-        scratch=(
-            ((width, own_units), BF),
-            ((own_units, width), BF),
-            (flat, BF),
-            ((group, own_units), BF),
-            ((group, own_units), BF),
-            ((width, own_units), BF),
-            ((own_units, width), BF),
-            ((n_seq, rows, 2 * width), F32),
-            ((8, width), F32),
-        ),
-        flops=12 * group * width * own_units,
-        megabytes=40,
-    )
-    mlp_sum = dp_sum(*results[:6])
-    give, keep = results[6:]
-
-    chip = lax.shift_right_logical(me, 1)
-    both = keep + lax.ppermute(give, "seq", CORE_SWAP).astype(F32)
+        with_waits(len(moved), mlp_grads_kernel),
+        (((2 * units + 8, width), BF),) * 4,
+        (*moved, *held[:3], dy, dy_other, held[3]),
+        scratch=(((width, half), BF), ((half, width), BF)),
+        flops=4 * group * width * 2 * half,
+        megabytes=24,
+        apart=len(moved),
+    )
+    terms = [results[3]] + [lax.ppermute(send, "dp", along(k)) for k, send in zip((1, 2, 3), results[:3])]
+
+    both = keep.astype(F32) + lax.ppermute(give, "seq", CORE_SWAP).astype(F32)
+    beyond = lax.ppermute(both[2:].astype(BF), "dp", SIDE_SWAP)
+    *terms, beyond = lax.optimization_barrier((*terms, beyond))
+    both = both[:2] + beyond.astype(F32)
     far = lax.ppermute(pick(both, 1 - chip).astype(BF), "seq", CHIP_SWAP)
     pair = pick(both, chip) + far.astype(F32)
     x = hidden_in.astype(F32)
@@ -845,21 +1026,38 @@
     )
     grad_in = grad_out.astype(F32) + inverse * inner
 
+    def from_heads(blocks):
+        split = jnp.moveaxis(blocks.reshape(n_seq, -1, 3, own), 0, 2)
+        return split.reshape(-1, 3 * width)
+
     qkv_back = attn_sum[:, : 3 * own].reshape(n_seq, deep, 3 * own).astype(BF)
     qkv_own = from_heads(seq_exchange(qkv_back).astype(F32))
     dense_own = attn_sum[:, 3 * own :].reshape(n_seq, deep, own)
     dense_own = jnp.swapaxes(dense_own, 0, 1).reshape(deep, width)
-    tail = mlp_sum[per_line + unit_rows :]
-    back = jnp.concatenate(
-        [mlp_sum[:per_line].reshape(n_seq, deep, own_units), jnp.broadcast_to(tail, (n_seq,) + tail.shape)], axis=1
-    )
-    back = seq_exchange(back.astype(BF)).astype(F32)
-    up_own = jnp.moveaxis(back[:, :deep].reshape(n_seq, deep, n_dp, unit_rows), 0, 2)
-    by_width = jnp.sum(back[:, deep : deep + 5], axis=0)
-    by_width = lax.dynamic_slice(by_width, (zero, device * deep), (5, deep))
-    qkv_bias_grad = from_heads(back[:, deep + 5 : deep + 6, : 3 * own])[0]
-    qkv_bias_grad = lax.dynamic_slice(qkv_bias_grad, (device * qkv_bias.shape[0],), qkv_bias.shape)
-    up_bias_grad = lax.dynamic_slice(tail[6], (dp_me * unit_rows,), (unit_rows,))
+    down_own, up_keep, up_give, tail = kernel_call(
+        mlp_sum_kernel,
+        (((units, width), F32), ((per_line, half), BF), ((per_line + 16, half), BF), ((8, width), F32)),
+        tuple(terms),
+        megabytes=8,
+    )
+    up_far = lax.ppermute(up_give, "dp", SIDE_SWAP)
+    blocks = kernel_call(
+        functools.partial(owners_kernel, deep),
+        (((deep + 8, width), BF),) * 4,
+        (up_keep, up_far, tail),
+        scratch=(((per_line, width), F32),),
+        megabytes=8,
+    )
+    up_own, vec_own = kernel_call(
+        functools.partial(owned_kernel, deep),
+        (((deep, hidden_units), F32), ((8, 128), F32)),
+        (*seq_shuffle(blocks), tail),
+        scratch=(((4, deep + 8, width), F32), ((8, 3 * width), F32)),
+        megabytes=8,
+    )
+    by_width = vec_own[:5, :deep]
+    qkv_bias_grad = vec_own[5, : 3 * deep]
+    up_bias_grad = vec_own[6, :units]
     return (
         block_out.astype(BF),
         grad_in.astype(BF),
@@ -871,9 +1069,9 @@
         qkv_bias_grad,
         dense_own,
         by_width[4],
-        up_own.reshape(deep, hidden_units),
+        up_own,
         up_bias_grad,
-        mlp_sum[per_line : per_line + unit_rows],
+        down_own,
         by_width[4],
     )
 

time: 200 us -> 181 us (0.905)
  the two profiles are of different devices: /device:TPU:0 before, /device:TPU:8 now
where the time goes in v4:
time: 181 us; the launch traced here: 180 us
  waiting for transfers between devices  66.5 us (37%)
  starting transfers between devices  48.5 us (27%)
  Pallas kernels  25.5 us (14%)
  local copies, waits for them, and re-layouts  19.8 us (11%)
  other arithmetic  18.9 us (10%)
    pallas_call x11, Pallas kernels, kernel_call(): pl.pallas_call(body, out_shape=tuple((jax.ShapeDtypeStruct(shape, kind) f...  25.5 us
    ppermute x3, waiting for transfers between devices, line_device(): lax.ppermute(send, 'dp', along(k))  23.1 us
    unnamed x66, local copies, waits for them, and re-layouts  13.3 us
    ppermute x12, waiting for transfers between devices, seq_shuffle(): got.append(lax.ppermute(blocks[other], 'seq', pairs))  8.17 us
    ppermute x12, starting transfers between devices, seq_shuffle(): got.append(lax.ppermute(blocks[other], 'seq', pairs))  8.09 us
    ppermute x1, waiting for transfers between devices, dp_pieces(): near2 = lax.ppermute(block, 'dp', along(2))  7.41 us
    ppermute x1, waiting for transfers between devices, line_device(): far = lax.ppermute(pick(both, 1 - chip).astype(BF), 'seq', CHIP_SWAP)  6.21 us
    ppermute x3, starting transfers between devices, line_device(): lax.ppermute(send, 'dp', along(k))  5.55 us
  transfers between devices with their start and end apart: 43, of which 21 were waited for; matrix products, arithmetic and copies ran while one was open for 13% of the time, Pallas kernels for 8%

profile of v4, /device:TPU:8, one launch (start us, length us, event | category | flops | bytes accessed | tf_op | source)
XLA Modules:
  0.0 180.5 jit_solution(12733140345248658070)
XLA Ops:
  7.4 1.6 collective-permute-start.1
  11.1 1.6 collective-permute-start.16
  15.5 1.6 collective-permute-start.4
  18.6 3.1 %collective-permute-done.4.refs_2_ = bf16[104,768]{1,0:T(8,128)(2,1)S(1)} collective-permute-done((bf16[104,768]{1,0:T(8,128)(2,1)S(1)}, bf16[104,768]{1,0:T(8,128)(2,1)S(1)}, u32[]{:S(2)}, u32[]{:S(2)}) %collective-permute-start.4) | collective-permute-done | bytes 159776 | tf_op jit(solution)/shard_map/ppermute | solution.py:447
  21.8 1.5 collective-permute-start.10
  23.3 2.6 %collective-permute-start.8 = (bf16[104,768]{1,0:T(8,128)(2,1)S(1)}, bf16[104,768]{1,0:T(8,128)(2,1)S(1)}, u32[]{:S(2)}, u32[]{:S(2)}) collective-permute-start(bf16[104,768]{1,0:T(8,128)(2,1)S(1)} %get-tuple-element.77.refs_0_), channel_id=1, source_target_pairs={{0,16},{4,20},{8,24},{12,28},{16,0},{20,4},{24,8},{28,12},{1,17},{... | collective-permute-start | bytes 479240 | tf_op jit(solution)/shard_map/ppermute | solution.py:450
  26.4 1.5 collective-permute-start.12
  27.9 7.4 %collective-permute-done.8.refs_6_ = bf16[104,768]{1,0:T(8,128)(2,1)S(1)} collective-permute-done((bf16[104,768]{1,0:T(8,128)(2,1)S(1)}, bf16[104,768]{1,0:T(8,128)(2,1)S(1)}, u32[]{:S(2)}, u32[]{:S(2)}) %collective-permute-start.8) | collective-permute-done | bytes 159776 | tf_op jit(solution)/shard_map/ppermute | solution.py:450
  38.1 1.6 collective-permute-start.3
  40.3 3.4 %collective-permute-start.15 = (bf16[192,768]{1,0:T(8,128)(2,1)S(1)}, bf16[192,768]{1,0:T(8,128)(2,1)S(1)}, u32[]{:S(2)}, u32[]{:S(2)}) collective-permute-start(bf16[192,768]{1,0:T(8,128)(2,1)S(1)} %maximum_maximum_fusion.refs_0_), channel_id=1, source_target_pairs={{0,16},{4,20},{8,24},{12,28},{16,0},{20,4},{24,8},{28,12},{1,17},{... | collective-permute-start | bytes 884744 | tf_op jit(solution)/shard_map/ppermute | solution.py:921
  43.7 4.4 %collective-permute-done.7.refs_5_ = bf16[104,768]{1,0:T(8,128)(2,1)S(1)} collective-permute-done((bf16[104,768]{1,0:T(8,128)(2,1)S(1)}, bf16[104,768]{1,0:T(8,128)(2,1)S(1)}, u32[]{:S(2)}, u32[]{:S(2)}) %collective-permute-start.7) | collective-permute-done | bytes 159776 | tf_op jit(solution)/shard_map/ppermute | solution.py:452
  48.1 1.5 collective-permute-start.5
  51.4 1.3 select_bitcast_fusion.3
  53.6 2.1 %collective-permute-start.14 = (bf16[192,768]{1,0:T(8,128)(2,1)S(1)}, bf16[192,768]{1,0:T(8,128)(2,1)S(1)}, u32[]{:S(2)}, u32[]{:S(2)}) collective-permute-start(bf16[192,768]{1,0:T(8,128)(2,1)S(1)} %maximum_maximum_fusion.refs_0_), channel_id=1, source_target_pairs={{0,24},{4,28},{8,0},{12,4},{16,8},{20,12},{24,16},{28,20},{1,25},{... | collective-permute-start | bytes 884744 | tf_op jit(solution)/shard_map/ppermute | solution.py:921
  55.6 1.7 collective-permute-done.9.refs_7_
  58.2 1.6 collective-permute-start.20
  60.4 1.5 shard_map.257
  62.4 1.1 collective-permute-done.21.refs_6_
  63.5 6.2 %shard_map.258 = (bf16[48,512]{1,0:T(8,128)(2,1)S(1)}, bf16[48,512]{1,0:T(8,128)(2,1)S(1)}, bf16[48,512]{1,0:T(8,128)(2,1)S(1)}, bf16[48,512]{1,0:T(8,128)(2,1)S(1)}, bf16[512,768]{1,0:T(8,128)(2,1)S(1)}) custom-call(bf16[192,768]{1,0:T(8,128)(2,1)S(1)} %collective-permute-done.15.refs_0_.refs_3_, bf16[512,384]{1,0:T(8,128)(2,1)S(1)} %get-tuple-element.85.refs_1_, ...), custom_call_target="tpu_custom_call" | custom-call | flops 704643072 | bytes 1871872 | tf_op jit(solution)/shard_map/pallas_call | solution.py:415
  70.2 1.2 collective-permute-start.23
  71.6 2.6 %collective-permute-done.23.refs_4_ = bf16[48,512]{1,0:T(8,128)(2,1)S(1)} collective-permute-done((bf16[48,512]{1,0:T(8,128)(2,1)S(1)}, bf16[48,512]{1,0:T(8,128)(2,1)S(1)}, u32[]{:S(2)}, u32[]{:S(2)}) %collective-permute-start.23) | collective-permute-done | bytes 49184 | tf_op jit(solution)/shard_map/ppermute | solution.py:499
  75.3 2.9 %shard_map.259 = (bf16[96,768]{1,0:T(8,128)(2,1)S(1)}, bf16[2,96,768]{2,1,0:T(8,128)(2,1)S(1)}, bf16[96,768]{1,0:T(8,128)(2,1)}, bf16[96,768]{1,0:T(8,128)(2,1)S...) custom-call(bf16[192,768]{1,0:T(8,128)(2,1)S(1)} %collective-permute, ...), custom_call_target="tpu_custom_call" | custom-call | flops 1509949440 | bytes 6217728 | tf_op jit(solution)/shard_map/pallas_call | solution.py:415
  80.1 9.2 %shard_map.260 = (bf16[4,128,1536]{2,1,0:T(8,128)(2,1)}, bf16[4,128,1536]{2,1,0:T(8,128)(2,1)S(1)}, bf16[1024,768]{1,0:T(8,128)(2,1)S(1)}, bf16[1024,384]{1,0:T(...) custom-call(bf16[192,768]{1,0:T(8,128)(2,1)S(1)} %maximum_maximum_fusion.refs_0_, ...), custom_call_target="tpu_custom_call" | custom-call | flops 2415919104 | bytes 9093120 | tf_op jit(solution)/shard_map/pallas_call | solution.py:415
  89.3 1.1 copy-done
  91.6 1.6 collective-permute-start.26
  93.9 1.6 collective-permute-start.37
  95.5 2.9 %collective-permute-done.26.refs_0_ = bf16[96,768]{1,0:T(8,128)(2,1)S(1)} collective-permute-done((bf16[96,768]{1,0:T(8,128)(2,1)S(1)}, bf16[96,768]{1,0:T(8,128)(2,1)S(1)}, u32[]{:S(2)}, u32[]{:S(2)}) %collective-permute-start.26) | collective-permute-done | bytes 147488 | tf_op jit(solution)/shard_map/ppermute | solution.py:463
  99.7 3.3 %collective-permute-start.38 = (bf16[96,768]{1,0:T(8,128)(2,1)}, bf16[96,768]{1,0:T(8,128)(2,1)}, u32[]{:S(2)}, u32[]{:S(2)}) collective-permute-start(bf16[96,768]{1,0:T(8,128)(2,1)} %add_convert_fusion.2), channel_id=1, source_target_pairs={{0,16},{4,20},{8,24},{12,28},{16,0},{20,4},{24,8},{28,12},{1,17},{... | collective-permute-start | bytes 442376 | tf_op jit(solution)/shard_map/ppermute | solution.py:469
  103.1 1.6 collective-permute-done.27.refs_1_
  105.5 3.7 %collective-permute-start.39 = (bf16[96,768]{1,0:T(8,128)(2,1)}, bf16[96,768]{1,0:T(8,128)(2,1)}, u32[]{:S(2)}, u32[]{:S(2)}) collective-permute-start(bf16[96,768]{1,0:T(8,128)(2,1)} %get-tuple-element.152), channel_id=1, source_target_pairs={{0,8},{4,12},{8,16},{12,20},{16,24},{20,28},{24,0},{28,4},{1,9},{5... | collective-permute-start | bytes 442376 | tf_op jit(solution)/shard_map/ppermute | solution.py:470
  109.1 1.2 collective-permute-start.40
  111.5 2.3 %collective-permute-done.39 = bf16[96,768]{1,0:T(8,128)(2,1)} collective-permute-done((bf16[96,768]{1,0:T(8,128)(2,1)}, bf16[96,768]{1,0:T(8,128)(2,1)}, u32[]{:S(2)}, u32[]{:S(2)}) %collective-permute-start.39) | collective-permute-done | bytes 147488 | tf_op jit(solution)/shard_map/ppermute | solution.py:470
  113.8 3.4 %collective-permute-done.40 = bf16[96,768]{1,0:T(8,128)(2,1)} collective-permute-done((bf16[96,768]{1,0:T(8,128)(2,1)}, bf16[96,768]{1,0:T(8,128)(2,1)}, u32[]{:S(2)}, u32[]{:S(2)}) %collective-permute-start.40) | collective-permute-done | bytes 147488 | tf_op jit(solution)/shard_map/ppermute | solution.py:471
  117.2 1.3 convert_add_fusion.2
  118.6 2.3 %convert_add_fusion = f32[4,128,1536]{2,1,0:T(8,128)S(1)} fusion(bf16[4,128,1536]{2,1,0:T(8,128)(2,1)} %collective-permute-done.25, bf16[4,128,1536]{2,1,0:T(8,128)(2,1)} %copy-done), kind=kLoop, calls=%fused_computation | loop fusion | flops 2359296 | bytes 6291456 | tf_op jit(solution)/shard_map/add | solution.py:1012
  122.0 1.5 collective-permute-start.31
  124.2 2.8 %shard_map.261 = (bf16[200,768]{1,0:T(8,128)(2,1)}, bf16[200,768]{1,0:T(8,128)(2,1)}, bf16[200,768]{1,0:T(8,128)(2,1)}, bf16[200,768]{1,0:T(8,128)(2,1)S(1)}) custom-call(bf16[96,768]{1,0:T(8,128)(2,1)S(1)} %copy-done.6, bf16[2,96,768]{2,1,0:T(8,128)(2,1)S(1)} %collective-permute-done.27.refs_1_, bf16[1024,768]{1,0:T(8,128)(2,1)S(1)} %get-tuple-element.105.refs_2_, ...), custom_call_target="tpu_custom_call" | custom-call | flops 1207959552 | bytes 5185536 | tf_op jit(solution)/shard_map/pallas_call | solution.py:415
  127.8 2.6 %collective-permute-start.28 = (bf16[200,768]{1,0:T(8,128)(2,1)}, bf16[200,768]{1,0:T(8,128)(2,1)S(1)}, u32[]{:S(2)}, u32[]{:S(2)}) collective-permute-start(bf16[200,768]{1,0:T(8,128)(2,1)} %get-tuple-element.110), channel_id=1, source_target_pairs={{0,8},{4,12},{8,16},{12,20},{16,24},{20,28},{24,0},{28,4},{1,9},{5... | collective-permute-start | bytes 921608 | tf_op jit(solution)/shard_map/ppermute | solution.py:1010
  130.4 1.7 collective-permute-start.29
  132.1 1.2 collective-permute-start.30
  136.4 15.1 %collective-permute-done.28.g1 = bf16[200,768]{1,0:T(8,128)(2,1)S(1)} collective-permute-done((bf16[200,768]{1,0:T(8,128)(2,1)}, bf16[200,768]{1,0:T(8,128)(2,1)S(1)}, u32[]{:S(2)}, u32[]{:S(2)}) %collective-permute-start.28) | collective-permute-done | bytes 307232 | tf_op jit(solution)/shard_map/ppermute | solution.py:1010
  151.5 6.2 %collective-permute-done.29.g2 = bf16[200,768]{1,0:T(8,128)(2,1)S(1)} collective-permute-done((bf16[200,768]{1,0:T(8,128)(2,1)}, bf16[200,768]{1,0:T(8,128)(2,1)S(1)}, u32[]{:S(2)}, u32[]{:S(2)}) %collective-permute-start.29) | collective-permute-done | bytes 307232 | tf_op jit(solution)/shard_map/ppermute | solution.py:1010
  157.7 1.8 %collective-permute-done.30.g3 = bf16[200,768]{1,0:T(8,128)(2,1)S(1)} collective-permute-done((bf16[200,768]{1,0:T(8,128)(2,1)}, bf16[200,768]{1,0:T(8,128)(2,1)S(1)}, u32[]{:S(2)}, u32[]{:S(2)}) %collective-permute-start.30) | collective-permute-done | bytes 307232 | tf_op jit(solution)/shard_map/ppermute | solution.py:1010
  160.8 1.8 slice_add_fusion
  162.6 2.2 %collective-permute-done.33.far = bf16[112,384]{1,0:T(8,128)(2,1)S(1)} collective-permute-done((bf16[112,384]{1,0:T(8,128)(2,1)S(1)}, bf16[112,384]{1,0:T(8,128)(2,1)S(1)}, u32[]{:S(2)}, u32[]{:S(2)}) %collective-permute-start.33) | collective-permute-done | bytes 86048 | tf_op jit(solution)/shard_map/ppermute | solution.py:1043
  164.9 1.2 collective-permute-start.35
  166.9 1.2 collective-permute-start.32
  172.4 6.2 %collective-permute-done.32 = bf16[128,1536]{1,0:T(8,128)(2,1)S(1)} collective-permute-done((bf16[128,1536]{1,0:T(8,128)(2,1)S(1)}, bf16[128,1536]{1,0:T(8,128)(2,1)S(1)}, u32[]{:S(2)}, u32[]{:S(2)}) %collective-permute-start.32) | collective-permute-done | bytes 393248 | tf_op jit(solution)/shard_map/ppermute | solution.py:1016
  (179 shorter events, 44.2 us)
Async XLA Ops:
  7.3 5.4 %collective-permute-start = (bf16[32,1344]{1,0:T(8,128)(2,1)S(1)}, bf16[32,1344]{1,0:T(8,128)(2,1)S(1)}, u32[]{:S(2)}, u32[]{:S(2)}) collective-permute-start(bf16[32,1344]{1,0:T(8,128)(2,1)S(1)} %get-tuple-element.74), channel_id=1, source_target_pairs={{0,1},{1,0},{2,3},{3,2},{4,5},{5,4},{6,7},{7,6},{8,9},{9,8},{10,11... | collective-permute-start | bytes 258056 | tf_op jit(solution)/shard_map/ppermute | solution.py:499
  7.4 5.5 %collective-permute-start.1 = (bf16[32,1344]{1,0:T(8,128)(2,1)S(1)}, bf16[32,1344]{1,0:T(8,128)(2,1)S(1)}, u32[]{:S(2)}, u32[]{:S(2)}) collective-permute-start(bf16[32,1344]{1,0:T(8,128)(2,1)S(1)} %get-tuple-element.75), channel_id=1, source_target_pairs={{0,2},{1,3},{2,0},{3,1},{4,6},{5,7},{6,4},{7,5},{8,10},{9,11},{10,... | collective-permute-start | bytes 258056 | tf_op jit(solution)/shard_map/ppermute | solution.py:499
  8.9 5.0 %collective-permute-start.2 = (bf16[32,1344]{1,0:T(8,128)(2,1)S(1)}, bf16[32,1344]{1,0:T(8,128)(2,1)S(1)}, u32[]{:S(2)}, u32[]{:S(2)}) collective-permute-start(bf16[32,1344]{1,0:T(8,128)(2,1)S(1)} %get-tuple-element.76), channel_id=1, source_target_pairs={{0,3},{1,2},{2,1},{3,0},{4,7},{5,6},{6,5},{7,4},{8,11},{9,10},{10,... | collective-permute-start | bytes 258056 | tf_op jit(solution)/shard_map/ppermute | solution.py:499
  11.1 24.2 %collective-permute-start.16 = (bf16[256,768]{1,0:T(8,128)(2,1)S(1)}, bf16[256,768]{1,0:T(8,128)(2,1)S(1)}, u32[]{:S(2)}, u32[]{:S(2)}) collective-permute-start(bf16[256,768]{1,0:T(8,128)(2,1)S(1)} %constant_dynamic-update-slice_fusion), channel_id=1, source_target_pairs={{0,4},{4,0},{8,12},{12,8},{16,20},{20,16},{24,28},{28,24},{1,5},{5... | collective-permute-start | bytes 1179656 | tf_op jit(solution)/shard_map/ppermute | solution.py:925
  15.5 6.3 %collective-permute-start.4 = (bf16[104,768]{1,0:T(8,128)(2,1)S(1)}, bf16[104,768]{1,0:T(8,128)(2,1)S(1)}, u32[]{:S(2)}, u32[]{:S(2)}) collective-permute-start(bf16[104,768]{1,0:T(8,128)(2,1)S(1)} %get-tuple-element.77.refs_0_), channel_id=1, source_target_pairs={{0,8},{4,12},{8,16},{12,20},{16,24},{20,28},{24,0},{28,4},{1,9},{5... | collective-permute-start | bytes 479240 | tf_op jit(solution)/shard_map/ppermute | solution.py:447
  21.8 14.1 %collective-permute-start.10 = (bf16[256,768]{1,0:T(8,128)(2,1)S(1)}, bf16[256,768]{1,0:T(8,128)(2,1)S(1)}, u32[]{:S(2)}, u32[]{:S(2)}) collective-permute-start(bf16[256,768]{1,0:T(8,128)(2,1)S(1)} %constant_dynamic-update-slice_fusion), channel_id=1, source_target_pairs={{0,2},{2,0},{1,3},{3,1},{4,6},{6,4},{5,7},{7,5},{8,10},{10,8},{9,1... | collective-permute-start | bytes 1179656 | tf_op jit(solution)/shard_map/ppermute | solution.py:928
  23.3 12.0 %collective-permute-start.8 = (bf16[104,768]{1,0:T(8,128)(2,1)S(1)}, bf16[104,768]{1,0:T(8,128)(2,1)S(1)}, u32[]{:S(2)}, u32[]{:S(2)}) collective-permute-start(bf16[104,768]{1,0:T(8,128)(2,1)S(1)} %get-tuple-element.77.refs_0_), channel_id=1, source_target_pairs={{0,16},{4,20},{8,24},{12,28},{16,0},{20,4},{24,8},{28,12},{1,17},{... | collective-permute-start | bytes 479240 | tf_op jit(solution)/shard_map/ppermute | solution.py:450
  25.9 13.8 %collective-permute-start.6 = (bf16[104,768]{1,0:T(8,128)(2,1)S(1)}, bf16[104,768]{1,0:T(8,128)(2,1)S(1)}, u32[]{:S(2)}, u32[]{:S(2)}) collective-permute-start(bf16[104,768]{1,0:T(8,128)(2,1)S(1)} %get-tuple-element.77.refs_0_), channel_id=1, source_target_pairs={{0,24},{4,28},{8,0},{12,4},{16,8},{20,12},{24,16},{28,20},{1,25},{... | collective-permute-start | bytes 479240 | tf_op jit(solution)/shard_map/ppermute | solution.py:449
  26.4 13.8 %collective-permute-start.12 = (bf16[96,384]{1,0:T(8,128)(2,1)S(1)}, bf16[96,384]{1,0:T(8,128)(2,1)S(1)}, u32[]{:S(2)}, u32[]{:S(2)}) collective-permute-start(bf16[96,384]{1,0:T(8,128)(2,1)S(1)} %get-tuple-element.82), channel_id=1, source_target_pairs={{0,4},{4,0},{8,12},{12,8},{16,20},{20,16},{24,28},{28,24},{1,5},{5... | collective-permute-start | bytes 221192 | tf_op jit(solution)/shard_map/ppermute | solution.py:916
  35.3 12.8 %collective-permute-start.17 = (bf16[256,768]{1,0:T(8,128)(2,1)S(1)}, bf16[256,768]{1,0:T(8,128)(2,1)}, u32[]{:S(2)}, u32[]{:S(2)}) collective-permute-start(bf16[256,768]{1,0:T(8,128)(2,1)S(1)} %collective-permute-done.16), channel_id=1, source_target_pairs={{0,2},{2,0},{1,3},{3,1},{4,6},{6,4},{5,7},{7,5},{8,10},{10,8},{9,1... | collective-permute-start | bytes 1179656 | tf_op jit(solution)/shard_map/ppermute | solution.py:928
  36.9 13.9 %collective-permute-start.11 = (bf16[2,256,768]{2,1,0:T(8,128)(2,1)}, bf16[2,256,768]{2,1,0:T(8,128)(2,1)}, u32[]{:S(2)}, u32[]{:S(2)}) collective-permute-start(bf16[2,256,768]{2,1,0:T(8,128)(2,1)} %pad_maximum_fusion.2), channel_id=1, source_target_pairs={{0,1},{1,0},{2,3},{3,2},{4,5},{5,4},{6,7},{7,6},{8,9},{9,8},{10,11... | collective-permute-start | bytes 2359304 | tf_op jit(solution)/shard_map/ppermute | solution.py:930
  38.1 15.4 %collective-permute-start.3 = (bf16[104,768]{1,0:T(8,128)(2,1)S(1)}, bf16[104,768]{1,0:T(8,128)(2,1)S(1)}, u32[]{:S(2)}, u32[]{:S(2)}) collective-permute-start(bf16[104,768]{1,0:T(8,128)(2,1)S(1)} %get-tuple-element.77.refs_0_), channel_id=1, source_target_pairs={{0,4},{4,0},{8,12},{12,8},{16,20},{20,16},{24,28},{28,24},{1,5},{5... | collective-permute-start | bytes 479240 | tf_op jit(solution)/shard_map/ppermute | solution.py:448
  39.7 8.4 %collective-permute-start.7 = (bf16[104,768]{1,0:T(8,128)(2,1)S(1)}, bf16[104,768]{1,0:T(8,128)(2,1)S(1)}, u32[]{:S(2)}, u32[]{:S(2)}) collective-permute-start(bf16[104,768]{1,0:T(8,128)(2,1)S(1)} %collective-permute-done.6.refs_4_), channel_id=1, source_target_pairs={{0,4},{4,0},{8,12},{12,8},{16,20},{20,16},{24,28},{28,24},{1,5},{5... | collective-permute-start | bytes 479240 | tf_op jit(solution)/shard_map/ppermute | solution.py:452
  40.3 17.9 %collective-permute-start.15 = (bf16[192,768]{1,0:T(8,128)(2,1)S(1)}, bf16[192,768]{1,0:T(8,128)(2,1)S(1)}, u32[]{:S(2)}, u32[]{:S(2)}) collective-permute-start(bf16[192,768]{1,0:T(8,128)(2,1)S(1)} %maximum_maximum_fusion.refs_0_), channel_id=1, source_target_pairs={{0,16},{4,20},{8,24},{12,28},{16,0},{20,4},{24,8},{28,12},{1,17},{... | collective-permute-start | bytes 884744 | tf_op jit(solution)/shard_map/ppermute | solution.py:921
  48.1 23.2 %collective-permute-start.13 = (bf16[192,768]{1,0:T(8,128)(2,1)S(1)}, bf16[192,768]{1,0:T(8,128)(2,1)S(1)}, u32[]{:S(2)}, u32[]{:S(2)}) collective-permute-start(bf16[192,768]{1,0:T(8,128)(2,1)S(1)} %maximum_maximum_fusion.refs_0_), channel_id=1, source_target_pairs={{0,8},{4,12},{8,16},{12,20},{16,24},{20,28},{24,0},{28,4},{1,9},{5... | collective-permute-start | bytes 884744 | tf_op jit(solution)/shard_map/ppermute | solution.py:921
  48.1 7.5 %collective-permute-start.5 = (bf16[104,768]{1,0:T(8,128)(2,1)S(1)}, bf16[104,768]{1,0:T(8,128)(2,1)S(1)}, u32[]{:S(2)}, u32[]{:S(2)}) collective-permute-start(bf16[104,768]{1,0:T(8,128)(2,1)S(1)} %collective-permute-done.4.refs_2_), channel_id=1, source_target_pairs={{0,4},{4,0},{8,12},{12,8},{16,20},{20,16},{24,28},{28,24},{1,5},{5... | collective-permute-start | bytes 479240 | tf_op jit(solution)/shard_map/ppermute | solution.py:451
  50.8 6.5 %collective-permute-start.9 = (bf16[104,768]{1,0:T(8,128)(2,1)S(1)}, bf16[104,768]{1,0:T(8,128)(2,1)S(1)}, u32[]{:S(2)}, u32[]{:S(2)}) collective-permute-start(bf16[104,768]{1,0:T(8,128)(2,1)S(1)} %collective-permute-done.8.refs_6_), channel_id=1, source_target_pairs={{0,4},{4,0},{8,12},{12,8},{16,20},{20,16},{24,28},{28,24},{1,5},{5... | collective-permute-start | bytes 479240 | tf_op jit(solution)/shard_map/ppermute | solution.py:453
  53.6 18.1 %collective-permute-start.14 = (bf16[192,768]{1,0:T(8,128)(2,1)S(1)}, bf16[192,768]{1,0:T(8,128)(2,1)S(1)}, u32[]{:S(2)}, u32[]{:S(2)}) collective-permute-start(bf16[192,768]{1,0:T(8,128)(2,1)S(1)} %maximum_maximum_fusion.refs_0_), channel_id=1, source_target_pairs={{0,24},{4,28},{8,0},{12,4},{16,8},{20,12},{24,16},{28,20},{1,25},{... | collective-permute-start | bytes 884744 | tf_op jit(solution)/shard_map/ppermute | solution.py:921
  55.6 22.6 %collective-permute-start.18 = (bf16[2,256,768]{2,1,0:T(8,128)(2,1)S(1)}, bf16[2,256,768]{2,1,0:T(8,128)(2,1)S(1)}, u32[]{:S(2)}, u32[]{:S(2)}) collective-permute-start(bf16[2,256,768]{2,1,0:T(8,128)(2,1)S(1)} %pad_maximum_fusion.3), channel_id=1, source_target_pairs={{0,1},{1,0},{2,3},{3,2},{4,5},{5,4},{6,7},{7,6},{8,9},{9,8},{10,11... | collective-permute-start | bytes 2359304 | tf_op jit(solution)/shard_map/ppermute | solution.py:930
  57.9 1.9 %collective-permute-start.19 = (bf16[48,512]{1,0:T(8,128)(2,1)S(1)}, bf16[48,512]{1,0:T(8,128)(2,1)S(1)}, u32[]{:S(2)}, u32[]{:S(2)}) collective-permute-start(bf16[48,512]{1,0:T(8,128)(2,1)S(1)} %get-tuple-element.88), channel_id=1, source_target_pairs={{0,1},{1,0},{2,3},{3,2},{4,5},{5,4},{6,7},{7,6},{8,9},{9,8},{10,11... | collective-permute-start | bytes 147464 | tf_op jit(solution)/shard_map/ppermute | solution.py:499
  58.2 4.2 %collective-permute-start.20 = (bf16[48,512]{1,0:T(8,128)(2,1)S(1)}, bf16[48,512]{1,0:T(8,128)(2,1)S(1)}, u32[]{:S(2)}, u32[]{:S(2)}) collective-permute-start(bf16[48,512]{1,0:T(8,128)(2,1)S(1)} %get-tuple-element.89), channel_id=1, source_target_pairs={{0,2},{1,3},{2,0},{3,1},{4,6},{5,7},{6,4},{7,5},{8,10},{9,11},{10,... | collective-permute-start | bytes 147464 | tf_op jit(solution)/shard_map/ppermute | solution.py:499
  59.8 3.7 %collective-permute-start.21 = (bf16[48,512]{1,0:T(8,128)(2,1)S(1)}, bf16[48,512]{1,0:T(8,128)(2,1)S(1)}, u32[]{:S(2)}, u32[]{:S(2)}) collective-permute-start(bf16[48,512]{1,0:T(8,128)(2,1)S(1)} %get-tuple-element.90), channel_id=1, source_target_pairs={{0,3},{1,2},{2,1},{3,0},{4,7},{5,6},{6,5},{7,4},{8,11},{9,10},{10,... | collective-permute-start | bytes 147464 | tf_op jit(solution)/shard_map/ppermute | solution.py:499
  69.7 1.9 %collective-permute-start.22 = (bf16[48,512]{1,0:T(8,128)(2,1)S(1)}, bf16[48,512]{1,0:T(8,128)(2,1)S(1)}, u32[]{:S(2)}, u32[]{:S(2)}) collective-permute-start(bf16[48,512]{1,0:T(8,128)(2,1)S(1)} %get-tuple-element.92), channel_id=1, source_target_pairs={{0,1},{1,0},{2,3},{3,2},{4,5},{5,4},{6,7},{7,6},{8,9},{9,8},{10,11... | collective-permute-start | bytes 147464 | tf_op jit(solution)/shard_map/ppermute | solution.py:499
  70.2 4.1 %collective-permute-start.23 = (bf16[48,512]{1,0:T(8,128)(2,1)S(1)}, bf16[48,512]{1,0:T(8,128)(2,1)S(1)}, u32[]{:S(2)}, u32[]{:S(2)}) collective-permute-start(bf16[48,512]{1,0:T(8,128)(2,1)S(1)} %get-tuple-element.93), channel_id=1, source_target_pairs={{0,2},{1,3},{2,0},{3,1},{4,6},{5,7},{6,4},{7,5},{8,10},{9,11},{10,... | collective-permute-start | bytes 147464 | tf_op jit(solution)/shard_map/ppermute | solution.py:499
  71.3 4.0 %collective-permute-start.24 = (bf16[48,512]{1,0:T(8,128)(2,1)S(1)}, bf16[48,512]{1,0:T(8,128)(2,1)S(1)}, u32[]{:S(2)}, u32[]{:S(2)}) collective-permute-start(bf16[48,512]{1,0:T(8,128)(2,1)S(1)} %get-tuple-element.94), channel_id=1, source_target_pairs={{0,3},{1,2},{2,1},{3,0},{4,7},{5,6},{6,5},{7,4},{8,11},{9,10},{10,... | collective-permute-start | bytes 147464 | tf_op jit(solution)/shard_map/ppermute | solution.py:499
  91.4 13.3 %copy-start.1 = (bf16[1024,384]{1,0:T(8,128)(2,1)}, bf16[1024,384]{1,0:T(8,128)(2,1)S(1)}, u32[]{:S(2)}) copy-start(bf16[1024,384]{1,0:T(8,128)(2,1)S(1)} %get-tuple-element.106.refs_3_) | copy-start | bytes 2359300
  91.4 27.2 %collective-permute-start.25 = (bf16[4,128,1536]{2,1,0:T(8,128)(2,1)}, bf16[4,128,1536]{2,1,0:T(8,128)(2,1)}, u32[]{:S(2)}, u32[]{:S(2)}) collective-permute-start(bf16[4,128,1536]{2,1,0:T(8,128)(2,1)} %get-tuple-element.102), channel_id=1, source_target_pairs={{0,1},{1,0},{2,3},{3,2},{4,5},{5,4},{6,7},{7,6},{8,9},{9,8},{10,11... | collective-permute-start | bytes 4718600 | tf_op jit(solution)/shard_map/ppermute | solution.py:1012
  91.6 6.8 %collective-permute-start.26 = (bf16[96,768]{1,0:T(8,128)(2,1)S(1)}, bf16[96,768]{1,0:T(8,128)(2,1)S(1)}, u32[]{:S(2)}, u32[]{:S(2)}) collective-permute-start(bf16[96,768]{1,0:T(8,128)(2,1)S(1)} %get-tuple-element.103), channel_id=1, source_target_pairs={{0,4},{4,0},{8,12},{12,8},{16,20},{20,16},{24,28},{28,24},{1,5},{5... | collective-permute-start | bytes 442376 | tf_op jit(solution)/shard_map/ppermute | solution.py:463
  93.2 11.5 %collective-permute-start.27 = (bf16[2,96,768]{2,1,0:T(8,128)(2,1)S(1)}, bf16[2,96,768]{2,1,0:T(8,128)(2,1)S(1)}, u32[]{:S(2)}, u32[]{:S(2)}) collective-permute-start(bf16[2,96,768]{2,1,0:T(8,128)(2,1)S(1)} %get-tuple-element.104), channel_id=1, source_target_pairs={{0,4},{4,0},{8,12},{12,8},{16,20},{20,16},{24,28},{28,24},{1,5},{5... | collective-permute-start | bytes 884744 | tf_op jit(solution)/shard_map/ppermute | solution.py:464
  93.9 17.5 %collective-permute-start.37 = (bf16[96,768]{1,0:T(8,128)(2,1)}, bf16[96,768]{1,0:T(8,128)(2,1)}, u32[]{:S(2)}, u32[]{:S(2)}) collective-permute-start(bf16[96,768]{1,0:T(8,128)(2,1)} %get-tuple-element.127), channel_id=1, source_target_pairs={{0,4},{4,0},{8,12},{12,8},{16,20},{20,16},{24,28},{28,24},{1,5},{5... | collective-permute-start | bytes 442376 | tf_op jit(solution)/shard_map/ppermute | solution.py:465
  99.7 11.7 %collective-permute-start.38 = (bf16[96,768]{1,0:T(8,128)(2,1)}, bf16[96,768]{1,0:T(8,128)(2,1)}, u32[]{:S(2)}, u32[]{:S(2)}) collective-permute-start(bf16[96,768]{1,0:T(8,128)(2,1)} %add_convert_fusion.2), channel_id=1, source_target_pairs={{0,16},{4,20},{8,24},{12,28},{16,0},{20,4},{24,8},{28,12},{1,17},{... | collective-permute-start | bytes 442376 | tf_op jit(solution)/shard_map/ppermute | solution.py:469
  105.5 8.3 %collective-permute-start.39 = (bf16[96,768]{1,0:T(8,128)(2,1)}, bf16[96,768]{1,0:T(8,128)(2,1)}, u32[]{:S(2)}, u32[]{:S(2)}) collective-permute-start(bf16[96,768]{1,0:T(8,128)(2,1)} %get-tuple-element.152), channel_id=1, source_target_pairs={{0,8},{4,12},{8,16},{12,20},{16,24},{20,28},{24,0},{28,4},{1,9},{5... | collective-permute-start | bytes 442376 | tf_op jit(solution)/shard_map/ppermute | solution.py:470
  109.1 8.0 %collective-permute-start.40 = (bf16[96,768]{1,0:T(8,128)(2,1)}, bf16[96,768]{1,0:T(8,128)(2,1)}, u32[]{:S(2)}, u32[]{:S(2)}) collective-permute-start(bf16[96,768]{1,0:T(8,128)(2,1)} %get-tuple-element.153), channel_id=1, source_target_pairs={{0,24},{4,28},{8,0},{12,4},{16,8},{20,12},{24,16},{28,20},{1,25},{... | collective-permute-start | bytes 442376 | tf_op jit(solution)/shard_map/ppermute | solution.py:471
  118.5 5.0 %collective-permute-start.41 = (bf16[2,24,576]{2,1,0:T(8,128)(2,1)S(1)}, bf16[2,24,576]{2,1,0:T(8,128)(2,1)S(1)}, u32[]{:S(2)}, u32[]{:S(2)}) collective-permute-start(bf16[2,24,576]{2,1,0:T(8,128)(2,1)S(1)} %dynamic-slice_bitcast_fusion), channel_id=1, source_target_pairs={{0,2},{2,0},{1,3},{3,1},{4,6},{6,4},{5,7},{7,5},{8,10},{10,8},{9,1... | collective-permute-start | bytes 165896 | tf_op jit(solution)/shard_map/ppermute | solution.py:64
  122.0 37.5 %collective-permute-start.31 = (bf16[2,128,1536]{2,1,0:T(8,128)(2,1)}, bf16[2,128,1536]{2,1,0:T(8,128)(2,1)}, u32[]{:S(2)}, u32[]{:S(2)}) collective-permute-start(bf16[2,128,1536]{2,1,0:T(8,128)(2,1)} %slice.143), channel_id=1, source_target_pairs={{0,4},{4,0},{8,12},{12,8},{16,20},{20,16},{24,28},{28,24},{1,5},{5... | collective-permute-start | bytes 2359304 | tf_op jit(solution)/shard_map/ppermute | solution.py:1013
  124.2 10.0 %collective-permute-start.42 = (bf16[2,24,576]{2,1,0:T(8,128)(2,1)}, bf16[2,24,576]{2,1,0:T(8,128)(2,1)}, u32[]{:S(2)}, u32[]{:S(2)}) collective-permute-start(bf16[2,24,576]{2,1,0:T(8,128)(2,1)} %fusion.27), channel_id=1, source_target_pairs={{0,1},{1,0},{2,3},{3,2},{4,5},{5,4},{6,7},{7,6},{8,9},{9,8},{10,11... | collective-permute-start | bytes 165896 | tf_op jit(solution)/shard_map/ppermute | solution.py:66
  127.8 31.7 %copy-start.8 = (bf16[200,768]{1,0:T(8,128)(2,1)S(1)}, bf16[200,768]{1,0:T(8,128)(2,1)}, u32[]{:S(2)}) copy-start(bf16[200,768]{1,0:T(8,128)(2,1)} %copy-done.7) | copy-start | bytes 921604
  127.8 23.7 %collective-permute-start.28 = (bf16[200,768]{1,0:T(8,128)(2,1)}, bf16[200,768]{1,0:T(8,128)(2,1)S(1)}, u32[]{:S(2)}, u32[]{:S(2)}) collective-permute-start(bf16[200,768]{1,0:T(8,128)(2,1)} %get-tuple-element.110), channel_id=1, source_target_pairs={{0,8},{4,12},{8,16},{12,20},{16,24},{20,28},{24,0},{28,4},{1,9},{5... | collective-permute-start | bytes 921608 | tf_op jit(solution)/shard_map/ppermute | solution.py:1010
  130.4 27.3 %collective-permute-start.29 = (bf16[200,768]{1,0:T(8,128)(2,1)}, bf16[200,768]{1,0:T(8,128)(2,1)S(1)}, u32[]{:S(2)}, u32[]{:S(2)}) collective-permute-start(bf16[200,768]{1,0:T(8,128)(2,1)} %get-tuple-element.111), channel_id=1, source_target_pairs={{0,16},{4,20},{8,24},{12,28},{16,0},{20,4},{24,8},{28,12},{1,17},{... | collective-permute-start | bytes 921608 | tf_op jit(solution)/shard_map/ppermute | solution.py:1010
  132.1 27.4 %collective-permute-start.30 = (bf16[200,768]{1,0:T(8,128)(2,1)}, bf16[200,768]{1,0:T(8,128)(2,1)S(1)}, u32[]{:S(2)}, u32[]{:S(2)}) collective-permute-start(bf16[200,768]{1,0:T(8,128)(2,1)} %get-tuple-element.112), channel_id=1, source_target_pairs={{0,24},{4,28},{8,0},{12,4},{16,8},{20,12},{24,16},{28,20},{1,25},{... | collective-permute-start | bytes 921608 | tf_op jit(solution)/shard_map/ppermute | solution.py:1010
  160.3 4.5 %collective-permute-start.33 = (bf16[112,384]{1,0:T(8,128)(2,1)S(1)}, bf16[112,384]{1,0:T(8,128)(2,1)S(1)}, u32[]{:S(2)}, u32[]{:S(2)}) collective-permute-start(bf16[112,384]{1,0:T(8,128)(2,1)S(1)} %get-tuple-element.119), channel_id=1, source_target_pairs={{0,4},{4,0},{8,12},{12,8},{16,20},{20,16},{24,28},{28,24},{1,5},{5... | collective-permute-start | bytes 258056 | tf_op jit(solution)/shard_map/ppermute | solution.py:1043
  164.8 14.0 %copy-start.23 = (bf16[128,768]{1,0:T(8,128)(2,1)S(1)}, bf16[128,768]{1,0:T(8,128)(2,1)}, u32[]{:S(2)}) copy-start(bf16[128,768]{1,0:T(8,128)(2,1)} %param.15) | copy-start | bytes 589828
  164.8 14.0 %copy-start.29 = (f32[128]{0:T(128)S(1)}, f32[128]{0:T(128)}, u32[]{:S(2)}) copy-start(f32[128]{0:T(128)} %copy-done.28) | copy-start | bytes 1540
  164.8 14.0 %copy-start.30 = (f32[128]{0:T(128)S(1)}, f32[128]{0:T(128)}, u32[]{:S(2)}) copy-start(f32[128]{0:T(128)} %add_rsqrt_fusion) | copy-start | bytes 1540
  164.9 3.3 %collective-permute-start.34 = (bf16[32,768]{1,0:T(8,128)(2,1)S(1)}, bf16[32,768]{1,0:T(8,128)(2,1)S(1)}, u32[]{:S(2)}, u32[]{:S(2)}) collective-permute-start(bf16[32,768]{1,0:T(8,128)(2,1)S(1)} %get-tuple-element.122), channel_id=1, source_target_pairs={{0,1},{1,0},{2,3},{3,2},{4,5},{5,4},{6,7},{7,6},{8,9},{9,8},{10,11... | collective-permute-start | bytes 147464 | tf_op jit(solution)/shard_map/ppermute | solution.py:499
  164.9 4.2 %collective-permute-start.35 = (bf16[32,768]{1,0:T(8,128)(2,1)S(1)}, bf16[32,768]{1,0:T(8,128)(2,1)S(1)}, u32[]{:S(2)}, u32[]{:S(2)}) collective-permute-start(bf16[32,768]{1,0:T(8,128)(2,1)S(1)} %get-tuple-element.123), channel_id=1, source_target_pairs={{0,2},{1,3},{2,0},{3,1},{4,6},{5,7},{6,4},{7,5},{8,10},{9,11},{10,... | collective-permute-start | bytes 147464 | tf_op jit(solution)/shard_map/ppermute | solution.py:499
  166.2 3.7 %collective-permute-start.36 = (bf16[32,768]{1,0:T(8,128)(2,1)S(1)}, bf16[32,768]{1,0:T(8,128)(2,1)S(1)}, u32[]{:S(2)}, u32[]{:S(2)}) collective-permute-start(bf16[32,768]{1,0:T(8,128)(2,1)S(1)} %get-tuple-element.124), channel_id=1, source_target_pairs={{0,3},{1,2},{2,1},{3,0},{4,7},{5,6},{6,5},{7,4},{8,11},{9,10},{10,... | collective-permute-start | bytes 147464 | tf_op jit(solution)/shard_map/ppermute | solution.py:499
  166.9 11.8 %collective-permute-start.32 = (bf16[128,1536]{1,0:T(8,128)(2,1)S(1)}, bf16[128,1536]{1,0:T(8,128)(2,1)S(1)}, u32[]{:S(2)}, u32[]{:S(2)}) collective-permute-start(bf16[128,1536]{1,0:T(8,128)(2,1)S(1)} %fusion.17), channel_id=1, source_target_pairs={{0,2},{2,0},{1,3},{3,1},{4,6},{6,4},{5,7},{7,5},{8,10},{10,8},{9,1... | collective-permute-start | bytes 1179656 | tf_op jit(solution)/shard_map/ppermute | solution.py:1016
  (27 other events, 86.4 us)

commit v5 on v4

--- a/solution.py
+++ b/solution.py
@@ -439,53 +439,39 @@
     return lax.shift_right_logical(me, 1), lax.bitwise_and(me, 1)
 
 
+PAIR_SWAP = [(i, i ^ 2) for i in range(8)]
+HALF_SWAP = [(i, i ^ 4) for i in range(8)]
+LINE_ORDER = (0, 2, 1, 3)
+
+
 def dp_index(line, step, side):
-    return 2 * lax.bitwise_and(line + step, 3) + side
-
-
-def dp_pieces(block):
-    near1 = lax.ppermute(block, "dp", along(1))
-    far0 = lax.ppermute(block, "dp", SIDE_SWAP)
-    near3 = lax.ppermute(block, "dp", along(3))
-    near2 = lax.ppermute(block, "dp", along(2))
-    far1 = lax.ppermute(near1, "dp", SIDE_SWAP)
-    far3 = lax.ppermute(near3, "dp", SIDE_SWAP)
-    far2 = lax.ppermute(once(near2, far3), "dp", SIDE_SWAP)
-    return (block, far0, near1, far1, near3, far3, near2, far2)
-
-
-def piece_owners():
+    return 2 * lax.bitwise_xor(line, step) + side
+
+
+def pick_blocks(block_of, send, keep):
     line, side = line_and_side()
-    return [dp_index(line, step, s) for step in (0, 3, 1, 2) for s in (side, 1 - side)]
-
-
-def dp_sum(send2, send13, send0, keep2, keep13, keep0):
-    moved2 = lax.ppermute(send2, "dp", SIDE_SWAP)
-    moved13 = lax.ppermute(send13, "dp", SIDE_SWAP)
-    moved0 = lax.ppermute(send0, "dp", SIDE_SWAP)
-    sum2 = (keep2.astype(F32) + moved2.astype(F32)).astype(BF)
-    sum1 = (keep13[0].astype(F32) + moved13[0].astype(F32)).astype(BF)
-    sum3 = (keep13[1].astype(F32) + moved13[1].astype(F32)).astype(BF)
-    got2 = lax.ppermute(sum2, "dp", along(2))
-    got1 = lax.ppermute(sum1, "dp", along(1))
-    got3 = lax.ppermute(sum3, "dp", along(3))
-    total = keep0.astype(F32) + moved0.astype(F32)
-    return (moved2, moved13), total + got2.astype(F32) + got1.astype(F32) + got3.astype(F32)
-
-
-def pick_blocks(block_of, send2, send13, send0, keep2, keep13, keep0):
-    line, side = line_and_side()
-    for far, (r2, r13, r0) in ((True, (send2, send13, send0)), (False, (keep2, keep13, keep0))):
-        s = 1 - side if far else side
-        r2[...] = block_of(dp_index(line, 2, s))
-        r13[0] = block_of(dp_index(line, 1, s))
-        r13[1] = block_of(dp_index(line, 3, s))
-        r0[...] = block_of(dp_index(line, 0, s))
-
-
-def pick_shapes(rows, width):
-    one, two = ((rows, width), BF), ((2, rows, width), BF)
-    return (one, two, one, one, two, one)
+    for j, step in enumerate(LINE_ORDER):
+        send[j] = block_of(dp_index(line, step, 1 - side))
+        keep[j] = block_of(dp_index(line, step, side))
+
+
+def add_kernel(here, there, *out):
+    place = 0
+    for ref in out:
+        for j in range(ref.shape[0]):
+            ref[j] = (here[place + j].astype(F32) + there[place + j].astype(F32)).astype(ref.dtype)
+        place += ref.shape[0]
+
+
+def add_blocks(here, there, *counts, waits=()):
+    shape = here.shape[1:]
+    return kernel_call(
+        with_waits(len(waits), add_kernel),
+        tuple(((count,) + shape, BF) for count in counts),
+        (*waits, here, there),
+        megabytes=8,
+        apart=len(waits),
+    )
 
 
 def once(values, *others):
@@ -501,12 +487,15 @@
 
 
 def place_kernel(deep, *refs):
-    pieces, (dy, weights, dense, vectors), d_blocks, (rows32, d_rows) = refs[:8], refs[8:12], refs[12:16], refs[16:]
+    pieces, (dy, weights, dense, vectors), d_blocks, (rows32, d_rows) = refs[:4], refs[4:8], refs[8:12], refs[12:]
+    line, side = line_and_side()
     per_line = 4 * deep
     quarter = dy.shape[1] // 4
     own = weights.shape[1] - quarter
     total = jnp.zeros(vectors.shape, F32)
-    for piece, owner in zip(pieces, piece_owners()):
+    for place in range(8):
+        piece = pieces[place // 2].at[place % 2]
+        owner = dp_index(line, LINE_ORDER[place % 4], side if place < 4 else 1 - side)
         weights[pl.ds(pl.multiple_of(owner * per_line, per_line), per_line), :] = piece[:per_line, :]
         total = total + piece[per_line:, :].astype(F32)
         beside = piece[:per_line, own:].astype(F32)
@@ -605,7 +594,7 @@
 
 def attention_grads_kernel(deep, *refs):
     r0, r1, r2, r3, dense, dy, attn_in, d_joined, weights, unit, vectors = refs[:11]
-    picks, (attn_out, scaled, sums), (rows_t, grads) = refs[11:17], refs[17:20], refs[20:]
+    picks, (attn_out, scaled, sums), (rows_t, grads) = refs[11:13], refs[13:16], refs[16:]
     me = lax.axis_index("seq")
     count = r0.shape[0]
     width = dy.shape[1]
@@ -642,72 +631,73 @@
 
 
 def pack_kernel(deep, *refs):
-    qkv, up, vectors_in, blocks, (all_blocks, row_block) = *refs[:2], refs[2:9], refs[9:13], refs[13:]
+    qkv, up, by_width, qkv_bias, x, dy, blocks, mine, (all_blocks, row_block) = *refs[:6], refs[6:10], *refs[10:11], refs[11:]
     width = qkv.shape[1] // 3
     own = width // 4
     units = up.shape[1] // 32
-    half = up.shape[1] // 8
     me = lax.axis_index("seq")
     device = 4 * lax.axis_index("dp") + me
     row_block[...] = jnp.zeros(row_block.shape, F32)
-    for r in range(6):
-        row_block[r : r + 1, :deep] = vectors_in[r][...].astype(F32)
+    row_block[:6, :deep] = by_width[...].astype(F32)
     vectors = pltpu.roll(row_block[:, :width], device * deep, 1)
     row_block[0:6, :] = jnp.zeros((6, row_block.shape[1]), F32)
-    row_block[6:7, : 3 * deep] = vectors_in[6][...].astype(F32)
+    row_block[6:7, : 3 * deep] = qkv_bias[...].astype(F32)
     bias_rows = pltpu.roll(row_block[...], device * (3 * deep), 1)
     up_values, qkv_values = up[...].astype(F32), qkv[...].astype(F32)
+    empty = jnp.zeros((deep + 8, own), F32)
+    both = jnp.concatenate([qkv_values, bias_rows], axis=0)
     for t in range(4):
         parts = [up_values[:, ((l * 2 + y) * 4 + t) * units :][:, :units] for y in range(2) for l in range(4)]
-        all_blocks[t, :deep, : 2 * half] = jnp.concatenate(parts, axis=1)
-        all_blocks[t, deep:, : 2 * half] = vectors
-        for part in range(3):
-            lanes = slice(part * width + t * own, part * width + (t + 1) * own)
-            place = slice(2 * half + part * own, 2 * half + (part + 1) * own)
-            all_blocks[t, :deep, place] = qkv_values[:, lanes]
-            all_blocks[t, deep:, place] = bias_rows[:, lanes]
+        all_blocks[t, :deep, :] = jnp.concatenate(parts, axis=1)
+        parts = [both[:, part * width + t * own : part * width + (t + 1) * own] for part in range(3)]
+        parts = jnp.concatenate(parts + [empty], axis=1)
+        all_blocks[t, deep : 2 * deep, :] = parts[:deep]
+        all_blocks[t, 2 * deep :, :] = parts[deep:] + vectors
+    rows = x.shape[0]
     for j in range(4):
         blocks[j][...] = all_blocks[lax.bitwise_xor(me, j)].astype(BF)
-
-
-def unpack_kernel(deep, r0, r1, r2, r3, dense, up_bias, attn_piece, up_keep, up_give, rows32, row_block):
+    mine[:rows, :] = x[...]
+    mine[rows:, :] = dy[...]
+
+
+def unpack_kernel(deep, r0, r1, r2, r3, dense, up_bias, attn_piece, up_keep, up_give, up32, qkv32, row_block):
     me = lax.axis_index("seq")
     line, side = line_and_side()
     width = dense.shape[1]
     quarter = width // 4
     half = up_keep.shape[1]
     own = 3 * quarter
-    extra = jnp.zeros((8, rows32.shape[1]), F32)
+    extra = jnp.zeros((8, width), F32)
     for j, ref in enumerate((r0, r1, r2, r3)):
         block = ref[...].astype(F32)
-        source = lax.bitwise_xor(me, j)
-        rows32[pl.ds(pl.multiple_of(source * deep, 8), deep), :] = block[:deep]
-        extra = extra + block[deep:]
+        place = pl.ds(pl.multiple_of(lax.bitwise_xor(me, j) * deep, 8), deep)
+        up32[place, :] = block[:deep]
+        qkv32[place, :] = block[deep : 2 * deep]
+        extra = extra + block[2 * deep :]
     rows = 4 * deep
-    first, second = rows32[:, :half], rows32[:, half : 2 * half]
+    first, second = up32[:, :half], up32[:, half:]
     up_keep[...] = jnp.where(side == 0, first, second).astype(BF)
     up_give[...] = jnp.where(side == 0, second, first).astype(BF)
-    attn_piece[:rows, :own] = rows32[:, 2 * half :].astype(BF)
+    attn_piece[:rows, :own] = qkv32[:, :own].astype(BF)
     dense_values = dense[...].astype(F32)
     beside = [dense_values[:, q * quarter : (q + 1) * quarter] for q in range(4)]
     attn_piece[:rows, own:] = jnp.concatenate(beside, axis=0).astype(BF)
     units = half // 4
     row_block[...] = jnp.zeros(row_block.shape, F32)
     row_block[7:8, :units] = up_bias[...].astype(F32)
-    up_row = pltpu.roll(row_block[...], side * half + line * units, 1)
-    qkv_row = jnp.concatenate([extra[:, 2 * half :], jnp.zeros((8, quarter), F32)], axis=1)
-    attn_piece[rows:, :] = (extra[:, : 2 * half] + up_row + qkv_row).astype(BF)
+    attn_piece[rows:, :] = (extra + pltpu.roll(row_block[...], side * half + line * units, 1)).astype(BF)
 
 
 def mlp_kernel(*refs):
-    pieces, (unit_own, unit_other, dy_own, dy_other, vectors, attn_out, scaled, sums_in) = refs[:4], refs[4:12]
-    give, keep, mlp_in, act, d_up, sums, up, down, done = refs[12:]
+    pieces, (unit_own, unit_other, dy_own, dy_other, vectors, attn_out, scaled, sums_in) = refs[:2], refs[2:10]
+    give, keep, keep_terms, send_terms, up, down, mlp_in, act, d_up, sums, up_grad, down_grad, done = refs[10:]
     line, side = line_and_side()
     width, half = up.shape
     units = half // 4
     copies = []
-    for step, piece in zip((0, 3, 1, 2), pieces):
-        l = lax.bitwise_and(line + step, 3)
+    for place, step in enumerate(LINE_ORDER):
+        piece = pieces[place // 2].at[place % 2]
+        l = lax.bitwise_xor(line, step)
         top, low = pl.ds(0, units), pl.ds(units, units)
         for source, target in (
             (piece.at[top, :], down.at[pl.ds(pl.multiple_of(l * units, 32), units), :]),
@@ -770,33 +760,26 @@
 
     tokens(unit_own, dy_own, 0, True)
     tokens(unit_other, dy_other, group, False)
-
-
-def mlp_grads_kernel(mlp_in, act, d_up, dy_own, dy_other, sums, send1, send2, send3, own_terms, up_grad, down_grad):
-    line, _ = line_and_side()
-    sends = (send1, send2, send3)
-    group, width = dy_own.shape
-    half = act.shape[1]
-    units = half // 4
     for c in range(0, width, 128):
         up_grad[c : c + 128, :] = dot_tn(mlp_in[:, c : c + 128], d_up[...]).astype(BF)
     for c in range(0, half, 128):
         total = dot_tn(act[:group, c : c + 128], dy_own[...]) + dot_tn(act[group:, c : c + 128], dy_other[...])
         down_grad[c : c + 128, :] = total.astype(BF)
     tail = sums[...].astype(BF)
-    for step, ref in zip((1, 2, 3, 0), (*sends, own_terms)):
-        l = lax.bitwise_and(line + step, 3)
+    for place, step in enumerate(LINE_ORDER):
+        ref = (keep_terms, send_terms)[place // 2].at[place % 2]
+        l = lax.bitwise_xor(line, step)
         ref[:units, :] = down_grad[pl.ds(pl.multiple_of(l * units, 32), units), :]
         ref[units : 2 * units, :half] = up_grad[pl.ds(pl.multiple_of(2 * l * units, 32), units), :]
         ref[units : 2 * units, half:] = up_grad[pl.ds(pl.multiple_of((2 * l + 1) * units, 32), units), :]
         ref[2 * units :, :] = tail
 
 
-def mlp_sum_kernel(own, g1, g2, g3, down_own, up_keep, up_give, tail):
+def mlp_sum_kernel(own, far, down_own, up_keep, up_give, tail):
     units, width = down_own.shape
     half = width // 2
     _, side = line_and_side()
-    refs = (own, g1, g2, g3)
+    refs = (own.at[0], far.at[0])
 
     def total(rows, lanes):
         return sum(ref[rows, lanes].astype(F32) for ref in refs)
@@ -853,6 +836,29 @@
     vec_own[5:6, :] = rolled[5:6, :128]
     rolled = pltpu.roll(tail[...], width - line * units, 1)
     vec_own[6:7, :] = rolled[6:7, :128]
+
+
+def attention_sum_kernel(deep, own, far, b0, b1, b2, b3, dense_own, total):
+    me = lax.axis_index("seq")
+    total[...] = own[0].astype(F32) + far[0].astype(F32)
+    quarter = total.shape[1] // 4
+    for q in range(4):
+        dense_own[:, q * quarter : (q + 1) * quarter] = total[q * deep : (q + 1) * deep, 3 * quarter :]
+    for j, ref in enumerate((b0, b1, b2, b3)):
+        target = lax.bitwise_xor(me, j)
+        ref[...] = total[pl.ds(pl.multiple_of(target * deep, 8), deep), : 3 * quarter].astype(BF)
+
+
+def attention_owned_kernel(b0, b1, b2, b3, qkv_own, sources):
+    me = lax.axis_index("seq")
+    width = qkv_own.shape[1] // 3
+    own = width // 4
+    for j, ref in enumerate((b0, b1, b2, b3)):
+        sources[lax.bitwise_xor(me, j)] = ref[...].astype(F32)
+    for part in range(3):
+        lanes = slice(part * own, (part + 1) * own)
+        whole = jnp.concatenate([sources[t, :, lanes] for t in range(4)], axis=1)
+        qkv_own[:, part * width : (part + 1) * width] = whole
 
 
 def with_waits(count, body):
@@ -896,43 +902,52 @@
     wide = 2 * half + 3 * own
     flat = (group, width)
 
-    vectors_in = (attn_gain, attn_shift, mlp_gain, mlp_shift, dense_bias, down_bias, qkv_bias)
-    blocks = kernel_call(
+    by_width = jnp.stack([attn_gain, attn_shift, mlp_gain, mlp_shift, dense_bias, down_bias])
+    *blocks, mine = kernel_call(
         functools.partial(pack_kernel, deep),
-        (((deep + 8, wide), BF),) * 4,
-        (qkv_weight, up_weight, *[v[None] for v in vectors_in]),
-        scratch=(((4, deep + 8, wide), F32), ((8, 3 * width), F32)),
+        (((2 * deep + 8, width), BF),) * 4 + (((2 * rows, width), BF),),
+        (qkv_weight, up_weight, by_width, qkv_bias[None], hidden_in, grad_out),
+        scratch=(((4, 2 * deep + 8, width), F32), ((8, 3 * width), F32)),
         megabytes=16,
     )
-    got = seq_shuffle(blocks)
     attn_piece, up_keep, up_give = kernel_call(
         functools.partial(unpack_kernel, deep),
         (((per_line + 8, width), BF), ((per_line, half), BF), ((per_line, half), BF)),
-        (*got, dense_weight, up_bias[None]),
-        scratch=(((per_line, wide), F32), ((8, width), F32)),
+        (*seq_shuffle(blocks), dense_weight, up_bias[None]),
+        scratch=(((per_line, width), F32), ((per_line, width), F32), ((8, width), F32)),
         megabytes=16,
     )
-    attn_pieces = dp_pieces(attn_piece)
+
+    across = lax.ppermute(mine, "dp", SIDE_SWAP)
+    attn_half = lax.ppermute(attn_piece, "dp", HALF_SWAP)
     up_far = lax.ppermute(up_give, "dp", SIDE_SWAP)
+    chip_far = lax.ppermute(once(mine, up_keep), "seq", CHIP_SWAP)
+
+    attn_two = once(jnp.stack([attn_piece, attn_half]), up_far)
+    attn_pair = lax.ppermute(attn_two, "dp", PAIR_SWAP)
+    attn_side = lax.ppermute(attn_two, "dp", SIDE_SWAP)
     up_both = jnp.concatenate(
         [jnp.where(side == 0, up_keep, up_far), jnp.where(side == 0, up_far, up_keep)], axis=1
     )
-    mlp_piece = jnp.concatenate([down_weight, up_both], axis=0)
-    from2, from1, from3 = [lax.ppermute(mlp_piece, "dp", along(k)) for k in (2, 1, 3)]
-    mlp_pieces = (mlp_piece, from1, from3, from2)
-
-    mine = jnp.concatenate([hidden_in, grad_out], axis=0)
-    across = lax.ppermute(mine, "dp", SIDE_SWAP)
-
-    def whole_group(values):
-        far = lax.ppermute(values, "seq", CHIP_SWAP)
-        by_chip = in_order(chip == 1, values, far)
-        over = lax.ppermute(by_chip, "seq", CORE_SWAP)
-        full = in_order(core == 1, by_chip, over, axis=1).reshape(n_seq, 2, rows, width)
+    mlp_piece = once(jnp.concatenate([down_weight, up_both], axis=0), attn_half)
+    mlp_half = lax.ppermute(mlp_piece, "dp", HALF_SWAP)
+    by_chip = once(in_order(chip == 1, mine, chip_far), attn_half, up_far)
+    core_far = lax.ppermute(by_chip, "seq", CORE_SWAP)
+
+    attn_far = lax.ppermute(once(attn_pair, mlp_half), "dp", SIDE_SWAP)
+    mlp_two = once(jnp.stack([mlp_piece, mlp_half]), attn_pair)
+    mlp_pair = lax.ppermute(mlp_two, "dp", PAIR_SWAP)
+    chip_beyond = lax.ppermute(once(across, mlp_half, attn_pair, attn_side), "seq", CHIP_SWAP)
+    by_chip_beyond = once(in_order(chip == 1, across, chip_beyond), mlp_pair, attn_far)
+    core_beyond = lax.ppermute(by_chip_beyond, "seq", CORE_SWAP)
+
+    def whole_group(values, over):
+        full = in_order(core == 1, values, over, axis=1).reshape(n_seq, 2, rows, width)
         return full[:, 0].reshape(flat), full[:, 1].reshape(flat)
 
-    hidden_group, dy = whole_group(once(mine, attn_pieces[2]))
-    hidden_other, dy_other = whole_group(once(across, attn_pieces[6]))
+    hidden_group, dy = whole_group(by_chip, core_far)
+    hidden_other, dy_other = whole_group(by_chip_beyond, core_beyond)
+    attn_pieces = (attn_two, attn_pair, attn_side, attn_far)
 
     row_lengths = lengths[0]
     segment, position = place(row_lengths, jnp.arange(group, dtype=jnp.int32))
@@ -970,7 +985,7 @@
     attended = kernel_call(
         with_waits(1, functools.partial(attention_kernel, deep)),
         (((2 * deep, group), BF),) * 4 + ((flat, BF),),
-        (from2, qk, v, *d_blocks, segment[:, None], segment[None, :], cosine, sine_a, sine_b),
+        (mlp_pair, qk, v, *d_blocks, segment[:, None], segment[None, :], cosine, sine_a, sine_b),
         scratch=(((own, group), F32),) * 4 + ((flat, F32),),
         flops=14 * group * group * own,
         apart=1,
@@ -978,43 +993,50 @@
     d_joined = attended[4]
     row_blocks = seq_shuffle(attended[:4])
     results = kernel_call(
-        with_waits(2, functools.partial(attention_grads_kernel, deep)),
-        pick_shapes(per_line, width) + ((flat, F32), (flat, F32), ((8, width), F32)),
-        (from1, from3, *row_blocks, dense, dy, attn_in, d_joined, weights, unit, vectors),
+        with_waits(1, functools.partial(attention_grads_kernel, deep)),
+        (((4, per_line, width), BF),) * 2 + ((flat, F32), (flat, F32), ((8, width), F32)),
+        (core_beyond, *row_blocks, dense, dy, attn_in, d_joined, weights, unit, vectors),
         scratch=(((n_dp * deep, group), BF), ((width, width), F32)),
         flops=5 * group * width * width,
         megabytes=32,
+        apart=1,
+    )
+    attn_send, attn_keep = results[:2]
+
+    give, keep, *results = kernel_call(
+        mlp_kernel,
+        (((4, rows, 2 * width), BF),) * 2 + (((2, 2 * units + 8, width), BF),) * 2,
+        (mlp_two, mlp_pair, unit, unit_other, dy, dy_other, vectors) + tuple(results[2:]),
+        scratch=(
+            ((width, half), BF),
+            ((half, width), BF),
+            ((2 * group, width), BF),
+            ((2 * group, half), BF),
+            ((2 * group, half), BF),
+            ((8, width), F32),
+            ((width, half), BF),
+            ((half, width), BF),
+            pltpu.SemaphoreType.DMA((12,)),
+        ),
+        flops=12 * group * width * 2 * half,
+        megabytes=32,
         apart=2,
     )
-    moved, attn_sum = dp_sum(*results[:6])
-
-    units_shape = ((2 * group, half), BF)
-    give, keep, *held = kernel_call(
-        mlp_kernel,
-        (((4, rows, 2 * width), BF),) * 2 + (((2 * group, width), BF), units_shape, units_shape, ((8, width), F32)),
-        (*mlp_pieces, unit, unit_other, dy, dy_other, vectors) + tuple(results[6:]),
-        scratch=(((width, half), BF), ((half, width), BF), pltpu.SemaphoreType.DMA((12,))),
-        flops=8 * group * width * 2 * half,
-        megabytes=32,
-        apart=4,
-    )
-    results = kernel_call(
-        with_waits(len(moved), mlp_grads_kernel),
-        (((2 * units + 8, width), BF),) * 4,
-        (*moved, *held[:3], dy, dy_other, held[3]),
-        scratch=(((width, half), BF), ((half, width), BF)),
-        flops=4 * group * width * 2 * half,
-        megabytes=24,
-        apart=len(moved),
-    )
-    terms = [results[3]] + [lax.ppermute(send, "dp", along(k)) for k, send in zip((1, 2, 3), results[:3])]
-
+    keep_terms, send_terms = results
+    mlp_got = lax.ppermute(send_terms, "dp", PAIR_SWAP)
+    attn_moved = lax.ppermute(once(attn_send, keep_terms), "dp", SIDE_SWAP)
     both = keep.astype(F32) + lax.ppermute(give, "seq", CORE_SWAP).astype(F32)
     beyond = lax.ppermute(both[2:].astype(BF), "dp", SIDE_SWAP)
-    *terms, beyond = lax.optimization_barrier((*terms, beyond))
+    mlp_mine, mlp_send = add_blocks(keep_terms, mlp_got, 1, 1)
+    mlp_last = lax.ppermute(mlp_send, "dp", HALF_SWAP)
+    attn_mine, attn_send = add_blocks(attn_keep, attn_moved, 2, 2, waits=(mlp_got,))
+    attn_got = lax.ppermute(attn_send, "dp", PAIR_SWAP)
+    attn_mine, attn_send = add_blocks(attn_mine, attn_got, 1, 1, waits=(mlp_send,))
+    attn_last = lax.ppermute(attn_send, "dp", HALF_SWAP)
+
     both = both[:2] + beyond.astype(F32)
-    far = lax.ppermute(pick(both, 1 - chip).astype(BF), "seq", CHIP_SWAP)
-    pair = pick(both, chip) + far.astype(F32)
+    chip_last = lax.ppermute(pick(both, 1 - chip).astype(BF), "seq", CHIP_SWAP)
+    pair = pick(both, chip) + chip_last.astype(F32)
     x = hidden_in.astype(F32)
     block_out = x + vectors[4] + vectors[5] + pair[:, :width]
     upstream = pair[:, width:]
@@ -1026,19 +1048,12 @@
     )
     grad_in = grad_out.astype(F32) + inverse * inner
 
-    def from_heads(blocks):
-        split = jnp.moveaxis(blocks.reshape(n_seq, -1, 3, own), 0, 2)
-        return split.reshape(-1, 3 * width)
-
-    qkv_back = attn_sum[:, : 3 * own].reshape(n_seq, deep, 3 * own).astype(BF)
-    qkv_own = from_heads(seq_exchange(qkv_back).astype(F32))
-    dense_own = attn_sum[:, 3 * own :].reshape(n_seq, deep, own)
-    dense_own = jnp.swapaxes(dense_own, 0, 1).reshape(deep, width)
     down_own, up_keep, up_give, tail = kernel_call(
-        mlp_sum_kernel,
+        with_waits(1, mlp_sum_kernel),
         (((units, width), F32), ((per_line, half), BF), ((per_line + 16, half), BF), ((8, width), F32)),
-        tuple(terms),
+        (beyond, mlp_mine, mlp_last),
         megabytes=8,
+        apart=1,
     )
     up_far = lax.ppermute(up_give, "dp", SIDE_SWAP)
     blocks = kernel_call(
@@ -1049,10 +1064,26 @@
         megabytes=8,
     )
     up_own, vec_own = kernel_call(
-        functools.partial(owned_kernel, deep),
+        with_waits(2, functools.partial(owned_kernel, deep)),
         (((deep, hidden_units), F32), ((8, 128), F32)),
-        (*seq_shuffle(blocks), tail),
+        (chip_last, attn_last, *seq_shuffle(blocks), tail),
         scratch=(((4, deep + 8, width), F32), ((8, 3 * width), F32)),
+        megabytes=8,
+        apart=2,
+    )
+    *blocks, dense_own = kernel_call(
+        with_waits(1, functools.partial(attention_sum_kernel, deep)),
+        (((deep, 3 * own), BF),) * 4 + (((deep, width), F32),),
+        (up_far, attn_mine, attn_last),
+        scratch=(((per_line, width), F32),),
+        megabytes=8,
+        apart=1,
+    )
+    (qkv_own,) = kernel_call(
+        attention_owned_kernel,
+        (((deep, 3 * width), F32),),
+        tuple(seq_shuffle(blocks)),
+        scratch=(((4, deep, 3 * own), F32),),
         megabytes=8,
     )
     by_width = vec_own[:5, :deep]

time: 181 us -> 151 us (0.83)
  the two profiles are of different devices: /device:TPU:8 before, /device:TPU:0 now
where the time goes in v5:
time: 151 us
  waiting for transfers between devices  65 us (43%)
  starting transfers between devices  38.8 us (26%)
  Pallas kernels  25.8 us (17%)
  local copies, waits for them, and re-layouts  11.6 us (8%)
  other arithmetic  8.46 us (6%)
    pallas_call x15, Pallas kernels, kernel_call(): pl.pallas_call(body, out_shape=tuple((jax.ShapeDtypeStruct(shape, kind) f...  25.8 us
    ppermute x15, waiting for transfers between devices, seq_shuffle(): got.append(lax.ppermute(blocks[other], 'seq', pairs))  14 us
    ppermute x1, waiting for transfers between devices, line_device(): attn_got = lax.ppermute(attn_send, 'dp', PAIR_SWAP)  12.1 us
    ppermute x15, starting transfers between devices, seq_shuffle(): got.append(lax.ppermute(blocks[other], 'seq', pairs))  10.3 us
    ppermute x1, waiting for transfers between devices, line_device(): mlp_half = lax.ppermute(mlp_piece, 'dp', HALF_SWAP)  9 us
    ppermute x1, waiting for transfers between devices, line_device(): mlp_got = lax.ppermute(send_terms, 'dp', PAIR_SWAP)  8.41 us
    unnamed x29, local copies, waits for them, and re-layouts  7.9 us
    ppermute x1, waiting for transfers between devices, line_device(): lax.ppermute(once(across, mlp_half, attn_pair, attn_side), 'seq', CHIP_SWAP)  4.99 us
  transfers between devices with their start and end apart: 36, of which 18 were waited for; matrix products, arithmetic and copies ran while one was open for 4% of the time, Pallas kernels for 3%

profile of v5, /device:TPU:0, one launch (start us, length us, event | category | flops | bytes accessed | tf_op | source)
XLA Modules:
  0.0 150.8 jit_solution(13010824949619682404)
XLA Ops:
  1.4 0.9 copy-done
  2.4 0.9 copy-done.2
  3.3 0.9 copy-done.4
  6.5 2.6 %collective-permute-start.1 = (bf16[56,768]{1,0:T(8,128)(2,1)S(1)}, bf16[56,768]{1,0:T(8,128)(2,1)S(1)}, u32[]{:S(2)}, u32[]{:S(2)}) collective-permute-start(bf16[56,768]{1,0:T(8,128)(2,1)S(1)} %get-tuple-element.78), channel_id=1, source_target_pairs={{0,2},{1,3},{2,0},{3,1},{4,6},{5,7},{6,4},{7,5},{8,10},{9,11},{10,... | collective-permute-start | bytes 258056 | tf_op jit(solution)/shard_map/ppermute | solution.py:485
  9.2 3.1 %collective-permute-done.1.r2 = bf16[56,768]{1,0:T(8,128)(2,1)S(1)} collective-permute-done((bf16[56,768]{1,0:T(8,128)(2,1)S(1)}, bf16[56,768]{1,0:T(8,128)(2,1)S(1)}, u32[]{:S(2)}, u32[]{:S(2)}) %collective-permute-start.1) | collective-permute-done | bytes 86048 | tf_op jit(solution)/shard_map/ppermute | solution.py:485
  12.3 1.6 %collective-permute-done.2.r3 = bf16[56,768]{1,0:T(8,128)(2,1)S(1)} collective-permute-done((bf16[56,768]{1,0:T(8,128)(2,1)S(1)}, bf16[56,768]{1,0:T(8,128)(2,1)S(1)}, u32[]{:S(2)}, u32[]{:S(2)}) %collective-permute-start.2) | collective-permute-done | bytes 86048 | tf_op jit(solution)/shard_map/ppermute | solution.py:485
  15.4 1.6 %collective-permute-start.4 = (bf16[96,384]{1,0:T(8,128)(2,1)S(1)}, bf16[96,384]{1,0:T(8,128)(2,1)S(1)}, u32[]{:S(2)}, u32[]{:S(2)}) collective-permute-start(bf16[96,384]{1,0:T(8,128)(2,1)S(1)} %get-tuple-element.81), channel_id=1, source_target_pairs={{0,4},{4,0},{8,12},{12,8},{16,20},{20,16},{24,28},{28,24},{1,5},{5... | collective-permute-start | bytes 221192 | tf_op jit(solution)/shard_map/ppermute | solution.py:923
  17.5 2.6 %collective-permute-start.3 = (bf16[104,768]{1,0:T(8,128)(2,1)S(1)}, bf16[104,768]{1,0:T(8,128)(2,1)S(1)}, u32[]{:S(2)}, u32[]{:S(2)}) collective-permute-start(bf16[104,768]{1,0:T(8,128)(2,1)S(1)} %get-tuple-element.80), channel_id=1, source_target_pairs={{0,16},{4,20},{8,24},{12,28},{16,0},{20,4},{24,8},{28,12},{1,17},{... | collective-permute-start | bytes 479240 | tf_op jit(solution)/shard_map/ppermute | solution.py:922
  20.1 1.5 collective-permute-start.9
  21.6 0.9 maximum_maximum_fusion
  22.6 5.0 %collective-permute-done.3 = bf16[104,768]{1,0:T(8,128)(2,1)S(1)} collective-permute-done((bf16[104,768]{1,0:T(8,128)(2,1)S(1)}, bf16[104,768]{1,0:T(8,128)(2,1)S(1)}, u32[]{:S(2)}, u32[]{:S(2)}) %collective-permute-start.3) | collective-permute-done | bytes 159776 | tf_op jit(solution)/shard_map/ppermute | solution.py:922
  27.6 4.2 %collective-permute-start.5 = (bf16[2,104,768]{2,1,0:T(8,128)(2,1)S(1)}, bf16[2,104,768]{2,1,0:T(8,128)(2,1)S(1)}, u32[]{:S(2)}, u32[]{:S(2)}) collective-permute-start(bf16[2,104,768]{2,1,0:T(8,128)(2,1)S(1)} %pad_maximum_fusion.5.refs_0_), channel_id=1, source_target_pairs={{0,8},{4,12},{8,0},{12,4},{16,24},{20,28},{24,16},{28,20},{1,9},{5... | collective-permute-start | bytes 958472 | tf_op jit(solution)/shard_map/ppermute | solution.py:927
  31.7 1.5 %collective-permute-start.6 = (bf16[2,104,768]{2,1,0:T(8,128)(2,1)S(1)}, bf16[2,104,768]{2,1,0:T(8,128)(2,1)S(1)}, u32[]{:S(2)}, u32[]{:S(2)}) collective-permute-start(bf16[2,104,768]{2,1,0:T(8,128)(2,1)S(1)} %pad_maximum_fusion.5.refs_0_), channel_id=1, source_target_pairs={{0,4},{4,0},{8,12},{12,8},{16,20},{20,16},{24,28},{28,24},{1,5},{5... | collective-permute-start | bytes 958472 | tf_op jit(solution)/shard_map/ppermute | solution.py:928
  33.7 9.0 %collective-permute-done.7 = bf16[192,768]{1,0:T(8,128)(2,1)S(1)} collective-permute-done((bf16[192,768]{1,0:T(8,128)(2,1)S(1)}, bf16[192,768]{1,0:T(8,128)(2,1)S(1)}, u32[]{:S(2)}, u32[]{:S(2)}) %collective-permute-start.7) | collective-permute-done | bytes 294944 | tf_op jit(solution)/shard_map/ppermute | solution.py:933
  43.4 1.6 %collective-permute-start.13 = (bf16[256,768]{1,0:T(8,128)(2,1)S(1)}, bf16[256,768]{1,0:T(8,128)(2,1)S(1)}, u32[]{:S(2)}, u32[]{:S(2)}) collective-permute-start(bf16[256,768]{1,0:T(8,128)(2,1)S(1)} %collective-permute-done.12), channel_id=1, source_target_pairs={{0,2},{2,0},{1,3},{3,1},{4,6},{6,4},{5,7},{7,5},{8,10},{10,8},{9,1... | collective-permute-start | bytes 1179656 | tf_op jit(solution)/shard_map/ppermute | solution.py:940
  45.2 1.6 %collective-permute-start.8 = (bf16[2,104,768]{2,1,0:T(8,128)(2,1)S(1)}, bf16[2,104,768]{2,1,0:T(8,128)(2,1)S(1)}, u32[]{:S(2)}, u32[]{:S(2)}) collective-permute-start(bf16[2,104,768]{2,1,0:T(8,128)(2,1)S(1)} %collective-permute-done.5.refs_1_), channel_id=1, source_target_pairs={{0,4},{4,0},{8,12},{12,8},{16,20},{20,16},{24,28},{28,24},{1,5},{5... | collective-permute-start | bytes 958472 | tf_op jit(solution)/shard_map/ppermute | solution.py:937
  46.8 5.0 %collective-permute-done.13 = bf16[256,768]{1,0:T(8,128)(2,1)S(1)} collective-permute-done((bf16[256,768]{1,0:T(8,128)(2,1)S(1)}, bf16[256,768]{1,0:T(8,128)(2,1)S(1)}, u32[]{:S(2)}, u32[]{:S(2)}) %collective-permute-start.13) | collective-permute-done | bytes 393248 | tf_op jit(solution)/shard_map/ppermute | solution.py:940
  51.9 3.2 %collective-permute-done.8.refs_3_ = bf16[2,104,768]{2,1,0:T(8,128)(2,1)S(1)} collective-permute-done((bf16[2,104,768]{2,1,0:T(8,128)(2,1)S(1)}, bf16[2,104,768]{2,1,0:T(8,128)(2,1)S(1)}, u32[]{:S(2)}, u32[]{:S(2)}) %collective-permute-start.8) | collective-permute-done | bytes 319520 | tf_op jit(solution)/shard_map/ppermute | solution.py:937
  55.2 2.2 %collective-permute-done.11.refs_0_.refs_1_ = bf16[2,192,768]{2,1,0:T(8,128)(2,1)S(1)} collective-permute-done((bf16[2,192,768]{2,1,0:T(8,128)(2,1)S(1)}, bf16[2,192,768]{2,1,0:T(8,128)(2,1)S(1)}, u32[]{:S(2)}, u32[]{:S(2)}) %collective-permute-start.11) | collective-permute-done | bytes 589856 | tf_op jit(solution)/shard_map/ppermute | solution.py:939
  57.4 1.0 fusion.18
  58.5 1.2 collective-permute-done.14.refs_0_
  62.8 1.3 collective-permute-start.17
  64.7 1.7 %shard_map.257 = (bf16[512,768]{1,0:T(8,128)(2,1)S(1)}, bf16[512,384]{1,0:T(8,128)(2,1)S(1)}, bf16[512,192]{1,0:T(8,128)(2,1)S(1)}) custom-call(f32[512,768]{1,0:T(8,128)S(1)} %fusion.1.unit.refs_10_.refs_2_, bf16[768,768]{1,0:T(8,128)(2,1)S(1)} %get-tuple-element.93.weights.refs_9_, f32[8,768]{1,0:T(8,128)S(1)} %get-tuple-element.89.vectors.refs_11_.refs_6_, ...), custom_call_target="tpu_custom_call" | custom-call | flops 603979776 | bytes 3563520 | tf_op jit(solution)/shard_map/pallas_call | solution.py:415
  66.9 6.2 %shard_map.258 = (bf16[48,512]{1,0:T(8,128)(2,1)S(1)}, bf16[48,512]{1,0:T(8,128)(2,1)S(1)}, bf16[48,512]{1,0:T(8,128)(2,1)S(1)}, bf16[48,512]{1,0:T(8,128)(2,1)S(1)}, bf16[512,768]{1,0:T(8,128)(2,1)S(1)}) custom-call(bf16[2,192,768]{2,1,0:T(8,128)(2,1)S(1)} %collective-permute-done.11.refs_0_.refs_1_, bf16[512,384]{1,0:T(8,128)(2,1)S(1)} %get-tuple-element.94.refs_1_, ...), custom_call_target="tpu_custom_call" | custom-call | flops 704643072 | bytes 2166784 | tf_op jit(solution)/shard_map/pallas_call | solution.py:415
  73.5 1.0 collective-permute-start.19
  75.3 2.5 %collective-permute-done.19.refs_3_ = bf16[48,512]{1,0:T(8,128)(2,1)S(1)} collective-permute-done((bf16[48,512]{1,0:T(8,128)(2,1)S(1)}, bf16[48,512]{1,0:T(8,128)(2,1)S(1)}, u32[]{:S(2)}, u32[]{:S(2)}) %collective-permute-start.19) | collective-permute-done | bytes 49184 | tf_op jit(solution)/shard_map/ppermute | solution.py:485
  78.4 2.6 %shard_map.259 = (bf16[4,96,768]{2,1,0:T(8,128)(2,1)}, bf16[4,96,768]{2,1,0:T(8,128)(2,1)S(1)}, f32[512,768]{1,0:T(8,128)S(1)}, f32[512,768]{1,0:T(8,128)S(1)}, f32[8,768]{1,0:T(8,128)S(1)}) custom-call(bf16[2,256,768]{2,1,0:T(8,128)(2,1)S(1)} %collective-permute-done.14.refs_0_, bf16[48,512]{1,0:T(8,128)(2,1)S(1)} %get-tuple-element.100.refs_1_, ...), custom_call_target="tpu_custom_call" | custom-call | flops 1509949440 | bytes 6414336 | tf_op jit(solution)/shard_map/pallas_call | solution.py:415
  81.0 10.7 %shard_map.260 = (bf16[4,128,1536]{2,1,0:T(8,128)(2,1)S(1)}, bf16[4,128,1536]{2,1,0:T(8,128)(2,1)S(1)}, bf16[2,200,768]{2,1,0:T(8,128)(2,1)S(1)}, bf16[2,200,768]{2,1,0:T(8,128)(2,1)}) custom-call(bf16[2,192,768]{2,1,0:T(8,128)(2,1)S(1)} %pad_maximum_fusion.4.refs_0_, bf16[2,192,768]{2,1,0:T(8,128)(2,1)S(1)} %collective-permute-done.11.refs_0_.refs_1_, ...), custom_call_target="tpu_custom_call" | custom-call | flops 3623878656 | bytes 9093120 | tf_op jit(solution)/shard_map/pallas_call | solution.py:415
  92.3 1.5 %collective-permute-start.25 = (bf16[4,96,768]{2,1,0:T(8,128)(2,1)}, bf16[4,96,768]{2,1,0:T(8,128)(2,1)S(1)}, u32[]{:S(2)}, u32[]{:S(2)}) collective-permute-start(bf16[4,96,768]{2,1,0:T(8,128)(2,1)} %get-tuple-element.117), channel_id=1, source_target_pairs={{0,4},{4,0},{8,12},{12,8},{16,20},{20,16},{24,28},{28,24},{1,5},{5... | collective-permute-start | bytes 1769480 | tf_op jit(solution)/shard_map/ppermute | solution.py:1027
  93.8 1.3 collective-permute-done.21
  95.7 1.6 %copy-done.9 = f32[4,128,1536]{2,1,0:T(8,128)} copy-done((f32[4,128,1536]{2,1,0:T(8,128)}, f32[4,128,1536]{2,1,0:T(8,128)S(1)}, u32[]{:S(2)}) %copy-start.9) | copy-done | bytes 3145752
  97.3 1.0 slice.109
  98.3 1.6 %collective-permute-start.22 = (bf16[2,128,1536]{2,1,0:T(8,128)(2,1)}, bf16[2,128,1536]{2,1,0:T(8,128)(2,1)S(1)}, u32[]{:S(2)}, u32[]{:S(2)}) collective-permute-start(bf16[2,128,1536]{2,1,0:T(8,128)(2,1)} %slice.109), channel_id=1, source_target_pairs={{0,4},{4,0},{8,12},{12,8},{16,20},{20,16},{24,28},{28,24},{1,5},{5... | collective-permute-start | bytes 2359304 | tf_op jit(solution)/shard_map/ppermute | solution.py:1029
  99.9 8.4 %collective-permute-done.24.refs_1_.refs_0_ = bf16[2,200,768]{2,1,0:T(8,128)(2,1)S(1)} collective-permute-done((bf16[2,200,768]{2,1,0:T(8,128)(2,1)}, bf16[2,200,768]{2,1,0:T(8,128)(2,1)S(1)}, u32[]{:S(2)}, u32[]{:S(2)}) %collective-permute-start.24) | collective-permute-done | bytes 614432 | tf_op jit(solution)/shard_map/ppermute | solution.py:1026
  108.4 4.4 %collective-permute-start.28 = (bf16[1,200,768]{2,1,0:T(8,128)(2,1)S(1)}, bf16[1,200,768]{2,1,0:T(8,128)(2,1)S(1)}, u32[]{:S(2)}, u32[]{:S(2)}) collective-permute-start(bf16[1,200,768]{2,1,0:T(8,128)(2,1)S(1)} %get-tuple-element.114.refs_0_), channel_id=1, source_target_pairs={{0,16},{4,20},{8,24},{12,28},{16,0},{20,4},{24,8},{28,12},{1,17},{... | collective-permute-start | bytes 921608 | tf_op jit(solution)/shard_map/ppermute | solution.py:1031
  113.0 1.6 %collective-permute-start.26 = (bf16[2,96,768]{2,1,0:T(8,128)(2,1)S(1)}, bf16[2,96,768]{2,1,0:T(8,128)(2,1)S(1)}, u32[]{:S(2)}, u32[]{:S(2)}) collective-permute-start(bf16[2,96,768]{2,1,0:T(8,128)(2,1)S(1)} %get-tuple-element.119), channel_id=1, source_target_pairs={{0,8},{4,12},{8,0},{12,4},{16,24},{20,28},{24,16},{28,20},{1,9},{5... | collective-permute-start | bytes 884744 | tf_op jit(solution)/shard_map/ppermute | solution.py:1033
  114.7 12.1 %collective-permute-done.26.refs_2_ = bf16[2,96,768]{2,1,0:T(8,128)(2,1)S(1)} collective-permute-done((bf16[2,96,768]{2,1,0:T(8,128)(2,1)S(1)}, bf16[2,96,768]{2,1,0:T(8,128)(2,1)S(1)}, u32[]{:S(2)}, u32[]{:S(2)}) %collective-permute-start.26) | collective-permute-done | bytes 294944 | tf_op jit(solution)/shard_map/ppermute | solution.py:1033
  126.9 1.0 collective-permute-start.27
  128.7 1.5 collective-permute-start.29
  130.5 1.1 collective-permute-start.23
  131.8 2.8 %collective-permute-done.27.refs_1_.refs_2_ = bf16[1,96,768]{2,1,0:T(8,128)(2,1)S(1)} collective-permute-done((bf16[1,96,768]{2,1,0:T(8,128)(2,1)S(1)}, bf16[1,96,768]{2,1,0:T(8,128)(2,1)S(1)}, u32[]{:S(2)}, u32[]{:S(2)}) %collective-permute-start.27) | collective-permute-done | bytes 147488 | tf_op jit(solution)/shard_map/ppermute | solution.py:1035
  135.4 1.1 collective-permute-start.34
  137.6 1.1 collective-permute-start.31
  138.7 2.9 %collective-permute-done.34.b2 = bf16[24,576]{1,0:T(8,128)(2,1)S(1)} collective-permute-done((bf16[24,576]{1,0:T(8,128)(2,1)S(1)}, bf16[24,576]{1,0:T(8,128)(2,1)S(1)}, u32[]{:S(2)}, u32[]{:S(2)}) %collective-permute-start.34) | collective-permute-done | bytes 27680 | tf_op jit(solution)/shard_map/ppermute | solution.py:485
  142.5 2.8 %collective-permute-done.32.refs_5_ = bf16[32,768]{1,0:T(8,128)(2,1)S(1)} collective-permute-done((bf16[32,768]{1,0:T(8,128)(2,1)S(1)}, bf16[32,768]{1,0:T(8,128)(2,1)S(1)}, u32[]{:S(2)}, u32[]{:S(2)}) %collective-permute-start.32) | collective-permute-done | bytes 49184 | tf_op jit(solution)/shard_map/ppermute | solution.py:485
  145.3 1.0 shard_map.266
  147.9 1.2 bitcast_add_fusion
  149.3 0.9 fusion.12
  (119 shorter events, 20.4 us)
Async XLA Ops:
  0.6 32.6 %copy-start.12 = (s32[1,4]{1,0:T(1,128)S(1)}, s32[1,4]{1,0:T(1,128)}, u32[]{:S(2)}) copy-start(s32[1,4]{1,0:T(1,128)} %param.16) | copy-start | bytes 52
  1.4 0.9 copy-start
  2.4 0.9 copy-start.2
  3.3 0.9 copy-start.4
  4.2 0.9 copy-start.5
  6.0 3.2 %collective-permute-start = (bf16[56,768]{1,0:T(8,128)(2,1)S(1)}, bf16[56,768]{1,0:T(8,128)(2,1)S(1)}, u32[]{:S(2)}, u32[]{:S(2)}) collective-permute-start(bf16[56,768]{1,0:T(8,128)(2,1)S(1)} %get-tuple-element.77), channel_id=1, source_target_pairs={{0,1},{1,0},{2,3},{3,2},{4,5},{5,4},{6,7},{7,6},{8,9},{9,8},{10,11... | collective-permute-start | bytes 258056 | tf_op jit(solution)/shard_map/ppermute | solution.py:485
  6.5 5.8 %collective-permute-start.1 = (bf16[56,768]{1,0:T(8,128)(2,1)S(1)}, bf16[56,768]{1,0:T(8,128)(2,1)S(1)}, u32[]{:S(2)}, u32[]{:S(2)}) collective-permute-start(bf16[56,768]{1,0:T(8,128)(2,1)S(1)} %get-tuple-element.78), channel_id=1, source_target_pairs={{0,2},{1,3},{2,0},{3,1},{4,6},{5,7},{6,4},{7,5},{8,10},{9,11},{10,... | collective-permute-start | bytes 258056 | tf_op jit(solution)/shard_map/ppermute | solution.py:485
  9.1 4.8 %collective-permute-start.2 = (bf16[56,768]{1,0:T(8,128)(2,1)S(1)}, bf16[56,768]{1,0:T(8,128)(2,1)S(1)}, u32[]{:S(2)}, u32[]{:S(2)}) collective-permute-start(bf16[56,768]{1,0:T(8,128)(2,1)S(1)} %get-tuple-element.79), channel_id=1, source_target_pairs={{0,3},{1,2},{2,1},{3,0},{4,7},{5,6},{6,5},{7,4},{8,11},{9,10},{10,... | collective-permute-start | bytes 258056 | tf_op jit(solution)/shard_map/ppermute | solution.py:485
  13.8 0.8 copy-start.6
  15.4 6.2 %collective-permute-start.4 = (bf16[96,384]{1,0:T(8,128)(2,1)S(1)}, bf16[96,384]{1,0:T(8,128)(2,1)S(1)}, u32[]{:S(2)}, u32[]{:S(2)}) collective-permute-start(bf16[96,384]{1,0:T(8,128)(2,1)S(1)} %get-tuple-element.81), channel_id=1, source_target_pairs={{0,4},{4,0},{8,12},{12,8},{16,20},{20,16},{24,28},{28,24},{1,5},{5... | collective-permute-start | bytes 221192 | tf_op jit(solution)/shard_map/ppermute | solution.py:923
  17.0 25.7 %collective-permute-start.12 = (bf16[256,768]{1,0:T(8,128)(2,1)S(1)}, bf16[256,768]{1,0:T(8,128)(2,1)S(1)}, u32[]{:S(2)}, u32[]{:S(2)}) collective-permute-start(bf16[256,768]{1,0:T(8,128)(2,1)S(1)} %get-tuple-element.87), channel_id=1, source_target_pairs={{0,4},{4,0},{8,12},{12,8},{16,20},{20,16},{24,28},{28,24},{1,5},{5... | collective-permute-start | bytes 1179656 | tf_op jit(solution)/shard_map/ppermute | solution.py:921
  17.5 10.0 %collective-permute-start.3 = (bf16[104,768]{1,0:T(8,128)(2,1)S(1)}, bf16[104,768]{1,0:T(8,128)(2,1)S(1)}, u32[]{:S(2)}, u32[]{:S(2)}) collective-permute-start(bf16[104,768]{1,0:T(8,128)(2,1)S(1)} %get-tuple-element.80), channel_id=1, source_target_pairs={{0,16},{4,20},{8,24},{12,28},{16,0},{20,4},{24,8},{28,12},{1,17},{... | collective-permute-start | bytes 479240 | tf_op jit(solution)/shard_map/ppermute | solution.py:922
  20.1 24.8 %collective-permute-start.9 = (bf16[256,768]{1,0:T(8,128)(2,1)S(1)}, bf16[256,768]{1,0:T(8,128)(2,1)S(1)}, u32[]{:S(2)}, u32[]{:S(2)}) collective-permute-start(bf16[256,768]{1,0:T(8,128)(2,1)S(1)} %get-tuple-element.87), channel_id=1, source_target_pairs={{0,2},{2,0},{1,3},{3,1},{4,6},{6,4},{5,7},{7,5},{8,10},{10,8},{9,1... | collective-permute-start | bytes 1179656 | tf_op jit(solution)/shard_map/ppermute | solution.py:924
  27.5 15.1 %collective-permute-start.7 = (bf16[192,768]{1,0:T(8,128)(2,1)S(1)}, bf16[192,768]{1,0:T(8,128)(2,1)S(1)}, u32[]{:S(2)}, u32[]{:S(2)}) collective-permute-start(bf16[192,768]{1,0:T(8,128)(2,1)S(1)} %maximum_maximum_fusion), channel_id=1, source_target_pairs={{0,16},{4,20},{8,24},{12,28},{16,0},{20,4},{24,8},{28,12},{1,17},{... | collective-permute-start | bytes 884744 | tf_op jit(solution)/shard_map/ppermute | solution.py:933
  27.6 15.8 %collective-permute-start.5 = (bf16[2,104,768]{2,1,0:T(8,128)(2,1)S(1)}, bf16[2,104,768]{2,1,0:T(8,128)(2,1)S(1)}, u32[]{:S(2)}, u32[]{:S(2)}) collective-permute-start(bf16[2,104,768]{2,1,0:T(8,128)(2,1)S(1)} %pad_maximum_fusion.5.refs_0_), channel_id=1, source_target_pairs={{0,8},{4,12},{8,0},{12,4},{16,24},{20,28},{24,16},{28,20},{1,9},{5... | collective-permute-start | bytes 958472 | tf_op jit(solution)/shard_map/ppermute | solution.py:927
  31.7 11.7 %collective-permute-start.6 = (bf16[2,104,768]{2,1,0:T(8,128)(2,1)S(1)}, bf16[2,104,768]{2,1,0:T(8,128)(2,1)S(1)}, u32[]{:S(2)}, u32[]{:S(2)}) collective-permute-start(bf16[2,104,768]{2,1,0:T(8,128)(2,1)S(1)} %pad_maximum_fusion.5.refs_0_), channel_id=1, source_target_pairs={{0,4},{4,0},{8,12},{12,8},{16,20},{20,16},{24,28},{28,24},{1,5},{5... | collective-permute-start | bytes 958472 | tf_op jit(solution)/shard_map/ppermute | solution.py:928
  43.4 8.4 %collective-permute-start.13 = (bf16[256,768]{1,0:T(8,128)(2,1)S(1)}, bf16[256,768]{1,0:T(8,128)(2,1)S(1)}, u32[]{:S(2)}, u32[]{:S(2)}) collective-permute-start(bf16[256,768]{1,0:T(8,128)(2,1)S(1)} %collective-permute-done.12), channel_id=1, source_target_pairs={{0,2},{2,0},{1,3},{3,1},{4,6},{6,4},{5,7},{7,5},{8,10},{10,8},{9,1... | collective-permute-start | bytes 1179656 | tf_op jit(solution)/shard_map/ppermute | solution.py:940
  45.0 12.4 %collective-permute-start.11 = (bf16[2,192,768]{2,1,0:T(8,128)(2,1)S(1)}, bf16[2,192,768]{2,1,0:T(8,128)(2,1)S(1)}, u32[]{:S(2)}, u32[]{:S(2)}) collective-permute-start(bf16[2,192,768]{2,1,0:T(8,128)(2,1)S(1)} %pad_maximum_fusion.4.refs_0_), channel_id=1, source_target_pairs={{0,8},{4,12},{8,0},{12,4},{16,24},{20,28},{24,16},{28,20},{1,9},{5... | collective-permute-start | bytes 1769480 | tf_op jit(solution)/shard_map/ppermute | solution.py:939
  45.1 13.3 %collective-permute-start.10 = (bf16[2,256,768]{2,1,0:T(8,128)(2,1)S(1)}, bf16[2,256,768]{2,1,0:T(8,128)(2,1)S(1)}, u32[]{:S(2)}, u32[]{:S(2)}) collective-permute-start(bf16[2,256,768]{2,1,0:T(8,128)(2,1)S(1)} %pad_maximum_fusion.2), channel_id=1, source_target_pairs={{0,1},{1,0},{2,3},{3,2},{4,5},{5,4},{6,7},{7,6},{8,9},{9,8},{10,11... | collective-permute-start | bytes 2359304 | tf_op jit(solution)/shard_map/ppermute | solution.py:935
  45.2 10.0 %collective-permute-start.8 = (bf16[2,104,768]{2,1,0:T(8,128)(2,1)S(1)}, bf16[2,104,768]{2,1,0:T(8,128)(2,1)S(1)}, u32[]{:S(2)}, u32[]{:S(2)}) collective-permute-start(bf16[2,104,768]{2,1,0:T(8,128)(2,1)S(1)} %collective-permute-done.5.refs_1_), channel_id=1, source_target_pairs={{0,4},{4,0},{8,12},{12,8},{16,20},{20,16},{24,28},{28,24},{1,5},{5... | collective-permute-start | bytes 958472 | tf_op jit(solution)/shard_map/ppermute | solution.py:937
  57.4 2.3 %collective-permute-start.14 = (bf16[2,256,768]{2,1,0:T(8,128)(2,1)S(1)}, bf16[2,256,768]{2,1,0:T(8,128)(2,1)S(1)}, u32[]{:S(2)}, u32[]{:S(2)}) collective-permute-start(bf16[2,256,768]{2,1,0:T(8,128)(2,1)S(1)} %pad_maximum_fusion.3), channel_id=1, source_target_pairs={{0,1},{1,0},{2,3},{3,2},{4,5},{5,4},{6,7},{7,6},{8,9},{9,8},{10,11... | collective-permute-start | bytes 2359304 | tf_op jit(solution)/shard_map/ppermute | solution.py:942
  62.2 4.3 %collective-permute-start.15 = (bf16[48,512]{1,0:T(8,128)(2,1)S(1)}, bf16[48,512]{1,0:T(8,128)(2,1)S(1)}, u32[]{:S(2)}, u32[]{:S(2)}) collective-permute-start(bf16[48,512]{1,0:T(8,128)(2,1)S(1)} %get-tuple-element.97), channel_id=1, source_target_pairs={{0,1},{1,0},{2,3},{3,2},{4,5},{5,4},{6,7},{7,6},{8,9},{9,8},{10,11... | collective-permute-start | bytes 147464 | tf_op jit(solution)/shard_map/ppermute | solution.py:485
  62.4 4.5 %collective-permute-start.16 = (bf16[48,512]{1,0:T(8,128)(2,1)S(1)}, bf16[48,512]{1,0:T(8,128)(2,1)S(1)}, u32[]{:S(2)}, u32[]{:S(2)}) collective-permute-start(bf16[48,512]{1,0:T(8,128)(2,1)S(1)} %get-tuple-element.98), channel_id=1, source_target_pairs={{0,2},{1,3},{2,0},{3,1},{4,6},{5,7},{6,4},{7,5},{8,10},{9,11},{10,... | collective-permute-start | bytes 147464 | tf_op jit(solution)/shard_map/ppermute | solution.py:485
  62.8 4.2 %collective-permute-start.17 = (bf16[48,512]{1,0:T(8,128)(2,1)S(1)}, bf16[48,512]{1,0:T(8,128)(2,1)S(1)}, u32[]{:S(2)}, u32[]{:S(2)}) collective-permute-start(bf16[48,512]{1,0:T(8,128)(2,1)S(1)} %get-tuple-element.99), channel_id=1, source_target_pairs={{0,3},{1,2},{2,1},{3,0},{4,7},{5,6},{6,5},{7,4},{8,11},{9,10},{10,... | collective-permute-start | bytes 147464 | tf_op jit(solution)/shard_map/ppermute | solution.py:485
  73.1 2.1 %collective-permute-start.18 = (bf16[48,512]{1,0:T(8,128)(2,1)S(1)}, bf16[48,512]{1,0:T(8,128)(2,1)S(1)}, u32[]{:S(2)}, u32[]{:S(2)}) collective-permute-start(bf16[48,512]{1,0:T(8,128)(2,1)S(1)} %get-tuple-element.101), channel_id=1, source_target_pairs={{0,1},{1,0},{2,3},{3,2},{4,5},{5,4},{6,7},{7,6},{8,9},{9,8},{10,11... | collective-permute-start | bytes 147464 | tf_op jit(solution)/shard_map/ppermute | solution.py:485
  73.5 4.2 %collective-permute-start.19 = (bf16[48,512]{1,0:T(8,128)(2,1)S(1)}, bf16[48,512]{1,0:T(8,128)(2,1)S(1)}, u32[]{:S(2)}, u32[]{:S(2)}) collective-permute-start(bf16[48,512]{1,0:T(8,128)(2,1)S(1)} %get-tuple-element.102), channel_id=1, source_target_pairs={{0,2},{1,3},{2,0},{3,1},{4,6},{5,7},{6,4},{7,5},{8,10},{9,11},{10,... | collective-permute-start | bytes 147464 | tf_op jit(solution)/shard_map/ppermute | solution.py:485
  74.6 3.8 %collective-permute-start.20 = (bf16[48,512]{1,0:T(8,128)(2,1)S(1)}, bf16[48,512]{1,0:T(8,128)(2,1)S(1)}, u32[]{:S(2)}, u32[]{:S(2)}) collective-permute-start(bf16[48,512]{1,0:T(8,128)(2,1)S(1)} %get-tuple-element.103), channel_id=1, source_target_pairs={{0,3},{1,2},{2,1},{3,0},{4,7},{5,6},{6,5},{7,4},{8,11},{9,10},{10,... | collective-permute-start | bytes 147464 | tf_op jit(solution)/shard_map/ppermute | solution.py:485
  91.7 3.5 %collective-permute-start.21 = (bf16[4,128,1536]{2,1,0:T(8,128)(2,1)S(1)}, bf16[4,128,1536]{2,1,0:T(8,128)(2,1)S(1)}, u32[]{:S(2)}, u32[]{:S(2)}) collective-permute-start(bf16[4,128,1536]{2,1,0:T(8,128)(2,1)S(1)} %get-tuple-element.111), channel_id=1, source_target_pairs={{0,1},{1,0},{2,3},{3,2},{4,5},{5,4},{6,7},{7,6},{8,9},{9,8},{10,11... | collective-permute-start | bytes 4718600 | tf_op jit(solution)/shard_map/ppermute | solution.py:1028
  91.9 16.4 %collective-permute-start.24 = (bf16[2,200,768]{2,1,0:T(8,128)(2,1)}, bf16[2,200,768]{2,1,0:T(8,128)(2,1)S(1)}, u32[]{:S(2)}, u32[]{:S(2)}) collective-permute-start(bf16[2,200,768]{2,1,0:T(8,128)(2,1)} %get-tuple-element.113), channel_id=1, source_target_pairs={{0,8},{4,12},{8,0},{12,4},{16,24},{20,28},{24,16},{28,20},{1,9},{5... | collective-permute-start | bytes 1843208 | tf_op jit(solution)/shard_map/ppermute | solution.py:1026
  92.3 20.6 %collective-permute-start.25 = (bf16[4,96,768]{2,1,0:T(8,128)(2,1)}, bf16[4,96,768]{2,1,0:T(8,128)(2,1)S(1)}, u32[]{:S(2)}, u32[]{:S(2)}) collective-permute-start(bf16[4,96,768]{2,1,0:T(8,128)(2,1)} %get-tuple-element.117), channel_id=1, source_target_pairs={{0,4},{4,0},{8,12},{12,8},{16,20},{20,16},{24,28},{28,24},{1,5},{5... | collective-permute-start | bytes 1769480 | tf_op jit(solution)/shard_map/ppermute | solution.py:1027
  95.7 1.6 %copy-start.9 = (f32[4,128,1536]{2,1,0:T(8,128)}, f32[4,128,1536]{2,1,0:T(8,128)S(1)}, u32[]{:S(2)}) copy-start(f32[4,128,1536]{2,1,0:T(8,128)S(1)} %convert_add_fusion) | copy-start | bytes 9437188
  98.3 16.3 %copy-start.1 = (bf16[128,768]{1,0:T(8,128)(2,1)S(1)}, bf16[128,768]{1,0:T(8,128)(2,1)}, u32[]{:S(2)}) copy-start(bf16[128,768]{1,0:T(8,128)(2,1)} %refs_4_.1) | copy-start | bytes 589828
  98.3 29.7 %collective-permute-start.22 = (bf16[2,128,1536]{2,1,0:T(8,128)(2,1)}, bf16[2,128,1536]{2,1,0:T(8,128)(2,1)S(1)}, u32[]{:S(2)}, u32[]{:S(2)}) collective-permute-start(bf16[2,128,1536]{2,1,0:T(8,128)(2,1)} %slice.109), channel_id=1, source_target_pairs={{0,4},{4,0},{8,12},{12,8},{16,20},{20,16},{24,28},{28,24},{1,5},{5... | collective-permute-start | bytes 2359304 | tf_op jit(solution)/shard_map/ppermute | solution.py:1029
  108.4 19.6 %collective-permute-start.28 = (bf16[1,200,768]{2,1,0:T(8,128)(2,1)S(1)}, bf16[1,200,768]{2,1,0:T(8,128)(2,1)S(1)}, u32[]{:S(2)}, u32[]{:S(2)}) collective-permute-start(bf16[1,200,768]{2,1,0:T(8,128)(2,1)S(1)} %get-tuple-element.114.refs_0_), channel_id=1, source_target_pairs={{0,16},{4,20},{8,24},{12,28},{16,0},{20,4},{24,8},{28,12},{1,17},{... | collective-permute-start | bytes 921608 | tf_op jit(solution)/shard_map/ppermute | solution.py:1031
  112.9 17.3 %copy-start.10 = (f32[4,128,1536]{2,1,0:T(8,128)S(1)}, f32[4,128,1536]{2,1,0:T(8,128)}, u32[]{:S(2)}) copy-start(f32[4,128,1536]{2,1,0:T(8,128)} %copy-done.9) | copy-start | bytes 9437188
  113.0 13.9 %collective-permute-start.26 = (bf16[2,96,768]{2,1,0:T(8,128)(2,1)S(1)}, bf16[2,96,768]{2,1,0:T(8,128)(2,1)S(1)}, u32[]{:S(2)}, u32[]{:S(2)}) collective-permute-start(bf16[2,96,768]{2,1,0:T(8,128)(2,1)S(1)} %get-tuple-element.119), channel_id=1, source_target_pairs={{0,8},{4,12},{8,0},{12,4},{16,24},{20,28},{24,16},{28,20},{1,9},{5... | collective-permute-start | bytes 884744 | tf_op jit(solution)/shard_map/ppermute | solution.py:1033
  126.9 7.7 %collective-permute-start.27 = (bf16[1,96,768]{2,1,0:T(8,128)(2,1)S(1)}, bf16[1,96,768]{2,1,0:T(8,128)(2,1)S(1)}, u32[]{:S(2)}, u32[]{:S(2)}) collective-permute-start(bf16[1,96,768]{2,1,0:T(8,128)(2,1)S(1)} %get-tuple-element.120), channel_id=1, source_target_pairs={{0,16},{4,20},{8,24},{12,28},{16,0},{20,4},{24,8},{28,12},{1,17},{... | collective-permute-start | bytes 442376 | tf_op jit(solution)/shard_map/ppermute | solution.py:1035
  128.7 5.9 %collective-permute-start.29 = (bf16[112,384]{1,0:T(8,128)(2,1)S(1)}, bf16[112,384]{1,0:T(8,128)(2,1)S(1)}, u32[]{:S(2)}, u32[]{:S(2)}) collective-permute-start(bf16[112,384]{1,0:T(8,128)(2,1)S(1)} %get-tuple-element.123), channel_id=1, source_target_pairs={{0,4},{4,0},{8,12},{12,8},{16,20},{20,16},{24,28},{28,24},{1,5},{5... | collective-permute-start | bytes 258056 | tf_op jit(solution)/shard_map/ppermute | solution.py:1058
  130.4 6.0 %copy-start.11 = (f32[2,128,1536]{2,1,0:T(8,128)}, f32[2,128,1536]{2,1,0:T(8,128)S(1)}, u32[]{:S(2)}) copy-start(f32[2,128,1536]{2,1,0:T(8,128)S(1)} %slice_add_fusion) | copy-start | bytes 4718596
  130.5 14.8 %collective-permute-start.23 = (bf16[128,1536]{1,0:T(8,128)(2,1)S(1)}, bf16[128,1536]{1,0:T(8,128)(2,1)S(1)}, u32[]{:S(2)}, u32[]{:S(2)}) collective-permute-start(bf16[128,1536]{1,0:T(8,128)(2,1)S(1)} %fusion.17), channel_id=1, source_target_pairs={{0,2},{2,0},{1,3},{3,1},{4,6},{6,4},{5,7},{7,5},{8,10},{10,8},{9,1... | collective-permute-start | bytes 1179656 | tf_op jit(solution)/shard_map/ppermute | solution.py:1038
  135.4 2.3 %collective-permute-start.33 = (bf16[24,576]{1,0:T(8,128)(2,1)S(1)}, bf16[24,576]{1,0:T(8,128)(2,1)S(1)}, u32[]{:S(2)}, u32[]{:S(2)}) collective-permute-start(bf16[24,576]{1,0:T(8,128)(2,1)S(1)} %get-tuple-element.132), channel_id=1, source_target_pairs={{0,1},{1,0},{2,3},{3,2},{4,5},{5,4},{6,7},{7,6},{8,9},{9,8},{10,11... | collective-permute-start | bytes 82952 | tf_op jit(solution)/shard_map/ppermute | solution.py:485
  135.4 6.3 %collective-permute-start.34 = (bf16[24,576]{1,0:T(8,128)(2,1)S(1)}, bf16[24,576]{1,0:T(8,128)(2,1)S(1)}, u32[]{:S(2)}, u32[]{:S(2)}) collective-permute-start(bf16[24,576]{1,0:T(8,128)(2,1)S(1)} %get-tuple-element.133), channel_id=1, source_target_pairs={{0,2},{1,3},{2,0},{3,1},{4,6},{5,7},{6,4},{7,5},{8,10},{9,11},{10,... | collective-permute-start | bytes 82952 | tf_op jit(solution)/shard_map/ppermute | solution.py:485
  136.4 5.2 %collective-permute-start.35 = (bf16[24,576]{1,0:T(8,128)(2,1)S(1)}, bf16[24,576]{1,0:T(8,128)(2,1)S(1)}, u32[]{:S(2)}, u32[]{:S(2)}) collective-permute-start(bf16[24,576]{1,0:T(8,128)(2,1)S(1)} %get-tuple-element.134), channel_id=1, source_target_pairs={{0,3},{1,2},{2,1},{3,0},{4,7},{5,6},{6,5},{7,4},{8,11},{9,10},{10,... | collective-permute-start | bytes 82952 | tf_op jit(solution)/shard_map/ppermute | solution.py:485
  137.3 5.2 %collective-permute-start.30 = (bf16[32,768]{1,0:T(8,128)(2,1)S(1)}, bf16[32,768]{1,0:T(8,128)(2,1)S(1)}, u32[]{:S(2)}, u32[]{:S(2)}) collective-permute-start(bf16[32,768]{1,0:T(8,128)(2,1)S(1)} %get-tuple-element.126), channel_id=1, source_target_pairs={{0,1},{1,0},{2,3},{3,2},{4,5},{5,4},{6,7},{7,6},{8,9},{9,8},{10,11... | collective-permute-start | bytes 147464 | tf_op jit(solution)/shard_map/ppermute | solution.py:485
  137.6 4.8 %collective-permute-start.31 = (bf16[32,768]{1,0:T(8,128)(2,1)S(1)}, bf16[32,768]{1,0:T(8,128)(2,1)S(1)}, u32[]{:S(2)}, u32[]{:S(2)}) collective-permute-start(bf16[32,768]{1,0:T(8,128)(2,1)S(1)} %get-tuple-element.127), channel_id=1, source_target_pairs={{0,2},{1,3},{2,0},{3,1},{4,6},{5,7},{6,4},{7,5},{8,10},{9,11},{10,... | collective-permute-start | bytes 147464 | tf_op jit(solution)/shard_map/ppermute | solution.py:485
  141.6 3.7 %collective-permute-start.32 = (bf16[32,768]{1,0:T(8,128)(2,1)S(1)}, bf16[32,768]{1,0:T(8,128)(2,1)S(1)}, u32[]{:S(2)}, u32[]{:S(2)}) collective-permute-start(bf16[32,768]{1,0:T(8,128)(2,1)S(1)} %get-tuple-element.128), channel_id=1, source_target_pairs={{0,3},{1,2},{2,1},{3,0},{4,7},{5,6},{6,5},{7,4},{8,11},{9,10},{10,... | collective-permute-start | bytes 147464 | tf_op jit(solution)/shard_map/ppermute | solution.py:485
  145.3 4.0 %copy-start.3 = (bf16[128,768]{1,0:T(8,128)(2,1)S(1)}, bf16[128,768]{1,0:T(8,128)(2,1)}, u32[]{:S(2)}) copy-start(bf16[128,768]{1,0:T(8,128)(2,1)} %refs_5_.1) | copy-start | bytes 589828
  146.8 3.4 %copy-start.13 = (f32[24]{0:T(128)}, f32[24]{0:T(128)S(1)}, u32[]{:S(2)}) copy-start(f32[24]{0:T(128)S(1)} %get-tuple-element.203) | copy-start | bytes 292
  (2 other events, 1.3 us)

commit v6 on v5

--- a/solution.py
+++ b/solution.py
@@ -593,41 +593,55 @@
 
 
 def attention_grads_kernel(deep, *refs):
-    r0, r1, r2, r3, dense, dy, attn_in, d_joined, weights, unit, vectors = refs[:11]
-    picks, (attn_out, scaled, sums), (rows_t, grads) = refs[11:13], refs[13:16], refs[16:]
-    me = lax.axis_index("seq")
+    r0, r1, r2, r3, dense, dy, attn_in, d_joined, weights, unit, vectors, own_pair = refs[:12]
+    picks, (give, keep), (rows_t, grads, sums) = refs[12:14], refs[14:16], refs[16:]
+    me = lax.axis_index("seq")
+    core = lax.bitwise_and(me, 1)
     count = r0.shape[0]
     width = dy.shape[1]
     quarter = width // 4
     own = width - quarter
     for j, ref in enumerate((r0, r1, r2, r3)):
         rows_t[pl.ds(pl.multiple_of(lax.bitwise_xor(me, j) * count, 16), count), :] = ref[...]
-    size = 128
-    for c in range(0, width, size):
-        grads[c : c + size, :] = dot_tn(attn_in[:, c : c + size], d_joined[...])
+    attended = jnp.transpose(rows_t[...].astype(F32)).astype(BF)
+    gain = vectors[0:1, :]
+    size = dy.shape[0] // 4
+    sums[...] = jnp.zeros(sums.shape, F32)
+    for i in range(4):
+        rows = slice(i * size, (i + 1) * size)
+        out = dot_nn(attended[rows], dense[...]) + own_pair[i, :, :width].astype(F32)
+        back = dot_nt(d_joined[rows, :], weights[...])
+        sums[0:1, :] += jnp.sum(back * unit[rows, :], axis=0, keepdims=True)
+        sums[1:2, :] += jnp.sum(back, axis=0, keepdims=True)
+        sums[5:6, :] += jnp.sum(d_joined[rows, :].astype(F32), axis=0, keepdims=True)
+        out = out.astype(BF)
+        back = (back * gain + own_pair[i, :, width:].astype(F32)).astype(BF)
+
+        @pl.when(core == i % 2)
+        def _():
+            keep[i // 2, :, :width] = out
+            keep[i // 2, :, width:] = back
+
+        @pl.when(core != i % 2)
+        def _():
+            give[i // 2, :, :width] = out
+            give[i // 2, :, width:] = back
+
+    for c in range(0, width, 128):
+        grads[c : c + 128, :] = dot_tn(attn_in[:, c : c + 128], d_joined[...])
     dense_grad = dot_nn(rows_t[...], dy[...])
     for p in range(8):
         for q in range(4):
             start = p * 4 * deep + q * deep
             grads[start : start + deep, own:] = dense_grad[p * deep : (p + 1) * deep, q * quarter : (q + 1) * quarter]
     per_line = 4 * deep
+    tail = sums[...]
 
     def block_of(index):
-        return grads[pl.ds(pl.multiple_of(index * per_line, per_line), per_line), :].astype(BF)
+        block = grads[pl.ds(pl.multiple_of(index * per_line, per_line), per_line), :]
+        return jnp.concatenate([block, tail], axis=0).astype(BF)
 
     pick_blocks(block_of, *picks)
-    attended = jnp.transpose(rows_t[...].astype(F32)).astype(BF)
-    gain = vectors[0:1, :]
-    tokens = dy.shape[0]
-    sums[...] = jnp.zeros(sums.shape, F32)
-    for c in range(0, tokens, size):
-        rows = slice(c, c + size)
-        attn_out[rows, :] = dot_nn(attended[rows], dense[...])
-        back = dot_nt(d_joined[rows, :], weights[...])
-        scaled[rows, :] = back * gain
-        sums[0:1, :] += jnp.sum(back * unit[rows, :], axis=0, keepdims=True)
-        sums[1:2, :] += jnp.sum(back, axis=0, keepdims=True)
-        sums[5:6, :] += jnp.sum(d_joined[rows, :].astype(F32), axis=0, keepdims=True)
 
 
 def pack_kernel(deep, *refs):
@@ -688,106 +702,119 @@
     attn_piece[rows:, :] = (extra + pltpu.roll(row_block[...], side * half + line * units, 1)).astype(BF)
 
 
+def mlp_tokens(unit, dy, vectors, up, down, mlp_in, act, d_up, sums, side, store):
+    half = up.shape[1]
+    gain, shift = vectors[2:3, :], vectors[3:4, :]
+    bias = jnp.where(side == 0, vectors[7:8, :half], vectors[7:8, half:])
+    sums[...] = jnp.zeros(sums.shape, F32)
+    size = unit.shape[0] // 4
+
+    def step(i, carry):
+        rows = pl.ds(pl.multiple_of(i * size, size), size)
+        u = unit[rows, :]
+        normed = (u * gain + shift).astype(BF)
+        mlp_in[rows, :] = normed
+        upper = dot_nn(normed, up[...]) + bias
+        cdf = 0.5 * (1.0 + lax.erf(upper * 0.7071067811865476))
+        pdf = jnp.exp(-0.5 * upper * upper) * 0.3989422804014327
+        act_rows = (upper * cdf).astype(BF)
+        act[rows, :] = act_rows
+        d_rows = (dot_nt(dy[rows, :], down[...]) * (cdf + upper * pdf)).astype(BF)
+        d_up[rows, :] = d_rows
+        out = dot_nn(act_rows, down[...]).astype(BF)
+        back = dot_nt(d_rows, up[...])
+        sums[2:3, :] += jnp.sum(back * u, axis=0, keepdims=True)
+        sums[3:4, :] += jnp.sum(back, axis=0, keepdims=True)
+        sums[6:7, :half] += jnp.sum(d_rows.astype(F32), axis=0, keepdims=True)
+        store(i, out, (back * gain).astype(BF))
+        return carry
+
+    lax.fori_loop(0, 4, step, 0)
+
+
 def mlp_kernel(*refs):
-    pieces, (unit_own, unit_other, dy_own, dy_other, vectors, attn_out, scaled, sums_in) = refs[:2], refs[2:10]
-    give, keep, keep_terms, send_terms, up, down, mlp_in, act, d_up, sums, up_grad, down_grad, done = refs[10:]
+    pieces, (unit, dy, vectors) = refs[:4], refs[4:7]
+    give, keep, mlp_in, act, d_up, sums, up, down, done = refs[7:]
     line, side = line_and_side()
     width, half = up.shape
     units = half // 4
     copies = []
     for place, step in enumerate(LINE_ORDER):
-        piece = pieces[place // 2].at[place % 2]
+        low, high = [pieces[k + place // 2].at[place % 2] for k in (0, 2)]
         l = lax.bitwise_xor(line, step)
-        top, low = pl.ds(0, units), pl.ds(units, units)
         for source, target in (
-            (piece.at[top, :], down.at[pl.ds(pl.multiple_of(l * units, 32), units), :]),
-            (piece.at[low, pl.ds(0, half)], up.at[pl.ds(pl.multiple_of(2 * l * units, 32), units), :]),
-            (piece.at[low, pl.ds(half, half)], up.at[pl.ds(pl.multiple_of((2 * l + 1) * units, 32), units), :]),
+            (low, down.at[pl.ds(pl.multiple_of(l * units, 32), units), :]),
+            (high.at[:, pl.ds(0, half)], up.at[pl.ds(pl.multiple_of(2 * l * units, 32), units), :]),
+            (high.at[:, pl.ds(half, half)], up.at[pl.ds(pl.multiple_of((2 * l + 1) * units, 32), units), :]),
         ):
             copies.append(pltpu.make_async_copy(source, target, done.at[len(copies)]))
     for copy in copies:
         copy.start()
-    gain, shift = vectors[2:3, :], vectors[3:4, :]
-    bias = jnp.where(side == 0, vectors[7:8, :half], vectors[7:8, half:])
-    sums[...] = sums_in[...]
-    group = unit_own.shape[0]
-    size = group // 4
     core = lax.bitwise_and(lax.axis_index("seq"), 1)
     for copy in copies:
         copy.wait()
 
-    def tokens(unit, dy, offset, own):
-        def step(i, carry):
-            rows = pl.ds(pl.multiple_of(i * size, size), size)
-            all_rows = pl.ds(pl.multiple_of(offset + i * size, size), size)
-            u = unit[rows, :]
-            normed = (u * gain + shift).astype(BF)
-            mlp_in[all_rows, :] = normed
-            upper = dot_nn(normed, up[...]) + bias
-            cdf = 0.5 * (1.0 + lax.erf(upper * 0.7071067811865476))
-            pdf = jnp.exp(-0.5 * upper * upper) * 0.3989422804014327
-            act_rows = (upper * cdf).astype(BF)
-            act[all_rows, :] = act_rows
-            g = dy[rows, :]
-            d_rows = (dot_nt(g, down[...]) * (cdf + upper * pdf)).astype(BF)
-            d_up[all_rows, :] = d_rows
-            out = dot_nn(act_rows, down[...])
-            back = dot_nt(d_rows, up[...])
-            sums[2:3, :] += jnp.sum(back * u, axis=0, keepdims=True)
-            sums[3:4, :] += jnp.sum(back, axis=0, keepdims=True)
-            sums[6:7, :half] += jnp.sum(d_rows.astype(F32), axis=0, keepdims=True)
-            back = back * gain
-            if own:
-                out = out + attn_out[rows, :]
-                back = back + scaled[rows, :]
-                sums[4:5, :] += 0.25 * jnp.sum(g.astype(F32), axis=0, keepdims=True)
-            place = (0 if own else 2) + lax.shift_right_logical(i, 1)
-            out, back = out.astype(BF), back.astype(BF)
-
-            @pl.when(lax.bitwise_and(i, 1) == core)
-            def _():
-                keep[place, :, :width] = out
-                keep[place, :, width:] = back
-
-            @pl.when(lax.bitwise_and(i, 1) != core)
-            def _():
-                give[place, :, :width] = out
-                give[place, :, width:] = back
-
-            return carry
-
-        lax.fori_loop(0, 4, step, 0)
-
-    tokens(unit_own, dy_own, 0, True)
-    tokens(unit_other, dy_other, group, False)
+    def store(i, out, back):
+        place = lax.shift_right_logical(i, 1)
+
+        @pl.when(lax.bitwise_and(i, 1) == core)
+        def _():
+            keep[place, :, :width] = out
+            keep[place, :, width:] = back
+
+        @pl.when(lax.bitwise_and(i, 1) != core)
+        def _():
+            give[place, :, :width] = out
+            give[place, :, width:] = back
+
+    mlp_tokens(unit, dy, vectors, up, down, mlp_in, act, d_up, sums, side, store)
+
+
+def mlp_own_kernel(unit, dy, vectors, up, down, own_pair, mlp_in, act, d_up, sums):
+    _, side = line_and_side()
+    width = up.shape[0]
+
+    def store(i, out, back):
+        own_pair[i, :, :width] = out
+        own_pair[i, :, width:] = back
+
+    mlp_tokens(unit, dy, vectors, up, down, mlp_in, act, d_up, sums, side, store)
+    sums[4:5, :] = 0.25 * jnp.sum(dy[...].astype(F32), axis=0, keepdims=True)
+
+
+def mlp_grads_kernel(*refs):
+    own, other = refs[:5], refs[5:10]
+    keep_up, send_up, keep_down, send_down, up_grad, down_grad = refs[10:]
+    line, _ = line_and_side()
+    half, width = down_grad.shape
+    units = half // 4
     for c in range(0, width, 128):
-        up_grad[c : c + 128, :] = dot_tn(mlp_in[:, c : c + 128], d_up[...]).astype(BF)
+        total = sum(dot_tn(mlp_in[:, c : c + 128], d_up[...]) for mlp_in, _, d_up, _, _ in (own, other))
+        up_grad[c : c + 128, :] = total.astype(BF)
     for c in range(0, half, 128):
-        total = dot_tn(act[:group, c : c + 128], dy_own[...]) + dot_tn(act[group:, c : c + 128], dy_other[...])
+        total = sum(dot_tn(act[:, c : c + 128], dy[...]) for _, act, _, dy, _ in (own, other))
         down_grad[c : c + 128, :] = total.astype(BF)
-    tail = sums[...].astype(BF)
+    tail = (own[4][...] + other[4][...]).astype(BF)
     for place, step in enumerate(LINE_ORDER):
-        ref = (keep_terms, send_terms)[place // 2].at[place % 2]
+        ups, downs = ((keep_up, keep_down), (send_up, send_down))[place // 2]
         l = lax.bitwise_xor(line, step)
-        ref[:units, :] = down_grad[pl.ds(pl.multiple_of(l * units, 32), units), :]
-        ref[units : 2 * units, :half] = up_grad[pl.ds(pl.multiple_of(2 * l * units, 32), units), :]
-        ref[units : 2 * units, half:] = up_grad[pl.ds(pl.multiple_of((2 * l + 1) * units, 32), units), :]
-        ref[2 * units :, :] = tail
-
-
-def mlp_sum_kernel(own, far, down_own, up_keep, up_give, tail):
-    units, width = down_own.shape
-    half = width // 2
+        downs[place % 2] = down_grad[pl.ds(pl.multiple_of(l * units, 32), units), :]
+        ref = ups.at[place % 2]
+        ref[:units, :half] = up_grad[pl.ds(pl.multiple_of(2 * l * units, 32), units), :]
+        ref[:units, half:] = up_grad[pl.ds(pl.multiple_of((2 * l + 1) * units, 32), units), :]
+        ref[units:, :] = tail
+
+
+def up_sum_kernel(own, far, up_keep, up_give, tail):
+    units, half = up_keep.shape
+    width = 2 * half
     _, side = line_and_side()
-    refs = (own.at[0], far.at[0])
 
     def total(rows, lanes):
-        return sum(ref[rows, lanes].astype(F32) for ref in refs)
-
-    down_own[...] = total(slice(0, units), slice(None))
-    first = total(slice(units, 2 * units), slice(0, half))
-    second = total(slice(units, 2 * units), slice(half, width))
-    last = total(slice(2 * units, 2 * units + 8), slice(None))
+        return own[0, rows, lanes].astype(F32) + far[0, rows, lanes].astype(F32)
+
+    first, second = total(slice(0, units), slice(0, half)), total(slice(0, units), slice(half, width))
+    last = total(slice(units, units + 8), slice(None))
     tail[...] = last
     up_keep[...] = jnp.where(side == 0, first, second).astype(BF)
     up_give[:units, :] = jnp.where(side == 0, second, first).astype(BF)
@@ -809,12 +836,12 @@
         ref[...] = jnp.concatenate([block, last], axis=0).astype(BF)
 
 
-def owned_kernel(deep, b0, b1, b2, b3, tail, up_own, vec_own, sources, row_block):
+def owned_kernel(deep, b0, b1, b2, b3, tail, up_own, vec_own, sources):
     line, _ = line_and_side()
     me = lax.axis_index("seq")
     device = 4 * lax.axis_index("dp") + me
     width = tail.shape[1]
-    half, own = width // 2, width // 4
+    half = width // 2
     units = half // 4
     for j, ref in enumerate((b0, b1, b2, b3)):
         sources[lax.bitwise_xor(me, j)] = ref[...].astype(F32)
@@ -826,14 +853,6 @@
     total = sources[0, deep:] + sources[1, deep:] + sources[2, deep:] + sources[3, deep:]
     rolled = pltpu.roll(total, width - device * deep, 1)
     vec_own[...] = rolled[:, :128]
-    row_block[...] = jnp.zeros(row_block.shape, F32)
-    for t in range(4):
-        row = sources[t, deep + 5 : deep + 6, :]
-        for part in range(3):
-            place = part * width + t * own
-            row_block[5:6, place : place + own] = row[:, part * own : (part + 1) * own]
-    rolled = pltpu.roll(row_block[...], 3 * width - device * (3 * deep), 1)
-    vec_own[5:6, :] = rolled[5:6, :128]
     rolled = pltpu.roll(tail[...], width - line * units, 1)
     vec_own[6:7, :] = rolled[6:7, :128]
 
@@ -842,23 +861,32 @@
     me = lax.axis_index("seq")
     total[...] = own[0].astype(F32) + far[0].astype(F32)
     quarter = total.shape[1] // 4
+    last = total[4 * deep :, :]
     for q in range(4):
         dense_own[:, q * quarter : (q + 1) * quarter] = total[q * deep : (q + 1) * deep, 3 * quarter :]
     for j, ref in enumerate((b0, b1, b2, b3)):
         target = lax.bitwise_xor(me, j)
-        ref[...] = total[pl.ds(pl.multiple_of(target * deep, 8), deep), : 3 * quarter].astype(BF)
-
-
-def attention_owned_kernel(b0, b1, b2, b3, qkv_own, sources):
-    me = lax.axis_index("seq")
-    width = qkv_own.shape[1] // 3
+        block = total[pl.ds(pl.multiple_of(target * deep, 8), deep), :]
+        ref[...] = jnp.concatenate([block, last], axis=0).astype(BF)
+
+
+def attention_owned_kernel(deep, b0, b1, b2, b3, qkv_own, vec_own, sources, row_block):
+    me = lax.axis_index("seq")
+    device = 4 * lax.axis_index("dp") + me
+    width = b0.shape[1]
     own = width // 4
     for j, ref in enumerate((b0, b1, b2, b3)):
         sources[lax.bitwise_xor(me, j)] = ref[...].astype(F32)
+    total = sources[0, deep:] + sources[1, deep:] + sources[2, deep:] + sources[3, deep:]
+    vec_own[...] = pltpu.roll(total, width - device * deep, 1)[:, :128]
+    row_block[...] = jnp.zeros(row_block.shape, F32)
     for part in range(3):
         lanes = slice(part * own, (part + 1) * own)
         whole = jnp.concatenate([sources[t, :, lanes] for t in range(4)], axis=1)
-        qkv_own[:, part * width : (part + 1) * width] = whole
+        qkv_own[:, part * width : (part + 1) * width] = whole[:deep]
+        row_block[5:6, part * width : (part + 1) * width] = whole[deep + 5 : deep + 6]
+    rolled = pltpu.roll(row_block[...], 3 * width - device * (3 * deep), 1)
+    vec_own[5:6, :] = rolled[5:6, :128]
 
 
 def with_waits(count, body):
@@ -919,6 +947,10 @@
     )
 
     across = lax.ppermute(mine, "dp", SIDE_SWAP)
+    down_half = lax.ppermute(down_weight, "dp", HALF_SWAP)
+    attn_piece, up_keep, up_give = once(attn_piece, down_half), up_keep, once(up_give, down_half)
+    down_two = jnp.stack([down_weight, down_half])
+    down_pair = lax.ppermute(down_two, "dp", PAIR_SWAP)
     attn_half = lax.ppermute(attn_piece, "dp", HALF_SWAP)
     up_far = lax.ppermute(up_give, "dp", SIDE_SWAP)
     chip_far = lax.ppermute(once(mine, up_keep), "seq", CHIP_SWAP)
@@ -929,24 +961,21 @@
     up_both = jnp.concatenate(
         [jnp.where(side == 0, up_keep, up_far), jnp.where(side == 0, up_far, up_keep)], axis=1
     )
-    mlp_piece = once(jnp.concatenate([down_weight, up_both], axis=0), attn_half)
+    mlp_piece = once(up_both, attn_half)
     mlp_half = lax.ppermute(mlp_piece, "dp", HALF_SWAP)
     by_chip = once(in_order(chip == 1, mine, chip_far), attn_half, up_far)
     core_far = lax.ppermute(by_chip, "seq", CORE_SWAP)
 
     attn_far = lax.ppermute(once(attn_pair, mlp_half), "dp", SIDE_SWAP)
-    mlp_two = once(jnp.stack([mlp_piece, mlp_half]), attn_pair)
+    mlp_two = once(jnp.stack([mlp_piece, mlp_half]), attn_pair, down_pair)
     mlp_pair = lax.ppermute(mlp_two, "dp", PAIR_SWAP)
     chip_beyond = lax.ppermute(once(across, mlp_half, attn_pair, attn_side), "seq", CHIP_SWAP)
-    by_chip_beyond = once(in_order(chip == 1, across, chip_beyond), mlp_pair, attn_far)
-    core_beyond = lax.ppermute(by_chip_beyond, "seq", CORE_SWAP)
 
     def whole_group(values, over):
         full = in_order(core == 1, values, over, axis=1).reshape(n_seq, 2, rows, width)
         return full[:, 0].reshape(flat), full[:, 1].reshape(flat)
 
     hidden_group, dy = whole_group(by_chip, core_far)
-    hidden_other, dy_other = whole_group(by_chip_beyond, core_beyond)
     attn_pieces = (attn_two, attn_pair, attn_side, attn_far)
 
     row_lengths = lengths[0]
@@ -965,16 +994,20 @@
         return centered * inverse, inverse
 
     unit = normed(hidden_group.astype(F32))[0]
-    unit_other = normed(hidden_other.astype(F32))[0]
 
     placed = kernel_call(
-        functools.partial(place_kernel, deep),
+        with_waits(1, functools.partial(place_kernel, deep)),
         ((flat[1:] * 2, BF), ((n_dp * deep, width), BF), ((8, width), F32)) + (((2 * deep, group), BF),) * 4,
-        attn_pieces + (dy,),
+        (mlp_pair,) + attn_pieces + (dy,),
         scratch=(((n_dp * deep, width), F32), ((n_dp * deep, group), BF)),
         flops=2 * n_dp * deep * width * group,
+        apart=1,
     )
     weights, dense, vectors = placed[:3]
+    by_chip_beyond = once(in_order(chip == 1, across, chip_beyond), weights)
+    core_beyond = lax.ppermute(by_chip_beyond, "seq", CORE_SWAP)
+    hidden_other, dy_other = whole_group(by_chip_beyond, core_beyond)
+    unit_other = normed(hidden_other.astype(F32))[0]
     d_blocks = seq_shuffle(placed[3:])
     attn_in, qk, v = kernel_call(
         project_kernel,
@@ -982,59 +1015,72 @@
         (unit, weights, vectors, cosine, sine_a, sine_b),
         flops=2 * group * width * width,
     )
+    held_shapes = ((flat, BF), ((group, half), BF), ((group, half), BF))
+    give, keep, *held_other, up_full, down_full = kernel_call(
+        mlp_kernel,
+        (((2, rows, 2 * width), BF),) * 2 + held_shapes + (((8, width), F32), ((width, half), BF), ((half, width), BF)),
+        (down_two, down_pair, mlp_two, mlp_pair, unit_other, dy_other, vectors),
+        scratch=(pltpu.SemaphoreType.DMA((12,)),),
+        flops=4 * group * width * 2 * half,
+        megabytes=16,
+        apart=4,
+    )
     attended = kernel_call(
         with_waits(1, functools.partial(attention_kernel, deep)),
         (((2 * deep, group), BF),) * 4 + ((flat, BF),),
-        (mlp_pair, qk, v, *d_blocks, segment[:, None], segment[None, :], cosine, sine_a, sine_b),
+        (held_other[2], qk, v, *d_blocks, segment[:, None], segment[None, :], cosine, sine_a, sine_b),
         scratch=(((own, group), F32),) * 4 + ((flat, F32),),
         flops=14 * group * group * own,
+        megabytes=16,
         apart=1,
     )
     d_joined = attended[4]
     row_blocks = seq_shuffle(attended[:4])
-    results = kernel_call(
-        with_waits(1, functools.partial(attention_grads_kernel, deep)),
-        (((4, per_line, width), BF),) * 2 + ((flat, F32), (flat, F32), ((8, width), F32)),
-        (core_beyond, *row_blocks, dense, dy, attn_in, d_joined, weights, unit, vectors),
-        scratch=(((n_dp * deep, group), BF), ((width, width), F32)),
+
+    own_pair, *held_own = kernel_call(
+        with_waits(1, mlp_own_kernel),
+        (((4, rows, 2 * width), BF),) + held_shapes + (((8, width), F32),),
+        (d_joined, unit, dy, vectors, up_full, down_full),
+        flops=4 * group * width * 2 * half,
+        megabytes=16,
+        apart=1,
+    )
+    attn_send, attn_keep, own_give, own_keep = kernel_call(
+        functools.partial(attention_grads_kernel, deep),
+        (((4, per_line + 8, width), BF),) * 2 + (((2, rows, 2 * width), BF),) * 2,
+        (*row_blocks, dense, dy, attn_in, d_joined, weights, unit, vectors, own_pair),
+        scratch=(((n_dp * deep, group), BF), ((width, width), F32), ((8, width), F32)),
         flops=5 * group * width * width,
-        megabytes=32,
+        megabytes=16,
+    )
+    up_shape, down_shape = ((2, units + 8, width), BF), ((2, units, width), BF)
+    keep_up, send_up, keep_down, send_down = kernel_call(
+        with_waits(1, mlp_grads_kernel),
+        (up_shape, up_shape, down_shape, down_shape),
+        (attn_send, *held_own[:3], dy, held_own[3], *held_other[:3], dy_other, held_other[3]),
+        scratch=(((width, half), BF), ((half, width), BF)),
+        flops=4 * group * width * 2 * half,
+        megabytes=16,
         apart=1,
     )
-    attn_send, attn_keep = results[:2]
-
-    give, keep, *results = kernel_call(
-        mlp_kernel,
-        (((4, rows, 2 * width), BF),) * 2 + (((2, 2 * units + 8, width), BF),) * 2,
-        (mlp_two, mlp_pair, unit, unit_other, dy, dy_other, vectors) + tuple(results[2:]),
-        scratch=(
-            ((width, half), BF),
-            ((half, width), BF),
-            ((2 * group, width), BF),
-            ((2 * group, half), BF),
-            ((2 * group, half), BF),
-            ((8, width), F32),
-            ((width, half), BF),
-            ((half, width), BF),
-            pltpu.SemaphoreType.DMA((12,)),
-        ),
-        flops=12 * group * width * 2 * half,
-        megabytes=32,
-        apart=2,
-    )
-    keep_terms, send_terms = results
-    mlp_got = lax.ppermute(send_terms, "dp", PAIR_SWAP)
-    attn_moved = lax.ppermute(once(attn_send, keep_terms), "dp", SIDE_SWAP)
-    both = keep.astype(F32) + lax.ppermute(give, "seq", CORE_SWAP).astype(F32)
-    beyond = lax.ppermute(both[2:].astype(BF), "dp", SIDE_SWAP)
-    mlp_mine, mlp_send = add_blocks(keep_terms, mlp_got, 1, 1)
-    mlp_last = lax.ppermute(mlp_send, "dp", HALF_SWAP)
-    attn_mine, attn_send = add_blocks(attn_keep, attn_moved, 2, 2, waits=(mlp_got,))
-    attn_got = lax.ppermute(attn_send, "dp", PAIR_SWAP)
-    attn_mine, attn_send = add_blocks(attn_mine, attn_got, 1, 1, waits=(mlp_send,))
+
+    attn_moved = lax.ppermute(attn_send, "dp", SIDE_SWAP)
+    up_got = lax.ppermute(send_up, "dp", PAIR_SWAP)
+    down_got = lax.ppermute(send_down, "dp", PAIR_SWAP)
+    both = keep.astype(F32) + lax.ppermute(once(give, keep_up), "seq", CORE_SWAP).astype(F32)
+    both = both.astype(BF)
+    first = (attn_moved, up_got, down_got, both)
+    up_mine, up_send = add_blocks(keep_up, up_got, 1, 1)
+    up_last = lax.ppermute(once(up_send, *first), "dp", HALF_SWAP)
+    attn_mine, attn_send = add_blocks(attn_keep, attn_moved, 2, 2)
+    attn_got = lax.ppermute(once(attn_send, *first), "dp", PAIR_SWAP)
+    down_mine, down_send = add_blocks(keep_down, down_got, 1, 1)
+    down_last = lax.ppermute(once(down_send, *first), "dp", HALF_SWAP)
+    beyond = lax.ppermute(once(both, *first), "dp", SIDE_SWAP)
+    attn_mine, attn_send = add_blocks(attn_mine, attn_got, 1, 1, waits=(up_last,))
     attn_last = lax.ppermute(attn_send, "dp", HALF_SWAP)
 
-    both = both[:2] + beyond.astype(F32)
+    both = own_keep.astype(F32) + lax.ppermute(own_give, "seq", CORE_SWAP).astype(F32) + beyond.astype(F32)
     chip_last = lax.ppermute(pick(both, 1 - chip).astype(BF), "seq", CHIP_SWAP)
     pair = pick(both, chip) + chip_last.astype(F32)
     x = hidden_in.astype(F32)
@@ -1048,52 +1094,55 @@
     )
     grad_in = grad_out.astype(F32) + inverse * inner
 
-    down_own, up_keep, up_give, tail = kernel_call(
-        with_waits(1, mlp_sum_kernel),
-        (((units, width), F32), ((per_line, half), BF), ((per_line + 16, half), BF), ((8, width), F32)),
-        (beyond, mlp_mine, mlp_last),
+    up_keep, up_give, tail = kernel_call(
+        with_waits(1, up_sum_kernel),
+        (((per_line, half), BF), ((per_line + 16, half), BF), ((8, width), F32)),
+        (attn_got, up_mine, up_last),
         megabytes=8,
         apart=1,
     )
+    down_own = down_mine[0].astype(F32) + down_last[0].astype(F32)
     up_far = lax.ppermute(up_give, "dp", SIDE_SWAP)
     blocks = kernel_call(
-        functools.partial(owners_kernel, deep),
+        with_waits(1, functools.partial(owners_kernel, deep)),
         (((deep + 8, width), BF),) * 4,
-        (up_keep, up_far, tail),
+        (attn_last, up_keep, up_far, tail),
         scratch=(((per_line, width), F32),),
         megabytes=8,
+        apart=1,
     )
     up_own, vec_own = kernel_call(
         with_waits(2, functools.partial(owned_kernel, deep)),
         (((deep, hidden_units), F32), ((8, 128), F32)),
         (chip_last, attn_last, *seq_shuffle(blocks), tail),
+        scratch=(((4, deep + 8, width), F32),),
+        megabytes=8,
+        apart=2,
+    )
+    *blocks, dense_own = kernel_call(
+        with_waits(1, functools.partial(attention_sum_kernel, deep)),
+        (((deep + 8, width), BF),) * 4 + (((deep, width), F32),),
+        (up_far, attn_mine, attn_last),
+        scratch=(((per_line + 8, width), F32),),
+        megabytes=8,
+        apart=1,
+    )
+    qkv_own, vec_attn = kernel_call(
+        with_waits(1, functools.partial(attention_owned_kernel, deep)),
+        (((deep, 3 * width), F32), ((8, 128), F32)),
+        (chip_last, *seq_shuffle(blocks)),
         scratch=(((4, deep + 8, width), F32), ((8, 3 * width), F32)),
         megabytes=8,
-        apart=2,
-    )
-    *blocks, dense_own = kernel_call(
-        with_waits(1, functools.partial(attention_sum_kernel, deep)),
-        (((deep, 3 * own), BF),) * 4 + (((deep, width), F32),),
-        (up_far, attn_mine, attn_last),
-        scratch=(((per_line, width), F32),),
-        megabytes=8,
         apart=1,
     )
-    (qkv_own,) = kernel_call(
-        attention_owned_kernel,
-        (((deep, 3 * width), F32),),
-        tuple(seq_shuffle(blocks)),
-        scratch=(((4, deep, 3 * own), F32),),
-        megabytes=8,
-    )
     by_width = vec_own[:5, :deep]
-    qkv_bias_grad = vec_own[5, : 3 * deep]
+    qkv_bias_grad = vec_attn[5, : 3 * deep]
     up_bias_grad = vec_own[6, :units]
     return (
         block_out.astype(BF),
         grad_in.astype(BF),
-        by_width[0],
-        by_width[1],
+        vec_attn[0, :deep],
+        vec_attn[1, :deep],
         by_width[2],
         by_width[3],
         qkv_own,

time: 151 us -> 147 us (0.974)
  starting transfers between devices: 38.8 us -> 35 us
  waiting for transfers between devices: 65 us -> 61.5 us
  Pallas kernels: 25.8 us -> 28 us
  other arithmetic: 8.46 us -> 10.4 us
    ppermute x15, waiting for transfers between devices: 14 us -> 3.02 us  [seq_shuffle(): got.append(lax.ppermute(blocks[other], 'seq', pairs))]
    ppermute x6 -> x11, waiting for transfers between devices: 21.9 us -> 32 us  [the longest x1 6.76 us: line_device(): down_got = lax.ppermute(send_down, 'dp', PAIR_SWAP)]
    ppermute x2, waiting for transfers between devices: 0.01 us -> 5.41 us  [line_device(): up_far = lax.ppermute(up_give, 'dp', SIDE_SWAP)]
    ppermute x1, waiting for transfers between devices: 4.99 us -> 0.37 us  [line_device(): lax.ppermute(once(across, mlp_half, attn_pair, attn_side), 'seq', CHIP_SWAP)]
    ppermute x1, starting transfers between devices: 4.17 us -> 0.07 us  [line_device(): attn_pair = lax.ppermute(attn_two, 'dp', PAIR_SWAP)]
    ppermute x6 -> x11, starting transfers between devices: 9.78 us -> 12.6 us  [the longest x1 2.82 us: line_device(): down_half = lax.ppermute(down_weight, 'dp', HALF_SWAP)]
    ppermute x1, waiting for transfers between devices: 2.82 us -> 0.01 us  [line_device(): attn_last = lax.ppermute(attn_send, 'dp', HALF_SWAP)]
    ppermute x1, starting transfers between devices: 2.65 us -> 0.01 us  [line_device(): attn_half = lax.ppermute(attn_piece, 'dp', HALF_SWAP)]
  transfers between devices with their start and end apart: 36 -> 41, of which waited for: 18 -> 19; matrix products, arithmetic and copies ran while one was open for 4% -> 7% of each run, Pallas kernels for 3% -> 9%
where the time goes in v6:
time: 147 us
  waiting for transfers between devices  61.5 us (42%)
  starting transfers between devices  35 us (24%)
  Pallas kernels  28 us (19%)
  local copies, waits for them, and re-layouts  10.7 us (7%)
  other arithmetic  10.4 us (7%)
    pallas_call x18, Pallas kernels, kernel_call(): pl.pallas_call(body, out_shape=tuple((jax.ShapeDtypeStruct(shape, kind) f...  28 us
    ppermute x15, starting transfers between devices, seq_shuffle(): got.append(lax.ppermute(blocks[other], 'seq', pairs))  11 us
    unnamed x27, local copies, waits for them, and re-layouts  7.44 us
    ppermute x1, waiting for transfers between devices, line_device(): attn_half = lax.ppermute(attn_piece, 'dp', HALF_SWAP)  7.42 us
    ppermute x1, waiting for transfers between devices, line_device(): down_got = lax.ppermute(send_down, 'dp', PAIR_SWAP)  6.76 us
    ppermute x1, waiting for transfers between devices, line_device(): mlp_half = lax.ppermute(mlp_piece, 'dp', HALF_SWAP)  6.51 us
    ppermute x1, waiting for transfers between devices, line_device(): up_got = lax.ppermute(send_up, 'dp', PAIR_SWAP)  5.66 us
    ppermute x1, waiting for transfers between devices, line_device(): down_pair = lax.ppermute(down_two, 'dp', PAIR_SWAP)  5.52 us
  transfers between devices with their start and end apart: 41, of which 19 were waited for; matrix products, arithmetic and copies ran while one was open for 7% of the time, Pallas kernels for 9%

profile of v6, /device:TPU:0, one launch (start us, length us, event | category | flops | bytes accessed | tf_op | source)
XLA Modules:
  0.0 146.8 jit_solution(11421755230540947548)
XLA Ops:
  1.4 0.9 copy-done
  2.3 0.9 copy-done.2
  3.3 0.9 copy-done.4
  4.2 0.9 copy-done.5
  6.5 2.6 %collective-permute-start.1 = (bf16[56,768]{1,0:T(8,128)(2,1)S(1)}, bf16[56,768]{1,0:T(8,128)(2,1)S(1)}, u32[]{:S(2)}, u32[]{:S(2)}) collective-permute-start(bf16[56,768]{1,0:T(8,128)(2,1)S(1)} %get-tuple-element.99), channel_id=1, source_target_pairs={{0,2},{1,3},{2,0},{3,1},{4,6},{5,7},{6,4},{7,5},{8,10},{9,11},{10,... | collective-permute-start | bytes 258056 | tf_op jit(solution)/shard_map/ppermute | solution.py:485
  9.1 2.8 %collective-permute-start.3 = (bf16[96,768]{1,0:T(8,128)(2,1)}, bf16[96,768]{1,0:T(8,128)(2,1)S(1)}, u32[]{:S(2)}, u32[]{:S(2)}) collective-permute-start(bf16[96,768]{1,0:T(8,128)(2,1)} %param.28), channel_id=1, source_target_pairs={{0,16},{4,20},{8,24},{12,28},{16,0},{20,4},{24,8},{28,12},{1,17},{... | collective-permute-start | bytes 442376 | tf_op jit(solution)/shard_map/ppermute | solution.py:950
  12.0 1.5 %collective-permute-start.14 = (bf16[256,768]{1,0:T(8,128)(2,1)S(1)}, bf16[256,768]{1,0:T(8,128)(2,1)S(1)}, u32[]{:S(2)}, u32[]{:S(2)}) collective-permute-start(bf16[256,768]{1,0:T(8,128)(2,1)S(1)} %get-tuple-element.111), channel_id=1, source_target_pairs={{0,4},{4,0},{8,12},{12,8},{16,20},{20,16},{24,28},{28,24},{1,5},{5... | collective-permute-start | bytes 1179656 | tf_op jit(solution)/shard_map/ppermute | solution.py:949
  16.9 2.8 %collective-permute-done.3 = bf16[96,768]{1,0:T(8,128)(2,1)S(1)} collective-permute-done((bf16[96,768]{1,0:T(8,128)(2,1)}, bf16[96,768]{1,0:T(8,128)(2,1)S(1)}, u32[]{:S(2)}, u32[]{:S(2)}) %collective-permute-start.3) | collective-permute-done | bytes 147488 | tf_op jit(solution)/shard_map/ppermute | solution.py:950
  19.7 1.6 %collective-permute-start.4 = (bf16[96,384]{1,0:T(8,128)(2,1)S(1)}, bf16[96,384]{1,0:T(8,128)(2,1)S(1)}, u32[]{:S(2)}, u32[]{:S(2)}) collective-permute-start(bf16[96,384]{1,0:T(8,128)(2,1)S(1)} %get-tuple-element.103), channel_id=1, source_target_pairs={{0,4},{4,0},{8,12},{12,8},{16,20},{20,16},{24,28},{28,24},{1,5},{5... | collective-permute-start | bytes 221192 | tf_op jit(solution)/shard_map/ppermute | solution.py:955
  21.3 1.5 %collective-permute-start.12 = (bf16[256,768]{1,0:T(8,128)(2,1)S(1)}, bf16[256,768]{1,0:T(8,128)(2,1)S(1)}, u32[]{:S(2)}, u32[]{:S(2)}) collective-permute-start(bf16[256,768]{1,0:T(8,128)(2,1)S(1)} %get-tuple-element.111), channel_id=1, source_target_pairs={{0,2},{2,0},{1,3},{3,1},{4,6},{6,4},{5,7},{7,5},{8,10},{10,8},{9,1... | collective-permute-start | bytes 1179656 | tf_op jit(solution)/shard_map/ppermute | solution.py:956
  22.8 1.9 %collective-permute-done.4 = bf16[96,384]{1,0:T(8,128)(2,1)S(1)} collective-permute-done((bf16[96,384]{1,0:T(8,128)(2,1)S(1)}, bf16[96,384]{1,0:T(8,128)(2,1)S(1)}, u32[]{:S(2)}, u32[]{:S(2)}) %collective-permute-start.4) | collective-permute-done | bytes 73760 | tf_op jit(solution)/shard_map/ppermute | solution.py:955
  24.7 7.4 %collective-permute-done.5 = bf16[104,768]{1,0:T(8,128)(2,1)S(1)} collective-permute-done((bf16[104,768]{1,0:T(8,128)(2,1)S(1)}, bf16[104,768]{1,0:T(8,128)(2,1)S(1)}, u32[]{:S(2)}, u32[]{:S(2)}) %collective-permute-start.5) | collective-permute-done | bytes 159776 | tf_op jit(solution)/shard_map/ppermute | solution.py:954
  32.8 1.7 %collective-permute-start.6 = (bf16[96,768]{1,0:T(8,128)(2,1)S(1)}, bf16[96,768]{1,0:T(8,128)(2,1)S(1)}, u32[]{:S(2)}, u32[]{:S(2)}) collective-permute-start(bf16[96,768]{1,0:T(8,128)(2,1)S(1)} %pad_maximum_fusion.7), channel_id=1, source_target_pairs={{0,16},{4,20},{8,24},{12,28},{16,0},{20,4},{24,8},{28,12},{1,17},{... | collective-permute-start | bytes 442376 | tf_op jit(solution)/shard_map/ppermute | solution.py:965
  34.7 6.5 %collective-permute-done.6 = bf16[96,768]{1,0:T(8,128)(2,1)S(1)} collective-permute-done((bf16[96,768]{1,0:T(8,128)(2,1)S(1)}, bf16[96,768]{1,0:T(8,128)(2,1)S(1)}, u32[]{:S(2)}, u32[]{:S(2)}) %collective-permute-start.6) | collective-permute-done | bytes 147488 | tf_op jit(solution)/shard_map/ppermute | solution.py:965
  41.2 2.2 %collective-permute-done.7.refs_2_ = bf16[2,104,768]{2,1,0:T(8,128)(2,1)S(1)} collective-permute-done((bf16[2,104,768]{2,1,0:T(8,128)(2,1)S(1)}, bf16[2,104,768]{2,1,0:T(8,128)(2,1)S(1)}, u32[]{:S(2)}, u32[]{:S(2)}) %collective-permute-start.7) | collective-permute-done | bytes 319520 | tf_op jit(solution)/shard_map/ppermute | solution.py:959
  44.6 1.0 fusion.18
  45.7 5.5 %collective-permute-done.8.refs_1_ = bf16[2,96,768]{2,1,0:T(8,128)(2,1)S(1)} collective-permute-done((bf16[2,96,768]{2,1,0:T(8,128)(2,1)S(1)}, bf16[2,96,768]{2,1,0:T(8,128)(2,1)S(1)}, u32[]{:S(2)}, u32[]{:S(2)}) %collective-permute-start.8) | collective-permute-done | bytes 294944 | tf_op jit(solution)/shard_map/ppermute | solution.py:953
  51.6 1.2 collective-permute-start.11
  54.1 3.9 %collective-permute-done.9.refs_0_.refs_3_ = bf16[2,96,768]{2,1,0:T(8,128)(2,1)S(1)} collective-permute-done((bf16[2,96,768]{2,1,0:T(8,128)(2,1)S(1)}, bf16[2,96,768]{2,1,0:T(8,128)(2,1)S(1)}, u32[]{:S(2)}, u32[]{:S(2)}) %collective-permute-start.9) | collective-permute-done | bytes 294944 | tf_op jit(solution)/shard_map/ppermute | solution.py:971
  59.8 1.6 %collective-permute-start.18 = (bf16[48,512]{1,0:T(8,128)(2,1)S(1)}, bf16[48,512]{1,0:T(8,128)(2,1)S(1)}, u32[]{:S(2)}, u32[]{:S(2)}) collective-permute-start(bf16[48,512]{1,0:T(8,128)(2,1)S(1)} %get-tuple-element.122), channel_id=1, source_target_pairs={{0,2},{1,3},{2,0},{3,1},{4,6},{5,7},{6,4},{7,5},{8,10},{9,11},{10,... | collective-permute-start | bytes 147464 | tf_op jit(solution)/shard_map/ppermute | solution.py:485
  62.0 1.7 %shard_map.258 = (bf16[512,768]{1,0:T(8,128)(2,1)S(1)}, bf16[512,384]{1,0:T(8,128)(2,1)S(1)}, bf16[512,192]{1,0:T(8,128)(2,1)S(1)}) custom-call(f32[512,768]{1,0:T(8,128)S(1)} %fusion.unit.refs_1_.refs_9_, bf16[768,768]{1,0:T(8,128)(2,1)S(1)} %get-tuple-element.115.weights.refs_8_, f32[8,768]{1,0:T(8,128)S(1)} %get-tuple-element.113.refs_6_.vectors.refs_3_.refs_10_, ...), custom_call_target="tpu_custom_call" | custom-call | flops 603979776 | bytes 3563520 | tf_op jit(solution)/shard_map/pallas_call | solution.py:415
  65.1 4.4 %shard_map.257 = (bf16[2,128,1536]{2,1,0:T(8,128)(2,1)S(1)}, bf16[2,128,1536]{2,1,0:T(8,128)(2,1)S(1)}, bf16[512,768]{1,0:T(8,128)(2,1)S(1)}, bf16[512,384]{1,0:...) custom-call(bf16[2,96,768]{2,1,0:T(8,128)(2,1)S(1)} %pad_maximum_fus, ...), custom_call_target="tpu_custom_call" | custom-call | flops 1207959552 | bytes 3563520 | tf_op jit(solution)/shard_map/pallas_call | solution.py:415
  69.6 6.2 %shard_map.259 = (bf16[48,512]{1,0:T(8,128)(2,1)S(1)}, bf16[48,512]{1,0:T(8,128)(2,1)S(1)}, bf16[48,512]{1,0:T(8,128)(2,1)S(1)}, bf16[48,512]{1,0:T(8,128)(2,1)S(1)}, bf16[512,768]{1,0:T(8,128)(2,1)S(1)}) custom-call(bf16[512,384]{1,0:T(8,128)(2,1)S(1)} %get-tuple-element.117.refs_0_.refs_8_, bf16[512,384]{1,0:T(8,128)(2,1)S(1)} %get-tuple-element.118.refs_1_, ...), custom_call_target="tpu_custom_call" | custom-call | flops 704643072 | bytes 1970176 | tf_op jit(solution)/shard_map/pallas_call | solution.py:415
  76.4 1.6 %collective-permute-start.21 = (bf16[48,512]{1,0:T(8,128)(2,1)S(1)}, bf16[48,512]{1,0:T(8,128)(2,1)S(1)}, u32[]{:S(2)}, u32[]{:S(2)}) collective-permute-start(bf16[48,512]{1,0:T(8,128)(2,1)S(1)} %get-tuple-element.126), channel_id=1, source_target_pairs={{0,2},{1,3},{2,0},{3,1},{4,6},{5,7},{6,4},{7,5},{8,10},{9,11},{10,... | collective-permute-start | bytes 147464 | tf_op jit(solution)/shard_map/ppermute | solution.py:485
  78.0 3.4 %shard_map.260 = (bf16[4,128,1536]{2,1,0:T(8,128)(2,1)S(1)}, bf16[512,768]{1,0:T(8,128)(2,1)S(1)}, bf16[512,384]{1,0:T(8,128)(2,1)S(1)}, bf16[512,384]{1,0:T(8,128)(2,1)S(1)}, f32[8,768]{1,0:T(8,128)S(1)}) custom-call(bf16[512,768]{1,0:T(8,128)(2,1)S(1)} %get-tuple-element.130.refs_0_.refs_7_, f32[512,768]{1,0:T(8,128)S(1)} %fusion.unit.refs_1_.refs_9_, ...), custom_call_target="tpu_custom_call" | custom-call | flops 1207959552 | bytes 4349952 | tf_op jit(solution)/shard_map/pallas_call | solution.py:415
  82.0 5.2 %shard_map.261 = (bf16[4,104,768]{2,1,0:T(8,128)(2,1)S(1)}, bf16[4,104,768]{2,1,0:T(8,128)(2,1)S(1)}, bf16[2,128,1536]{2,1,0:T(8,128)(2,1)}, bf16[2,128,1536]{2,1,0:T(8,128)(2,1)S(1)}) custom-call(bf16[48,512]{1,0:T(8,128)(2,1)S(1)} %get-tuple-element.124.refs_0_, bf16[48,512]{1,0:T(8,128)(2,1)S(1)} %collective-permute-done.20.refs_1_, ...), custom_call_target="tpu_custom_call" | custom-call | flops 1509949440 | bytes 7200768 | tf_op jit(solution)/shard_map/pallas_call | solution.py:415
  87.2 1.8 %shard_map.262 = (bf16[2,104,768]{2,1,0:T(8,128)(2,1)S(1)}, bf16[2,104,768]{2,1,0:T(8,128)(2,1)S(1)}, bf16[2,96,768]{2,1,0:T(8,128)(2,1)S(1)}, bf16[2,96,768]{2,1,0:T(8,128)(2,1)S(1)}) custom-call(bf16[4,104,768]{2,1,0:T(8,128)(2,1)S(1)} %get-tuple-element.138.refs_0_, bf16[512,768]{1,0:T(8,128)(2,1)S(1)} %get-tuple-element.139.refs_1_, ...), custom_call_target="tpu_custom_call" | custom-call | flops 1207959552 | bytes 5406720 | tf_op jit(solution)/shard_map/pallas_call | solution.py:415
  89.1 1.1 collective-permute-start.25
  90.2 1.3 collective-permute-start.27
  92.2 1.1 add_convert_fusion
  93.4 6.8 %collective-permute-done.27.refs_1_ = bf16[2,96,768]{2,1,0:T(8,128)(2,1)S(1)} collective-permute-done((bf16[2,96,768]{2,1,0:T(8,128)(2,1)S(1)}, bf16[2,96,768]{2,1,0:T(8,128)(2,1)S(1)}, u32[]{:S(2)}, u32[]{:S(2)}) %collective-permute-start.27) | collective-permute-done | bytes 294944 | tf_op jit(solution)/shard_map/ppermute | solution.py:1069
  100.1 5.7 %collective-permute-done.26.refs_1_ = bf16[2,104,768]{2,1,0:T(8,128)(2,1)S(1)} collective-permute-done((bf16[2,104,768]{2,1,0:T(8,128)(2,1)S(1)}, bf16[2,104,768]{2,1,0:T(8,128)(2,1)S(1)}, u32[]{:S(2)}, u32[]{:S(2)}) %collective-permute-start.26) | collective-permute-done | bytes 319520 | tf_op jit(solution)/shard_map/ppermute | solution.py:1068
  105.9 1.2 collective-permute-start.28
  108.1 2.0 %collective-permute-start.31 = (bf16[1,104,768]{2,1,0:T(8,128)(2,1)S(1)}, bf16[1,104,768]{2,1,0:T(8,128)(2,1)S(1)}, u32[]{:S(2)}, u32[]{:S(2)}) collective-permute-start(bf16[1,104,768]{2,1,0:T(8,128)(2,1)S(1)} %get-tuple-element.156), channel_id=1, source_target_pairs={{0,16},{4,20},{8,24},{12,28},{16,0},{20,4},{24,8},{28,12},{1,17},{... | collective-permute-start | bytes 479240 | tf_op jit(solution)/shard_map/ppermute | solution.py:1074
  111.3 2.3 %collective-permute-start.40 = (bf16[1,96,768]{2,1,0:T(8,128)(2,1)}, bf16[1,96,768]{2,1,0:T(8,128)(2,1)S(1)}, u32[]{:S(2)}, u32[]{:S(2)}) collective-permute-start(bf16[1,96,768]{2,1,0:T(8,128)(2,1)} %get-tuple-element.179), channel_id=1, source_target_pairs={{0,16},{4,20},{8,24},{12,28},{16,0},{20,4},{24,8},{28,12},{1,17},{... | collective-permute-start | bytes 442376 | tf_op jit(solution)/shard_map/ppermute | solution.py:1078
  113.7 5.2 %collective-permute-done.31.refs_2_.refs_0_ = bf16[1,104,768]{2,1,0:T(8,128)(2,1)S(1)} collective-permute-done((bf16[1,104,768]{2,1,0:T(8,128)(2,1)S(1)}, bf16[1,104,768]{2,1,0:T(8,128)(2,1)S(1)}, u32[]{:S(2)}, u32[]{:S(2)}) %collective-permute-start.31) | collective-permute-done | bytes 159776 | tf_op jit(solution)/shard_map/ppermute | solution.py:1074
  118.9 5.2 %collective-permute-done.30.refs_0_.refs_2_ = bf16[2,104,768]{2,1,0:T(8,128)(2,1)S(1)} collective-permute-done((bf16[2,104,768]{2,1,0:T(8,128)(2,1)}, bf16[2,104,768]{2,1,0:T(8,128)(2,1)S(1)}, u32[]{:S(2)}, u32[]{:S(2)}) %collective-permute-start.30) | collective-permute-done | bytes 319520 | tf_op jit(solution)/shard_map/ppermute | solution.py:1076
  125.3 1.6 %convert_add_fusion = f32[2,128,1536]{2,1,0:T(8,128)S(1)} fusion(bf16[2,128,1536]{2,1,0:T(8,128)(2,1)} %collective-permute-done.28, bf16[2,128,1536]{2,1,0:T(8,128)(2,1)} %collective-permute-done.23, bf16[2,128,1536]{2,1,0:T(8,128)(2,1)S(1)} %get-tuple-element.134), kind=kLoop, calls=%fused_computation.6 | loop fusion | flops 1966080 | bytes 3932160 | tf_op jit(solution)/shard_map/add | solution.py:1083
  126.9 1.2 copy-done.9
  129.0 1.0 collective-permute-start.32
  130.0 3.6 %collective-permute-done.32.refs_0_.refs_2_ = bf16[112,384]{1,0:T(8,128)(2,1)S(1)} collective-permute-done((bf16[112,384]{1,0:T(8,128)(2,1)S(1)}, bf16[112,384]{1,0:T(8,128)(2,1)S(1)}, u32[]{:S(2)}, u32[]{:S(2)}) %collective-permute-start.32) | collective-permute-done | bytes 86048 | tf_op jit(solution)/shard_map/ppermute | solution.py:1105
  133.7 1.4 collective-permute-start.38
  137.4 1.3 collective-permute-start.35
  138.7 0.9 collective-permute-done.38.refs_4_
  139.6 0.9 shard_map.270
  141.6 1.5 %collective-permute-done.36.refs_4_ = bf16[32,768]{1,0:T(8,128)(2,1)S(1)} collective-permute-done((bf16[32,768]{1,0:T(8,128)(2,1)S(1)}, bf16[32,768]{1,0:T(8,128)(2,1)S(1)}, u32[]{:S(2)}, u32[]{:S(2)}) %collective-permute-start.36) | collective-permute-done | bytes 49184 | tf_op jit(solution)/shard_map/ppermute | solution.py:485
  143.1 0.9 shard_map.268
  145.3 0.9 fusion.12
  (133 shorter events, 24.9 us)
Async XLA Ops:
  2.3 0.9 copy-start.2
  6.0 9.3 %collective-permute-start = (bf16[56,768]{1,0:T(8,128)(2,1)S(1)}, bf16[56,768]{1,0:T(8,128)(2,1)S(1)}, u32[]{:S(2)}, u32[]{:S(2)}) collective-permute-start(bf16[56,768]{1,0:T(8,128)(2,1)S(1)} %get-tuple-element.98), channel_id=1, source_target_pairs={{0,1},{1,0},{2,3},{3,2},{4,5},{5,4},{6,7},{7,6},{8,9},{9,8},{10,11... | collective-permute-start | bytes 258056 | tf_op jit(solution)/shard_map/ppermute | solution.py:485
  6.5 8.8 %collective-permute-start.1 = (bf16[56,768]{1,0:T(8,128)(2,1)S(1)}, bf16[56,768]{1,0:T(8,128)(2,1)S(1)}, u32[]{:S(2)}, u32[]{:S(2)}) collective-permute-start(bf16[56,768]{1,0:T(8,128)(2,1)S(1)} %get-tuple-element.99), channel_id=1, source_target_pairs={{0,2},{1,3},{2,0},{3,1},{4,6},{5,7},{6,4},{7,5},{8,10},{9,11},{10,... | collective-permute-start | bytes 258056 | tf_op jit(solution)/shard_map/ppermute | solution.py:485
  9.1 6.2 %collective-permute-start.2 = (bf16[56,768]{1,0:T(8,128)(2,1)S(1)}, bf16[56,768]{1,0:T(8,128)(2,1)S(1)}, u32[]{:S(2)}, u32[]{:S(2)}) collective-permute-start(bf16[56,768]{1,0:T(8,128)(2,1)S(1)} %get-tuple-element.100), channel_id=1, source_target_pairs={{0,3},{1,2},{2,1},{3,0},{4,7},{5,6},{6,5},{7,4},{8,11},{9,10},{10,... | collective-permute-start | bytes 258056 | tf_op jit(solution)/shard_map/ppermute | solution.py:485
  9.1 10.6 %collective-permute-start.3 = (bf16[96,768]{1,0:T(8,128)(2,1)}, bf16[96,768]{1,0:T(8,128)(2,1)S(1)}, u32[]{:S(2)}, u32[]{:S(2)}) collective-permute-start(bf16[96,768]{1,0:T(8,128)(2,1)} %param.28), channel_id=1, source_target_pairs={{0,16},{4,20},{8,24},{12,28},{16,0},{20,4},{24,8},{28,12},{1,17},{... | collective-permute-start | bytes 442376 | tf_op jit(solution)/shard_map/ppermute | solution.py:950
  12.0 22.7 %collective-permute-start.14 = (bf16[256,768]{1,0:T(8,128)(2,1)S(1)}, bf16[256,768]{1,0:T(8,128)(2,1)S(1)}, u32[]{:S(2)}, u32[]{:S(2)}) collective-permute-start(bf16[256,768]{1,0:T(8,128)(2,1)S(1)} %get-tuple-element.111), channel_id=1, source_target_pairs={{0,4},{4,0},{8,12},{12,8},{16,20},{20,16},{24,28},{28,24},{1,5},{5... | collective-permute-start | bytes 1179656 | tf_op jit(solution)/shard_map/ppermute | solution.py:949
  19.7 4.9 %collective-permute-start.4 = (bf16[96,384]{1,0:T(8,128)(2,1)S(1)}, bf16[96,384]{1,0:T(8,128)(2,1)S(1)}, u32[]{:S(2)}, u32[]{:S(2)}) collective-permute-start(bf16[96,384]{1,0:T(8,128)(2,1)S(1)} %get-tuple-element.103), channel_id=1, source_target_pairs={{0,4},{4,0},{8,12},{12,8},{16,20},{20,16},{24,28},{28,24},{1,5},{5... | collective-permute-start | bytes 221192 | tf_op jit(solution)/shard_map/ppermute | solution.py:955
  21.3 13.2 %collective-permute-start.12 = (bf16[256,768]{1,0:T(8,128)(2,1)S(1)}, bf16[256,768]{1,0:T(8,128)(2,1)S(1)}, u32[]{:S(2)}, u32[]{:S(2)}) collective-permute-start(bf16[256,768]{1,0:T(8,128)(2,1)S(1)} %get-tuple-element.111), channel_id=1, source_target_pairs={{0,2},{2,0},{1,3},{3,1},{4,6},{6,4},{5,7},{7,5},{8,10},{10,8},{9,1... | collective-permute-start | bytes 1179656 | tf_op jit(solution)/shard_map/ppermute | solution.py:956
  22.8 9.3 %collective-permute-start.5 = (bf16[104,768]{1,0:T(8,128)(2,1)S(1)}, bf16[104,768]{1,0:T(8,128)(2,1)S(1)}, u32[]{:S(2)}, u32[]{:S(2)}) collective-permute-start(bf16[104,768]{1,0:T(8,128)(2,1)S(1)} %get-tuple-element.105), channel_id=1, source_target_pairs={{0,16},{4,20},{8,24},{12,28},{16,0},{20,4},{24,8},{28,12},{1,17},{... | collective-permute-start | bytes 479240 | tf_op jit(solution)/shard_map/ppermute | solution.py:954
  32.1 11.8 %copy-start.11 = (bf16[96,768]{1,0:T(8,128)(2,1)S(1)}, bf16[96,768]{1,0:T(8,128)(2,1)}, u32[]{:S(2)}) copy-start(bf16[96,768]{1,0:T(8,128)(2,1)} %param.28) | copy-start | bytes 442372
  32.1 11.3 %collective-permute-start.7 = (bf16[2,104,768]{2,1,0:T(8,128)(2,1)S(1)}, bf16[2,104,768]{2,1,0:T(8,128)(2,1)S(1)}, u32[]{:S(2)}, u32[]{:S(2)}) collective-permute-start(bf16[2,104,768]{2,1,0:T(8,128)(2,1)S(1)} %pad_maximum_fusion.4.refs_1_), channel_id=1, source_target_pairs={{0,8},{4,12},{8,0},{12,4},{16,24},{20,28},{24,16},{28,20},{1,9},{5... | collective-permute-start | bytes 958472 | tf_op jit(solution)/shard_map/ppermute | solution.py:959
  32.2 11.2 %collective-permute-start.10 = (bf16[2,104,768]{2,1,0:T(8,128)(2,1)S(1)}, bf16[2,104,768]{2,1,0:T(8,128)(2,1)S(1)}, u32[]{:S(2)}, u32[]{:S(2)}) collective-permute-start(bf16[2,104,768]{2,1,0:T(8,128)(2,1)S(1)} %pad_maximum_fusion.4.refs_1_), channel_id=1, source_target_pairs={{0,4},{4,0},{8,12},{12,8},{16,20},{20,16},{24,28},{28,24},{1,5},{5... | collective-permute-start | bytes 958472 | tf_op jit(solution)/shard_map/ppermute | solution.py:960
  32.8 8.4 %collective-permute-start.6 = (bf16[96,768]{1,0:T(8,128)(2,1)S(1)}, bf16[96,768]{1,0:T(8,128)(2,1)S(1)}, u32[]{:S(2)}, u32[]{:S(2)}) collective-permute-start(bf16[96,768]{1,0:T(8,128)(2,1)S(1)} %pad_maximum_fusion.7), channel_id=1, source_target_pairs={{0,16},{4,20},{8,24},{12,28},{16,0},{20,4},{24,8},{28,12},{1,17},{... | collective-permute-start | bytes 442376 | tf_op jit(solution)/shard_map/ppermute | solution.py:965
  34.6 18.7 %collective-permute-start.13 = (bf16[2,256,768]{2,1,0:T(8,128)(2,1)S(1)}, bf16[2,256,768]{2,1,0:T(8,128)(2,1)S(1)}, u32[]{:S(2)}, u32[]{:S(2)}) collective-permute-start(bf16[2,256,768]{2,1,0:T(8,128)(2,1)S(1)} %pad_maximum_fusion.2), channel_id=1, source_target_pairs={{0,1},{1,0},{2,3},{3,2},{4,5},{5,4},{6,7},{7,6},{8,9},{9,8},{10,11... | collective-permute-start | bytes 2359304 | tf_op jit(solution)/shard_map/ppermute | solution.py:967
  43.4 9.8 %collective-permute-start.15 = (bf16[256,768]{1,0:T(8,128)(2,1)S(1)}, bf16[256,768]{1,0:T(8,128)(2,1)S(1)}, u32[]{:S(2)}, u32[]{:S(2)}) collective-permute-start(bf16[256,768]{1,0:T(8,128)(2,1)S(1)} %collective-permute-done.14), channel_id=1, source_target_pairs={{0,2},{2,0},{1,3},{3,1},{4,6},{6,4},{5,7},{7,5},{8,10},{10,8},{9,1... | collective-permute-start | bytes 1179656 | tf_op jit(solution)/shard_map/ppermute | solution.py:972
  44.0 7.2 %collective-permute-start.8 = (bf16[2,96,768]{2,1,0:T(8,128)(2,1)S(1)}, bf16[2,96,768]{2,1,0:T(8,128)(2,1)S(1)}, u32[]{:S(2)}, u32[]{:S(2)}) collective-permute-start(bf16[2,96,768]{2,1,0:T(8,128)(2,1)S(1)} %pad_maximum_fusion.6.refs_0_), channel_id=1, source_target_pairs={{0,8},{4,12},{8,0},{12,4},{16,24},{20,28},{24,16},{28,20},{1,9},{5... | collective-permute-start | bytes 884744 | tf_op jit(solution)/shard_map/ppermute | solution.py:953
  51.2 6.7 %collective-permute-start.9 = (bf16[2,96,768]{2,1,0:T(8,128)(2,1)S(1)}, bf16[2,96,768]{2,1,0:T(8,128)(2,1)S(1)}, u32[]{:S(2)}, u32[]{:S(2)}) collective-permute-start(bf16[2,96,768]{2,1,0:T(8,128)(2,1)S(1)} %pad_maximum_fusion.5.refs_2_), channel_id=1, source_target_pairs={{0,8},{4,12},{8,0},{12,4},{16,24},{20,28},{24,16},{28,20},{1,9},{5... | collective-permute-start | bytes 884744 | tf_op jit(solution)/shard_map/ppermute | solution.py:971
  51.6 7.0 %collective-permute-start.11 = (bf16[2,104,768]{2,1,0:T(8,128)(2,1)S(1)}, bf16[2,104,768]{2,1,0:T(8,128)(2,1)S(1)}, u32[]{:S(2)}, u32[]{:S(2)}) collective-permute-start(bf16[2,104,768]{2,1,0:T(8,128)(2,1)S(1)} %collective-permute-done.7.refs_2_), channel_id=1, source_target_pairs={{0,4},{4,0},{8,12},{12,8},{16,20},{20,16},{24,28},{28,24},{1,5},{5... | collective-permute-start | bytes 958472 | tf_op jit(solution)/shard_map/ppermute | solution.py:969
  59.2 4.5 %collective-permute-start.16 = (bf16[2,256,768]{2,1,0:T(8,128)(2,1)S(1)}, bf16[2,256,768]{2,1,0:T(8,128)(2,1)S(1)}, u32[]{:S(2)}, u32[]{:S(2)}) collective-permute-start(bf16[2,256,768]{2,1,0:T(8,128)(2,1)S(1)} %pad_maximum_fusion.3), channel_id=1, source_target_pairs={{0,1},{1,0},{2,3},{3,2},{4,5},{5,4},{6,7},{7,6},{8,9},{9,8},{10,11... | collective-permute-start | bytes 2359304 | tf_op jit(solution)/shard_map/ppermute | solution.py:1008
  59.3 10.3 %collective-permute-start.17 = (bf16[48,512]{1,0:T(8,128)(2,1)S(1)}, bf16[48,512]{1,0:T(8,128)(2,1)S(1)}, u32[]{:S(2)}, u32[]{:S(2)}) collective-permute-start(bf16[48,512]{1,0:T(8,128)(2,1)S(1)} %get-tuple-element.121), channel_id=1, source_target_pairs={{0,1},{1,0},{2,3},{3,2},{4,5},{5,4},{6,7},{7,6},{8,9},{9,8},{10,11... | collective-permute-start | bytes 147464 | tf_op jit(solution)/shard_map/ppermute | solution.py:485
  59.8 9.8 %collective-permute-start.18 = (bf16[48,512]{1,0:T(8,128)(2,1)S(1)}, bf16[48,512]{1,0:T(8,128)(2,1)S(1)}, u32[]{:S(2)}, u32[]{:S(2)}) collective-permute-start(bf16[48,512]{1,0:T(8,128)(2,1)S(1)} %get-tuple-element.122), channel_id=1, source_target_pairs={{0,2},{1,3},{2,0},{3,1},{4,6},{5,7},{6,4},{7,5},{8,10},{9,11},{10,... | collective-permute-start | bytes 147464 | tf_op jit(solution)/shard_map/ppermute | solution.py:485
  61.4 8.2 %collective-permute-start.19 = (bf16[48,512]{1,0:T(8,128)(2,1)S(1)}, bf16[48,512]{1,0:T(8,128)(2,1)S(1)}, u32[]{:S(2)}, u32[]{:S(2)}) collective-permute-start(bf16[48,512]{1,0:T(8,128)(2,1)S(1)} %get-tuple-element.123), channel_id=1, source_target_pairs={{0,3},{1,2},{2,1},{3,0},{4,7},{5,6},{6,5},{7,4},{8,11},{9,10},{10,... | collective-permute-start | bytes 147464 | tf_op jit(solution)/shard_map/ppermute | solution.py:485
  75.8 5.6 %collective-permute-start.20 = (bf16[48,512]{1,0:T(8,128)(2,1)S(1)}, bf16[48,512]{1,0:T(8,128)(2,1)S(1)}, u32[]{:S(2)}, u32[]{:S(2)}) collective-permute-start(bf16[48,512]{1,0:T(8,128)(2,1)S(1)} %get-tuple-element.125), channel_id=1, source_target_pairs={{0,1},{1,0},{2,3},{3,2},{4,5},{5,4},{6,7},{7,6},{8,9},{9,8},{10,11... | collective-permute-start | bytes 147464 | tf_op jit(solution)/shard_map/ppermute | solution.py:485
  76.4 5.0 %collective-permute-start.21 = (bf16[48,512]{1,0:T(8,128)(2,1)S(1)}, bf16[48,512]{1,0:T(8,128)(2,1)S(1)}, u32[]{:S(2)}, u32[]{:S(2)}) collective-permute-start(bf16[48,512]{1,0:T(8,128)(2,1)S(1)} %get-tuple-element.126), channel_id=1, source_target_pairs={{0,2},{1,3},{2,0},{3,1},{4,6},{5,7},{6,4},{7,5},{8,10},{9,11},{10,... | collective-permute-start | bytes 147464 | tf_op jit(solution)/shard_map/ppermute | solution.py:485
  78.0 4.0 %collective-permute-start.22 = (bf16[48,512]{1,0:T(8,128)(2,1)S(1)}, bf16[48,512]{1,0:T(8,128)(2,1)S(1)}, u32[]{:S(2)}, u32[]{:S(2)}) collective-permute-start(bf16[48,512]{1,0:T(8,128)(2,1)S(1)} %get-tuple-element.127), channel_id=1, source_target_pairs={{0,3},{1,2},{2,1},{3,0},{4,7},{5,6},{6,5},{7,4},{8,11},{9,10},{10,... | collective-permute-start | bytes 147464 | tf_op jit(solution)/shard_map/ppermute | solution.py:485
  89.0 18.1 %copy-start.1 = (bf16[128,768]{1,0:T(8,128)(2,1)S(1)}, bf16[128,768]{1,0:T(8,128)(2,1)}, u32[]{:S(2)}) copy-start(bf16[128,768]{1,0:T(8,128)(2,1)} %refs_4_.1) | copy-start | bytes 589828
  89.0 3.2 %collective-permute-start.24 = (bf16[2,128,1536]{2,1,0:T(8,128)(2,1)S(1)}, bf16[2,128,1536]{2,1,0:T(8,128)(2,1)S(1)}, u32[]{:S(2)}, u32[]{:S(2)}) collective-permute-start(bf16[2,128,1536]{2,1,0:T(8,128)(2,1)S(1)} %get-tuple-element.147), channel_id=1, source_target_pairs={{0,1},{1,0},{2,3},{3,2},{4,5},{5,4},{6,7},{7,6},{8,9},{9,8},{10,11... | collective-permute-start | bytes 2359304 | tf_op jit(solution)/shard_map/ppermute | solution.py:1070
  89.1 16.7 %collective-permute-start.25 = (bf16[4,104,768]{2,1,0:T(8,128)(2,1)S(1)}, bf16[4,104,768]{2,1,0:T(8,128)(2,1)S(1)}, u32[]{:S(2)}, u32[]{:S(2)}) collective-permute-start(bf16[4,104,768]{2,1,0:T(8,128)(2,1)S(1)} %get-tuple-element.138.refs_0_), channel_id=1, source_target_pairs={{0,4},{4,0},{8,12},{12,8},{16,20},{20,16},{24,28},{28,24},{1,5},{5... | collective-permute-start | bytes 1916936 | tf_op jit(solution)/shard_map/ppermute | solution.py:1067
  90.2 9.9 %collective-permute-start.27 = (bf16[2,96,768]{2,1,0:T(8,128)(2,1)S(1)}, bf16[2,96,768]{2,1,0:T(8,128)(2,1)S(1)}, u32[]{:S(2)}, u32[]{:S(2)}) collective-permute-start(bf16[2,96,768]{2,1,0:T(8,128)(2,1)S(1)} %get-tuple-element.149), channel_id=1, source_target_pairs={{0,8},{4,12},{8,0},{12,4},{16,24},{20,28},{24,16},{28,20},{1,9},{5... | collective-permute-start | bytes 884744 | tf_op jit(solution)/shard_map/ppermute | solution.py:1069
  91.5 14.3 %collective-permute-start.26 = (bf16[2,104,768]{2,1,0:T(8,128)(2,1)S(1)}, bf16[2,104,768]{2,1,0:T(8,128)(2,1)S(1)}, u32[]{:S(2)}, u32[]{:S(2)}) collective-permute-start(bf16[2,104,768]{2,1,0:T(8,128)(2,1)S(1)} %get-tuple-element.148), channel_id=1, source_target_pairs={{0,8},{4,12},{8,0},{12,4},{16,24},{20,28},{24,16},{28,20},{1,9},{5... | collective-permute-start | bytes 958472 | tf_op jit(solution)/shard_map/ppermute | solution.py:1068
  92.2 32.3 %collective-permute-start.23 = (bf16[2,128,1536]{2,1,0:T(8,128)(2,1)}, bf16[2,128,1536]{2,1,0:T(8,128)(2,1)}, u32[]{:S(2)}, u32[]{:S(2)}) collective-permute-start(bf16[2,128,1536]{2,1,0:T(8,128)(2,1)} %get-tuple-element.135), channel_id=1, source_target_pairs={{0,1},{1,0},{2,3},{3,2},{4,5},{5,4},{6,7},{7,6},{8,9},{9,8},{10,11... | collective-permute-start | bytes 2359304 | tf_op jit(solution)/shard_map/ppermute | solution.py:1083
  105.9 19.4 %collective-permute-start.28 = (bf16[2,128,1536]{2,1,0:T(8,128)(2,1)}, bf16[2,128,1536]{2,1,0:T(8,128)(2,1)}, u32[]{:S(2)}, u32[]{:S(2)}) collective-permute-start(bf16[2,128,1536]{2,1,0:T(8,128)(2,1)} %add_convert_fusion), channel_id=1, source_target_pairs={{0,4},{4,0},{8,12},{12,8},{16,20},{20,16},{24,28},{28,24},{1,5},{5... | collective-permute-start | bytes 2359304 | tf_op jit(solution)/shard_map/ppermute | solution.py:1079
  108.1 10.8 %collective-permute-start.31 = (bf16[1,104,768]{2,1,0:T(8,128)(2,1)S(1)}, bf16[1,104,768]{2,1,0:T(8,128)(2,1)S(1)}, u32[]{:S(2)}, u32[]{:S(2)}) collective-permute-start(bf16[1,104,768]{2,1,0:T(8,128)(2,1)S(1)} %get-tuple-element.156), channel_id=1, source_target_pairs={{0,16},{4,20},{8,24},{12,28},{16,0},{20,4},{24,8},{28,12},{1,17},{... | collective-permute-start | bytes 479240 | tf_op jit(solution)/shard_map/ppermute | solution.py:1074
  110.1 14.0 %collective-permute-start.30 = (bf16[2,104,768]{2,1,0:T(8,128)(2,1)}, bf16[2,104,768]{2,1,0:T(8,128)(2,1)S(1)}, u32[]{:S(2)}, u32[]{:S(2)}) collective-permute-start(bf16[2,104,768]{2,1,0:T(8,128)(2,1)} %get-tuple-element.153), channel_id=1, source_target_pairs={{0,8},{4,12},{8,0},{12,4},{16,24},{20,28},{24,16},{28,20},{1,9},{5... | collective-permute-start | bytes 958472 | tf_op jit(solution)/shard_map/ppermute | solution.py:1076
  111.3 24.2 %collective-permute-start.40 = (bf16[1,96,768]{2,1,0:T(8,128)(2,1)}, bf16[1,96,768]{2,1,0:T(8,128)(2,1)S(1)}, u32[]{:S(2)}, u32[]{:S(2)}) collective-permute-start(bf16[1,96,768]{2,1,0:T(8,128)(2,1)} %get-tuple-element.179), channel_id=1, source_target_pairs={{0,16},{4,20},{8,24},{12,28},{16,0},{20,4},{24,8},{28,12},{1,17},{... | collective-permute-start | bytes 442376 | tf_op jit(solution)/shard_map/ppermute | solution.py:1078
  124.1 9.4 %collective-permute-start.33 = (bf16[1,104,768]{2,1,0:T(8,128)(2,1)S(1)}, bf16[1,104,768]{2,1,0:T(8,128)(2,1)S(1)}, u32[]{:S(2)}, u32[]{:S(2)}) collective-permute-start(bf16[1,104,768]{2,1,0:T(8,128)(2,1)S(1)} %get-tuple-element.160), channel_id=1, source_target_pairs={{0,16},{4,20},{8,24},{12,28},{16,0},{20,4},{24,8},{28,12},{1,17},{... | collective-permute-start | bytes 479240 | tf_op jit(solution)/shard_map/ppermute | solution.py:1081
  126.9 1.2 copy-start.9
  128.2 11.4 %collective-permute-start.29 = (bf16[128,1536]{1,0:T(8,128)(2,1)S(1)}, bf16[128,1536]{1,0:T(8,128)(2,1)S(1)}, u32[]{:S(2)}, u32[]{:S(2)}) collective-permute-start(bf16[128,1536]{1,0:T(8,128)(2,1)S(1)} %fusion.17), channel_id=1, source_target_pairs={{0,2},{2,0},{1,3},{3,1},{4,6},{6,4},{5,7},{7,5},{8,10},{10,8},{9,1... | collective-permute-start | bytes 1179656 | tf_op jit(solution)/shard_map/ppermute | solution.py:1084
  128.9 16.1 %copy-start.10 = (f32[2,128,1536]{2,1,0:T(8,128)S(1)}, f32[2,128,1536]{2,1,0:T(8,128)}, u32[]{:S(2)}) copy-start(f32[2,128,1536]{2,1,0:T(8,128)} %copy-done.9) | copy-start | bytes 4718596
  129.0 4.6 %collective-permute-start.32 = (bf16[112,384]{1,0:T(8,128)(2,1)S(1)}, bf16[112,384]{1,0:T(8,128)(2,1)S(1)}, u32[]{:S(2)}, u32[]{:S(2)}) collective-permute-start(bf16[112,384]{1,0:T(8,128)(2,1)S(1)} %get-tuple-element.157), channel_id=1, source_target_pairs={{0,4},{4,0},{8,12},{12,8},{16,20},{20,16},{24,28},{28,24},{1,5},{5... | collective-permute-start | bytes 258056 | tf_op jit(solution)/shard_map/ppermute | solution.py:1105
  133.6 3.8 %collective-permute-start.37 = (bf16[32,768]{1,0:T(8,128)(2,1)S(1)}, bf16[32,768]{1,0:T(8,128)(2,1)S(1)}, u32[]{:S(2)}, u32[]{:S(2)}) collective-permute-start(bf16[32,768]{1,0:T(8,128)(2,1)S(1)} %get-tuple-element.169), channel_id=1, source_target_pairs={{0,1},{1,0},{2,3},{3,2},{4,5},{5,4},{6,7},{7,6},{8,9},{9,8},{10,11... | collective-permute-start | bytes 147464 | tf_op jit(solution)/shard_map/ppermute | solution.py:485
  133.7 5.9 %collective-permute-start.38 = (bf16[32,768]{1,0:T(8,128)(2,1)S(1)}, bf16[32,768]{1,0:T(8,128)(2,1)S(1)}, u32[]{:S(2)}, u32[]{:S(2)}) collective-permute-start(bf16[32,768]{1,0:T(8,128)(2,1)S(1)} %get-tuple-element.170), channel_id=1, source_target_pairs={{0,2},{1,3},{2,0},{3,1},{4,6},{5,7},{6,4},{7,5},{8,10},{9,11},{10,... | collective-permute-start | bytes 147464 | tf_op jit(solution)/shard_map/ppermute | solution.py:485
  135.1 4.5 %collective-permute-start.39 = (bf16[32,768]{1,0:T(8,128)(2,1)S(1)}, bf16[32,768]{1,0:T(8,128)(2,1)S(1)}, u32[]{:S(2)}, u32[]{:S(2)}) collective-permute-start(bf16[32,768]{1,0:T(8,128)(2,1)S(1)} %get-tuple-element.171), channel_id=1, source_target_pairs={{0,3},{1,2},{2,1},{3,0},{4,7},{5,6},{6,5},{7,4},{8,11},{9,10},{10,... | collective-permute-start | bytes 147464 | tf_op jit(solution)/shard_map/ppermute | solution.py:485
  137.0 4.5 %collective-permute-start.34 = (bf16[32,768]{1,0:T(8,128)(2,1)S(1)}, bf16[32,768]{1,0:T(8,128)(2,1)S(1)}, u32[]{:S(2)}, u32[]{:S(2)}) collective-permute-start(bf16[32,768]{1,0:T(8,128)(2,1)S(1)} %get-tuple-element.162), channel_id=1, source_target_pairs={{0,1},{1,0},{2,3},{3,2},{4,5},{5,4},{6,7},{7,6},{8,9},{9,8},{10,11... | collective-permute-start | bytes 147464 | tf_op jit(solution)/shard_map/ppermute | solution.py:485
  137.4 4.2 %collective-permute-start.35 = (bf16[32,768]{1,0:T(8,128)(2,1)S(1)}, bf16[32,768]{1,0:T(8,128)(2,1)S(1)}, u32[]{:S(2)}, u32[]{:S(2)}) collective-permute-start(bf16[32,768]{1,0:T(8,128)(2,1)S(1)} %get-tuple-element.163), channel_id=1, source_target_pairs={{0,2},{1,3},{2,0},{3,1},{4,6},{5,7},{6,4},{7,5},{8,10},{9,11},{10,... | collective-permute-start | bytes 147464 | tf_op jit(solution)/shard_map/ppermute | solution.py:485
  139.6 3.5 %collective-permute-start.36 = (bf16[32,768]{1,0:T(8,128)(2,1)S(1)}, bf16[32,768]{1,0:T(8,128)(2,1)S(1)}, u32[]{:S(2)}, u32[]{:S(2)}) collective-permute-start(bf16[32,768]{1,0:T(8,128)(2,1)S(1)} %get-tuple-element.164), channel_id=1, source_target_pairs={{0,3},{1,2},{2,1},{3,0},{4,7},{5,6},{6,5},{7,4},{8,11},{9,10},{10,... | collective-permute-start | bytes 147464 | tf_op jit(solution)/shard_map/ppermute | solution.py:485
  141.0 5.2 %copy-start.12 = (f32[24]{0:T(128)}, f32[24]{0:T(128)S(1)}, u32[]{:S(2)}) copy-start(f32[24]{0:T(128)S(1)} %get-tuple-element.243) | copy-start | bytes 292
  143.1 2.2 %copy-start.3 = (bf16[128,768]{1,0:T(8,128)(2,1)S(1)}, bf16[128,768]{1,0:T(8,128)(2,1)}, u32[]{:S(2)}) copy-start(bf16[128,768]{1,0:T(8,128)(2,1)} %refs_5_.1) | copy-start | bytes 589828
  (6 other events, 4.8 us)

commit v7 on v6

--- a/solution.py
+++ b/solution.py
@@ -996,12 +996,11 @@
     unit = normed(hidden_group.astype(F32))[0]
 
     placed = kernel_call(
-        with_waits(1, functools.partial(place_kernel, deep)),
+        functools.partial(place_kernel, deep),
         ((flat[1:] * 2, BF), ((n_dp * deep, width), BF), ((8, width), F32)) + (((2 * deep, group), BF),) * 4,
-        (mlp_pair,) + attn_pieces + (dy,),
+        attn_pieces + (dy,),
         scratch=(((n_dp * deep, width), F32), ((n_dp * deep, group), BF)),
         flops=2 * n_dp * deep * width * group,
-        apart=1,
     )
     weights, dense, vectors = placed[:3]
     by_chip_beyond = once(in_order(chip == 1, across, chip_beyond), weights)
@@ -1015,26 +1014,26 @@
         (unit, weights, vectors, cosine, sine_a, sine_b),
         flops=2 * group * width * width,
     )
-    held_shapes = ((flat, BF), ((group, half), BF), ((group, half), BF))
-    give, keep, *held_other, up_full, down_full = kernel_call(
-        mlp_kernel,
-        (((2, rows, 2 * width), BF),) * 2 + held_shapes + (((8, width), F32), ((width, half), BF), ((half, width), BF)),
-        (down_two, down_pair, mlp_two, mlp_pair, unit_other, dy_other, vectors),
-        scratch=(pltpu.SemaphoreType.DMA((12,)),),
-        flops=4 * group * width * 2 * half,
-        megabytes=16,
-        apart=4,
-    )
     attended = kernel_call(
         with_waits(1, functools.partial(attention_kernel, deep)),
         (((2 * deep, group), BF),) * 4 + ((flat, BF),),
-        (held_other[2], qk, v, *d_blocks, segment[:, None], segment[None, :], cosine, sine_a, sine_b),
+        (mlp_pair, qk, v, *d_blocks, segment[:, None], segment[None, :], cosine, sine_a, sine_b),
         scratch=(((own, group), F32),) * 4 + ((flat, F32),),
         flops=14 * group * group * own,
         megabytes=16,
         apart=1,
     )
     d_joined = attended[4]
+    held_shapes = ((flat, BF), ((group, half), BF), ((group, half), BF))
+    give, keep, *held_other, up_full, down_full = kernel_call(
+        with_waits(1, mlp_kernel),
+        (((2, rows, 2 * width), BF),) * 2 + held_shapes + (((8, width), F32), ((width, half), BF), ((half, width), BF)),
+        (d_joined, down_two, down_pair, mlp_two, mlp_pair, unit_other, dy_other, vectors),
+        scratch=(pltpu.SemaphoreType.DMA((12,)),),
+        flops=4 * group * width * 2 * half,
+        megabytes=16,
+        apart=5,
+    )
     row_blocks = seq_shuffle(attended[:4])
 
     own_pair, *held_own = kernel_call(

time: 147 us -> 142 us (0.966)
  waiting for transfers between devices: 61.5 us -> 57.3 us
    ppermute x1, waiting for transfers between devices: 3.88 us -> 0.01 us  [line_device(): mlp_pair = lax.ppermute(mlp_two, 'dp', PAIR_SWAP)]
  transfers between devices with their start and end apart: 41 -> 41, of which waited for: 19 -> 18; matrix products, arithmetic and copies ran while one was open for 7% -> 8% of each run, Pallas kernels for 9% -> 14%
where the time goes in v7:
time: 142 us
  waiting for transfers between devices  57.3 us (40%)
  starting transfers between devices  34 us (24%)
  Pallas kernels  28 us (20%)
  local copies, waits for them, and re-layouts  10.7 us (8%)
  other arithmetic  10.5 us (7%)
    pallas_call x18, Pallas kernels, kernel_call(): pl.pallas_call(body, out_shape=tuple((jax.ShapeDtypeStruct(shape, kind) f...  28 us
    ppermute x15, starting transfers between devices, seq_shuffle(): got.append(lax.ppermute(blocks[other], 'seq', pairs))  10.5 us
    unnamed x27, local copies, waits for them, and re-layouts  7.44 us
    ppermute x1, waiting for transfers between devices, line_device(): attn_half = lax.ppermute(attn_piece, 'dp', HALF_SWAP)  7.42 us
    ppermute x1, waiting for transfers between devices, line_device(): down_got = lax.ppermute(send_down, 'dp', PAIR_SWAP)  6.73 us
    ppermute x1, waiting for transfers between devices, line_device(): mlp_half = lax.ppermute(mlp_piece, 'dp', HALF_SWAP)  6.51 us
    ppermute x1, waiting for transfers between devices, line_device(): up_got = lax.ppermute(send_up, 'dp', PAIR_SWAP)  5.87 us
    ppermute x2, waiting for transfers between devices, line_device(): up_far = lax.ppermute(up_give, 'dp', SIDE_SWAP)  5.41 us
  transfers between devices with their start and end apart: 41, of which 18 were waited for; matrix products, arithmetic and copies ran while one was open for 8% of the time, Pallas kernels for 14%

profile of v7, /device:TPU:0, one launch (start us, length us, event | category | flops | bytes accessed | tf_op | source)
XLA Modules:
  0.0 141.7 jit_solution(1711310868775106226)
XLA Ops:
  1.4 0.9 copy-done
  2.3 0.9 copy-done.2
  3.3 0.9 copy-done.4
  4.2 0.9 copy-done.5
  6.5 2.6 %collective-permute-start.1 = (bf16[56,768]{1,0:T(8,128)(2,1)S(1)}, bf16[56,768]{1,0:T(8,128)(2,1)S(1)}, u32[]{:S(2)}, u32[]{:S(2)}) collective-permute-start(bf16[56,768]{1,0:T(8,128)(2,1)S(1)} %get-tuple-element.99), channel_id=1, source_target_pairs={{0,2},{1,3},{2,0},{3,1},{4,6},{5,7},{6,4},{7,5},{8,10},{9,11},{10,... | collective-permute-start | bytes 258056 | tf_op jit(solution)/shard_map/ppermute | solution.py:485
  9.1 2.8 %collective-permute-start.3 = (bf16[96,768]{1,0:T(8,128)(2,1)}, bf16[96,768]{1,0:T(8,128)(2,1)S(1)}, u32[]{:S(2)}, u32[]{:S(2)}) collective-permute-start(bf16[96,768]{1,0:T(8,128)(2,1)} %param.28), channel_id=1, source_target_pairs={{0,16},{4,20},{8,24},{12,28},{16,0},{20,4},{24,8},{28,12},{1,17},{... | collective-permute-start | bytes 442376 | tf_op jit(solution)/shard_map/ppermute | solution.py:950
  12.0 1.5 %collective-permute-start.20 = (bf16[256,768]{1,0:T(8,128)(2,1)S(1)}, bf16[256,768]{1,0:T(8,128)(2,1)S(1)}, u32[]{:S(2)}, u32[]{:S(2)}) collective-permute-start(bf16[256,768]{1,0:T(8,128)(2,1)S(1)} %get-tuple-element.110), channel_id=1, source_target_pairs={{0,4},{4,0},{8,12},{12,8},{16,20},{20,16},{24,28},{28,24},{1,5},{5... | collective-permute-start | bytes 1179656 | tf_op jit(solution)/shard_map/ppermute | solution.py:949
  13.5 0.8 reduce-window.8
  16.9 2.8 %collective-permute-done.3 = bf16[96,768]{1,0:T(8,128)(2,1)S(1)} collective-permute-done((bf16[96,768]{1,0:T(8,128)(2,1)}, bf16[96,768]{1,0:T(8,128)(2,1)S(1)}, u32[]{:S(2)}, u32[]{:S(2)}) %collective-permute-start.3) | collective-permute-done | bytes 147488 | tf_op jit(solution)/shard_map/ppermute | solution.py:950
  19.7 1.6 %collective-permute-start.5 = (bf16[96,384]{1,0:T(8,128)(2,1)S(1)}, bf16[96,384]{1,0:T(8,128)(2,1)S(1)}, u32[]{:S(2)}, u32[]{:S(2)}) collective-permute-start(bf16[96,384]{1,0:T(8,128)(2,1)S(1)} %get-tuple-element.104), channel_id=1, source_target_pairs={{0,4},{4,0},{8,12},{12,8},{16,20},{20,16},{24,28},{28,24},{1,5},{5... | collective-permute-start | bytes 221192 | tf_op jit(solution)/shard_map/ppermute | solution.py:955
  21.3 1.5 %collective-permute-start.10 = (bf16[256,768]{1,0:T(8,128)(2,1)S(1)}, bf16[256,768]{1,0:T(8,128)(2,1)S(1)}, u32[]{:S(2)}, u32[]{:S(2)}) collective-permute-start(bf16[256,768]{1,0:T(8,128)(2,1)S(1)} %get-tuple-element.110), channel_id=1, source_target_pairs={{0,2},{2,0},{1,3},{3,1},{4,6},{6,4},{5,7},{7,5},{8,10},{10,8},{9,1... | collective-permute-start | bytes 1179656 | tf_op jit(solution)/shard_map/ppermute | solution.py:956
  22.8 1.9 %collective-permute-done.5 = bf16[96,384]{1,0:T(8,128)(2,1)S(1)} collective-permute-done((bf16[96,384]{1,0:T(8,128)(2,1)S(1)}, bf16[96,384]{1,0:T(8,128)(2,1)S(1)}, u32[]{:S(2)}, u32[]{:S(2)}) %collective-permute-start.5) | collective-permute-done | bytes 73760 | tf_op jit(solution)/shard_map/ppermute | solution.py:955
  24.7 7.4 %collective-permute-done.4 = bf16[104,768]{1,0:T(8,128)(2,1)S(1)} collective-permute-done((bf16[104,768]{1,0:T(8,128)(2,1)S(1)}, bf16[104,768]{1,0:T(8,128)(2,1)S(1)}, u32[]{:S(2)}, u32[]{:S(2)}) %collective-permute-start.4) | collective-permute-done | bytes 159776 | tf_op jit(solution)/shard_map/ppermute | solution.py:954
  32.8 1.7 %collective-permute-start.8 = (bf16[96,768]{1,0:T(8,128)(2,1)S(1)}, bf16[96,768]{1,0:T(8,128)(2,1)S(1)}, u32[]{:S(2)}, u32[]{:S(2)}) collective-permute-start(bf16[96,768]{1,0:T(8,128)(2,1)S(1)} %pad_maximum_fusion.7), channel_id=1, source_target_pairs={{0,16},{4,20},{8,24},{12,28},{16,0},{20,4},{24,8},{28,12},{1,17},{... | collective-permute-start | bytes 442376 | tf_op jit(solution)/shard_map/ppermute | solution.py:965
  34.7 6.5 %collective-permute-done.8 = bf16[96,768]{1,0:T(8,128)(2,1)S(1)} collective-permute-done((bf16[96,768]{1,0:T(8,128)(2,1)S(1)}, bf16[96,768]{1,0:T(8,128)(2,1)S(1)}, u32[]{:S(2)}, u32[]{:S(2)}) %collective-permute-start.8) | collective-permute-done | bytes 147488 | tf_op jit(solution)/shard_map/ppermute | solution.py:965
  41.2 2.2 %collective-permute-done.6.refs_1_ = bf16[2,104,768]{2,1,0:T(8,128)(2,1)S(1)} collective-permute-done((bf16[2,104,768]{2,1,0:T(8,128)(2,1)S(1)}, bf16[2,104,768]{2,1,0:T(8,128)(2,1)S(1)}, u32[]{:S(2)}, u32[]{:S(2)}) %collective-permute-start.6) | collective-permute-done | bytes 319520 | tf_op jit(solution)/shard_map/ppermute | solution.py:959
  44.6 1.0 fusion.18
  45.7 0.9 collective-permute-start.9
  46.6 4.6 %collective-permute-done.12.refs_2_ = bf16[2,96,768]{2,1,0:T(8,128)(2,1)S(1)} collective-permute-done((bf16[2,96,768]{2,1,0:T(8,128)(2,1)S(1)}, bf16[2,96,768]{2,1,0:T(8,128)(2,1)S(1)}, u32[]{:S(2)}, u32[]{:S(2)}) %collective-permute-start.12) | collective-permute-done | bytes 294944 | tf_op jit(solution)/shard_map/ppermute | solution.py:953
  51.6 1.6 %collective-permute-done.21 = bf16[256,768]{1,0:T(8,128)(2,1)S(1)} collective-permute-done((bf16[256,768]{1,0:T(8,128)(2,1)S(1)}, bf16[256,768]{1,0:T(8,128)(2,1)S(1)}, u32[]{:S(2)}, u32[]{:S(2)}) %collective-permute-start.21) | collective-permute-done | bytes 393248 | tf_op jit(solution)/shard_map/ppermute | solution.py:972
  55.7 0.9 collective-permute-start.16
  57.3 1.7 %shard_map.257 = (bf16[512,768]{1,0:T(8,128)(2,1)S(1)}, bf16[512,384]{1,0:T(8,128)(2,1)S(1)}, bf16[512,192]{1,0:T(8,128)(2,1)S(1)}) custom-call(f32[512,768]{1,0:T(8,128)S(1)} %fusion.1.unit.refs_1_.refs_9_, bf16[768,768]{1,0:T(8,128)(2,1)S(1)} %get-tuple-element.114.weights.refs_8_, f32[8,768]{1,0:T(8,128)S(1)} %get-tuple-element.112.vectors.refs_7_.refs_3_.refs_10_, ...), custom_call_target="tpu_custom_call" | custom-call | flops 603979776 | bytes 3563520 | tf_op jit(solution)/shard_map/pallas_call | solution.py:415
  59.8 6.2 %shard_map.258 = (bf16[48,512]{1,0:T(8,128)(2,1)S(1)}, bf16[48,512]{1,0:T(8,128)(2,1)S(1)}, bf16[48,512]{1,0:T(8,128)(2,1)S(1)}, bf16[48,512]{1,0:T(8,128)(2,1)S(1)}, bf16[512,768]{1,0:T(8,128)(2,1)S(1)}) custom-call(bf16[2,96,768]{2,1,0:T(8,128)(2,1)S(1)} %collective-permute-done.13.refs_0_.refs_4_, bf16[512,384]{1,0:T(8,128)(2,1)S(1)} %get-tuple-element.115.refs_1_, ...), custom_call_target="tpu_custom_call" | custom-call | flops 704643072 | bytes 1871872 | tf_op jit(solution)/shard_map/pallas_call | solution.py:415
  66.4 1.3 collective-permute-start.18
  69.4 4.4 %shard_map.259 = (bf16[2,128,1536]{2,1,0:T(8,128)(2,1)S(1)}, bf16[2,128,1536]{2,1,0:T(8,128)(2,1)S(1)}, bf16[512,768]{1,0:T(8,128)(2,1)S(1)}, bf16[512,384]{1,0:...) custom-call(bf16[512,768]{1,0:T(8,128)(2,1)S(1)} %get-tuple-element., ...), custom_call_target="tpu_custom_call" | custom-call | flops 1207959552 | bytes 4349952 | tf_op jit(solution)/shard_map/pallas_call | solution.py:415
  73.8 3.4 %shard_map.260 = (bf16[4,128,1536]{2,1,0:T(8,128)(2,1)S(1)}, bf16[512,768]{1,0:T(8,128)(2,1)S(1)}, bf16[512,384]{1,0:T(8,128)(2,1)S(1)}, bf16[512,384]{1,0:T(8,128)(2,1)S(1)}, f32[8,768]{1,0:T(8,128)S(1)}) custom-call(bf16[512,768]{1,0:T(8,128)(2,1)S(1)} %get-tuple-element.127.refs_0_.refs_7_, f32[512,768]{1,0:T(8,128)S(1)} %fusion.1.unit.refs_1_.refs_9_, ...), custom_call_target="tpu_custom_call" | custom-call | flops 1207959552 | bytes 4349952 | tf_op jit(solution)/shard_map/pallas_call | solution.py:415
  77.3 5.2 %shard_map.261 = (bf16[4,104,768]{2,1,0:T(8,128)(2,1)S(1)}, bf16[4,104,768]{2,1,0:T(8,128)(2,1)S(1)}, bf16[2,128,1536]{2,1,0:T(8,128)(2,1)}, bf16[2,128,1536]{2,1,0:T(8,128)(2,1)S(1)}) custom-call(bf16[48,512]{1,0:T(8,128)(2,1)S(1)} %get-tuple-element.121.refs_0_, bf16[48,512]{1,0:T(8,128)(2,1)S(1)} %collective-permute-done.17.refs_1_, ...), custom_call_target="tpu_custom_call" | custom-call | flops 1509949440 | bytes 7200768 | tf_op jit(solution)/shard_map/pallas_call | solution.py:415
  82.5 1.8 %shard_map.262 = (bf16[2,104,768]{2,1,0:T(8,128)(2,1)S(1)}, bf16[2,104,768]{2,1,0:T(8,128)(2,1)S(1)}, bf16[2,96,768]{2,1,0:T(8,128)(2,1)S(1)}, bf16[2,96,768]{2,1,0:T(8,128)(2,1)S(1)}) custom-call(bf16[4,104,768]{2,1,0:T(8,128)(2,1)S(1)} %get-tuple-element.137.refs_0_, bf16[512,768]{1,0:T(8,128)(2,1)S(1)} %get-tuple-element.138.refs_1_, ...), custom_call_target="tpu_custom_call" | custom-call | flops 1207959552 | bytes 5406720 | tf_op jit(solution)/shard_map/pallas_call | solution.py:415
  85.1 1.6 %collective-permute-start.27 = (bf16[2,96,768]{2,1,0:T(8,128)(2,1)S(1)}, bf16[2,96,768]{2,1,0:T(8,128)(2,1)S(1)}, u32[]{:S(2)}, u32[]{:S(2)}) collective-permute-start(bf16[2,96,768]{2,1,0:T(8,128)(2,1)S(1)} %get-tuple-element.149), channel_id=1, source_target_pairs={{0,8},{4,12},{8,0},{12,4},{16,24},{20,28},{24,16},{28,20},{1,9},{5... | collective-permute-start | bytes 884744 | tf_op jit(solution)/shard_map/ppermute | solution.py:1068
  87.2 1.1 add_convert_fusion
  88.3 6.7 %collective-permute-done.27.refs_1_ = bf16[2,96,768]{2,1,0:T(8,128)(2,1)S(1)} collective-permute-done((bf16[2,96,768]{2,1,0:T(8,128)(2,1)S(1)}, bf16[2,96,768]{2,1,0:T(8,128)(2,1)S(1)}, u32[]{:S(2)}, u32[]{:S(2)}) %collective-permute-start.27) | collective-permute-done | bytes 294944 | tf_op jit(solution)/shard_map/ppermute | solution.py:1068
  95.0 5.9 %collective-permute-done.26.refs_1_ = bf16[2,104,768]{2,1,0:T(8,128)(2,1)S(1)} collective-permute-done((bf16[2,104,768]{2,1,0:T(8,128)(2,1)S(1)}, bf16[2,104,768]{2,1,0:T(8,128)(2,1)S(1)}, u32[]{:S(2)}, u32[]{:S(2)}) %collective-permute-start.26) | collective-permute-done | bytes 319520 | tf_op jit(solution)/shard_map/ppermute | solution.py:1067
  101.3 1.2 collective-permute-start.28
  103.5 1.8 %collective-permute-start.31 = (bf16[1,104,768]{2,1,0:T(8,128)(2,1)S(1)}, bf16[1,104,768]{2,1,0:T(8,128)(2,1)S(1)}, u32[]{:S(2)}, u32[]{:S(2)}) collective-permute-start(bf16[1,104,768]{2,1,0:T(8,128)(2,1)S(1)} %get-tuple-element.156), channel_id=1, source_target_pairs={{0,16},{4,20},{8,24},{12,28},{16,0},{20,4},{24,8},{28,12},{1,17},{... | collective-permute-start | bytes 479240 | tf_op jit(solution)/shard_map/ppermute | solution.py:1073
  106.8 2.1 %collective-permute-start.40 = (bf16[1,96,768]{2,1,0:T(8,128)(2,1)}, bf16[1,96,768]{2,1,0:T(8,128)(2,1)S(1)}, u32[]{:S(2)}, u32[]{:S(2)}) collective-permute-start(bf16[1,96,768]{2,1,0:T(8,128)(2,1)} %get-tuple-element.179), channel_id=1, source_target_pairs={{0,16},{4,20},{8,24},{12,28},{16,0},{20,4},{24,8},{28,12},{1,17},{... | collective-permute-start | bytes 442376 | tf_op jit(solution)/shard_map/ppermute | solution.py:1077
  108.9 4.8 %collective-permute-done.31.refs_2_.refs_0_ = bf16[1,104,768]{2,1,0:T(8,128)(2,1)S(1)} collective-permute-done((bf16[1,104,768]{2,1,0:T(8,128)(2,1)S(1)}, bf16[1,104,768]{2,1,0:T(8,128)(2,1)S(1)}, u32[]{:S(2)}, u32[]{:S(2)}) %collective-permute-start.31) | collective-permute-done | bytes 159776 | tf_op jit(solution)/shard_map/ppermute | solution.py:1073
  113.7 5.4 %collective-permute-done.30.refs_0_.refs_2_ = bf16[2,104,768]{2,1,0:T(8,128)(2,1)S(1)} collective-permute-done((bf16[2,104,768]{2,1,0:T(8,128)(2,1)}, bf16[2,104,768]{2,1,0:T(8,128)(2,1)S(1)}, u32[]{:S(2)}, u32[]{:S(2)}) %collective-permute-start.30) | collective-permute-done | bytes 319520 | tf_op jit(solution)/shard_map/ppermute | solution.py:1075
  119.3 1.0 collective-permute-done.28
  120.3 1.6 %convert_add_fusion = f32[2,128,1536]{2,1,0:T(8,128)S(1)} fusion(bf16[2,128,1536]{2,1,0:T(8,128)(2,1)} %collective-permute-done.28, bf16[2,128,1536]{2,1,0:T(8,128)(2,1)} %collective-permute-done.23, bf16[2,128,1536]{2,1,0:T(8,128)(2,1)S(1)} %get-tuple-element.133), kind=kLoop, calls=%fused_computation.6 | loop fusion | flops 1966080 | bytes 3932160 | tf_op jit(solution)/shard_map/add | solution.py:1082
  122.0 1.2 copy-done.9
  123.2 1.5 %collective-permute-start.29 = (bf16[128,1536]{1,0:T(8,128)(2,1)S(1)}, bf16[128,1536]{1,0:T(8,128)(2,1)S(1)}, u32[]{:S(2)}, u32[]{:S(2)}) collective-permute-start(bf16[128,1536]{1,0:T(8,128)(2,1)S(1)} %fusion.17), channel_id=1, source_target_pairs={{0,2},{2,0},{1,3},{3,1},{4,6},{6,4},{5,7},{7,5},{8,10},{10,8},{9,1... | collective-permute-start | bytes 1179656 | tf_op jit(solution)/shard_map/ppermute | solution.py:1083
  124.7 1.0 collective-permute-start.32
  125.7 3.6 %collective-permute-done.32.refs_0_.refs_2_ = bf16[112,384]{1,0:T(8,128)(2,1)S(1)} collective-permute-done((bf16[112,384]{1,0:T(8,128)(2,1)S(1)}, bf16[112,384]{1,0:T(8,128)(2,1)S(1)}, u32[]{:S(2)}, u32[]{:S(2)}) %collective-permute-start.32) | collective-permute-done | bytes 86048 | tf_op jit(solution)/shard_map/ppermute | solution.py:1104
  130.1 1.2 collective-permute-start.39
  134.6 0.9 shard_map.270
  136.6 0.8 collective-permute-done.35.refs_3_
  138.0 0.9 shard_map.268
  140.2 0.9 fusion.12
  (133 shorter events, 25.3 us)
Async XLA Ops:
  2.3 0.9 copy-start.2
  6.0 9.3 %collective-permute-start = (bf16[56,768]{1,0:T(8,128)(2,1)S(1)}, bf16[56,768]{1,0:T(8,128)(2,1)S(1)}, u32[]{:S(2)}, u32[]{:S(2)}) collective-permute-start(bf16[56,768]{1,0:T(8,128)(2,1)S(1)} %get-tuple-element.98), channel_id=1, source_target_pairs={{0,1},{1,0},{2,3},{3,2},{4,5},{5,4},{6,7},{7,6},{8,9},{9,8},{10,11... | collective-permute-start | bytes 258056 | tf_op jit(solution)/shard_map/ppermute | solution.py:485
  6.5 8.8 %collective-permute-start.1 = (bf16[56,768]{1,0:T(8,128)(2,1)S(1)}, bf16[56,768]{1,0:T(8,128)(2,1)S(1)}, u32[]{:S(2)}, u32[]{:S(2)}) collective-permute-start(bf16[56,768]{1,0:T(8,128)(2,1)S(1)} %get-tuple-element.99), channel_id=1, source_target_pairs={{0,2},{1,3},{2,0},{3,1},{4,6},{5,7},{6,4},{7,5},{8,10},{9,11},{10,... | collective-permute-start | bytes 258056 | tf_op jit(solution)/shard_map/ppermute | solution.py:485
  9.1 6.2 %collective-permute-start.2 = (bf16[56,768]{1,0:T(8,128)(2,1)S(1)}, bf16[56,768]{1,0:T(8,128)(2,1)S(1)}, u32[]{:S(2)}, u32[]{:S(2)}) collective-permute-start(bf16[56,768]{1,0:T(8,128)(2,1)S(1)} %get-tuple-element.100), channel_id=1, source_target_pairs={{0,3},{1,2},{2,1},{3,0},{4,7},{5,6},{6,5},{7,4},{8,11},{9,10},{10,... | collective-permute-start | bytes 258056 | tf_op jit(solution)/shard_map/ppermute | solution.py:485
  9.1 10.6 %collective-permute-start.3 = (bf16[96,768]{1,0:T(8,128)(2,1)}, bf16[96,768]{1,0:T(8,128)(2,1)S(1)}, u32[]{:S(2)}, u32[]{:S(2)}) collective-permute-start(bf16[96,768]{1,0:T(8,128)(2,1)} %param.28), channel_id=1, source_target_pairs={{0,16},{4,20},{8,24},{12,28},{16,0},{20,4},{24,8},{28,12},{1,17},{... | collective-permute-start | bytes 442376 | tf_op jit(solution)/shard_map/ppermute | solution.py:950
  12.0 22.7 %collective-permute-start.20 = (bf16[256,768]{1,0:T(8,128)(2,1)S(1)}, bf16[256,768]{1,0:T(8,128)(2,1)S(1)}, u32[]{:S(2)}, u32[]{:S(2)}) collective-permute-start(bf16[256,768]{1,0:T(8,128)(2,1)S(1)} %get-tuple-element.110), channel_id=1, source_target_pairs={{0,4},{4,0},{8,12},{12,8},{16,20},{20,16},{24,28},{28,24},{1,5},{5... | collective-permute-start | bytes 1179656 | tf_op jit(solution)/shard_map/ppermute | solution.py:949
  19.7 4.9 %collective-permute-start.5 = (bf16[96,384]{1,0:T(8,128)(2,1)S(1)}, bf16[96,384]{1,0:T(8,128)(2,1)S(1)}, u32[]{:S(2)}, u32[]{:S(2)}) collective-permute-start(bf16[96,384]{1,0:T(8,128)(2,1)S(1)} %get-tuple-element.104), channel_id=1, source_target_pairs={{0,4},{4,0},{8,12},{12,8},{16,20},{20,16},{24,28},{28,24},{1,5},{5... | collective-permute-start | bytes 221192 | tf_op jit(solution)/shard_map/ppermute | solution.py:955
  21.3 13.2 %collective-permute-start.10 = (bf16[256,768]{1,0:T(8,128)(2,1)S(1)}, bf16[256,768]{1,0:T(8,128)(2,1)S(1)}, u32[]{:S(2)}, u32[]{:S(2)}) collective-permute-start(bf16[256,768]{1,0:T(8,128)(2,1)S(1)} %get-tuple-element.110), channel_id=1, source_target_pairs={{0,2},{2,0},{1,3},{3,1},{4,6},{6,4},{5,7},{7,5},{8,10},{10,8},{9,1... | collective-permute-start | bytes 1179656 | tf_op jit(solution)/shard_map/ppermute | solution.py:956
  22.8 9.3 %collective-permute-start.4 = (bf16[104,768]{1,0:T(8,128)(2,1)S(1)}, bf16[104,768]{1,0:T(8,128)(2,1)S(1)}, u32[]{:S(2)}, u32[]{:S(2)}) collective-permute-start(bf16[104,768]{1,0:T(8,128)(2,1)S(1)} %get-tuple-element.102), channel_id=1, source_target_pairs={{0,16},{4,20},{8,24},{12,28},{16,0},{20,4},{24,8},{28,12},{1,17},{... | collective-permute-start | bytes 479240 | tf_op jit(solution)/shard_map/ppermute | solution.py:954
  32.1 11.8 %copy-start.11 = (bf16[96,768]{1,0:T(8,128)(2,1)S(1)}, bf16[96,768]{1,0:T(8,128)(2,1)}, u32[]{:S(2)}) copy-start(bf16[96,768]{1,0:T(8,128)(2,1)} %param.28) | copy-start | bytes 442372
  32.1 11.3 %collective-permute-start.6 = (bf16[2,104,768]{2,1,0:T(8,128)(2,1)S(1)}, bf16[2,104,768]{2,1,0:T(8,128)(2,1)S(1)}, u32[]{:S(2)}, u32[]{:S(2)}) collective-permute-start(bf16[2,104,768]{2,1,0:T(8,128)(2,1)S(1)} %pad_maximum_fusion.4.refs_0_), channel_id=1, source_target_pairs={{0,8},{4,12},{8,0},{12,4},{16,24},{20,28},{24,16},{28,20},{1,9},{5... | collective-permute-start | bytes 958472 | tf_op jit(solution)/shard_map/ppermute | solution.py:959
  32.2 11.2 %collective-permute-start.7 = (bf16[2,104,768]{2,1,0:T(8,128)(2,1)S(1)}, bf16[2,104,768]{2,1,0:T(8,128)(2,1)S(1)}, u32[]{:S(2)}, u32[]{:S(2)}) collective-permute-start(bf16[2,104,768]{2,1,0:T(8,128)(2,1)S(1)} %pad_maximum_fusion.4.refs_0_), channel_id=1, source_target_pairs={{0,4},{4,0},{8,12},{12,8},{16,20},{20,16},{24,28},{28,24},{1,5},{5... | collective-permute-start | bytes 958472 | tf_op jit(solution)/shard_map/ppermute | solution.py:960
  32.8 8.4 %collective-permute-start.8 = (bf16[96,768]{1,0:T(8,128)(2,1)S(1)}, bf16[96,768]{1,0:T(8,128)(2,1)S(1)}, u32[]{:S(2)}, u32[]{:S(2)}) collective-permute-start(bf16[96,768]{1,0:T(8,128)(2,1)S(1)} %pad_maximum_fusion.7), channel_id=1, source_target_pairs={{0,16},{4,20},{8,24},{12,28},{16,0},{20,4},{24,8},{28,12},{1,17},{... | collective-permute-start | bytes 442376 | tf_op jit(solution)/shard_map/ppermute | solution.py:965
  34.6 18.7 %collective-permute-start.11 = (bf16[2,256,768]{2,1,0:T(8,128)(2,1)S(1)}, bf16[2,256,768]{2,1,0:T(8,128)(2,1)S(1)}, u32[]{:S(2)}, u32[]{:S(2)}) collective-permute-start(bf16[2,256,768]{2,1,0:T(8,128)(2,1)S(1)} %pad_maximum_fusion.2), channel_id=1, source_target_pairs={{0,1},{1,0},{2,3},{3,2},{4,5},{5,4},{6,7},{7,6},{8,9},{9,8},{10,11... | collective-permute-start | bytes 2359304 | tf_op jit(solution)/shard_map/ppermute | solution.py:967
  43.4 9.8 %collective-permute-start.21 = (bf16[256,768]{1,0:T(8,128)(2,1)S(1)}, bf16[256,768]{1,0:T(8,128)(2,1)S(1)}, u32[]{:S(2)}, u32[]{:S(2)}) collective-permute-start(bf16[256,768]{1,0:T(8,128)(2,1)S(1)} %collective-permute-done.20), channel_id=1, source_target_pairs={{0,2},{2,0},{1,3},{3,1},{4,6},{6,4},{5,7},{7,5},{8,10},{10,8},{9,1... | collective-permute-start | bytes 1179656 | tf_op jit(solution)/shard_map/ppermute | solution.py:972
  44.0 7.2 %collective-permute-start.12 = (bf16[2,96,768]{2,1,0:T(8,128)(2,1)S(1)}, bf16[2,96,768]{2,1,0:T(8,128)(2,1)S(1)}, u32[]{:S(2)}, u32[]{:S(2)}) collective-permute-start(bf16[2,96,768]{2,1,0:T(8,128)(2,1)S(1)} %pad_maximum_fusion.6.refs_1_), channel_id=1, source_target_pairs={{0,8},{4,12},{8,0},{12,4},{16,24},{20,28},{24,16},{28,20},{1,9},{5... | collective-permute-start | bytes 884744 | tf_op jit(solution)/shard_map/ppermute | solution.py:953
  45.7 8.4 %collective-permute-start.9 = (bf16[2,104,768]{2,1,0:T(8,128)(2,1)S(1)}, bf16[2,104,768]{2,1,0:T(8,128)(2,1)S(1)}, u32[]{:S(2)}, u32[]{:S(2)}) collective-permute-start(bf16[2,104,768]{2,1,0:T(8,128)(2,1)S(1)} %collective-permute-done.6.refs_1_), channel_id=1, source_target_pairs={{0,4},{4,0},{8,12},{12,8},{16,20},{20,16},{24,28},{28,24},{1,5},{5... | collective-permute-start | bytes 958472 | tf_op jit(solution)/shard_map/ppermute | solution.py:969
  51.2 7.8 %collective-permute-start.13 = (bf16[2,96,768]{2,1,0:T(8,128)(2,1)S(1)}, bf16[2,96,768]{2,1,0:T(8,128)(2,1)S(1)}, u32[]{:S(2)}, u32[]{:S(2)}) collective-permute-start(bf16[2,96,768]{2,1,0:T(8,128)(2,1)S(1)} %pad_maximum_fusion.5.refs_3_), channel_id=1, source_target_pairs={{0,8},{4,12},{8,0},{12,4},{16,24},{20,28},{24,16},{28,20},{1,9},{5... | collective-permute-start | bytes 884744 | tf_op jit(solution)/shard_map/ppermute | solution.py:971
  54.7 13.3 %collective-permute-start.22 = (bf16[2,256,768]{2,1,0:T(8,128)(2,1)S(1)}, bf16[2,256,768]{2,1,0:T(8,128)(2,1)S(1)}, u32[]{:S(2)}, u32[]{:S(2)}) collective-permute-start(bf16[2,256,768]{2,1,0:T(8,128)(2,1)S(1)} %pad_maximum_fusion.3), channel_id=1, source_target_pairs={{0,1},{1,0},{2,3},{3,2},{4,5},{5,4},{6,7},{7,6},{8,9},{9,8},{10,11... | collective-permute-start | bytes 2359304 | tf_op jit(solution)/shard_map/ppermute | solution.py:1007
  54.8 4.3 %collective-permute-start.14 = (bf16[48,512]{1,0:T(8,128)(2,1)S(1)}, bf16[48,512]{1,0:T(8,128)(2,1)S(1)}, u32[]{:S(2)}, u32[]{:S(2)}) collective-permute-start(bf16[48,512]{1,0:T(8,128)(2,1)S(1)} %get-tuple-element.118), channel_id=1, source_target_pairs={{0,1},{1,0},{2,3},{3,2},{4,5},{5,4},{6,7},{7,6},{8,9},{9,8},{10,11... | collective-permute-start | bytes 147464 | tf_op jit(solution)/shard_map/ppermute | solution.py:485
  55.2 4.5 %collective-permute-start.15 = (bf16[48,512]{1,0:T(8,128)(2,1)S(1)}, bf16[48,512]{1,0:T(8,128)(2,1)S(1)}, u32[]{:S(2)}, u32[]{:S(2)}) collective-permute-start(bf16[48,512]{1,0:T(8,128)(2,1)S(1)} %get-tuple-element.119), channel_id=1, source_target_pairs={{0,2},{1,3},{2,0},{3,1},{4,6},{5,7},{6,4},{7,5},{8,10},{9,11},{10,... | collective-permute-start | bytes 147464 | tf_op jit(solution)/shard_map/ppermute | solution.py:485
  55.7 4.0 %collective-permute-start.16 = (bf16[48,512]{1,0:T(8,128)(2,1)S(1)}, bf16[48,512]{1,0:T(8,128)(2,1)S(1)}, u32[]{:S(2)}, u32[]{:S(2)}) collective-permute-start(bf16[48,512]{1,0:T(8,128)(2,1)S(1)} %get-tuple-element.120), channel_id=1, source_target_pairs={{0,3},{1,2},{2,1},{3,0},{4,7},{5,6},{6,5},{7,4},{8,11},{9,10},{10,... | collective-permute-start | bytes 147464 | tf_op jit(solution)/shard_map/ppermute | solution.py:485
  66.0 11.2 %collective-permute-start.17 = (bf16[48,512]{1,0:T(8,128)(2,1)S(1)}, bf16[48,512]{1,0:T(8,128)(2,1)S(1)}, u32[]{:S(2)}, u32[]{:S(2)}) collective-permute-start(bf16[48,512]{1,0:T(8,128)(2,1)S(1)} %get-tuple-element.122), channel_id=1, source_target_pairs={{0,1},{1,0},{2,3},{3,2},{4,5},{5,4},{6,7},{7,6},{8,9},{9,8},{10,11... | collective-permute-start | bytes 147464 | tf_op jit(solution)/shard_map/ppermute | solution.py:485
  66.4 10.8 %collective-permute-start.18 = (bf16[48,512]{1,0:T(8,128)(2,1)S(1)}, bf16[48,512]{1,0:T(8,128)(2,1)S(1)}, u32[]{:S(2)}, u32[]{:S(2)}) collective-permute-start(bf16[48,512]{1,0:T(8,128)(2,1)S(1)} %get-tuple-element.123), channel_id=1, source_target_pairs={{0,2},{1,3},{2,0},{3,1},{4,6},{5,7},{6,4},{7,5},{8,10},{9,11},{10,... | collective-permute-start | bytes 147464 | tf_op jit(solution)/shard_map/ppermute | solution.py:485
  67.7 9.6 %collective-permute-start.19 = (bf16[48,512]{1,0:T(8,128)(2,1)S(1)}, bf16[48,512]{1,0:T(8,128)(2,1)S(1)}, u32[]{:S(2)}, u32[]{:S(2)}) collective-permute-start(bf16[48,512]{1,0:T(8,128)(2,1)S(1)} %get-tuple-element.124), channel_id=1, source_target_pairs={{0,3},{1,2},{2,1},{3,0},{4,7},{5,6},{6,5},{7,4},{8,11},{9,10},{10,... | collective-permute-start | bytes 147464 | tf_op jit(solution)/shard_map/ppermute | solution.py:485
  84.2 18.3 %copy-start.1 = (bf16[128,768]{1,0:T(8,128)(2,1)S(1)}, bf16[128,768]{1,0:T(8,128)(2,1)}, u32[]{:S(2)}) copy-start(bf16[128,768]{1,0:T(8,128)(2,1)} %refs_4_.1) | copy-start | bytes 589828
  84.3 2.9 %collective-permute-start.24 = (bf16[2,128,1536]{2,1,0:T(8,128)(2,1)S(1)}, bf16[2,128,1536]{2,1,0:T(8,128)(2,1)S(1)}, u32[]{:S(2)}, u32[]{:S(2)}) collective-permute-start(bf16[2,128,1536]{2,1,0:T(8,128)(2,1)S(1)} %get-tuple-element.147), channel_id=1, source_target_pairs={{0,1},{1,0},{2,3},{3,2},{4,5},{5,4},{6,7},{7,6},{8,9},{9,8},{10,11... | collective-permute-start | bytes 2359304 | tf_op jit(solution)/shard_map/ppermute | solution.py:1069
  85.0 16.4 %collective-permute-start.25 = (bf16[4,104,768]{2,1,0:T(8,128)(2,1)S(1)}, bf16[4,104,768]{2,1,0:T(8,128)(2,1)S(1)}, u32[]{:S(2)}, u32[]{:S(2)}) collective-permute-start(bf16[4,104,768]{2,1,0:T(8,128)(2,1)S(1)} %get-tuple-element.137.refs_0_), channel_id=1, source_target_pairs={{0,4},{4,0},{8,12},{12,8},{16,20},{20,16},{24,28},{28,24},{1,5},{5... | collective-permute-start | bytes 1916936 | tf_op jit(solution)/shard_map/ppermute | solution.py:1066
  85.1 9.9 %collective-permute-start.27 = (bf16[2,96,768]{2,1,0:T(8,128)(2,1)S(1)}, bf16[2,96,768]{2,1,0:T(8,128)(2,1)S(1)}, u32[]{:S(2)}, u32[]{:S(2)}) collective-permute-start(bf16[2,96,768]{2,1,0:T(8,128)(2,1)S(1)} %get-tuple-element.149), channel_id=1, source_target_pairs={{0,8},{4,12},{8,0},{12,4},{16,24},{20,28},{24,16},{28,20},{1,9},{5... | collective-permute-start | bytes 884744 | tf_op jit(solution)/shard_map/ppermute | solution.py:1068
  86.7 14.2 %collective-permute-start.26 = (bf16[2,104,768]{2,1,0:T(8,128)(2,1)S(1)}, bf16[2,104,768]{2,1,0:T(8,128)(2,1)S(1)}, u32[]{:S(2)}, u32[]{:S(2)}) collective-permute-start(bf16[2,104,768]{2,1,0:T(8,128)(2,1)S(1)} %get-tuple-element.148), channel_id=1, source_target_pairs={{0,8},{4,12},{8,0},{12,4},{16,24},{20,28},{24,16},{28,20},{1,9},{5... | collective-permute-start | bytes 958472 | tf_op jit(solution)/shard_map/ppermute | solution.py:1067
  87.2 32.1 %collective-permute-start.23 = (bf16[2,128,1536]{2,1,0:T(8,128)(2,1)}, bf16[2,128,1536]{2,1,0:T(8,128)(2,1)}, u32[]{:S(2)}, u32[]{:S(2)}) collective-permute-start(bf16[2,128,1536]{2,1,0:T(8,128)(2,1)} %get-tuple-element.134), channel_id=1, source_target_pairs={{0,1},{1,0},{2,3},{3,2},{4,5},{5,4},{6,7},{7,6},{8,9},{9,8},{10,11... | collective-permute-start | bytes 2359304 | tf_op jit(solution)/shard_map/ppermute | solution.py:1082
  101.3 19.0 %collective-permute-start.28 = (bf16[2,128,1536]{2,1,0:T(8,128)(2,1)}, bf16[2,128,1536]{2,1,0:T(8,128)(2,1)}, u32[]{:S(2)}, u32[]{:S(2)}) collective-permute-start(bf16[2,128,1536]{2,1,0:T(8,128)(2,1)} %add_convert_fusion), channel_id=1, source_target_pairs={{0,4},{4,0},{8,12},{12,8},{16,20},{20,16},{24,28},{28,24},{1,5},{5... | collective-permute-start | bytes 2359304 | tf_op jit(solution)/shard_map/ppermute | solution.py:1078
  103.5 10.2 %collective-permute-start.31 = (bf16[1,104,768]{2,1,0:T(8,128)(2,1)S(1)}, bf16[1,104,768]{2,1,0:T(8,128)(2,1)S(1)}, u32[]{:S(2)}, u32[]{:S(2)}) collective-permute-start(bf16[1,104,768]{2,1,0:T(8,128)(2,1)S(1)} %get-tuple-element.156), channel_id=1, source_target_pairs={{0,16},{4,20},{8,24},{12,28},{16,0},{20,4},{24,8},{28,12},{1,17},{... | collective-permute-start | bytes 479240 | tf_op jit(solution)/shard_map/ppermute | solution.py:1073
  105.4 13.7 %collective-permute-start.30 = (bf16[2,104,768]{2,1,0:T(8,128)(2,1)}, bf16[2,104,768]{2,1,0:T(8,128)(2,1)S(1)}, u32[]{:S(2)}, u32[]{:S(2)}) collective-permute-start(bf16[2,104,768]{2,1,0:T(8,128)(2,1)} %get-tuple-element.153), channel_id=1, source_target_pairs={{0,8},{4,12},{8,0},{12,4},{16,24},{20,28},{24,16},{28,20},{1,9},{5... | collective-permute-start | bytes 958472 | tf_op jit(solution)/shard_map/ppermute | solution.py:1075
  106.8 24.5 %collective-permute-start.40 = (bf16[1,96,768]{2,1,0:T(8,128)(2,1)}, bf16[1,96,768]{2,1,0:T(8,128)(2,1)S(1)}, u32[]{:S(2)}, u32[]{:S(2)}) collective-permute-start(bf16[1,96,768]{2,1,0:T(8,128)(2,1)} %get-tuple-element.179), channel_id=1, source_target_pairs={{0,16},{4,20},{8,24},{12,28},{16,0},{20,4},{24,8},{28,12},{1,17},{... | collective-permute-start | bytes 442376 | tf_op jit(solution)/shard_map/ppermute | solution.py:1077
  119.2 10.1 %collective-permute-start.33 = (bf16[1,104,768]{2,1,0:T(8,128)(2,1)S(1)}, bf16[1,104,768]{2,1,0:T(8,128)(2,1)S(1)}, u32[]{:S(2)}, u32[]{:S(2)}) collective-permute-start(bf16[1,104,768]{2,1,0:T(8,128)(2,1)S(1)} %get-tuple-element.160), channel_id=1, source_target_pairs={{0,16},{4,20},{8,24},{12,28},{16,0},{20,4},{24,8},{28,12},{1,17},{... | collective-permute-start | bytes 479240 | tf_op jit(solution)/shard_map/ppermute | solution.py:1080
  122.0 1.2 copy-start.9
  123.2 11.4 %collective-permute-start.29 = (bf16[128,1536]{1,0:T(8,128)(2,1)S(1)}, bf16[128,1536]{1,0:T(8,128)(2,1)S(1)}, u32[]{:S(2)}, u32[]{:S(2)}) collective-permute-start(bf16[128,1536]{1,0:T(8,128)(2,1)S(1)} %fusion.17), channel_id=1, source_target_pairs={{0,2},{2,0},{1,3},{3,1},{4,6},{6,4},{5,7},{7,5},{8,10},{10,8},{9,1... | collective-permute-start | bytes 1179656 | tf_op jit(solution)/shard_map/ppermute | solution.py:1083
  124.7 15.2 %copy-start.10 = (f32[2,128,1536]{2,1,0:T(8,128)S(1)}, f32[2,128,1536]{2,1,0:T(8,128)}, u32[]{:S(2)}) copy-start(f32[2,128,1536]{2,1,0:T(8,128)} %copy-done.9) | copy-start | bytes 4718596
  124.7 4.6 %collective-permute-start.32 = (bf16[112,384]{1,0:T(8,128)(2,1)S(1)}, bf16[112,384]{1,0:T(8,128)(2,1)S(1)}, u32[]{:S(2)}, u32[]{:S(2)}) collective-permute-start(bf16[112,384]{1,0:T(8,128)(2,1)S(1)} %get-tuple-element.157), channel_id=1, source_target_pairs={{0,4},{4,0},{8,12},{12,8},{16,20},{20,16},{24,28},{28,24},{1,5},{5... | collective-permute-start | bytes 258056 | tf_op jit(solution)/shard_map/ppermute | solution.py:1104
  129.3 3.8 %collective-permute-start.37 = (bf16[32,768]{1,0:T(8,128)(2,1)S(1)}, bf16[32,768]{1,0:T(8,128)(2,1)S(1)}, u32[]{:S(2)}, u32[]{:S(2)}) collective-permute-start(bf16[32,768]{1,0:T(8,128)(2,1)S(1)} %get-tuple-element.169), channel_id=1, source_target_pairs={{0,1},{1,0},{2,3},{3,2},{4,5},{5,4},{6,7},{7,6},{8,9},{9,8},{10,11... | collective-permute-start | bytes 147464 | tf_op jit(solution)/shard_map/ppermute | solution.py:485
  129.4 4.6 %collective-permute-start.38 = (bf16[32,768]{1,0:T(8,128)(2,1)S(1)}, bf16[32,768]{1,0:T(8,128)(2,1)S(1)}, u32[]{:S(2)}, u32[]{:S(2)}) collective-permute-start(bf16[32,768]{1,0:T(8,128)(2,1)S(1)} %get-tuple-element.170), channel_id=1, source_target_pairs={{0,2},{1,3},{2,0},{3,1},{4,6},{5,7},{6,4},{7,5},{8,10},{9,11},{10,... | collective-permute-start | bytes 147464 | tf_op jit(solution)/shard_map/ppermute | solution.py:485
  130.1 4.5 %collective-permute-start.39 = (bf16[32,768]{1,0:T(8,128)(2,1)S(1)}, bf16[32,768]{1,0:T(8,128)(2,1)S(1)}, u32[]{:S(2)}, u32[]{:S(2)}) collective-permute-start(bf16[32,768]{1,0:T(8,128)(2,1)S(1)} %get-tuple-element.171), channel_id=1, source_target_pairs={{0,3},{1,2},{2,1},{3,0},{4,7},{5,6},{6,5},{7,4},{8,11},{9,10},{10,... | collective-permute-start | bytes 147464 | tf_op jit(solution)/shard_map/ppermute | solution.py:485
  132.8 3.9 %collective-permute-start.34 = (bf16[32,768]{1,0:T(8,128)(2,1)S(1)}, bf16[32,768]{1,0:T(8,128)(2,1)S(1)}, u32[]{:S(2)}, u32[]{:S(2)}) collective-permute-start(bf16[32,768]{1,0:T(8,128)(2,1)S(1)} %get-tuple-element.162), channel_id=1, source_target_pairs={{0,1},{1,0},{2,3},{3,2},{4,5},{5,4},{6,7},{7,6},{8,9},{9,8},{10,11... | collective-permute-start | bytes 147464 | tf_op jit(solution)/shard_map/ppermute | solution.py:485
  133.1 4.4 %collective-permute-start.35 = (bf16[32,768]{1,0:T(8,128)(2,1)S(1)}, bf16[32,768]{1,0:T(8,128)(2,1)S(1)}, u32[]{:S(2)}, u32[]{:S(2)}) collective-permute-start(bf16[32,768]{1,0:T(8,128)(2,1)S(1)} %get-tuple-element.163), channel_id=1, source_target_pairs={{0,2},{1,3},{2,0},{3,1},{4,6},{5,7},{6,4},{7,5},{8,10},{9,11},{10,... | collective-permute-start | bytes 147464 | tf_op jit(solution)/shard_map/ppermute | solution.py:485
  134.0 3.9 %collective-permute-start.36 = (bf16[32,768]{1,0:T(8,128)(2,1)S(1)}, bf16[32,768]{1,0:T(8,128)(2,1)S(1)}, u32[]{:S(2)}, u32[]{:S(2)}) collective-permute-start(bf16[32,768]{1,0:T(8,128)(2,1)S(1)} %get-tuple-element.164), channel_id=1, source_target_pairs={{0,3},{1,2},{2,1},{3,0},{4,7},{5,6},{6,5},{7,4},{8,11},{9,10},{10,... | collective-permute-start | bytes 147464 | tf_op jit(solution)/shard_map/ppermute | solution.py:485
  136.1 5.1 %copy-start.12 = (f32[24]{0:T(128)}, f32[24]{0:T(128)S(1)}, u32[]{:S(2)}) copy-start(f32[24]{0:T(128)S(1)} %get-tuple-element.243) | copy-start | bytes 292
  138.0 2.2 %copy-start.3 = (bf16[128,768]{1,0:T(8,128)(2,1)S(1)}, bf16[128,768]{1,0:T(8,128)(2,1)}, u32[]{:S(2)}) copy-start(bf16[128,768]{1,0:T(8,128)(2,1)} %refs_5_.1) | copy-start | bytes 589828
  (6 other events, 4.8 us)

commit v8 on v7

--- a/solution.py
+++ b/solution.py
@@ -565,12 +565,12 @@
         for first in range(0, tokens, size):
             rows = slice(first, first + size)
             n = first + size
-            scores = dot_nt(q_h[rows], k_h[:n]) * SCALE
+            scores = dot_nt(q_h[rows] * SCALE, k_h[:n])
             query = lax.broadcasted_iota(jnp.int32, (size, n), 0) + first
             key = lax.broadcasted_iota(jnp.int32, (size, n), 1)
             allowed = (seg_column[rows, :] == seg_row[:, :n]) & (key <= query)
             scores = jnp.where(allowed, scores, NEGATIVE)
-            weights = jnp.where(allowed, jnp.exp(scores - jnp.max(scores, axis=1, keepdims=True)), 0.0)
+            weights = jnp.exp(scores - jnp.max(scores, axis=1, keepdims=True))
             probs = weights * (1.0 / jnp.sum(weights, axis=1, keepdims=True))
             probs_r = probs.astype(BF)
             out_t[lanes, rows] = jnp.transpose(dot_nn(probs_r, v_h[:n]))

time: 142 us -> 142 us (level)
  no operation moved by 1% of the time
where the time goes in v8:
time: 142 us
  waiting for transfers between devices  57.2 us (40%)
  starting transfers between devices  34 us (24%)
  Pallas kernels  28.4 us (20%)
  local copies, waits for them, and re-layouts  10.7 us (8%)
  other arithmetic  10.5 us (7%)
    pallas_call x18, Pallas kernels, kernel_call(): pl.pallas_call(body, out_shape=tuple((jax.ShapeDtypeStruct(shape, kind) f...  28.4 us
    ppermute x15, starting transfers between devices, seq_shuffle(): got.append(lax.ppermute(blocks[other], 'seq', pairs))  10.5 us
    unnamed x27, local copies, waits for them, and re-layouts  7.44 us
    ppermute x1, waiting for transfers between devices, line_device(): attn_half = lax.ppermute(attn_piece, 'dp', HALF_SWAP)  7.42 us
    ppermute x1, waiting for transfers between devices, line_device(): down_got = lax.ppermute(send_down, 'dp', PAIR_SWAP)  6.73 us
    ppermute x1, waiting for transfers between devices, line_device(): mlp_half = lax.ppermute(mlp_piece, 'dp', HALF_SWAP)  6.51 us
    ppermute x1, waiting for transfers between devices, line_device(): up_got = lax.ppermute(send_up, 'dp', PAIR_SWAP)  5.86 us
    ppermute x2, waiting for transfers between devices, line_device(): up_far = lax.ppermute(up_give, 'dp', SIDE_SWAP)  5.41 us
  transfers between devices with their start and end apart: 41, of which 18 were waited for; matrix products, arithmetic and copies ran while one was open for 8% of the time, Pallas kernels for 14%

profile of v8, /device:TPU:0, one launch (start us, length us, event | category | flops | bytes accessed | tf_op | source)
XLA Modules:
  0.0 142.0 jit_solution(17165386850269843633)
XLA Ops:
  1.4 0.9 copy-done
  2.3 0.9 copy-done.2
  3.3 0.9 copy-done.4
  4.2 0.9 copy-done.5
  6.5 2.6 %collective-permute-start.1 = (bf16[56,768]{1,0:T(8,128)(2,1)S(1)}, bf16[56,768]{1,0:T(8,128)(2,1)S(1)}, u32[]{:S(2)}, u32[]{:S(2)}) collective-permute-start(bf16[56,768]{1,0:T(8,128)(2,1)S(1)} %get-tuple-element.99), channel_id=1, source_target_pairs={{0,2},{1,3},{2,0},{3,1},{4,6},{5,7},{6,4},{7,5},{8,10},{9,11},{10,... | collective-permute-start | bytes 258056 | tf_op jit(solution)/shard_map/ppermute | solution.py:485
  9.1 2.8 %collective-permute-start.3 = (bf16[96,768]{1,0:T(8,128)(2,1)}, bf16[96,768]{1,0:T(8,128)(2,1)S(1)}, u32[]{:S(2)}, u32[]{:S(2)}) collective-permute-start(bf16[96,768]{1,0:T(8,128)(2,1)} %param.28), channel_id=1, source_target_pairs={{0,16},{4,20},{8,24},{12,28},{16,0},{20,4},{24,8},{28,12},{1,17},{... | collective-permute-start | bytes 442376 | tf_op jit(solution)/shard_map/ppermute | solution.py:950
  12.0 1.5 %collective-permute-start.20 = (bf16[256,768]{1,0:T(8,128)(2,1)S(1)}, bf16[256,768]{1,0:T(8,128)(2,1)S(1)}, u32[]{:S(2)}, u32[]{:S(2)}) collective-permute-start(bf16[256,768]{1,0:T(8,128)(2,1)S(1)} %get-tuple-element.110), channel_id=1, source_target_pairs={{0,4},{4,0},{8,12},{12,8},{16,20},{20,16},{24,28},{28,24},{1,5},{5... | collective-permute-start | bytes 1179656 | tf_op jit(solution)/shard_map/ppermute | solution.py:949
  13.5 0.8 reduce-window.8
  16.9 2.8 %collective-permute-done.3 = bf16[96,768]{1,0:T(8,128)(2,1)S(1)} collective-permute-done((bf16[96,768]{1,0:T(8,128)(2,1)}, bf16[96,768]{1,0:T(8,128)(2,1)S(1)}, u32[]{:S(2)}, u32[]{:S(2)}) %collective-permute-start.3) | collective-permute-done | bytes 147488 | tf_op jit(solution)/shard_map/ppermute | solution.py:950
  19.7 1.6 %collective-permute-start.5 = (bf16[96,384]{1,0:T(8,128)(2,1)S(1)}, bf16[96,384]{1,0:T(8,128)(2,1)S(1)}, u32[]{:S(2)}, u32[]{:S(2)}) collective-permute-start(bf16[96,384]{1,0:T(8,128)(2,1)S(1)} %get-tuple-element.104), channel_id=1, source_target_pairs={{0,4},{4,0},{8,12},{12,8},{16,20},{20,16},{24,28},{28,24},{1,5},{5... | collective-permute-start | bytes 221192 | tf_op jit(solution)/shard_map/ppermute | solution.py:955
  21.3 1.5 %collective-permute-start.10 = (bf16[256,768]{1,0:T(8,128)(2,1)S(1)}, bf16[256,768]{1,0:T(8,128)(2,1)S(1)}, u32[]{:S(2)}, u32[]{:S(2)}) collective-permute-start(bf16[256,768]{1,0:T(8,128)(2,1)S(1)} %get-tuple-element.110), channel_id=1, source_target_pairs={{0,2},{2,0},{1,3},{3,1},{4,6},{6,4},{5,7},{7,5},{8,10},{10,8},{9,1... | collective-permute-start | bytes 1179656 | tf_op jit(solution)/shard_map/ppermute | solution.py:956
  22.8 1.9 %collective-permute-done.5 = bf16[96,384]{1,0:T(8,128)(2,1)S(1)} collective-permute-done((bf16[96,384]{1,0:T(8,128)(2,1)S(1)}, bf16[96,384]{1,0:T(8,128)(2,1)S(1)}, u32[]{:S(2)}, u32[]{:S(2)}) %collective-permute-start.5) | collective-permute-done | bytes 73760 | tf_op jit(solution)/shard_map/ppermute | solution.py:955
  24.7 7.4 %collective-permute-done.4 = bf16[104,768]{1,0:T(8,128)(2,1)S(1)} collective-permute-done((bf16[104,768]{1,0:T(8,128)(2,1)S(1)}, bf16[104,768]{1,0:T(8,128)(2,1)S(1)}, u32[]{:S(2)}, u32[]{:S(2)}) %collective-permute-start.4) | collective-permute-done | bytes 159776 | tf_op jit(solution)/shard_map/ppermute | solution.py:954
  32.8 1.7 %collective-permute-start.8 = (bf16[96,768]{1,0:T(8,128)(2,1)S(1)}, bf16[96,768]{1,0:T(8,128)(2,1)S(1)}, u32[]{:S(2)}, u32[]{:S(2)}) collective-permute-start(bf16[96,768]{1,0:T(8,128)(2,1)S(1)} %pad_maximum_fusion.7), channel_id=1, source_target_pairs={{0,16},{4,20},{8,24},{12,28},{16,0},{20,4},{24,8},{28,12},{1,17},{... | collective-permute-start | bytes 442376 | tf_op jit(solution)/shard_map/ppermute | solution.py:965
  34.7 6.5 %collective-permute-done.8 = bf16[96,768]{1,0:T(8,128)(2,1)S(1)} collective-permute-done((bf16[96,768]{1,0:T(8,128)(2,1)S(1)}, bf16[96,768]{1,0:T(8,128)(2,1)S(1)}, u32[]{:S(2)}, u32[]{:S(2)}) %collective-permute-start.8) | collective-permute-done | bytes 147488 | tf_op jit(solution)/shard_map/ppermute | solution.py:965
  41.2 2.2 %collective-permute-done.6.refs_1_ = bf16[2,104,768]{2,1,0:T(8,128)(2,1)S(1)} collective-permute-done((bf16[2,104,768]{2,1,0:T(8,128)(2,1)S(1)}, bf16[2,104,768]{2,1,0:T(8,128)(2,1)S(1)}, u32[]{:S(2)}, u32[]{:S(2)}) %collective-permute-start.6) | collective-permute-done | bytes 319520 | tf_op jit(solution)/shard_map/ppermute | solution.py:959
  44.6 1.0 fusion.18
  45.7 0.9 collective-permute-start.9
  46.6 4.6 %collective-permute-done.12.refs_2_ = bf16[2,96,768]{2,1,0:T(8,128)(2,1)S(1)} collective-permute-done((bf16[2,96,768]{2,1,0:T(8,128)(2,1)S(1)}, bf16[2,96,768]{2,1,0:T(8,128)(2,1)S(1)}, u32[]{:S(2)}, u32[]{:S(2)}) %collective-permute-start.12) | collective-permute-done | bytes 294944 | tf_op jit(solution)/shard_map/ppermute | solution.py:953
  51.6 1.6 %collective-permute-done.21 = bf16[256,768]{1,0:T(8,128)(2,1)S(1)} collective-permute-done((bf16[256,768]{1,0:T(8,128)(2,1)S(1)}, bf16[256,768]{1,0:T(8,128)(2,1)S(1)}, u32[]{:S(2)}, u32[]{:S(2)}) %collective-permute-start.21) | collective-permute-done | bytes 393248 | tf_op jit(solution)/shard_map/ppermute | solution.py:972
  55.7 0.9 collective-permute-start.16
  57.3 1.7 %shard_map.257 = (bf16[512,768]{1,0:T(8,128)(2,1)S(1)}, bf16[512,384]{1,0:T(8,128)(2,1)S(1)}, bf16[512,192]{1,0:T(8,128)(2,1)S(1)}) custom-call(f32[512,768]{1,0:T(8,128)S(1)} %fusion.1.unit.refs_1_.refs_9_, bf16[768,768]{1,0:T(8,128)(2,1)S(1)} %get-tuple-element.114.weights.refs_8_, f32[8,768]{1,0:T(8,128)S(1)} %get-tuple-element.112.vectors.refs_7_.refs_3_.refs_10_, ...), custom_call_target="tpu_custom_call" | custom-call | flops 603979776 | bytes 3563520 | tf_op jit(solution)/shard_map/pallas_call | solution.py:415
  59.8 6.6 %shard_map.258 = (bf16[48,512]{1,0:T(8,128)(2,1)S(1)}, bf16[48,512]{1,0:T(8,128)(2,1)S(1)}, bf16[48,512]{1,0:T(8,128)(2,1)S(1)}, bf16[48,512]{1,0:T(8,128)(2,1)S(1)}, bf16[512,768]{1,0:T(8,128)(2,1)S(1)}) custom-call(bf16[2,96,768]{2,1,0:T(8,128)(2,1)S(1)} %collective-permute-done.13.refs_0_.refs_4_, bf16[512,384]{1,0:T(8,128)(2,1)S(1)} %get-tuple-element.115.refs_1_, ...), custom_call_target="tpu_custom_call" | custom-call | flops 704643072 | bytes 1871872 | tf_op jit(solution)/shard_map/pallas_call | solution.py:415
  66.8 1.3 collective-permute-start.18
  69.7 4.4 %shard_map.259 = (bf16[2,128,1536]{2,1,0:T(8,128)(2,1)S(1)}, bf16[2,128,1536]{2,1,0:T(8,128)(2,1)S(1)}, bf16[512,768]{1,0:T(8,128)(2,1)S(1)}, bf16[512,384]{1,0:...) custom-call(bf16[512,768]{1,0:T(8,128)(2,1)S(1)} %get-tuple-element., ...), custom_call_target="tpu_custom_call" | custom-call | flops 1207959552 | bytes 4349952 | tf_op jit(solution)/shard_map/pallas_call | solution.py:415
  74.1 3.4 %shard_map.260 = (bf16[4,128,1536]{2,1,0:T(8,128)(2,1)S(1)}, bf16[512,768]{1,0:T(8,128)(2,1)S(1)}, bf16[512,384]{1,0:T(8,128)(2,1)S(1)}, bf16[512,384]{1,0:T(8,128)(2,1)S(1)}, f32[8,768]{1,0:T(8,128)S(1)}) custom-call(bf16[512,768]{1,0:T(8,128)(2,1)S(1)} %get-tuple-element.127.refs_0_.refs_7_, f32[512,768]{1,0:T(8,128)S(1)} %fusion.1.unit.refs_1_.refs_9_, ...), custom_call_target="tpu_custom_call" | custom-call | flops 1207959552 | bytes 4349952 | tf_op jit(solution)/shard_map/pallas_call | solution.py:415
  77.6 5.2 %shard_map.261 = (bf16[4,104,768]{2,1,0:T(8,128)(2,1)S(1)}, bf16[4,104,768]{2,1,0:T(8,128)(2,1)S(1)}, bf16[2,128,1536]{2,1,0:T(8,128)(2,1)}, bf16[2,128,1536]{2,1,0:T(8,128)(2,1)S(1)}) custom-call(bf16[48,512]{1,0:T(8,128)(2,1)S(1)} %get-tuple-element.121.refs_0_, bf16[48,512]{1,0:T(8,128)(2,1)S(1)} %collective-permute-done.17.refs_1_, ...), custom_call_target="tpu_custom_call" | custom-call | flops 1509949440 | bytes 7200768 | tf_op jit(solution)/shard_map/pallas_call | solution.py:415
  82.8 1.8 %shard_map.262 = (bf16[2,104,768]{2,1,0:T(8,128)(2,1)S(1)}, bf16[2,104,768]{2,1,0:T(8,128)(2,1)S(1)}, bf16[2,96,768]{2,1,0:T(8,128)(2,1)S(1)}, bf16[2,96,768]{2,1,0:T(8,128)(2,1)S(1)}) custom-call(bf16[4,104,768]{2,1,0:T(8,128)(2,1)S(1)} %get-tuple-element.137.refs_0_, bf16[512,768]{1,0:T(8,128)(2,1)S(1)} %get-tuple-element.138.refs_1_, ...), custom_call_target="tpu_custom_call" | custom-call | flops 1207959552 | bytes 5406720 | tf_op jit(solution)/shard_map/pallas_call | solution.py:415
  85.5 1.6 %collective-permute-start.27 = (bf16[2,96,768]{2,1,0:T(8,128)(2,1)S(1)}, bf16[2,96,768]{2,1,0:T(8,128)(2,1)S(1)}, u32[]{:S(2)}, u32[]{:S(2)}) collective-permute-start(bf16[2,96,768]{2,1,0:T(8,128)(2,1)S(1)} %get-tuple-element.149), channel_id=1, source_target_pairs={{0,8},{4,12},{8,0},{12,4},{16,24},{20,28},{24,16},{28,20},{1,9},{5... | collective-permute-start | bytes 884744 | tf_op jit(solution)/shard_map/ppermute | solution.py:1068
  87.5 1.1 add_convert_fusion
  88.6 6.7 %collective-permute-done.27.refs_1_ = bf16[2,96,768]{2,1,0:T(8,128)(2,1)S(1)} collective-permute-done((bf16[2,96,768]{2,1,0:T(8,128)(2,1)S(1)}, bf16[2,96,768]{2,1,0:T(8,128)(2,1)S(1)}, u32[]{:S(2)}, u32[]{:S(2)}) %collective-permute-start.27) | collective-permute-done | bytes 294944 | tf_op jit(solution)/shard_map/ppermute | solution.py:1068
  95.3 5.9 %collective-permute-done.26.refs_1_ = bf16[2,104,768]{2,1,0:T(8,128)(2,1)S(1)} collective-permute-done((bf16[2,104,768]{2,1,0:T(8,128)(2,1)S(1)}, bf16[2,104,768]{2,1,0:T(8,128)(2,1)S(1)}, u32[]{:S(2)}, u32[]{:S(2)}) %collective-permute-start.26) | collective-permute-done | bytes 319520 | tf_op jit(solution)/shard_map/ppermute | solution.py:1067
  101.7 1.2 collective-permute-start.28
  103.9 1.8 %collective-permute-start.31 = (bf16[1,104,768]{2,1,0:T(8,128)(2,1)S(1)}, bf16[1,104,768]{2,1,0:T(8,128)(2,1)S(1)}, u32[]{:S(2)}, u32[]{:S(2)}) collective-permute-start(bf16[1,104,768]{2,1,0:T(8,128)(2,1)S(1)} %get-tuple-element.156), channel_id=1, source_target_pairs={{0,16},{4,20},{8,24},{12,28},{16,0},{20,4},{24,8},{28,12},{1,17},{... | collective-permute-start | bytes 479240 | tf_op jit(solution)/shard_map/ppermute | solution.py:1073
  107.1 2.1 %collective-permute-start.40 = (bf16[1,96,768]{2,1,0:T(8,128)(2,1)}, bf16[1,96,768]{2,1,0:T(8,128)(2,1)S(1)}, u32[]{:S(2)}, u32[]{:S(2)}) collective-permute-start(bf16[1,96,768]{2,1,0:T(8,128)(2,1)} %get-tuple-element.179), channel_id=1, source_target_pairs={{0,16},{4,20},{8,24},{12,28},{16,0},{20,4},{24,8},{28,12},{1,17},{... | collective-permute-start | bytes 442376 | tf_op jit(solution)/shard_map/ppermute | solution.py:1077
  109.3 4.9 %collective-permute-done.31.refs_2_.refs_0_ = bf16[1,104,768]{2,1,0:T(8,128)(2,1)S(1)} collective-permute-done((bf16[1,104,768]{2,1,0:T(8,128)(2,1)S(1)}, bf16[1,104,768]{2,1,0:T(8,128)(2,1)S(1)}, u32[]{:S(2)}, u32[]{:S(2)}) %collective-permute-start.31) | collective-permute-done | bytes 159776 | tf_op jit(solution)/shard_map/ppermute | solution.py:1073
  114.1 5.3 %collective-permute-done.30.refs_0_.refs_2_ = bf16[2,104,768]{2,1,0:T(8,128)(2,1)S(1)} collective-permute-done((bf16[2,104,768]{2,1,0:T(8,128)(2,1)}, bf16[2,104,768]{2,1,0:T(8,128)(2,1)S(1)}, u32[]{:S(2)}, u32[]{:S(2)}) %collective-permute-start.30) | collective-permute-done | bytes 319520 | tf_op jit(solution)/shard_map/ppermute | solution.py:1075
  119.7 1.0 collective-permute-done.28
  120.7 1.6 %convert_add_fusion = f32[2,128,1536]{2,1,0:T(8,128)S(1)} fusion(bf16[2,128,1536]{2,1,0:T(8,128)(2,1)} %collective-permute-done.28, bf16[2,128,1536]{2,1,0:T(8,128)(2,1)} %collective-permute-done.23, bf16[2,128,1536]{2,1,0:T(8,128)(2,1)S(1)} %get-tuple-element.133), kind=kLoop, calls=%fused_computation.6 | loop fusion | flops 1966080 | bytes 3932160 | tf_op jit(solution)/shard_map/add | solution.py:1082
  122.3 1.2 copy-done.9
  123.5 1.5 %collective-permute-start.29 = (bf16[128,1536]{1,0:T(8,128)(2,1)S(1)}, bf16[128,1536]{1,0:T(8,128)(2,1)S(1)}, u32[]{:S(2)}, u32[]{:S(2)}) collective-permute-start(bf16[128,1536]{1,0:T(8,128)(2,1)S(1)} %fusion.17), channel_id=1, source_target_pairs={{0,2},{2,0},{1,3},{3,1},{4,6},{6,4},{5,7},{7,5},{8,10},{10,8},{9,1... | collective-permute-start | bytes 1179656 | tf_op jit(solution)/shard_map/ppermute | solution.py:1083
  125.1 1.0 collective-permute-start.32
  126.1 3.6 %collective-permute-done.32.refs_0_.refs_2_ = bf16[112,384]{1,0:T(8,128)(2,1)S(1)} collective-permute-done((bf16[112,384]{1,0:T(8,128)(2,1)S(1)}, bf16[112,384]{1,0:T(8,128)(2,1)S(1)}, u32[]{:S(2)}, u32[]{:S(2)}) %collective-permute-start.32) | collective-permute-done | bytes 86048 | tf_op jit(solution)/shard_map/ppermute | solution.py:1104
  130.5 1.2 collective-permute-start.39
  135.0 0.9 shard_map.270
  137.0 0.8 collective-permute-done.35.refs_3_
  138.3 0.9 shard_map.268
  140.6 0.9 fusion.12
  (133 shorter events, 25.3 us)
Async XLA Ops:
  1.4 0.9 copy-start
  6.0 9.3 %collective-permute-start = (bf16[56,768]{1,0:T(8,128)(2,1)S(1)}, bf16[56,768]{1,0:T(8,128)(2,1)S(1)}, u32[]{:S(2)}, u32[]{:S(2)}) collective-permute-start(bf16[56,768]{1,0:T(8,128)(2,1)S(1)} %get-tuple-element.98), channel_id=1, source_target_pairs={{0,1},{1,0},{2,3},{3,2},{4,5},{5,4},{6,7},{7,6},{8,9},{9,8},{10,11... | collective-permute-start | bytes 258056 | tf_op jit(solution)/shard_map/ppermute | solution.py:485
  6.5 8.8 %collective-permute-start.1 = (bf16[56,768]{1,0:T(8,128)(2,1)S(1)}, bf16[56,768]{1,0:T(8,128)(2,1)S(1)}, u32[]{:S(2)}, u32[]{:S(2)}) collective-permute-start(bf16[56,768]{1,0:T(8,128)(2,1)S(1)} %get-tuple-element.99), channel_id=1, source_target_pairs={{0,2},{1,3},{2,0},{3,1},{4,6},{5,7},{6,4},{7,5},{8,10},{9,11},{10,... | collective-permute-start | bytes 258056 | tf_op jit(solution)/shard_map/ppermute | solution.py:485
  9.1 6.2 %collective-permute-start.2 = (bf16[56,768]{1,0:T(8,128)(2,1)S(1)}, bf16[56,768]{1,0:T(8,128)(2,1)S(1)}, u32[]{:S(2)}, u32[]{:S(2)}) collective-permute-start(bf16[56,768]{1,0:T(8,128)(2,1)S(1)} %get-tuple-element.100), channel_id=1, source_target_pairs={{0,3},{1,2},{2,1},{3,0},{4,7},{5,6},{6,5},{7,4},{8,11},{9,10},{10,... | collective-permute-start | bytes 258056 | tf_op jit(solution)/shard_map/ppermute | solution.py:485
  9.1 10.6 %collective-permute-start.3 = (bf16[96,768]{1,0:T(8,128)(2,1)}, bf16[96,768]{1,0:T(8,128)(2,1)S(1)}, u32[]{:S(2)}, u32[]{:S(2)}) collective-permute-start(bf16[96,768]{1,0:T(8,128)(2,1)} %param.28), channel_id=1, source_target_pairs={{0,16},{4,20},{8,24},{12,28},{16,0},{20,4},{24,8},{28,12},{1,17},{... | collective-permute-start | bytes 442376 | tf_op jit(solution)/shard_map/ppermute | solution.py:950
  12.0 22.7 %collective-permute-start.20 = (bf16[256,768]{1,0:T(8,128)(2,1)S(1)}, bf16[256,768]{1,0:T(8,128)(2,1)S(1)}, u32[]{:S(2)}, u32[]{:S(2)}) collective-permute-start(bf16[256,768]{1,0:T(8,128)(2,1)S(1)} %get-tuple-element.110), channel_id=1, source_target_pairs={{0,4},{4,0},{8,12},{12,8},{16,20},{20,16},{24,28},{28,24},{1,5},{5... | collective-permute-start | bytes 1179656 | tf_op jit(solution)/shard_map/ppermute | solution.py:949
  19.7 4.9 %collective-permute-start.5 = (bf16[96,384]{1,0:T(8,128)(2,1)S(1)}, bf16[96,384]{1,0:T(8,128)(2,1)S(1)}, u32[]{:S(2)}, u32[]{:S(2)}) collective-permute-start(bf16[96,384]{1,0:T(8,128)(2,1)S(1)} %get-tuple-element.104), channel_id=1, source_target_pairs={{0,4},{4,0},{8,12},{12,8},{16,20},{20,16},{24,28},{28,24},{1,5},{5... | collective-permute-start | bytes 221192 | tf_op jit(solution)/shard_map/ppermute | solution.py:955
  21.3 13.2 %collective-permute-start.10 = (bf16[256,768]{1,0:T(8,128)(2,1)S(1)}, bf16[256,768]{1,0:T(8,128)(2,1)S(1)}, u32[]{:S(2)}, u32[]{:S(2)}) collective-permute-start(bf16[256,768]{1,0:T(8,128)(2,1)S(1)} %get-tuple-element.110), channel_id=1, source_target_pairs={{0,2},{2,0},{1,3},{3,1},{4,6},{6,4},{5,7},{7,5},{8,10},{10,8},{9,1... | collective-permute-start | bytes 1179656 | tf_op jit(solution)/shard_map/ppermute | solution.py:956
  22.8 9.3 %collective-permute-start.4 = (bf16[104,768]{1,0:T(8,128)(2,1)S(1)}, bf16[104,768]{1,0:T(8,128)(2,1)S(1)}, u32[]{:S(2)}, u32[]{:S(2)}) collective-permute-start(bf16[104,768]{1,0:T(8,128)(2,1)S(1)} %get-tuple-element.102), channel_id=1, source_target_pairs={{0,16},{4,20},{8,24},{12,28},{16,0},{20,4},{24,8},{28,12},{1,17},{... | collective-permute-start | bytes 479240 | tf_op jit(solution)/shard_map/ppermute | solution.py:954
  32.1 11.8 %copy-start.11 = (bf16[96,768]{1,0:T(8,128)(2,1)S(1)}, bf16[96,768]{1,0:T(8,128)(2,1)}, u32[]{:S(2)}) copy-start(bf16[96,768]{1,0:T(8,128)(2,1)} %param.28) | copy-start | bytes 442372
  32.1 11.3 %collective-permute-start.6 = (bf16[2,104,768]{2,1,0:T(8,128)(2,1)S(1)}, bf16[2,104,768]{2,1,0:T(8,128)(2,1)S(1)}, u32[]{:S(2)}, u32[]{:S(2)}) collective-permute-start(bf16[2,104,768]{2,1,0:T(8,128)(2,1)S(1)} %pad_maximum_fusion.4.refs_0_), channel_id=1, source_target_pairs={{0,8},{4,12},{8,0},{12,4},{16,24},{20,28},{24,16},{28,20},{1,9},{5... | collective-permute-start | bytes 958472 | tf_op jit(solution)/shard_map/ppermute | solution.py:959
  32.2 11.2 %collective-permute-start.7 = (bf16[2,104,768]{2,1,0:T(8,128)(2,1)S(1)}, bf16[2,104,768]{2,1,0:T(8,128)(2,1)S(1)}, u32[]{:S(2)}, u32[]{:S(2)}) collective-permute-start(bf16[2,104,768]{2,1,0:T(8,128)(2,1)S(1)} %pad_maximum_fusion.4.refs_0_), channel_id=1, source_target_pairs={{0,4},{4,0},{8,12},{12,8},{16,20},{20,16},{24,28},{28,24},{1,5},{5... | collective-permute-start | bytes 958472 | tf_op jit(solution)/shard_map/ppermute | solution.py:960
  32.8 8.4 %collective-permute-start.8 = (bf16[96,768]{1,0:T(8,128)(2,1)S(1)}, bf16[96,768]{1,0:T(8,128)(2,1)S(1)}, u32[]{:S(2)}, u32[]{:S(2)}) collective-permute-start(bf16[96,768]{1,0:T(8,128)(2,1)S(1)} %pad_maximum_fusion.7), channel_id=1, source_target_pairs={{0,16},{4,20},{8,24},{12,28},{16,0},{20,4},{24,8},{28,12},{1,17},{... | collective-permute-start | bytes 442376 | tf_op jit(solution)/shard_map/ppermute | solution.py:965
  34.6 18.7 %collective-permute-start.11 = (bf16[2,256,768]{2,1,0:T(8,128)(2,1)S(1)}, bf16[2,256,768]{2,1,0:T(8,128)(2,1)S(1)}, u32[]{:S(2)}, u32[]{:S(2)}) collective-permute-start(bf16[2,256,768]{2,1,0:T(8,128)(2,1)S(1)} %pad_maximum_fusion.2), channel_id=1, source_target_pairs={{0,1},{1,0},{2,3},{3,2},{4,5},{5,4},{6,7},{7,6},{8,9},{9,8},{10,11... | collective-permute-start | bytes 2359304 | tf_op jit(solution)/shard_map/ppermute | solution.py:967
  43.4 9.8 %collective-permute-start.21 = (bf16[256,768]{1,0:T(8,128)(2,1)S(1)}, bf16[256,768]{1,0:T(8,128)(2,1)S(1)}, u32[]{:S(2)}, u32[]{:S(2)}) collective-permute-start(bf16[256,768]{1,0:T(8,128)(2,1)S(1)} %collective-permute-done.20), channel_id=1, source_target_pairs={{0,2},{2,0},{1,3},{3,1},{4,6},{6,4},{5,7},{7,5},{8,10},{10,8},{9,1... | collective-permute-start | bytes 1179656 | tf_op jit(solution)/shard_map/ppermute | solution.py:972
  44.0 7.2 %collective-permute-start.12 = (bf16[2,96,768]{2,1,0:T(8,128)(2,1)S(1)}, bf16[2,96,768]{2,1,0:T(8,128)(2,1)S(1)}, u32[]{:S(2)}, u32[]{:S(2)}) collective-permute-start(bf16[2,96,768]{2,1,0:T(8,128)(2,1)S(1)} %pad_maximum_fusion.6.refs_1_), channel_id=1, source_target_pairs={{0,8},{4,12},{8,0},{12,4},{16,24},{20,28},{24,16},{28,20},{1,9},{5... | collective-permute-start | bytes 884744 | tf_op jit(solution)/shard_map/ppermute | solution.py:953
  45.7 8.4 %collective-permute-start.9 = (bf16[2,104,768]{2,1,0:T(8,128)(2,1)S(1)}, bf16[2,104,768]{2,1,0:T(8,128)(2,1)S(1)}, u32[]{:S(2)}, u32[]{:S(2)}) collective-permute-start(bf16[2,104,768]{2,1,0:T(8,128)(2,1)S(1)} %collective-permute-done.6.refs_1_), channel_id=1, source_target_pairs={{0,4},{4,0},{8,12},{12,8},{16,20},{20,16},{24,28},{28,24},{1,5},{5... | collective-permute-start | bytes 958472 | tf_op jit(solution)/shard_map/ppermute | solution.py:969
  51.2 7.8 %collective-permute-start.13 = (bf16[2,96,768]{2,1,0:T(8,128)(2,1)S(1)}, bf16[2,96,768]{2,1,0:T(8,128)(2,1)S(1)}, u32[]{:S(2)}, u32[]{:S(2)}) collective-permute-start(bf16[2,96,768]{2,1,0:T(8,128)(2,1)S(1)} %pad_maximum_fusion.5.refs_3_), channel_id=1, source_target_pairs={{0,8},{4,12},{8,0},{12,4},{16,24},{20,28},{24,16},{28,20},{1,9},{5... | collective-permute-start | bytes 884744 | tf_op jit(solution)/shard_map/ppermute | solution.py:971
  54.7 13.6 %collective-permute-start.22 = (bf16[2,256,768]{2,1,0:T(8,128)(2,1)S(1)}, bf16[2,256,768]{2,1,0:T(8,128)(2,1)S(1)}, u32[]{:S(2)}, u32[]{:S(2)}) collective-permute-start(bf16[2,256,768]{2,1,0:T(8,128)(2,1)S(1)} %pad_maximum_fusion.3), channel_id=1, source_target_pairs={{0,1},{1,0},{2,3},{3,2},{4,5},{5,4},{6,7},{7,6},{8,9},{9,8},{10,11... | collective-permute-start | bytes 2359304 | tf_op jit(solution)/shard_map/ppermute | solution.py:1007
  54.8 4.3 %collective-permute-start.14 = (bf16[48,512]{1,0:T(8,128)(2,1)S(1)}, bf16[48,512]{1,0:T(8,128)(2,1)S(1)}, u32[]{:S(2)}, u32[]{:S(2)}) collective-permute-start(bf16[48,512]{1,0:T(8,128)(2,1)S(1)} %get-tuple-element.118), channel_id=1, source_target_pairs={{0,1},{1,0},{2,3},{3,2},{4,5},{5,4},{6,7},{7,6},{8,9},{9,8},{10,11... | collective-permute-start | bytes 147464 | tf_op jit(solution)/shard_map/ppermute | solution.py:485
  55.2 4.5 %collective-permute-start.15 = (bf16[48,512]{1,0:T(8,128)(2,1)S(1)}, bf16[48,512]{1,0:T(8,128)(2,1)S(1)}, u32[]{:S(2)}, u32[]{:S(2)}) collective-permute-start(bf16[48,512]{1,0:T(8,128)(2,1)S(1)} %get-tuple-element.119), channel_id=1, source_target_pairs={{0,2},{1,3},{2,0},{3,1},{4,6},{5,7},{6,4},{7,5},{8,10},{9,11},{10,... | collective-permute-start | bytes 147464 | tf_op jit(solution)/shard_map/ppermute | solution.py:485
  55.7 4.0 %collective-permute-start.16 = (bf16[48,512]{1,0:T(8,128)(2,1)S(1)}, bf16[48,512]{1,0:T(8,128)(2,1)S(1)}, u32[]{:S(2)}, u32[]{:S(2)}) collective-permute-start(bf16[48,512]{1,0:T(8,128)(2,1)S(1)} %get-tuple-element.120), channel_id=1, source_target_pairs={{0,3},{1,2},{2,1},{3,0},{4,7},{5,6},{6,5},{7,4},{8,11},{9,10},{10,... | collective-permute-start | bytes 147464 | tf_op jit(solution)/shard_map/ppermute | solution.py:485
  66.3 11.2 %collective-permute-start.17 = (bf16[48,512]{1,0:T(8,128)(2,1)S(1)}, bf16[48,512]{1,0:T(8,128)(2,1)S(1)}, u32[]{:S(2)}, u32[]{:S(2)}) collective-permute-start(bf16[48,512]{1,0:T(8,128)(2,1)S(1)} %get-tuple-element.122), channel_id=1, source_target_pairs={{0,1},{1,0},{2,3},{3,2},{4,5},{5,4},{6,7},{7,6},{8,9},{9,8},{10,11... | collective-permute-start | bytes 147464 | tf_op jit(solution)/shard_map/ppermute | solution.py:485
  66.8 10.8 %collective-permute-start.18 = (bf16[48,512]{1,0:T(8,128)(2,1)S(1)}, bf16[48,512]{1,0:T(8,128)(2,1)S(1)}, u32[]{:S(2)}, u32[]{:S(2)}) collective-permute-start(bf16[48,512]{1,0:T(8,128)(2,1)S(1)} %get-tuple-element.123), channel_id=1, source_target_pairs={{0,2},{1,3},{2,0},{3,1},{4,6},{5,7},{6,4},{7,5},{8,10},{9,11},{10,... | collective-permute-start | bytes 147464 | tf_op jit(solution)/shard_map/ppermute | solution.py:485
  68.0 9.6 %collective-permute-start.19 = (bf16[48,512]{1,0:T(8,128)(2,1)S(1)}, bf16[48,512]{1,0:T(8,128)(2,1)S(1)}, u32[]{:S(2)}, u32[]{:S(2)}) collective-permute-start(bf16[48,512]{1,0:T(8,128)(2,1)S(1)} %get-tuple-element.124), channel_id=1, source_target_pairs={{0,3},{1,2},{2,1},{3,0},{4,7},{5,6},{6,5},{7,4},{8,11},{9,10},{10,... | collective-permute-start | bytes 147464 | tf_op jit(solution)/shard_map/ppermute | solution.py:485
  84.6 18.3 %copy-start.1 = (bf16[128,768]{1,0:T(8,128)(2,1)S(1)}, bf16[128,768]{1,0:T(8,128)(2,1)}, u32[]{:S(2)}) copy-start(bf16[128,768]{1,0:T(8,128)(2,1)} %refs_4_.1) | copy-start | bytes 589828
  84.6 2.9 %collective-permute-start.24 = (bf16[2,128,1536]{2,1,0:T(8,128)(2,1)S(1)}, bf16[2,128,1536]{2,1,0:T(8,128)(2,1)S(1)}, u32[]{:S(2)}, u32[]{:S(2)}) collective-permute-start(bf16[2,128,1536]{2,1,0:T(8,128)(2,1)S(1)} %get-tuple-element.147), channel_id=1, source_target_pairs={{0,1},{1,0},{2,3},{3,2},{4,5},{5,4},{6,7},{7,6},{8,9},{9,8},{10,11... | collective-permute-start | bytes 2359304 | tf_op jit(solution)/shard_map/ppermute | solution.py:1069
  85.3 16.4 %collective-permute-start.25 = (bf16[4,104,768]{2,1,0:T(8,128)(2,1)S(1)}, bf16[4,104,768]{2,1,0:T(8,128)(2,1)S(1)}, u32[]{:S(2)}, u32[]{:S(2)}) collective-permute-start(bf16[4,104,768]{2,1,0:T(8,128)(2,1)S(1)} %get-tuple-element.137.refs_0_), channel_id=1, source_target_pairs={{0,4},{4,0},{8,12},{12,8},{16,20},{20,16},{24,28},{28,24},{1,5},{5... | collective-permute-start | bytes 1916936 | tf_op jit(solution)/shard_map/ppermute | solution.py:1066
  85.5 9.9 %collective-permute-start.27 = (bf16[2,96,768]{2,1,0:T(8,128)(2,1)S(1)}, bf16[2,96,768]{2,1,0:T(8,128)(2,1)S(1)}, u32[]{:S(2)}, u32[]{:S(2)}) collective-permute-start(bf16[2,96,768]{2,1,0:T(8,128)(2,1)S(1)} %get-tuple-element.149), channel_id=1, source_target_pairs={{0,8},{4,12},{8,0},{12,4},{16,24},{20,28},{24,16},{28,20},{1,9},{5... | collective-permute-start | bytes 884744 | tf_op jit(solution)/shard_map/ppermute | solution.py:1068
  87.1 14.2 %collective-permute-start.26 = (bf16[2,104,768]{2,1,0:T(8,128)(2,1)S(1)}, bf16[2,104,768]{2,1,0:T(8,128)(2,1)S(1)}, u32[]{:S(2)}, u32[]{:S(2)}) collective-permute-start(bf16[2,104,768]{2,1,0:T(8,128)(2,1)S(1)} %get-tuple-element.148), channel_id=1, source_target_pairs={{0,8},{4,12},{8,0},{12,4},{16,24},{20,28},{24,16},{28,20},{1,9},{5... | collective-permute-start | bytes 958472 | tf_op jit(solution)/shard_map/ppermute | solution.py:1067
  87.5 32.2 %collective-permute-start.23 = (bf16[2,128,1536]{2,1,0:T(8,128)(2,1)}, bf16[2,128,1536]{2,1,0:T(8,128)(2,1)}, u32[]{:S(2)}, u32[]{:S(2)}) collective-permute-start(bf16[2,128,1536]{2,1,0:T(8,128)(2,1)} %get-tuple-element.134), channel_id=1, source_target_pairs={{0,1},{1,0},{2,3},{3,2},{4,5},{5,4},{6,7},{7,6},{8,9},{9,8},{10,11... | collective-permute-start | bytes 2359304 | tf_op jit(solution)/shard_map/ppermute | solution.py:1082
  101.7 19.0 %collective-permute-start.28 = (bf16[2,128,1536]{2,1,0:T(8,128)(2,1)}, bf16[2,128,1536]{2,1,0:T(8,128)(2,1)}, u32[]{:S(2)}, u32[]{:S(2)}) collective-permute-start(bf16[2,128,1536]{2,1,0:T(8,128)(2,1)} %add_convert_fusion), channel_id=1, source_target_pairs={{0,4},{4,0},{8,12},{12,8},{16,20},{20,16},{24,28},{28,24},{1,5},{5... | collective-permute-start | bytes 2359304 | tf_op jit(solution)/shard_map/ppermute | solution.py:1078
  103.9 10.3 %collective-permute-start.31 = (bf16[1,104,768]{2,1,0:T(8,128)(2,1)S(1)}, bf16[1,104,768]{2,1,0:T(8,128)(2,1)S(1)}, u32[]{:S(2)}, u32[]{:S(2)}) collective-permute-start(bf16[1,104,768]{2,1,0:T(8,128)(2,1)S(1)} %get-tuple-element.156), channel_id=1, source_target_pairs={{0,16},{4,20},{8,24},{12,28},{16,0},{20,4},{24,8},{28,12},{1,17},{... | collective-permute-start | bytes 479240 | tf_op jit(solution)/shard_map/ppermute | solution.py:1073
  105.7 13.7 %collective-permute-start.30 = (bf16[2,104,768]{2,1,0:T(8,128)(2,1)}, bf16[2,104,768]{2,1,0:T(8,128)(2,1)S(1)}, u32[]{:S(2)}, u32[]{:S(2)}) collective-permute-start(bf16[2,104,768]{2,1,0:T(8,128)(2,1)} %get-tuple-element.153), channel_id=1, source_target_pairs={{0,8},{4,12},{8,0},{12,4},{16,24},{20,28},{24,16},{28,20},{1,9},{5... | collective-permute-start | bytes 958472 | tf_op jit(solution)/shard_map/ppermute | solution.py:1075
  107.1 24.5 %collective-permute-start.40 = (bf16[1,96,768]{2,1,0:T(8,128)(2,1)}, bf16[1,96,768]{2,1,0:T(8,128)(2,1)S(1)}, u32[]{:S(2)}, u32[]{:S(2)}) collective-permute-start(bf16[1,96,768]{2,1,0:T(8,128)(2,1)} %get-tuple-element.179), channel_id=1, source_target_pairs={{0,16},{4,20},{8,24},{12,28},{16,0},{20,4},{24,8},{28,12},{1,17},{... | collective-permute-start | bytes 442376 | tf_op jit(solution)/shard_map/ppermute | solution.py:1077
  119.5 10.1 %collective-permute-start.33 = (bf16[1,104,768]{2,1,0:T(8,128)(2,1)S(1)}, bf16[1,104,768]{2,1,0:T(8,128)(2,1)S(1)}, u32[]{:S(2)}, u32[]{:S(2)}) collective-permute-start(bf16[1,104,768]{2,1,0:T(8,128)(2,1)S(1)} %get-tuple-element.160), channel_id=1, source_target_pairs={{0,16},{4,20},{8,24},{12,28},{16,0},{20,4},{24,8},{28,12},{1,17},{... | collective-permute-start | bytes 479240 | tf_op jit(solution)/shard_map/ppermute | solution.py:1080
  122.3 1.2 copy-start.9
  123.5 11.4 %collective-permute-start.29 = (bf16[128,1536]{1,0:T(8,128)(2,1)S(1)}, bf16[128,1536]{1,0:T(8,128)(2,1)S(1)}, u32[]{:S(2)}, u32[]{:S(2)}) collective-permute-start(bf16[128,1536]{1,0:T(8,128)(2,1)S(1)} %fusion.17), channel_id=1, source_target_pairs={{0,2},{2,0},{1,3},{3,1},{4,6},{6,4},{5,7},{7,5},{8,10},{10,8},{9,1... | collective-permute-start | bytes 1179656 | tf_op jit(solution)/shard_map/ppermute | solution.py:1083
  125.0 15.2 %copy-start.10 = (f32[2,128,1536]{2,1,0:T(8,128)S(1)}, f32[2,128,1536]{2,1,0:T(8,128)}, u32[]{:S(2)}) copy-start(f32[2,128,1536]{2,1,0:T(8,128)} %copy-done.9) | copy-start | bytes 4718596
  125.1 4.6 %collective-permute-start.32 = (bf16[112,384]{1,0:T(8,128)(2,1)S(1)}, bf16[112,384]{1,0:T(8,128)(2,1)S(1)}, u32[]{:S(2)}, u32[]{:S(2)}) collective-permute-start(bf16[112,384]{1,0:T(8,128)(2,1)S(1)} %get-tuple-element.157), channel_id=1, source_target_pairs={{0,4},{4,0},{8,12},{12,8},{16,20},{20,16},{24,28},{28,24},{1,5},{5... | collective-permute-start | bytes 258056 | tf_op jit(solution)/shard_map/ppermute | solution.py:1104
  129.7 3.8 %collective-permute-start.37 = (bf16[32,768]{1,0:T(8,128)(2,1)S(1)}, bf16[32,768]{1,0:T(8,128)(2,1)S(1)}, u32[]{:S(2)}, u32[]{:S(2)}) collective-permute-start(bf16[32,768]{1,0:T(8,128)(2,1)S(1)} %get-tuple-element.169), channel_id=1, source_target_pairs={{0,1},{1,0},{2,3},{3,2},{4,5},{5,4},{6,7},{7,6},{8,9},{9,8},{10,11... | collective-permute-start | bytes 147464 | tf_op jit(solution)/shard_map/ppermute | solution.py:485
  129.8 4.6 %collective-permute-start.38 = (bf16[32,768]{1,0:T(8,128)(2,1)S(1)}, bf16[32,768]{1,0:T(8,128)(2,1)S(1)}, u32[]{:S(2)}, u32[]{:S(2)}) collective-permute-start(bf16[32,768]{1,0:T(8,128)(2,1)S(1)} %get-tuple-element.170), channel_id=1, source_target_pairs={{0,2},{1,3},{2,0},{3,1},{4,6},{5,7},{6,4},{7,5},{8,10},{9,11},{10,... | collective-permute-start | bytes 147464 | tf_op jit(solution)/shard_map/ppermute | solution.py:485
  130.5 4.5 %collective-permute-start.39 = (bf16[32,768]{1,0:T(8,128)(2,1)S(1)}, bf16[32,768]{1,0:T(8,128)(2,1)S(1)}, u32[]{:S(2)}, u32[]{:S(2)}) collective-permute-start(bf16[32,768]{1,0:T(8,128)(2,1)S(1)} %get-tuple-element.171), channel_id=1, source_target_pairs={{0,3},{1,2},{2,1},{3,0},{4,7},{5,6},{6,5},{7,4},{8,11},{9,10},{10,... | collective-permute-start | bytes 147464 | tf_op jit(solution)/shard_map/ppermute | solution.py:485
  133.1 3.9 %collective-permute-start.34 = (bf16[32,768]{1,0:T(8,128)(2,1)S(1)}, bf16[32,768]{1,0:T(8,128)(2,1)S(1)}, u32[]{:S(2)}, u32[]{:S(2)}) collective-permute-start(bf16[32,768]{1,0:T(8,128)(2,1)S(1)} %get-tuple-element.162), channel_id=1, source_target_pairs={{0,1},{1,0},{2,3},{3,2},{4,5},{5,4},{6,7},{7,6},{8,9},{9,8},{10,11... | collective-permute-start | bytes 147464 | tf_op jit(solution)/shard_map/ppermute | solution.py:485
  133.5 4.4 %collective-permute-start.35 = (bf16[32,768]{1,0:T(8,128)(2,1)S(1)}, bf16[32,768]{1,0:T(8,128)(2,1)S(1)}, u32[]{:S(2)}, u32[]{:S(2)}) collective-permute-start(bf16[32,768]{1,0:T(8,128)(2,1)S(1)} %get-tuple-element.163), channel_id=1, source_target_pairs={{0,2},{1,3},{2,0},{3,1},{4,6},{5,7},{6,4},{7,5},{8,10},{9,11},{10,... | collective-permute-start | bytes 147464 | tf_op jit(solution)/shard_map/ppermute | solution.py:485
  134.4 3.9 %collective-permute-start.36 = (bf16[32,768]{1,0:T(8,128)(2,1)S(1)}, bf16[32,768]{1,0:T(8,128)(2,1)S(1)}, u32[]{:S(2)}, u32[]{:S(2)}) collective-permute-start(bf16[32,768]{1,0:T(8,128)(2,1)S(1)} %get-tuple-element.164), channel_id=1, source_target_pairs={{0,3},{1,2},{2,1},{3,0},{4,7},{5,6},{6,5},{7,4},{8,11},{9,10},{10,... | collective-permute-start | bytes 147464 | tf_op jit(solution)/shard_map/ppermute | solution.py:485
  136.4 5.1 %copy-start.12 = (f32[24]{0:T(128)}, f32[24]{0:T(128)S(1)}, u32[]{:S(2)}) copy-start(f32[24]{0:T(128)S(1)} %get-tuple-element.243) | copy-start | bytes 292
  138.3 2.2 %copy-start.3 = (bf16[128,768]{1,0:T(8,128)(2,1)S(1)}, bf16[128,768]{1,0:T(8,128)(2,1)}, u32[]{:S(2)}) copy-start(bf16[128,768]{1,0:T(8,128)(2,1)} %refs_5_.1) | copy-start | bytes 589828
  (6 other events, 4.8 us)
